TPU v7x, 128 devices: a whole 4x4x4 slice. The times are simulated.
128 devices in a mesh: band: 4 (over x), dom: 32 (over y, z, core).
Axes of the slice: x: 4, y: 4, z: 4, core: 2. Of those that a mesh axis runs over, the one named last changes fastest.
Arguments:
- grid_vars: bfloat16 [65536, 227], P(('band', 'dom')), may hold values from -6 to 6
- cotangent: bfloat16 [65536, 227], P(('band', 'dom')), may hold values from -0.011962891 to 0.011962891
- mesh_static: bfloat16 [32768, 512], P(('band', 'dom')), may hold values from -6 to 6
- embed_weight: bfloat16 [227, 512], replicated, may hold values from -0.375 to 0.375
- encode_weight: bfloat16 [512, 512], replicated, may hold values from -0.25 to 0.25
- self_weight: bfloat16 [2, 512, 512], replicated, may hold values from -0.25 to 0.25
- neighbor_weight: bfloat16 [2, 512, 512], replicated, may hold values from -0.25 to 0.25
- decode_weight: bfloat16 [512, 512], replicated, may hold values from -0.25 to 0.25
- output_weight: bfloat16 [512, 227], replicated, may hold values from -0.25 to 0.25
- grid_sender: int32 [491520], P(('band', 'dom')), may hold values from 0 to 511
- mesh_receiver: int32 [491520], P(('band', 'dom')), may hold values from 0 to 256, as said below
- neighbors: int32 [32768, 6], P(('band', 'dom')), may hold values from 0 to 383, as said below
- mesh_sender: int32 [491520], P(('band', 'dom')), may hold values from 0 to 255
- grid_receiver: int32 [491520], P(('band', 'dom')), may hold values from 0 to 512, as said below
Outputs:
- prediction: bfloat16 [65536, 227], P(('band', 'dom'))
- grad_static: float32 [32768, 512], P(('band', 'dom'))
- grad_embed: float32 [227, 512], replicated
- grad_encode: float32 [512, 512], replicated
- grad_self: float32 [2, 512, 512], replicated
- grad_neighbor: float32 [2, 512, 512], replicated
- grad_decode: float32 [512, 512], replicated
- grad_output: float32 [512, 227], replicated
Inputs may be any that keep to these rules, and one draw needn't show every extreme that they name: `mesh_receiver`: each device's receiving slots are present with a share that differs from device to device; 256 marks an absent edge. Slots whose sending device would lie outside the bands are absent. `grid_receiver`: each device's receiving slots are present with a share that differs from device to device; 512 marks an absent edge. Slots whose sending device would lie outside the bands are absent. `neighbors`: local row i of a partition has neighbours among extended rows i to i + 128.
All inputs are finite; a program needn't handle non-finite values.
Results may differ from a plain program's by a relative error of at most 0.025.
Values may be sent and summed in bfloat16 or wider, within the bound.
No kernel may reach another device: no remote copies, remote signals or barrier semaphores. Data moves between devices by JAX's collectives and lax.ppermute only.
A program may use at most 64 MiB of HBM per device.

v0:
```python
import jax
import jax.numpy as jnp
from jax import lax
from jax.sharding import PartitionSpec as P

LAYERS = 2
NEAR = 6
RIM = 64


def shifted(block, axis, distance):
    devices = range(lax.axis_size(axis))
    route = [((i - distance) % len(devices), i) for i in devices]
    return lax.ppermute(block, axis, route)


def shifted_2(value, axis, steps):
    count = lax.axis_size(axis)
    first, last = (max(0, -steps), min(count, count - steps))
    return lax.ppermute(value, axis, [(source, source + steps) for source in range(first, last)])


def extended_2(cells, sides, width):
    for axis, dim in sides:
        count = lax.axis_size(axis)
        head = lax.slice_in_dim(cells, 0, width, axis=dim)
        tail = lax.slice_in_dim(cells, cells.shape[dim] - width, cells.shape[dim], axis=dim)
        cells = jnp.concatenate(
            [
                lax.ppermute(tail, axis, [(i, (i + 1) % count) for i in range(count)]),
                cells,
                lax.ppermute(head, axis, [((i + 1) % count, i) for i in range(count)]),
            ],
            axis=dim,
        )
    return cells


def silu_slope(values):
    sigma = jax.nn.sigmoid(values)
    return sigma * (1.0 + values * (1.0 - sigma))


def matmul(left, right):
    return jnp.dot(left, right, preferred_element_type=jnp.float32)


def outer_sum(left, right):
    return lax.dot_general(
        left, right, (((0,), (0,)), ((), ())), preferred_element_type=jnp.float32
    )


def back_mul(left, right):
    return lax.dot_general(
        left, right, (((1,), (1,)), ((), ())), preferred_element_type=jnp.float32
    )


def select_rows(table, index):
    picks = (index[:, None] == jnp.arange(table.shape[0], dtype=jnp.int32)[None, :]).astype(
        table.dtype
    )
    return matmul(picks, table).astype(table.dtype)


def collect_rows(values, receivers, count):
    picks = (jnp.arange(count, dtype=jnp.int32)[:, None] == receivers[None, :]).astype(values.dtype)
    return matmul(picks, values)


def neighbor_counts(neighbors, width):
    columns = jnp.arange(width, dtype=jnp.int32)[None, :]
    counts = jnp.zeros((neighbors.shape[0], width), jnp.float32)
    for column in range(NEAR):
        counts = counts + (neighbors[:, column][:, None] == columns).astype(jnp.float32)
    return counts


def relay_rows(edge_rows, sign):
    groups = edge_rows.reshape(5, -1, edge_rows.shape[1])
    east = shifted(groups[1], "dom", sign)
    west = shifted(groups[2], "dom", -sign)
    north = shifted_2(groups[3], "band", sign)
    south = shifted_2(groups[4], "band", -sign)
    moved = jnp.stack([groups[0], east, west, north, south])
    return moved.reshape(edge_rows.shape)


def shards(
    grid_vars,
    cotangent,
    mesh_static,
    embed_weight,
    encode_weight,
    self_weight,
    neighbor_weight,
    decode_weight,
    output_weight,
    grid_sender,
    mesh_receiver,
    neighbors,
    mesh_sender,
    grid_receiver,
):
    grid_count = grid_vars.shape[0]
    mesh_count = mesh_static.shape[0]
    rim_rows = RIM
    counts = neighbor_counts(neighbors, mesh_count + 2 * rim_rows)
    counts_half = counts.astype(jnp.bfloat16)
    embed_pre = matmul(grid_vars, embed_weight)
    latent = jax.nn.silu(embed_pre).astype(jnp.bfloat16)
    arrived = relay_rows(select_rows(latent, grid_sender), 1)
    encode_in = collect_rows(arrived, mesh_receiver, mesh_count).astype(jnp.bfloat16)
    encode_pre = matmul(encode_in, encode_weight)
    state = mesh_static.astype(jnp.float32) + jax.nn.silu(encode_pre)
    saved = []
    for layer_index in range(LAYERS):
        state_half = state.astype(jnp.bfloat16)
        extended = extended_2(state_half, (("dom", 0),), RIM)
        nearby_half = (matmul(counts_half, extended) * (1.0 / NEAR)).astype(jnp.bfloat16)
        layer_pre = matmul(state_half, self_weight[layer_index]) + matmul(
            nearby_half, neighbor_weight[layer_index]
        )
        saved.append((state_half, nearby_half, layer_pre))
        state = state + jax.nn.silu(layer_pre)
    final_half = state.astype(jnp.bfloat16)
    arrived = relay_rows(select_rows(final_half, mesh_sender), 1)
    decode_in = collect_rows(arrived, grid_receiver, grid_count).astype(jnp.bfloat16)
    decode_pre = matmul(decode_in, decode_weight)
    hidden = jax.nn.silu(decode_pre).astype(jnp.bfloat16)
    prediction = (grid_vars.astype(jnp.float32) + matmul(hidden, output_weight)).astype(
        jnp.bfloat16
    )
    grad_output = outer_sum(hidden, cotangent)
    hidden_grad = back_mul(cotangent, output_weight)
    decode_grad = (hidden_grad * silu_slope(decode_pre)).astype(jnp.bfloat16)
    grad_decode = outer_sum(decode_in, decode_grad)
    decode_in_grad = back_mul(decode_grad, decode_weight).astype(jnp.bfloat16)
    returned = relay_rows(select_rows(decode_in_grad, grid_receiver), -1)
    state_grad = collect_rows(returned, mesh_sender, mesh_count)
    self_list = []
    near_list = []
    for layer_index in range(LAYERS - 1, -1, -1):
        state_half, nearby_half, layer_pre = saved[layer_index]
        layer_grad = (state_grad * silu_slope(layer_pre)).astype(jnp.bfloat16)
        self_list.append(outer_sum(state_half, layer_grad))
        near_list.append(outer_sum(nearby_half, layer_grad))
        own_grad = back_mul(layer_grad, self_weight[layer_index])
        near_grad = back_mul(layer_grad, neighbor_weight[layer_index]) * (1.0 / NEAR)
        extended_grad = lax.dot_general(
            counts,
            near_grad,
            (((0,), (0,)), ((), ())),
            precision=lax.Precision.HIGHEST,
            preferred_element_type=jnp.float32,
        )
        upper_rim = extended_grad[:rim_rows]
        lower_rim = extended_grad[rim_rows + mesh_count :]
        from_next = shifted(upper_rim, "dom", -1)
        from_prev = shifted(lower_rim, "dom", 1)
        spread_grad = extended_grad[rim_rows : rim_rows + mesh_count]
        spread_grad = spread_grad.at[:rim_rows].add(from_prev)
        spread_grad = spread_grad.at[mesh_count - rim_rows :].add(from_next)
        state_grad = state_grad + own_grad + spread_grad
    encode_grad = (state_grad * silu_slope(encode_pre)).astype(jnp.bfloat16)
    grad_encode = outer_sum(encode_in, encode_grad)
    encode_in_grad = back_mul(encode_grad, encode_weight).astype(jnp.bfloat16)
    returned = relay_rows(select_rows(encode_in_grad, mesh_receiver), -1)
    latent_grad = collect_rows(returned, grid_sender, grid_count)
    embed_grad = (latent_grad * silu_slope(embed_pre)).astype(jnp.bfloat16)
    grad_embed = outer_sum(grid_vars, embed_grad)
    grad_self = jnp.stack(self_list[::-1])
    grad_neighbor = jnp.stack(near_list[::-1])
    grad_embed, grad_encode, grad_self, grad_neighbor, grad_decode, grad_output = lax.psum(
        (grad_embed, grad_encode, grad_self, grad_neighbor, grad_decode, grad_output),
        ("band", "dom"),
    )
    return (
        prediction,
        state_grad,
        grad_embed,
        grad_encode,
        grad_self,
        grad_neighbor,
        grad_decode,
        grad_output,
    )


def solution(mesh):
    placed = (
        P(("band", "dom"), None),
        P(("band", "dom"), None),
        P(("band", "dom"), None),
        P(),
        P(),
        P(),
        P(),
        P(),
        P(),
        P(("band", "dom")),
        P(("band", "dom")),
        P(("band", "dom"), None),
        P(("band", "dom")),
        P(("band", "dom")),
    )
    return jax.shard_map(
        shards,
        mesh=mesh,
        in_specs=placed,
        out_specs=(
            P(("band", "dom"), None),
            P(("band", "dom"), None),
            P(),
            P(),
            P(),
            P(),
            P(),
            P(),
        ),
        check_vma=False,
    )
```

profile of v0, /device:TPU:1, one launch (start us, length us, event | category | flops | bytes accessed | tf_op | source)
XLA Modules:
  0.0 372.2 jit_solution(12686846474547495305)
XLA Ops:
  7.2 1.4 fusion.102
  8.7 3.7 fusion.5
  12.6 3.1 collective-permute-start
  15.7 3.2 collective-permute-start.2
  18.9 1.3 collective-permute-start.3
  20.3 4.4 %collective-permute-done = bf16[768,512]{1,0:T(8,128)(2,1)S(1)} collective-permute-done((bf16[768,512]{1,0:T(8,128)(2,1)S(1)}, bf16[768,512]{1,0:T(8,128)(2,1)S(1)}, u32[]{:S(2)}, u32[]{:S(2)}) %collective-permute-start) | collective-permute-done | bytes 786464 | tf_op jit(solution)/shard_map/ppermute | solution.py:14
  24.7 2.7 collective-permute-done.1
  27.5 3.7 collective-permute-done.2
  31.3 3.8 %collective-permute-done.3 = bf16[768,512]{1,0:T(8,128)(2,1)S(1)} collective-permute-done((bf16[768,512]{1,0:T(8,128)(2,1)S(1)}, bf16[768,512]{1,0:T(8,128)(2,1)S(1)}, u32[]{:S(2)}, u32[]{:S(2)}) %collective-permute-start.3) | collective-permute-done | bytes 786464 | tf_op jit(solution)/shard_map/ppermute | solution.py:20
  35.2 1.2 fusion.22
  36.9 5.7 %collective-permute-start.5 = (bf16[64,512]{1,0:T(8,128)(2,1)S(1)}, bf16[64,512]{1,0:T(8,128)(2,1)S(1)}, u32[]{:S(2)}, u32[]{:S(2)}) collective-permute-start(bf16[64,512]{1,0:T(8,128)(2,1)S(1)} %get-tuple-element.87), channel_id=1, source_target_pairs={{1,0},{2,1},{3,2},{4,3},{5,4},{6,5},{7,6},{8,7},{9,8},{10,9},{11,1... | collective-permute-start | bytes 196616 | tf_op jit(solution)/shard_map/ppermute | solution.py:32
  42.6 1.6 collective-permute-start.4
  44.5 1.6 collective-permute-done.5
  46.6 1.2 fusion.92
  47.8 5.9 %collective-permute-start.7 = (bf16[64,512]{1,0:T(8,128)(2,1)S(1)}, bf16[64,512]{1,0:T(8,128)(2,1)S(1)}, u32[]{:S(2)}, u32[]{:S(2)}) collective-permute-start(bf16[64,512]{1,0:T(8,128)(2,1)S(1)} %get-tuple-element.85), channel_id=1, source_target_pairs={{1,0},{2,1},{3,2},{4,3},{5,4},{6,5},{7,6},{8,7},{9,8},{10,9},{11,1... | collective-permute-start | bytes 196616 | tf_op jit(solution)/shard_map/ppermute | solution.py:32
  55.9 2.0 convolution_convert_fusion.1
  58.2 2.4 collective-permute-start.8
  60.6 3.5 collective-permute-start.9
  64.1 3.1 collective-permute-start.10
  67.2 1.5 collective-permute-start.11
  69.6 2.7 collective-permute-done.9
  72.4 6.6 %collective-permute-done.10 = bf16[768,512]{1,0:T(8,128)(2,1)S(1)} collective-permute-done((bf16[768,512]{1,0:T(8,128)(2,1)S(1)}, bf16[768,512]{1,0:T(8,128)(2,1)S(1)}, u32[]{:S(2)}, u32[]{:S(2)}) %collective-permute-start.10) | collective-permute-done | bytes 786464 | tf_op jit(solution)/shard_map/ppermute | solution.py:20
  79.1 3.8 %collective-permute-done.11 = bf16[768,512]{1,0:T(8,128)(2,1)S(1)} collective-permute-done((bf16[768,512]{1,0:T(8,128)(2,1)S(1)}, bf16[768,512]{1,0:T(8,128)(2,1)S(1)}, u32[]{:S(2)}, u32[]{:S(2)}) %collective-permute-start.11) | collective-permute-done | bytes 786464 | tf_op jit(solution)/shard_map/ppermute | solution.py:20
  83.0 2.2 fusion.17
  85.2 0.8 copy-done.15
  87.0 1.3 fusion.18
  88.3 5.9 %fusion.4 = bf16[3840,512]{1,0:T(8,128)(2,1)} fusion(s32[3840]{0:T(1024)S(1)} %copy-done.30, bf16[512,512]{1,0:T(8,128)(2,1)} %fusion.18, bf16[512,512]{1,0:T(8,128)(2,1)S(1)} %copy-done), kind=kOutput, calls=%fused_computation.8 | convolution fusion | flops 2285895680 | bytes 4996096 | tf_op jit(solution)/shard_map/dot_general | solution.py:45
  94.3 2.1 fusion.94
  96.4 6.3 %collective-permute-start.12 = (bf16[768,512]{1,0:T(8,128)(2,1)S(1)}, bf16[768,512]{1,0:T(8,128)(2,1)S(1)}, u32[]{:S(2)}, u32[]{:S(2)}) collective-permute-start(bf16[768,512]{1,0:T(8,128)(2,1)S(1)} %get-tuple-element.71), channel_id=1, source_target_pairs={{1,0},{2,1},{3,2},{4,3},{5,4},{6,5},{7,6},{8,7},{9,8},{10,9},{11,1... | collective-permute-start | bytes 2359304 | tf_op jit(solution)/shard_map/ppermute | solution.py:14
  102.7 1.5 fusion.104
  104.1 1.3 collective-permute-start.14
  105.4 1.2 fusion.31
  106.6 4.0 %collective-permute-start.15 = (bf16[768,512]{1,0:T(8,128)(2,1)S(1)}, bf16[768,512]{1,0:T(8,128)(2,1)S(1)}, u32[]{:S(2)}, u32[]{:S(2)}) collective-permute-start(bf16[768,512]{1,0:T(8,128)(2,1)S(1)} %get-tuple-element.68), channel_id=1, source_target_pairs={{0,32},{32,64},{64,96},{1,33},{33,65},{65,97},{2,34},{34,66},{66,9... | collective-permute-start | bytes 2359304 | tf_op jit(solution)/shard_map/ppermute | solution.py:20
  110.7 1.1 fusion.105
  111.9 12.8 %collective-permute-done.14 = bf16[768,512]{1,0:T(8,128)(2,1)S(1)} collective-permute-done((bf16[768,512]{1,0:T(8,128)(2,1)S(1)}, bf16[768,512]{1,0:T(8,128)(2,1)S(1)}, u32[]{:S(2)}, u32[]{:S(2)}) %collective-permute-start.14) | collective-permute-done | bytes 786464 | tf_op jit(solution)/shard_map/ppermute | solution.py:20
  124.7 2.0 collective-permute-done.15
  126.7 1.2 multiply_convert_fusion.5
  128.4 1.1 fusion.65
  130.0 2.0 collective-permute-start.17
  132.5 2.2 collective-permute-done.17
  135.5 1.1 fusion.64
  136.8 4.8 %collective-permute-start.19 = (f32[64,512]{1,0:T(8,128)S(1)}, f32[64,512]{1,0:T(8,128)S(1)}, u32[]{:S(2)}, u32[]{:S(2)}) collective-permute-start(f32[64,512]{1,0:T(8,128)S(1)} %get-tuple-element.80), channel_id=1, source_target_pairs={{1,0},{2,1},{3,2},{4,3},{5,4},{6,5},{7,6},{8,7},{9,8},{10,9},{11,1... | collective-permute-start | bytes 393224 | tf_op jit(solution)/shard_map/ppermute | solution.py:14
  141.6 1.3 convolution_bitcast_fusion.3
  143.0 1.2 multiply_convert_fusion.3
  144.2 4.8 %convolution_convert_fusion = bf16[3840,512]{1,0:T(8,128)(2,1)} fusion(s32[3840]{0:T(1024)S(1)} %copy-done.27, bf16[256,512]{1,0:T(8,128)(2,1)S(1)} %get-tuple-element.103, bf16[512,512]{1,0:T(8,128)(2,1)} %param.26), kind=kOutput, calls=%fused_computation.10 | convolution fusion | flops 1143930880 | bytes 4733952 | tf_op jit(solution)/shard_map/dot_general | solution.py:45
  149.0 2.1 fusion.93
  151.1 6.4 %collective-permute-start.20 = (bf16[768,512]{1,0:T(8,128)(2,1)S(1)}, bf16[768,512]{1,0:T(8,128)(2,1)S(1)}, u32[]{:S(2)}, u32[]{:S(2)}) collective-permute-start(bf16[768,512]{1,0:T(8,128)(2,1)S(1)} %get-tuple-element.67), channel_id=1, source_target_pairs={{1,0},{2,1},{3,2},{4,3},{5,4},{6,5},{7,6},{8,7},{9,8},{10,9},{11,1... | collective-permute-start | bytes 2359304 | tf_op jit(solution)/shard_map/ppermute | solution.py:14
  157.9 2.5 pad_maximum_fusion
  160.4 1.3 collective-permute-start.22
  161.6 4.8 %collective-permute-start.23 = (bf16[768,512]{1,0:T(8,128)(2,1)S(1)}, bf16[768,512]{1,0:T(8,128)(2,1)S(1)}, u32[]{:S(2)}, u32[]{:S(2)}) collective-permute-start(bf16[768,512]{1,0:T(8,128)(2,1)S(1)} %get-tuple-element.64), channel_id=1, source_target_pairs={{0,32},{32,64},{64,96},{1,33},{33,65},{65,97},{2,34},{34,66},{66,9... | collective-permute-start | bytes 2359304 | tf_op jit(solution)/shard_map/ppermute | solution.py:20
  166.4 1.2 fusion.30
  167.7 1.3 fusion.103
  169.3 7.9 %collective-permute-done.22 = bf16[768,512]{1,0:T(8,128)(2,1)S(1)} collective-permute-done((bf16[768,512]{1,0:T(8,128)(2,1)S(1)}, bf16[768,512]{1,0:T(8,128)(2,1)S(1)}, u32[]{:S(2)}, u32[]{:S(2)}) %collective-permute-start.22) | collective-permute-done | bytes 786464 | tf_op jit(solution)/shard_map/ppermute | solution.py:20
  177.3 0.8 collective-permute-done.23
  178.2 1.9 copy-done.26
  180.1 5.5 %convolution_bitcast_fusion.4 = f32[227,512]{1,0:T(8,128)} fusion(bf16[512,227]{0,1:T(8,128)(2,1)S(1)} %copy-done.13, bf16[3840,512]{1,0:T(8,128)(2,1)} %bitcast.138, s32[3840]{0:T(1024)S(1)} %copy-done.32, f32[512,512]{1,0:T(8,128)S(1)} %copy-done.7), kind=kOutput, calls=%fused_computation.48 | convolution fusion | flops 2136604672 | bytes 5693440 | tf_op jit(solution)/shard_map/dot_general | solution.py:49
  185.6 0.9 copy-done.25
  186.5 1.0 fusion.25
  187.6 167.3 %all-reduce.3.cloned.1.call-done = (f32[227,512]{1,0:T(8,128)}, f32[512,512]{1,0:T(8,128)}, f32[2,512,512]{2,1,0:T(8,128)}, f32[2,512,512]{2,1,0:T(8,128)}, f32[512,512]{1,0:T(8,128)}, /*index=5*/f32[512,227]{0,1:T(8,128)}) async-done(((f32[227,512]{1,0:T(8,128)}, f32[512,512]{1,0:T(8,128)}, f32[2,512,512]{2,1,0:T(8,128)}, f32[2,512,512]{2,1,0:T(8,128)}, f32[512,512]{1,0:T(8,128)}, ...) | async-done | bytes 7221264 | tf_op jit(solution)/shard_map/psum | solution.py:175
  354.9 2.0 copy.48
  356.8 2.3 copy.49
  359.1 3.2 copy.50
  362.3 1.3 copy.51
  363.6 1.0 copy.52
  (133 shorter events, 10.5 us)
Async XLA Ops:
  7.2 78.8 %copy-start = (bf16[512,512]{1,0:T(8,128)(2,1)S(1)}, bf16[512,512]{1,0:T(8,128)(2,1)}, u32[]{:S(2)}) copy-start(bf16[512,512]{1,0:T(8,128)(2,1)} %param.29) | copy-start | bytes 1572868
  7.2 347.7 %all-reduce.3.cloned.1.call-start = ((), (), s32[]{:S(2)}) async-start(), calls=%async_computation | async-start | bytes 14483456 | tf_op jit(solution)/shard_map/psum | solution.py:175
  8.7 3.7 %copy-start.6 = (f32[512,512]{1,0:T(8,128)}, f32[512,512]{1,0:T(8,128)S(1)}, u32[]{:S(2)}) copy-start(f32[512,512]{1,0:T(8,128)S(1)} %fusion.102) | copy-start | bytes 3145732
  12.4 7.8 %copy-start.28 = (s32[256,6]{0,1:T(8,128)S(1)}, s32[256,6]{0,1:T(8,128)}, u32[]{:S(2)}) copy-start(s32[256,6]{0,1:T(8,128)} %param.33) | copy-start | bytes 18436
  12.6 12.0 %collective-permute-start = (bf16[768,512]{1,0:T(8,128)(2,1)S(1)}, bf16[768,512]{1,0:T(8,128)(2,1)S(1)}, u32[]{:S(2)}, u32[]{:S(2)}) collective-permute-start(bf16[768,512]{1,0:T(8,128)(2,1)S(1)} %get-tuple-element.79), channel_id=1, source_target_pairs={{31,0},{0,1},{1,2},{2,3},{3,4},{4,5},{5,6},{6,7},{7,8},{8,9},{9,10... | collective-permute-start | bytes 2359304 | tf_op jit(solution)/shard_map/ppermute | solution.py:14
  15.7 11.7 %collective-permute-start.1 = (bf16[768,512]{1,0:T(8,128)(2,1)S(1)}, bf16[768,512]{1,0:T(8,128)(2,1)S(1)}, u32[]{:S(2)}, u32[]{:S(2)}) collective-permute-start(bf16[768,512]{1,0:T(8,128)(2,1)S(1)} %get-tuple-element.78), channel_id=1, source_target_pairs={{1,0},{2,1},{3,2},{4,3},{5,4},{6,5},{7,6},{8,7},{9,8},{10,9},{11,1... | collective-permute-start | bytes 2359304 | tf_op jit(solution)/shard_map/ppermute | solution.py:14
  15.7 15.5 %collective-permute-start.2 = (bf16[768,512]{1,0:T(8,128)(2,1)S(1)}, bf16[768,512]{1,0:T(8,128)(2,1)S(1)}, u32[]{:S(2)}, u32[]{:S(2)}) collective-permute-start(bf16[768,512]{1,0:T(8,128)(2,1)S(1)} %get-tuple-element.77), channel_id=1, source_target_pairs={{0,32},{32,64},{64,96},{1,33},{33,65},{65,97},{2,34},{34,66},{66,9... | collective-permute-start | bytes 2359304 | tf_op jit(solution)/shard_map/ppermute | solution.py:20
  18.9 16.2 %collective-permute-start.3 = (bf16[768,512]{1,0:T(8,128)(2,1)S(1)}, bf16[768,512]{1,0:T(8,128)(2,1)S(1)}, u32[]{:S(2)}, u32[]{:S(2)}) collective-permute-start(bf16[768,512]{1,0:T(8,128)(2,1)S(1)} %get-tuple-element.76), channel_id=1, source_target_pairs={{32,0},{64,32},{96,64},{33,1},{65,33},{97,65},{34,2},{66,34},{98,6... | collective-permute-start | bytes 2359304 | tf_op jit(solution)/shard_map/ppermute | solution.py:20
  20.2 14.9 %copy-start.27 = (s32[3840]{0:T(1024)S(1)}, s32[3840]{0:T(1024)}, u32[]{:S(2)}) copy-start(s32[3840]{0:T(1024)} %param.32) | copy-start | bytes 46084
  35.1 1.2 copy-start.14
  35.2 1.2 copy-start.29
  35.2 9.0 %copy-start.8 = (bf16[2,512,512]{2,1,0:T(8,128)(2,1)S(1)}, bf16[2,512,512]{2,1,0:T(8,128)(2,1)}, u32[]{:S(2)}) copy-start(bf16[2,512,512]{2,1,0:T(8,128)(2,1)} %param.27) | copy-start | bytes 3145732
  36.4 11.4 %copy-start.19 = (bf16[256,512]{1,0:T(8,128)(2,1)}, bf16[256,512]{1,0:T(8,128)(2,1)S(1)}, u32[]{:S(2)}) copy-start(bf16[256,512]{1,0:T(8,128)(2,1)S(1)} %fusion.22) | copy-start | bytes 786436
  36.4 10.2 %copy-start.3 = (bf16[2,512,512]{2,1,0:T(8,128)(2,1)S(1)}, bf16[2,512,512]{2,1,0:T(8,128)(2,1)}, u32[]{:S(2)}) copy-start(bf16[2,512,512]{2,1,0:T(8,128)(2,1)} %param.28) | copy-start | bytes 3145732
  36.8 11.0 %copy-start.33 = (f32[256,512]{1,0:T(8,128)}, f32[256,512]{1,0:T(8,128)S(1)}, u32[]{:S(2)}) copy-start(f32[256,512]{1,0:T(8,128)S(1)} %get-tuple-element.95) | copy-start | bytes 1572868
  36.9 9.2 %collective-permute-start.5 = (bf16[64,512]{1,0:T(8,128)(2,1)S(1)}, bf16[64,512]{1,0:T(8,128)(2,1)S(1)}, u32[]{:S(2)}, u32[]{:S(2)}) collective-permute-start(bf16[64,512]{1,0:T(8,128)(2,1)S(1)} %get-tuple-element.87), channel_id=1, source_target_pairs={{1,0},{2,1},{3,2},{4,3},{5,4},{6,5},{7,6},{8,7},{9,8},{10,9},{11,1... | collective-permute-start | bytes 196616 | tf_op jit(solution)/shard_map/ppermute | solution.py:32
  42.6 3.5 collective-permute-start.4
  46.6 9.0 %copy-start.21 = (bf16[256,512]{1,0:T(8,128)(2,1)}, bf16[256,512]{1,0:T(8,128)(2,1)S(1)}, u32[]{:S(2)}) copy-start(bf16[256,512]{1,0:T(8,128)(2,1)S(1)} %fusion.23) | copy-start | bytes 786436
  47.8 8.1 %copy-start.31 = (s32[3840]{0:T(1024)S(1)}, s32[3840]{0:T(1024)}, u32[]{:S(2)}) copy-start(s32[3840]{0:T(1024)} %param.34) | copy-start | bytes 46084
  47.8 6.8 %collective-permute-start.7 = (bf16[64,512]{1,0:T(8,128)(2,1)S(1)}, bf16[64,512]{1,0:T(8,128)(2,1)S(1)}, u32[]{:S(2)}, u32[]{:S(2)}) collective-permute-start(bf16[64,512]{1,0:T(8,128)(2,1)S(1)} %get-tuple-element.85), channel_id=1, source_target_pairs={{1,0},{2,1},{3,2},{4,3},{5,4},{6,5},{7,6},{8,7},{9,8},{10,9},{11,1... | collective-permute-start | bytes 196616 | tf_op jit(solution)/shard_map/ppermute | solution.py:32
  53.7 1.3 collective-permute-start.6
  55.6 2.4 copy-start.11
  58.2 11.4 %collective-permute-start.8 = (bf16[768,512]{1,0:T(8,128)(2,1)S(1)}, bf16[768,512]{1,0:T(8,128)(2,1)S(1)}, u32[]{:S(2)}, u32[]{:S(2)}) collective-permute-start(bf16[768,512]{1,0:T(8,128)(2,1)S(1)} %get-tuple-element.75), channel_id=1, source_target_pairs={{31,0},{0,1},{1,2},{2,3},{3,4},{4,5},{5,6},{6,7},{7,8},{8,9},{9,10... | collective-permute-start | bytes 2359304 | tf_op jit(solution)/shard_map/ppermute | solution.py:14
  60.6 11.7 %collective-permute-start.9 = (bf16[768,512]{1,0:T(8,128)(2,1)S(1)}, bf16[768,512]{1,0:T(8,128)(2,1)S(1)}, u32[]{:S(2)}, u32[]{:S(2)}) collective-permute-start(bf16[768,512]{1,0:T(8,128)(2,1)S(1)} %get-tuple-element.74), channel_id=1, source_target_pairs={{1,0},{2,1},{3,2},{4,3},{5,4},{6,5},{7,6},{8,7},{9,8},{10,9},{11,1... | collective-permute-start | bytes 2359304 | tf_op jit(solution)/shard_map/ppermute | solution.py:14
  64.1 14.9 %collective-permute-start.10 = (bf16[768,512]{1,0:T(8,128)(2,1)S(1)}, bf16[768,512]{1,0:T(8,128)(2,1)S(1)}, u32[]{:S(2)}, u32[]{:S(2)}) collective-permute-start(bf16[768,512]{1,0:T(8,128)(2,1)S(1)} %get-tuple-element.73), channel_id=1, source_target_pairs={{0,32},{32,64},{64,96},{1,33},{33,65},{65,97},{2,34},{34,66},{66,9... | collective-permute-start | bytes 2359304 | tf_op jit(solution)/shard_map/ppermute | solution.py:20
  67.2 15.7 %copy-start.30 = (s32[3840]{0:T(1024)S(1)}, s32[3840]{0:T(1024)}, u32[]{:S(2)}) copy-start(s32[3840]{0:T(1024)} %param.35) | copy-start | bytes 46084
  67.2 15.7 %collective-permute-start.11 = (bf16[768,512]{1,0:T(8,128)(2,1)S(1)}, bf16[768,512]{1,0:T(8,128)(2,1)S(1)}, u32[]{:S(2)}, u32[]{:S(2)}) collective-permute-start(bf16[768,512]{1,0:T(8,128)(2,1)S(1)} %get-tuple-element.72), channel_id=1, source_target_pairs={{32,0},{64,32},{96,64},{33,1},{65,33},{97,65},{34,2},{66,34},{98,6... | collective-permute-start | bytes 2359304 | tf_op jit(solution)/shard_map/ppermute | solution.py:20
  85.2 0.8 copy-start.15
  86.0 0.9 copy-start.23
  86.0 1.1 copy-start.24
  94.2 8.4 %copy-start.16 = (bf16[512,512]{1,0:T(8,128)(2,1)S(1)}, bf16[512,512]{1,0:T(8,128)(2,1)}, u32[]{:S(2)}) copy-start(bf16[512,512]{1,0:T(8,128)(2,1)} %copy-done.15) | copy-start | bytes 1572868
  94.3 8.4 %copy-start.17 = (bf16[512,512]{1,0:T(8,128)(2,1)S(1)}, bf16[512,512]{1,0:T(8,128)(2,1)}, u32[]{:S(2)}) copy-start(bf16[512,512]{1,0:T(8,128)(2,1)} %fusion.18) | copy-start | bytes 1572868
  96.4 15.3 %collective-permute-start.12 = (bf16[768,512]{1,0:T(8,128)(2,1)S(1)}, bf16[768,512]{1,0:T(8,128)(2,1)S(1)}, u32[]{:S(2)}, u32[]{:S(2)}) collective-permute-start(bf16[768,512]{1,0:T(8,128)(2,1)S(1)} %get-tuple-element.71), channel_id=1, source_target_pairs={{1,0},{2,1},{3,2},{4,3},{5,4},{6,5},{7,6},{8,7},{9,8},{10,9},{11,1... | collective-permute-start | bytes 2359304 | tf_op jit(solution)/shard_map/ppermute | solution.py:14
  102.6 9.1 %collective-permute-start.13 = (bf16[768,512]{1,0:T(8,128)(2,1)S(1)}, bf16[768,512]{1,0:T(8,128)(2,1)S(1)}, u32[]{:S(2)}, u32[]{:S(2)}) collective-permute-start(bf16[768,512]{1,0:T(8,128)(2,1)S(1)} %get-tuple-element.70), channel_id=1, source_target_pairs={{31,0},{0,1},{1,2},{2,3},{3,4},{4,5},{5,6},{6,7},{7,8},{8,9},{9,10... | collective-permute-start | bytes 2359304 | tf_op jit(solution)/shard_map/ppermute | solution.py:14
  104.1 20.5 %collective-permute-start.14 = (bf16[768,512]{1,0:T(8,128)(2,1)S(1)}, bf16[768,512]{1,0:T(8,128)(2,1)S(1)}, u32[]{:S(2)}, u32[]{:S(2)}) collective-permute-start(bf16[768,512]{1,0:T(8,128)(2,1)S(1)} %get-tuple-element.69), channel_id=1, source_target_pairs={{32,0},{64,32},{96,64},{33,1},{65,33},{97,65},{34,2},{66,34},{98,6... | collective-permute-start | bytes 2359304 | tf_op jit(solution)/shard_map/ppermute | solution.py:20
  106.6 20.1 %collective-permute-start.15 = (bf16[768,512]{1,0:T(8,128)(2,1)S(1)}, bf16[768,512]{1,0:T(8,128)(2,1)S(1)}, u32[]{:S(2)}, u32[]{:S(2)}) collective-permute-start(bf16[768,512]{1,0:T(8,128)(2,1)S(1)} %get-tuple-element.68), channel_id=1, source_target_pairs={{0,32},{32,64},{64,96},{1,33},{33,65},{65,97},{2,34},{34,66},{66,9... | collective-permute-start | bytes 2359304 | tf_op jit(solution)/shard_map/ppermute | solution.py:20
  128.0 4.0 %copy-start.12 = (bf16[256,512]{1,0:T(8,128)(2,1)S(1)}, bf16[256,512]{1,0:T(8,128)(2,1)}, u32[]{:S(2)}) copy-start(bf16[256,512]{1,0:T(8,128)(2,1)} %copy-done.11) | copy-start | bytes 786436
  128.0 6.7 %copy-start.9 = (bf16[2,512,512]{2,1,0:T(8,128)(2,1)S(1)}, bf16[2,512,512]{2,1,0:T(8,128)(2,1)}, u32[]{:S(2)}) copy-start(bf16[2,512,512]{2,1,0:T(8,128)(2,1)} %param.27) | copy-start | bytes 3145732
  128.0 6.7 %copy-start.35 = (f32[256,512]{1,0:T(8,128)S(1)}, f32[256,512]{1,0:T(8,128)}, u32[]{:S(2)}) copy-start(f32[256,512]{1,0:T(8,128)} %get-tuple-element.96) | copy-start | bytes 1572868
  129.6 5.6 %copy-start.4 = (bf16[2,512,512]{2,1,0:T(8,128)(2,1)S(1)}, bf16[2,512,512]{2,1,0:T(8,128)(2,1)}, u32[]{:S(2)}) copy-start(bf16[2,512,512]{2,1,0:T(8,128)(2,1)} %param.28) | copy-start | bytes 3145732
  129.9 2.6 collective-permute-start.16
  130.0 4.7 %collective-permute-start.17 = (f32[64,512]{1,0:T(8,128)S(1)}, f32[64,512]{1,0:T(8,128)S(1)}, u32[]{:S(2)}, u32[]{:S(2)}) collective-permute-start(f32[64,512]{1,0:T(8,128)S(1)} %get-tuple-element.82), channel_id=1, source_target_pairs={{1,0},{2,1},{3,2},{4,3},{5,4},{6,5},{7,6},{8,7},{9,8},{10,9},{11,1... | collective-permute-start | bytes 393224 | tf_op jit(solution)/shard_map/ppermute | solution.py:14
  135.2 7.8 %copy-start.34 = (f32[256,512]{1,0:T(8,128)S(1)}, f32[256,512]{1,0:T(8,128)}, u32[]{:S(2)}) copy-start(f32[256,512]{1,0:T(8,128)} %copy-done.33) | copy-start | bytes 1572868
  136.7 6.2 %collective-permute-start.18 = (f32[64,512]{1,0:T(8,128)S(1)}, f32[64,512]{1,0:T(8,128)S(1)}, u32[]{:S(2)}, u32[]{:S(2)}) collective-permute-start(f32[64,512]{1,0:T(8,128)S(1)} %get-tuple-element.81), channel_id=1, source_target_pairs={{31,0},{0,1},{1,2},{2,3},{3,4},{4,5},{5,6},{6,7},{7,8},{8,9},{9,10... | collective-permute-start | bytes 393224 | tf_op jit(solution)/shard_map/ppermute | solution.py:14
  136.8 6.1 %collective-permute-start.19 = (f32[64,512]{1,0:T(8,128)S(1)}, f32[64,512]{1,0:T(8,128)S(1)}, u32[]{:S(2)}, u32[]{:S(2)}) collective-permute-start(f32[64,512]{1,0:T(8,128)S(1)} %get-tuple-element.80), channel_id=1, source_target_pairs={{1,0},{2,1},{3,2},{4,3},{5,4},{6,5},{7,6},{8,7},{9,8},{10,9},{11,1... | collective-permute-start | bytes 393224 | tf_op jit(solution)/shard_map/ppermute | solution.py:14
  149.0 8.6 %copy-start.22 = (bf16[256,512]{1,0:T(8,128)(2,1)S(1)}, bf16[256,512]{1,0:T(8,128)(2,1)}, u32[]{:S(2)}) copy-start(bf16[256,512]{1,0:T(8,128)(2,1)} %copy-done.21) | copy-start | bytes 786436
  149.0 8.9 %copy-start.2 = (f32[1,512,512]{2,1,0:T(8,128)S(1)}, f32[1,512,512]{2,1,0:T(8,128)}, u32[]{:S(2)}) copy-start(f32[1,512,512]{2,1,0:T(8,128)} %convolution_bitcast_fusion.3) | copy-start | bytes 3145732
  151.1 17.9 %collective-permute-start.20 = (bf16[768,512]{1,0:T(8,128)(2,1)S(1)}, bf16[768,512]{1,0:T(8,128)(2,1)S(1)}, u32[]{:S(2)}, u32[]{:S(2)}) collective-permute-start(bf16[768,512]{1,0:T(8,128)(2,1)S(1)} %get-tuple-element.67), channel_id=1, source_target_pairs={{1,0},{2,1},{3,2},{4,3},{5,4},{6,5},{7,6},{8,7},{9,8},{10,9},{11,1... | collective-permute-start | bytes 2359304 | tf_op jit(solution)/shard_map/ppermute | solution.py:14
  157.9 9.8 %copy-start.20 = (bf16[256,512]{1,0:T(8,128)(2,1)S(1)}, bf16[256,512]{1,0:T(8,128)(2,1)}, u32[]{:S(2)}) copy-start(bf16[256,512]{1,0:T(8,128)(2,1)} %copy-done.19) | copy-start | bytes 786436
  160.3 8.9 %collective-permute-start.21 = (bf16[768,512]{1,0:T(8,128)(2,1)S(1)}, bf16[768,512]{1,0:T(8,128)(2,1)S(1)}, u32[]{:S(2)}, u32[]{:S(2)}) collective-permute-start(bf16[768,512]{1,0:T(8,128)(2,1)S(1)} %get-tuple-element.66), channel_id=1, source_target_pairs={{31,0},{0,1},{1,2},{2,3},{3,4},{4,5},{5,6},{6,7},{7,8},{8,9},{9,10... | collective-permute-start | bytes 2359304 | tf_op jit(solution)/shard_map/ppermute | solution.py:14
  160.4 16.9 %collective-permute-start.22 = (bf16[768,512]{1,0:T(8,128)(2,1)S(1)}, bf16[768,512]{1,0:T(8,128)(2,1)S(1)}, u32[]{:S(2)}, u32[]{:S(2)}) collective-permute-start(bf16[768,512]{1,0:T(8,128)(2,1)S(1)} %get-tuple-element.65), channel_id=1, source_target_pairs={{32,0},{64,32},{96,64},{33,1},{65,33},{97,65},{34,2},{66,34},{98,6... | collective-permute-start | bytes 2359304 | tf_op jit(solution)/shard_map/ppermute | solution.py:20
  161.6 16.5 %collective-permute-start.23 = (bf16[768,512]{1,0:T(8,128)(2,1)S(1)}, bf16[768,512]{1,0:T(8,128)(2,1)S(1)}, u32[]{:S(2)}, u32[]{:S(2)}) collective-permute-start(bf16[768,512]{1,0:T(8,128)(2,1)S(1)} %get-tuple-element.64), channel_id=1, source_target_pairs={{0,32},{32,64},{64,96},{1,33},{33,65},{65,97},{2,34},{34,66},{66,9... | collective-permute-start | bytes 2359304 | tf_op jit(solution)/shard_map/ppermute | solution.py:20
  167.6 12.5 %copy-start.7 = (f32[512,512]{1,0:T(8,128)S(1)}, f32[512,512]{1,0:T(8,128)}, u32[]{:S(2)}) copy-start(f32[512,512]{1,0:T(8,128)} %copy-done.6) | copy-start | bytes 3145732
  167.6 12.5 %copy-start.13 = (bf16[512,227]{0,1:T(8,128)(2,1)S(1)}, bf16[512,227]{0,1:T(8,128)(2,1)}, u32[]{:S(2)}) copy-start(bf16[512,227]{0,1:T(8,128)(2,1)} %param.22) | copy-start | bytes 697348
  167.7 12.5 %copy-start.32 = (s32[3840]{0:T(1024)S(1)}, s32[3840]{0:T(1024)}, u32[]{:S(2)}) copy-start(s32[3840]{0:T(1024)} %param.31) | copy-start | bytes 46084
  178.2 1.9 copy-start.26
  185.6 0.9 copy-start.25
  354.9 7.4 %copy-start.5 = (f32[2,512,512]{2,1,0:T(8,128)S(1)}, f32[2,512,512]{2,1,0:T(8,128)}, u32[]{:S(2)}) copy-start(f32[2,512,512]{2,1,0:T(8,128)} %get-tuple-element.112) | copy-start | bytes 6291460
  359.1 4.5 %copy-start.10 = (f32[512,512]{1,0:T(8,128)S(1)}, f32[512,512]{1,0:T(8,128)}, u32[]{:S(2)}) copy-start(f32[512,512]{1,0:T(8,128)} %get-tuple-element.113) | copy-start | bytes 3145732
  359.1 6.3 %copy-start.1 = (bf16[512,512]{1,0:T(8,128)(2,1)S(1)}, bf16[512,512]{1,0:T(8,128)(2,1)}, u32[]{:S(2)}) copy-start(bf16[512,512]{1,0:T(8,128)(2,1)} %param.29) | copy-start | bytes 1572868
  362.3 2.3 copy-start.18
Sparse Core Ops, SparseCore 0:
  185.8 169.0 all-reduce.2
where the time goes:
time: 373 us; the launch traced here: 372 us
  waiting for transfers between devices  225 us (60%)
  starting transfers between devices  62.3 us (17%)
  matrix products  45.1 us (12%)
  local copies, waits for them, and re-layouts  22.9 us (6%)
  between operations  14.8 us (4%)
    psum x1, waiting for transfers between devices, shards(): lax.psum((grad_embed, grad_encode, grad_self, grad_neighbor, grad_decode,...  167 us
    ppermute x8, waiting for transfers between devices, shifted_2(): lax.ppermute(value, axis, [(source, source + steps) for source in range(f...  41.5 us
    ppermute x12, starting transfers between devices, shifted(): return lax.ppermute(block, axis, route)  28.6 us
    dot_general x17, matrix products, matmul(): return jnp.dot(left, right, preferred_element_type=jnp.float32)  27.6 us
    ppermute x8, starting transfers between devices, shifted_2(): lax.ppermute(value, axis, [(source, source + steps) for source in range(f...  20.4 us
    unnamed x94, local copies, waits for them, and re-layouts  17.8 us
    ppermute x12, waiting for transfers between devices, shifted(): return lax.ppermute(block, axis, route)  13.2 us
    ppermute x2, starting transfers between devices, extended_2(): lax.ppermute(head, axis, [((i + 1) % count, i) for i in range(count)])  11.6 us
  transfers between devices with their start and end apart: 25, of which 19 were waited for; matrix products, arithmetic and copies ran while one was open for 3% of the time, Pallas kernels for 0%

commit v1 on v0

v1 whole, which is shorter than its diff:
```python
import jax
import jax.numpy as jnp
from jax import lax
from jax.sharding import PartitionSpec as P

NEAR = 6
RIM = 64
GROUPS = 5
HALF = jnp.bfloat16
SINGLE = jnp.float32


def silu_slope(values):
    sigma = jax.nn.sigmoid(values)
    return sigma * (1.0 + values * (1.0 - sigma))


def matmul(left, right):
    return jnp.dot(left, right, preferred_element_type=SINGLE)


def outer_sum(left, right):
    return lax.dot_general(
        left, right, (((0,), (0,)), ((), ())), preferred_element_type=SINGLE
    )


def back_mul(left, right):
    return lax.dot_general(
        left, right, (((1,), (1,)), ((), ())), preferred_element_type=SINGLE
    )


def swap_on(value):
    count = lax.axis_size("dom")
    return lax.ppermute(value, "dom", [(i, i ^ 1) for i in range(count)])


def swap_off(value):
    count = lax.axis_size("dom")
    return lax.ppermute(
        value, "dom", [(i, (i + (1 if i % 2 else -1)) % count) for i in range(count)]
    )


def swap_band(value, first):
    count = lax.axis_size("band")
    pairs = []
    for low in range(first, count - 1, 2):
        pairs += [(low, low + 1), (low + 1, low)]
    return lax.ppermute(value, "band", pairs)


def swap_all(on, off, north, south):
    return swap_on(on), swap_off(off), swap_band(north, 0), swap_band(south, 1)


def by_partner(slots, odd_dom, odd_band, incoming):
    flip_dom = odd_dom != incoming
    flip_band = odd_band != incoming
    return [
        slots[0],
        jnp.where(flip_dom, slots[2], slots[1]),
        jnp.where(flip_dom, slots[1], slots[2]),
        jnp.where(flip_band, slots[4], slots[3]),
        jnp.where(flip_band, slots[3], slots[4]),
    ]


def pair_counts(rows, row_count, columns, column_count):
    row_hot = (jnp.arange(row_count, dtype=jnp.int32)[:, None] == rows[None, :]).astype(HALF)
    column_hot = (columns[:, None] == jnp.arange(column_count, dtype=jnp.int32)[None, :]).astype(HALF)
    return matmul(row_hot, column_hot).astype(HALF)


def reduce_all(stacked):
    rows = stacked.shape[0]
    odd = lax.axis_index("dom") % 2
    count = lax.axis_size("dom")
    groups = [list(range(c, count, 2)) for c in range(2)]
    halves = stacked.reshape(2, rows // 2, -1)
    mine = jnp.where(odd == 1, halves[1], halves[0])
    other = jnp.where(odd == 1, halves[0], halves[1])
    part = (mine.astype(SINGLE) + swap_on(other).astype(SINGLE)).astype(HALF)
    pieces = lax.all_to_all(
        part.reshape(count // 2, -1, part.shape[1]), "dom", 0, 0, axis_index_groups=groups
    )
    piece = jnp.sum(pieces.astype(SINGLE), 0).astype(HALF)
    pieces = lax.all_gather(piece, "band", axis=0)
    piece = jnp.sum(pieces.astype(SINGLE), 0).astype(HALF)
    part = lax.all_gather(piece, "dom", axis=0, tiled=True, axis_index_groups=groups)
    other = swap_on(part)
    return jnp.concatenate(
        [jnp.where(odd == 1, other, part), jnp.where(odd == 1, part, other)], 0
    )


def shards(
    grid_vars,
    cotangent,
    mesh_static,
    embed_weight,
    encode_weight,
    self_weight,
    neighbor_weight,
    decode_weight,
    output_weight,
    grid_sender,
    mesh_receiver,
    neighbors,
    mesh_sender,
    grid_receiver,
):
    grid_count, variables = grid_vars.shape
    mesh_count, width = mesh_static.shape
    rim = RIM
    odd_dom = lax.axis_index("dom") % 2 == 1
    odd_band = lax.axis_index("band") % 2 == 1

    def sides_out(first, last):
        return jnp.where(odd_dom, first, last), jnp.where(odd_dom, last, first)

    def sides_in(on, off):
        return jnp.where(odd_dom, on, off), jnp.where(odd_dom, off, on)

    grid_send = by_partner(grid_sender.reshape(GROUPS, -1), odd_dom, odd_band, False)
    mesh_recv = by_partner(mesh_receiver.reshape(GROUPS, -1), odd_dom, odd_band, True)
    mesh_send = by_partner(mesh_sender.reshape(GROUPS, -1), odd_dom, odd_band, False)
    grid_recv = by_partner(grid_receiver.reshape(GROUPS, -1), odd_dom, odd_band, True)
    near_on, near_off = sides_out(
        neighbors[: 2 * rim].reshape(-1), neighbors[mesh_count - 2 * rim :].reshape(-1)
    )
    near_out = [near_on, near_off, near_off[:0], near_off[:0]]
    packed = [
        jnp.concatenate([mesh_recv[p], mesh_send[p], near_out[p - 1]]) for p in range(1, GROUPS)
    ]
    packed = swap_all(*packed)
    cap = mesh_recv[0].shape[0]
    far_recv = [mesh_recv[0]] + [block[:cap] for block in packed]
    far_send = [mesh_send[0]] + [block[cap : 2 * cap] for block in packed]
    near_left, near_right = sides_in(packed[0][2 * cap :], packed[1][2 * cap :])
    wide = mesh_count + 4 * rim
    near_rows = jnp.concatenate(
        [
            near_left.reshape(-1, NEAR) + (rim - mesh_count),
            neighbors + rim,
            near_right.reshape(-1, NEAR) + (rim + mesh_count),
        ],
        0,
    )
    columns = jnp.arange(wide, dtype=jnp.int32)[None, :]
    counts = jnp.zeros((wide, wide), SINGLE)
    for column in range(NEAR):
        counts = counts + (near_rows[:, column][:, None] == columns).astype(SINGLE)
    counts = counts.astype(HALF)
    own = slice(2 * rim, 2 * rim + mesh_count)
    rims = slice(rim, 3 * rim + mesh_count)
    inner = slice(rim, rim + mesh_count)

    embed_pre = matmul(grid_vars, embed_weight)
    latent = jax.nn.silu(embed_pre).astype(HALF)
    to_mesh = [
        pair_counts(far_recv[p], mesh_count, grid_send[p], grid_count) for p in range(GROUPS)
    ]
    to_grid = [
        pair_counts(grid_recv[p], grid_count, far_send[p], mesh_count) for p in range(GROUPS)
    ]
    sums = [matmul(to_mesh[p], latent) for p in range(GROUPS)]
    arrived = swap_all(*[block.astype(HALF) for block in sums[1:]])
    encode_sum = sums[0]
    for block in arrived:
        encode_sum = encode_sum + block.astype(SINGLE)
    encode_in = encode_sum.astype(HALF)
    encode_pre = matmul(encode_in, encode_weight)
    state = mesh_static.astype(SINGLE) + jax.nn.silu(encode_pre)

    half = state.astype(HALF)
    left, right = sides_in(
        *[
            swap(block)
            for swap, block in zip(
                (swap_on, swap_off),
                sides_out(half[: 2 * rim], half[mesh_count - 2 * rim :]),
                strict=True,
            )
        ]
    )
    half_0 = jnp.concatenate([left, half, right], 0)
    state_0 = jnp.concatenate(
        [left[rim:].astype(SINGLE), state, right[:rim].astype(SINGLE)], 0
    )
    nearby_0 = (matmul(counts[rims], half_0) * (1.0 / NEAR)).astype(HALF)
    pre_0 = matmul(half_0[rims], self_weight[0]) + matmul(nearby_0, neighbor_weight[0])
    state_1 = state_0 + jax.nn.silu(pre_0)
    half_1 = state_1.astype(HALF)
    nearby_1 = (matmul(counts[own, rims], half_1) * (1.0 / NEAR)).astype(HALF)
    pre_1 = matmul(half_1[inner], self_weight[1]) + matmul(nearby_1, neighbor_weight[1])
    state_2 = state_1[inner] + jax.nn.silu(pre_1)
    final_half = state_2.astype(HALF)

    finals = (final_half,) + swap_all(*[final_half] * 4)
    decode_sum = matmul(to_grid[0], finals[0])
    for p in range(1, GROUPS):
        decode_sum = decode_sum + matmul(to_grid[p], finals[p])
    decode_in = decode_sum.astype(HALF)
    decode_pre = matmul(decode_in, decode_weight)
    hidden = jax.nn.silu(decode_pre).astype(HALF)
    prediction = (grid_vars.astype(SINGLE) + matmul(hidden, output_weight)).astype(HALF)
    grad_output = outer_sum(cotangent, hidden)
    hidden_grad = back_mul(cotangent, output_weight)
    decode_grad = (hidden_grad * silu_slope(decode_pre)).astype(HALF)
    grad_decode = outer_sum(decode_in, decode_grad)
    decode_in_grad = back_mul(decode_grad, decode_weight).astype(HALF)
    sums = [outer_sum(to_grid[p], decode_in_grad) for p in range(GROUPS)]
    arrived = swap_all(*[block.astype(HALF) for block in sums[1:]])
    state_grad = sums[0]
    for block in arrived:
        state_grad = state_grad + block.astype(SINGLE)

    layer_grad = (state_grad * silu_slope(pre_1)).astype(HALF)
    grad_self_1 = outer_sum(half_1[inner], layer_grad)
    grad_near_1 = outer_sum(nearby_1, layer_grad)
    state_grad_half = state_grad.astype(HALF)
    heads = jnp.concatenate([layer_grad[: 2 * rim], state_grad_half[:rim]], 0)
    tails = jnp.concatenate(
        [layer_grad[mesh_count - 2 * rim :], state_grad_half[mesh_count - rim :]], 0
    )
    left, right = sides_in(
        *[
            swap(block)
            for swap, block in zip((swap_on, swap_off), sides_out(heads, tails), strict=True)
        ]
    )
    layer_grad = jnp.concatenate([left[: 2 * rim], layer_grad, right[: 2 * rim]], 0)
    state_grad = jnp.concatenate(
        [left[2 * rim :].astype(SINGLE), state_grad, right[2 * rim :].astype(SINGLE)], 0
    )
    spread = (outer_sum(counts[:, rims], layer_grad) * (1.0 / NEAR)).astype(HALF)
    state_grad = (
        state_grad
        + back_mul(layer_grad[rims], self_weight[1])
        + back_mul(spread, neighbor_weight[1])
    )
    layer_grad = (state_grad * silu_slope(pre_0)).astype(HALF)
    grad_self_0 = outer_sum(half, layer_grad[inner])
    grad_near_0 = outer_sum(nearby_0[inner], layer_grad[inner])
    spread = (outer_sum(counts[rims, own], layer_grad) * (1.0 / NEAR)).astype(HALF)
    state_grad = (
        state_grad[inner]
        + back_mul(layer_grad[inner], self_weight[0])
        + back_mul(spread, neighbor_weight[0])
    )
    encode_grad = (state_grad * silu_slope(encode_pre)).astype(HALF)
    grad_encode = outer_sum(encode_in, encode_grad)
    encode_in_grad = back_mul(encode_grad, encode_weight).astype(HALF)
    returned = (encode_in_grad,) + swap_all(*[encode_in_grad] * 4)
    latent_grad = outer_sum(to_mesh[0], returned[0])
    for p in range(1, GROUPS):
        latent_grad = latent_grad + outer_sum(to_mesh[p], returned[p])
    embed_grad = (latent_grad * silu_slope(embed_pre)).astype(HALF)
    grad_embed = outer_sum(grid_vars, embed_grad)

    filler = jnp.zeros((-variables % 32, width), HALF)
    pieces = [
        grad_self_0,
        grad_self_1,
        grad_near_0,
        grad_near_1,
        grad_encode,
        grad_decode,
        grad_output,
        filler,
        grad_embed,
        filler,
    ]
    total = reduce_all(jnp.concatenate([piece.astype(HALF) for piece in pieces], 0))
    total = total.astype(SINGLE)
    square = total[: 6 * width].reshape(6, width, width)
    rest = total[6 * width :].reshape(2, -1, width)[:, :variables]
    return (
        prediction,
        state_grad,
        rest[1],
        square[4],
        square[0:2],
        square[2:4],
        square[5],
        rest[0].T,
    )


def solution(mesh):
    placed = (
        P(("band", "dom"), None),
        P(("band", "dom"), None),
        P(("band", "dom"), None),
        P(),
        P(),
        P(),
        P(),
        P(),
        P(),
        P(("band", "dom")),
        P(("band", "dom")),
        P(("band", "dom"), None),
        P(("band", "dom")),
        P(("band", "dom")),
    )
    return jax.shard_map(
        shards,
        mesh=mesh,
        in_specs=placed,
        out_specs=(
            P(("band", "dom"), None),
            P(("band", "dom"), None),
            P(),
            P(),
            P(),
            P(),
            P(),
            P(),
        ),
        check_vma=False,
    )
```

time: 373 us -> 244 us (0.65)
  waiting for transfers between devices: 225 us -> 65.8 us
  blocking collectives: 0 us -> 38.5 us
  local copies, waits for them, and re-layouts: 22.9 us -> 9.08 us
  other arithmetic: 2.58 us -> 15.5 us
  starting transfers between devices: 62.3 us -> 51.4 us
    psum x1 -> x0, waiting for transfers between devices: 167 us -> none  [shards(): lax.psum((grad_embed, grad_encode, grad_self, grad_neighbor, grad_decode,...]
    all_gather x0 -> x1, waiting for transfers between devices: none -> 43.2 us  [reduce_all(): lax.all_gather(piece, 'dom', axis=0, tiled=True, axis_index_groups=groups)]
    ppermute x24 -> x26, waiting for transfers between devices: 57.3 us -> 22.6 us  [the longest x7 14.5 us: swap_off(): lax.ppermute(value, 'dom', [(i, (i + (1 if i % 2 else -1)) % count) for i...]
    all_to_all x0 -> x1, blocking collectives: none -> 27.3 us  [reduce_all(): lax.all_to_all(part.reshape(count // 2, -1, part.shape[1]), 'dom', 0, 0,...]
    unnamed x94 -> x64, local copies, waits for them, and re-layouts: 17.8 us -> 1.73 us
    all_gather x0 -> x1, blocking collectives: none -> 11.3 us  [reduce_all(): pieces = lax.all_gather(piece, 'band', axis=0)]
    ppermute x24 -> x26, starting transfers between devices: 62.2 us -> 51.3 us  [the longest x9 32.4 us: swap_on(): return lax.ppermute(value, 'dom', [(i, i ^ 1) for i in range(count)])]
    dot_general x5 -> x7, matrix products: 3.6 us -> 12.8 us  [back_mul(): lax.dot_general(left, right, (((1,), (1,)), ((), ())), preferred_element_...]
  transfers between devices with their start and end apart: 25 -> 27, of which waited for: 19 -> 11; matrix products, arithmetic and copies ran while one was open for 3% -> 11% of each run, Pallas kernels for 0% -> 0%
where the time goes in v1:
time: 244 us; the launch traced here: 243 us
  waiting for transfers between devices  65.8 us (27%)
  starting transfers between devices  51.4 us (21%)
  matrix products  47.9 us (20%)
  blocking collectives  38.5 us (16%)
  other arithmetic  15.5 us (6%)
  between operations  14.8 us (6%)
  local copies, waits for them, and re-layouts  9.08 us (4%)
    all_gather x1, waiting for transfers between devices, reduce_all(): lax.all_gather(piece, 'dom', axis=0, tiled=True, axis_index_groups=groups)  43.2 us
    ppermute x9, starting transfers between devices, swap_on(): return lax.ppermute(value, 'dom', [(i, i ^ 1) for i in range(count)])  32.4 us
    all_to_all x1, blocking collectives, reduce_all(): lax.all_to_all(part.reshape(count // 2, -1, part.shape[1]), 'dom', 0, 0,...  27.3 us
    dot_general x30, matrix products, matmul(): return jnp.dot(left, right, preferred_element_type=SINGLE)  21.5 us
    ppermute x10, starting transfers between devices, swap_band(): return lax.ppermute(value, 'band', pairs)  15.9 us
    ppermute x7, waiting for transfers between devices, swap_off(): lax.ppermute(value, 'dom', [(i, (i + (1 if i % 2 else -1)) % count) for i...  14.5 us
    dot_general x17, matrix products, outer_sum(): lax.dot_general(left, right, (((0,), (0,)), ((), ())), preferred_element_...  13.6 us
    dot_general x7, matrix products, back_mul(): lax.dot_general(left, right, (((1,), (1,)), ((), ())), preferred_element_...  12.8 us
  transfers between devices with their start and end apart: 27, of which 11 were waited for; matrix products, arithmetic and copies ran while one was open for 11% of the time, Pallas kernels for 0%

profile of v1, /device:TPU:1, one launch (start us, length us, event | category | flops | bytes accessed | tf_op | source)
XLA Modules:
  0.0 242.9 jit_solution(4323309121745881318)
XLA Ops:
  7.3 0.8 fusion.134
  8.1 0.8 slice_select_fusion.17
  9.5 4.6 %collective-permute-start.4 = (s32[1536]{0:T(1024)S(1)}, s32[1536]{0:T(1024)S(1)}, u32[]{:S(2)}, u32[]{:S(2)}) collective-permute-start(s32[1536]{0:T(1024)S(1)} %pad_add_fusion.2), channel_id=1, source_target_pairs={{0,32},{32,0},{64,96},{96,64},{1,33},{33,1},{65,97},{97,65},{2,34}... | collective-permute-start | bytes 18440 | tf_op jit(solution)/shard_map/ppermute | solution.py:51
  15.1 2.8 %collective-permute-start.2 = (s32[2304]{0:T(1024)S(1)}, s32[2304]{0:T(1024)S(1)}, u32[]{:S(2)}, u32[]{:S(2)}) collective-permute-start(s32[2304]{0:T(1024)S(1)} %pad_add_fusion.1), channel_id=1, source_target_pairs={{0,31},{1,2},{2,1},{3,4},{4,3},{5,6},{6,5},{7,8},{8,7},{9,10},{10,... | collective-permute-start | bytes 27656 | tf_op jit(solution)/shard_map/ppermute | solution.py:41
  18.2 3.9 %collective-permute-start = (s32[2304]{0:T(1024)S(1)}, s32[2304]{0:T(1024)S(1)}, u32[]{:S(2)}, u32[]{:S(2)}) collective-permute-start(s32[2304]{0:T(1024)S(1)} %pad_add_fusion), channel_id=1, source_target_pairs={{0,1},{1,0},{2,3},{3,2},{4,5},{5,4},{6,7},{7,6},{8,9},{9,8},{10,11... | collective-permute-start | bytes 27656 | tf_op jit(solution)/shard_map/ppermute | solution.py:36
  22.1 0.8 slice_select_fusion.2
  22.9 0.8 slice_select_fusion.11
  23.7 2.4 %multiply_convert_fusion.1 = (bf16[512,512]{1,0:T(8,128)(2,1)S(1)}, f32[512,512]{1,0:T(8,128)}) fusion(bf16[512,227]{0,1:T(8,128)(2,1)} %param.14, bf16[227,512]{1,0:T(8,128)(2,1)} %param.17), kind=kOutput, calls=%fused_computation.101 | convolution fusion | flops 120324096 | bytes 2037760 | tf_op jit(solution)/shard_map/dot_general | solution.py:19
  26.7 1.2 fusion.30
  28.8 1.4 collective-permute-start.7
  31.1 0.9 collective-permute-start.5
  32.0 1.2 fusion.21
  33.2 1.2 fusion.22
  35.1 1.0 convolution_convert_fusion.14
  36.6 1.0 convolution_convert_fusion.15
  37.7 1.0 collective-permute-start.1
  39.6 0.9 add_convert_fusion.1
  40.6 1.6 collective-permute-done.3
  42.2 1.6 add_convert_fusion.2
  43.8 1.1 fusion.131
  44.9 4.0 %collective-permute-start.8 = (bf16[128,512]{1,0:T(8,128)(2,1)S(1)}, bf16[128,512]{1,0:T(8,128)(2,1)S(1)}, u32[]{:S(2)}, u32[]{:S(2)}) collective-permute-start(bf16[128,512]{1,0:T(8,128)(2,1)S(1)} %get-tuple-element.33), channel_id=1, source_target_pairs={{0,1},{1,0},{2,3},{3,2},{4,5},{5,4},{6,7},{7,6},{8,9},{9,8},{10,11... | collective-permute-start | bytes 393224 | tf_op jit(solution)/shard_map/ppermute | solution.py:36
  49.9 3.4 %collective-permute-done.9 = bf16[128,512]{1,0:T(8,128)(2,1)S(1)} collective-permute-done((bf16[128,512]{1,0:T(8,128)(2,1)S(1)}, bf16[128,512]{1,0:T(8,128)(2,1)S(1)}, u32[]{:S(2)}, u32[]{:S(2)}) %collective-permute-start.9) | collective-permute-done | bytes 131104 | tf_op jit(solution)/shard_map/ppermute | solution.py:41
  54.6 1.3 fusion.130
  57.0 0.8 collective-permute-start.13
  57.8 2.4 %collective-permute-start.12 = (bf16[256,512]{1,0:T(8,128)(2,1)S(1)}, bf16[256,512]{1,0:T(8,128)(2,1)S(1)}, u32[]{:S(2)}, u32[]{:S(2)}) collective-permute-start(bf16[256,512]{1,0:T(8,128)(2,1)S(1)} %get-tuple-element.77), channel_id=1, source_target_pairs={{0,32},{32,0},{64,96},{96,64},{1,33},{33,1},{65,97},{97,65},{2,34}... | collective-permute-start | bytes 786440 | tf_op jit(solution)/shard_map/ppermute | solution.py:51
  60.3 4.0 %collective-permute-start.10 = (bf16[256,512]{1,0:T(8,128)(2,1)S(1)}, bf16[256,512]{1,0:T(8,128)(2,1)S(1)}, u32[]{:S(2)}, u32[]{:S(2)}) collective-permute-start(bf16[256,512]{1,0:T(8,128)(2,1)S(1)} %get-tuple-element.77), channel_id=1, source_target_pairs={{0,1},{1,0},{2,3},{3,2},{4,5},{5,4},{6,7},{7,6},{8,9},{9,8},{10,11... | collective-permute-start | bytes 786440 | tf_op jit(solution)/shard_map/ppermute | solution.py:36
  64.6 0.8 collective-permute-done.10
  66.3 4.0 %collective-permute-done.11 = bf16[256,512]{1,0:T(8,128)(2,1)S(1)} collective-permute-done((bf16[256,512]{1,0:T(8,128)(2,1)S(1)}, bf16[256,512]{1,0:T(8,128)(2,1)S(1)}, u32[]{:S(2)}, u32[]{:S(2)}) %collective-permute-start.11) | collective-permute-done | bytes 262176 | tf_op jit(solution)/shard_map/ppermute | solution.py:41
  74.7 2.0 collective-permute-start.16
  77.0 3.5 %collective-permute-start.14 = (bf16[256,512]{1,0:T(8,128)(2,1)S(1)}, bf16[256,512]{1,0:T(8,128)(2,1)S(1)}, u32[]{:S(2)}, u32[]{:S(2)}) collective-permute-start(bf16[256,512]{1,0:T(8,128)(2,1)S(1)} %convolution_convert_fusion.11), channel_id=1, source_target_pairs={{0,1},{1,0},{2,3},{3,2},{4,5},{5,4},{6,7},{7,6},{8,9},{9,8},{10,11... | collective-permute-start | bytes 786440 | tf_op jit(solution)/shard_map/ppermute | solution.py:36
  80.5 1.0 fusion.36
  81.5 1.3 convolution_convert_fusion
  83.8 6.8 %collective-permute-start.18 = (bf16[192,512]{1,0:T(8,128)(2,1)S(1)}, bf16[192,512]{1,0:T(8,128)(2,1)S(1)}, u32[]{:S(2)}, u32[]{:S(2)}) collective-permute-start(bf16[192,512]{1,0:T(8,128)(2,1)S(1)} %get-tuple-element.25), channel_id=1, source_target_pairs={{0,1},{1,0},{2,3},{3,2},{4,5},{5,4},{6,7},{7,6},{8,9},{9,8},{10,11... | collective-permute-start | bytes 589832 | tf_op jit(solution)/shard_map/ppermute | solution.py:36
  90.9 0.7 collective-permute-done.18
  91.7 4.0 %collective-permute-done.19 = bf16[192,512]{1,0:T(8,128)(2,1)S(1)} collective-permute-done((bf16[192,512]{1,0:T(8,128)(2,1)S(1)}, bf16[192,512]{1,0:T(8,128)(2,1)S(1)}, u32[]{:S(2)}, u32[]{:S(2)}) %collective-permute-start.19) | collective-permute-done | bytes 196640 | tf_op jit(solution)/shard_map/ppermute | solution.py:41
  96.5 1.3 fusion.70
  97.8 3.9 %multiply_convert_fusion.2 = (bf16[384,512]{1,0:T(8,128)(2,1)}, f32[384,512]{1,0:T(8,128)}) fusion(f32[384,512]{1,0:T(8,128)} %get-tuple-element.76, bf16[2,512,512]{2,1,0:T(8,128)(2,1)} %param.20, bf16[128,512]{1,0:T(8,128)(2,1)} %copy-done.27, bf16[256,512]{1,0:T(8,128)(2,1)S(1)} %get-tuple-element.8, bf16[128,512]{1,0:T(8,128)(2,1)} %copy-done.28, ...), kind=kOutput, calls=%fused_computation.105 | convolution fusion | flops 407175168 | bytes 4980736 | tf_op jit(solution)/shard_map/dot_general | solution.py:29
  101.7 2.3 convolution_add_fusion.7
  104.0 2.9 %multiply_convert_fusion.3 = (bf16[256,512]{1,0:T(8,128)(2,1)S(1)}, f32[256,512]{1,0:T(8,128)}) fusion(f32[256,512]{1,0:T(8,128)} %get-tuple-element.75, f32[256,512]{1,0:T(8,128)} %convolution_add_fusion.7, bf16[2,512,512]{2,1,0:T(8,128)(2,1)} %param.20, bf16[384,512]{1,0:T(8,128)(2,1)} %get-tuple-element.81, bf16[512,512]{1,0:T(8,128)(2,1)} %copy-done.17), kind=kOutput, calls=%fused_computation.154 | convolution fusion | flops 236453888 | bytes 2949120 | tf_op jit(solution)/shard_map/dot_general | solution.py:29
  106.9 1.1 convolution_convert_fusion.5
  108.0 1.4 convolution_convert_fusion.7
  110.1 1.7 collective-permute-start.22
  111.9 4.0 %collective-permute-start.20 = (bf16[256,512]{1,0:T(8,128)(2,1)S(1)}, bf16[256,512]{1,0:T(8,128)(2,1)S(1)}, u32[]{:S(2)}, u32[]{:S(2)}) collective-permute-start(bf16[256,512]{1,0:T(8,128)(2,1)S(1)} %convolution_convert_fusion.7), channel_id=1, source_target_pairs={{0,1},{1,0},{2,3},{3,2},{4,5},{5,4},{6,7},{7,6},{8,9},{9,8},{10,11... | collective-permute-start | bytes 786440 | tf_op jit(solution)/shard_map/ppermute | solution.py:36
  115.8 1.1 convolution_convert_fusion.2
  117.0 1.1 convolution_convert_fusion.4
  118.4 1.3 convolution_add_fusion.1
  120.4 1.5 collective-permute-done.21
  122.6 3.2 %fusion.35 = bf16[227,512]{1,0:T(8,128)(2,1)} fusion(bf16[512,227]{0,1:T(8,128)(2,1)} %param.14, f32[512,512]{1,0:T(8,128)S(1)} %fusion.148, f32[512,512]{1,0:T(8,128)S(1)} %fusion.147, f32[512,512]{1,0:T(8,128)} %convolution_add_fusion.1, bf16[256,512]{1,0:T(8,128)(2,1)} %copy-done.21, bf16[256,512]{1,0:T(8,128)(2,1)} %copy-done.31, ...), kind=kOutput, calls=%fused_computation.84 | convolution fusion | flops 256493056 | bytes 5183488 | tf_op jit(solution)/shard_map/dot_general | solution.py:23
  125.9 5.4 %concatenate.54 = bf16[2048,512]{1,0:T(8,128)(2,1)S(1)} concatenate(bf16[512,512]{1,0:T(8,128)(2,1)S(1)} %convolution_convert_fusion.6, bf16[512,512]{1,0:T(8,128)(2,1)} %convolution_convert_fusion.5, bf16[512,512]{1,0:T(8,128)(2,1)} %convolution_convert_fusion, bf16[227,512]{1,0:T(8,128)(2,1)S(1)} %copy-done.13, bf16[29,512]{1,0:T(8,128)(2,1)S(1)} %broadcast_in_dim.2, ...), dimensions={0} | concatenate | bytes 4194304 | tf_op jit(solution)/shard_map/concatenate | solution.py:276
  131.3 1.8 broadcast_select_fusion.2
  133.1 3.1 %collective-permute-start.24 = (bf16[1792,512]{1,0:T(8,128)(2,1)S(1)}, bf16[1792,512]{1,0:T(8,128)(2,1)S(1)}, u32[]{:S(2)}, u32[]{:S(2)}) collective-permute-start(bf16[1792,512]{1,0:T(8,128)(2,1)S(1)} %broadcast_select_fusion.2), channel_id=1, source_target_pairs={{0,1},{1,0},{2,3},{3,2},{4,5},{5,4},{6,7},{7,6},{8,9},{9,8},{10,11... | collective-permute-start | bytes 5505032 | tf_op jit(solution)/shard_map/ppermute | solution.py:36
  136.2 3.4 %collective-permute-done.24 = bf16[1792,512]{1,0:T(8,128)(2,1)S(1)} collective-permute-done((bf16[1792,512]{1,0:T(8,128)(2,1)S(1)}, bf16[1792,512]{1,0:T(8,128)(2,1)S(1)}, u32[]{:S(2)}, u32[]{:S(2)}) %collective-permute-start.24) | collective-permute-done | bytes 1835040 | tf_op jit(solution)/shard_map/ppermute | solution.py:36
  139.7 0.8 add_convert_fusion
  140.5 27.3 %all_to_all.5 = bf16[16,112,512]{2,1,0:T(8,128)(2,1)S(1)} all-to-all(bf16[16,112,512]{2,1,0:T(8,128)(2,1)S(1)} %bitcast.118), channel_id=1, replica_groups={{0,2,4,6,8,10,12,14,16,18,20,22,24,26,28,30},{1,3,5,7,9,11,13,15,17,19,..., dimensions={0} | all-to-all | bytes 3670016 | tf_op jit(solution)/shard_map/all_to_all | solution.py:85
  168.0 11.3 %all-gather = bf16[448,512]{1,0:T(8,128)(2,1)S(1)} all-gather(bf16[112,512]{1,0:T(8,128)(2,1)S(1)} %reduce_sum.24), channel_id=2, replica_groups=mesh['band'=4,'dom'=32] {'band'}, dimensions={0}, use_global_device_ids=true | all-gather | bytes 573440 | tf_op jit(solution)/shard_map/all_gather | solution.py:89
  179.3 0.7 reduce_sum.25
  180.1 43.2 %all-gather.3.cloned.1.call-done = bf16[1792,512]{1,0:T(8,128)(2,1)} async-done(((bf16[112,512]{1,0:T(8,128)(2,1)}), bf16[1792,512]{1,0:T(8,128)(2,1)}) %all-gather.3.cloned.1.call-update) | async-done | bytes 1835024 | tf_op jit(solution)/shard_map/all_gather | solution.py:91
  223.2 2.1 collective-permute-start.25
  225.4 1.0 fusion.33
  226.4 2.6 %collective-permute-done.25 = bf16[1792,512]{1,0:T(8,128)(2,1)S(1)} collective-permute-done((bf16[1792,512]{1,0:T(8,128)(2,1)}, bf16[1792,512]{1,0:T(8,128)(2,1)S(1)}, u32[]{:S(2)}, u32[]{:S(2)}) %collective-permute-start.25) | collective-permute-done | bytes 1835040 | tf_op jit(solution)/shard_map/ppermute | solution.py:36
  229.0 1.7 broadcast_select_fusion.1
  230.7 1.8 fusion.51
  232.5 2.6 %maximum_convert_fusion = (f32[1024,512]{1,0:T(8,128)}, f32[1024,512]{1,0:T(8,128)}) fusion(bf16[1792,512]{1,0:T(8,128)(2,1)S(1)} %get-tuple-element.20, bf16[1792,512]{1,0:T(8,128)(2,1)S(1)} %get-tuple-element.19), kind=kLoop, calls=%fused_computation.86 | loop fusion | flops 4194304 | bytes 7864320 | tf_op jit(solution)/shard_map/slice | solution.py:286
  235.1 1.0 slice_bitcast_fusion
  (156 shorter events, 20.1 us)
Async XLA Ops:
  7.2 63.5 %copy-start = (bf16[512,512]{1,0:T(8,128)(2,1)S(1)}, bf16[512,512]{1,0:T(8,128)(2,1)}, u32[]{:S(2)}) copy-start(bf16[512,512]{1,0:T(8,128)(2,1)} %param.21) | copy-start | bytes 1572868
  7.2 216.1 %all-gather.3.cloned.1.call-start = ((), (), s32[]{:S(2)}) async-start(), calls=%async_computation.1 | async-start | bytes 1949696 | tf_op jit(solution)/shard_map/all_gather | solution.py:91
  8.8 19.1 %collective-permute-start.6 = (s32[1536]{0:T(1024)S(1)}, s32[1536]{0:T(1024)S(1)}, u32[]{:S(2)}, u32[]{:S(2)}) collective-permute-start(s32[1536]{0:T(1024)S(1)} %pad_add_fusion.3), channel_id=1, source_target_pairs={{32,64},{64,32},{33,65},{65,33},{34,66},{66,34},{35,67},{67,35},{3... | collective-permute-start | bytes 18440 | tf_op jit(solution)/shard_map/ppermute | solution.py:51
  9.5 20.7 %collective-permute-start.4 = (s32[1536]{0:T(1024)S(1)}, s32[1536]{0:T(1024)S(1)}, u32[]{:S(2)}, u32[]{:S(2)}) collective-permute-start(s32[1536]{0:T(1024)S(1)} %pad_add_fusion.2), channel_id=1, source_target_pairs={{0,32},{32,0},{64,96},{96,64},{1,33},{33,1},{65,97},{97,65},{2,34}... | collective-permute-start | bytes 18440 | tf_op jit(solution)/shard_map/ppermute | solution.py:51
  15.1 19.4 %collective-permute-start.2 = (s32[2304]{0:T(1024)S(1)}, s32[2304]{0:T(1024)S(1)}, u32[]{:S(2)}, u32[]{:S(2)}) collective-permute-start(s32[2304]{0:T(1024)S(1)} %pad_add_fusion.1), channel_id=1, source_target_pairs={{0,31},{1,2},{2,1},{3,4},{4,3},{5,6},{6,5},{7,8},{8,7},{9,10},{10,... | collective-permute-start | bytes 27656 | tf_op jit(solution)/shard_map/ppermute | solution.py:41
  18.2 16.3 %collective-permute-start = (s32[2304]{0:T(1024)S(1)}, s32[2304]{0:T(1024)S(1)}, u32[]{:S(2)}, u32[]{:S(2)}) collective-permute-start(s32[2304]{0:T(1024)S(1)} %pad_add_fusion), channel_id=1, source_target_pairs={{0,1},{1,0},{2,3},{3,2},{4,5},{5,4},{6,7},{7,6},{8,9},{9,8},{10,11... | collective-permute-start | bytes 27656 | tf_op jit(solution)/shard_map/ppermute | solution.py:36
  26.1 1.8 copy-start.29
  26.7 15.5 %copy-start.9 = (bf16[256,512]{1,0:T(8,128)(2,1)}, bf16[256,512]{1,0:T(8,128)(2,1)S(1)}, u32[]{:S(2)}) copy-start(bf16[256,512]{1,0:T(8,128)(2,1)S(1)} %fusion.29) | copy-start | bytes 786436
  28.8 11.7 %collective-permute-start.7 = (bf16[256,512]{1,0:T(8,128)(2,1)S(1)}, bf16[256,512]{1,0:T(8,128)(2,1)}, u32[]{:S(2)}, u32[]{:S(2)}) collective-permute-start(bf16[256,512]{1,0:T(8,128)(2,1)S(1)} %convolution_convert_fusion.12), channel_id=1, source_target_pairs={{32,64},{64,32},{33,65},{65,33},{34,66},{66,34},{35,67},{67,35},{3... | collective-permute-start | bytes 786440 | tf_op jit(solution)/shard_map/ppermute | solution.py:51
  31.1 9.5 %collective-permute-start.5 = (bf16[256,512]{1,0:T(8,128)(2,1)S(1)}, bf16[256,512]{1,0:T(8,128)(2,1)}, u32[]{:S(2)}, u32[]{:S(2)}) collective-permute-start(bf16[256,512]{1,0:T(8,128)(2,1)S(1)} %convolution_convert_fusion.13), channel_id=1, source_target_pairs={{0,32},{32,0},{64,96},{96,64},{1,33},{33,1},{65,97},{97,65},{2,34}... | collective-permute-start | bytes 786440 | tf_op jit(solution)/shard_map/ppermute | solution.py:51
  35.1 3.6 %copy-start.21 = (bf16[256,512]{1,0:T(8,128)(2,1)}, bf16[256,512]{1,0:T(8,128)(2,1)S(1)}, u32[]{:S(2)}) copy-start(bf16[256,512]{1,0:T(8,128)(2,1)S(1)} %fusion.27) | copy-start | bytes 786436
  36.1 6.1 %collective-permute-start.3 = (bf16[256,512]{1,0:T(8,128)(2,1)}, bf16[256,512]{1,0:T(8,128)(2,1)}, u32[]{:S(2)}, u32[]{:S(2)}) collective-permute-start(bf16[256,512]{1,0:T(8,128)(2,1)} %convolution_convert_fusion.14), channel_id=1, source_target_pairs={{0,31},{1,2},{2,1},{3,4},{4,3},{5,6},{6,5},{7,8},{8,7},{9,10},{10,... | collective-permute-start | bytes 786440 | tf_op jit(solution)/shard_map/ppermute | solution.py:41
  37.7 4.5 %collective-permute-start.1 = (bf16[256,512]{1,0:T(8,128)(2,1)}, bf16[256,512]{1,0:T(8,128)(2,1)}, u32[]{:S(2)}, u32[]{:S(2)}) collective-permute-start(bf16[256,512]{1,0:T(8,128)(2,1)} %convolution_convert_fusion.15), channel_id=1, source_target_pairs={{0,1},{1,0},{2,3},{3,2},{4,5},{5,4},{6,7},{7,6},{8,9},{9,8},{10,11... | collective-permute-start | bytes 786440 | tf_op jit(solution)/shard_map/ppermute | solution.py:36
  39.0 4.7 %copy-start.16 = (bf16[512,512]{1,0:T(8,128)(2,1)S(1)}, bf16[512,512]{1,0:T(8,128)(2,1)}, u32[]{:S(2)}) copy-start(bf16[512,512]{1,0:T(8,128)(2,1)} %param.18) | copy-start | bytes 1572868
  39.0 4.7 %copy-start.30 = (bf16[256,512]{1,0:T(8,128)(2,1)S(1)}, bf16[256,512]{1,0:T(8,128)(2,1)}, u32[]{:S(2)}) copy-start(bf16[256,512]{1,0:T(8,128)(2,1)} %param.16) | copy-start | bytes 786436
  40.6 15.7 %copy-start.17 = (bf16[512,512]{1,0:T(8,128)(2,1)}, bf16[512,512]{1,0:T(8,128)(2,1)S(1)}, u32[]{:S(2)}) copy-start(bf16[512,512]{1,0:T(8,128)(2,1)S(1)} %add_convert_fusion.1) | copy-start | bytes 1572868
  43.8 1.1 copy-start.11
  44.9 5.0 %collective-permute-start.8 = (bf16[128,512]{1,0:T(8,128)(2,1)S(1)}, bf16[128,512]{1,0:T(8,128)(2,1)S(1)}, u32[]{:S(2)}, u32[]{:S(2)}) collective-permute-start(bf16[128,512]{1,0:T(8,128)(2,1)S(1)} %get-tuple-element.33), channel_id=1, source_target_pairs={{0,1},{1,0},{2,3},{3,2},{4,5},{5,4},{6,7},{7,6},{8,9},{9,8},{10,11... | collective-permute-start | bytes 393224 | tf_op jit(solution)/shard_map/ppermute | solution.py:36
  48.9 4.4 %collective-permute-start.9 = (bf16[128,512]{1,0:T(8,128)(2,1)S(1)}, bf16[128,512]{1,0:T(8,128)(2,1)S(1)}, u32[]{:S(2)}, u32[]{:S(2)}) collective-permute-start(bf16[128,512]{1,0:T(8,128)(2,1)S(1)} %get-tuple-element.34), channel_id=1, source_target_pairs={{0,31},{1,2},{2,1},{3,4},{4,3},{5,6},{6,5},{7,8},{8,7},{9,10},{10,... | collective-permute-start | bytes 393224 | tf_op jit(solution)/shard_map/ppermute | solution.py:41
  49.5 4.3 %copy-start.20 = (bf16[2,512,512]{2,1,0:T(8,128)(2,1)S(1)}, bf16[2,512,512]{2,1,0:T(8,128)(2,1)}, u32[]{:S(2)}) copy-start(bf16[2,512,512]{2,1,0:T(8,128)(2,1)} %param.20) | copy-start | bytes 3145732
  53.4 1.2 copy-start.6
  53.8 2.2 copy-start.18
  56.6 7.7 %copy-start.22 = (bf16[512,256]{1,0:T(8,128)(2,1)S(1)}, bf16[512,256]{1,0:T(8,128)(2,1)}, u32[]{:S(2)}) copy-start(bf16[512,256]{1,0:T(8,128)(2,1)} %fusion.30) | copy-start | bytes 786436
  57.0 8.7 %copy-start.7 = (bf16[512,256]{1,0:T(8,128)(2,1)S(1)}, bf16[512,256]{1,0:T(8,128)(2,1)}, u32[]{:S(2)}) copy-start(bf16[512,256]{1,0:T(8,128)(2,1)} %fusion.21) | copy-start | bytes 786436
  57.0 8.7 %collective-permute-start.13 = (bf16[256,512]{1,0:T(8,128)(2,1)S(1)}, bf16[256,512]{1,0:T(8,128)(2,1)S(1)}, u32[]{:S(2)}, u32[]{:S(2)}) collective-permute-start(bf16[256,512]{1,0:T(8,128)(2,1)S(1)} %get-tuple-element.77), channel_id=1, source_target_pairs={{32,64},{64,32},{33,65},{65,33},{34,66},{66,34},{35,67},{67,35},{3... | collective-permute-start | bytes 786440 | tf_op jit(solution)/shard_map/ppermute | solution.py:51
  57.8 8.2 %collective-permute-start.12 = (bf16[256,512]{1,0:T(8,128)(2,1)S(1)}, bf16[256,512]{1,0:T(8,128)(2,1)S(1)}, u32[]{:S(2)}, u32[]{:S(2)}) collective-permute-start(bf16[256,512]{1,0:T(8,128)(2,1)S(1)} %get-tuple-element.77), channel_id=1, source_target_pairs={{0,32},{32,0},{64,96},{96,64},{1,33},{33,1},{65,97},{97,65},{2,34}... | collective-permute-start | bytes 786440 | tf_op jit(solution)/shard_map/ppermute | solution.py:51
  60.3 5.1 %collective-permute-start.10 = (bf16[256,512]{1,0:T(8,128)(2,1)S(1)}, bf16[256,512]{1,0:T(8,128)(2,1)S(1)}, u32[]{:S(2)}, u32[]{:S(2)}) collective-permute-start(bf16[256,512]{1,0:T(8,128)(2,1)S(1)} %get-tuple-element.77), channel_id=1, source_target_pairs={{0,1},{1,0},{2,3},{3,2},{4,5},{5,4},{6,7},{7,6},{8,9},{9,8},{10,11... | collective-permute-start | bytes 786440 | tf_op jit(solution)/shard_map/ppermute | solution.py:36
  64.3 6.1 %collective-permute-start.11 = (bf16[256,512]{1,0:T(8,128)(2,1)S(1)}, bf16[256,512]{1,0:T(8,128)(2,1)S(1)}, u32[]{:S(2)}, u32[]{:S(2)}) collective-permute-start(bf16[256,512]{1,0:T(8,128)(2,1)S(1)} %get-tuple-element.77), channel_id=1, source_target_pairs={{0,31},{1,2},{2,1},{3,4},{4,3},{5,6},{6,5},{7,8},{8,7},{9,10},{10,... | collective-permute-start | bytes 786440 | tf_op jit(solution)/shard_map/ppermute | solution.py:41
  64.6 1.5 copy-start.8
  70.7 0.9 copy-start.24
  70.7 1.0 copy-start.26
  71.3 9.2 %copy-start.3 = (bf16[512,512]{1,0:T(8,128)(2,1)}, bf16[512,512]{1,0:T(8,128)(2,1)S(1)}, u32[]{:S(2)}) copy-start(bf16[512,512]{1,0:T(8,128)(2,1)S(1)} %get-tuple-element.79) | copy-start | bytes 1572868
  74.0 8.8 %collective-permute-start.17 = (bf16[256,512]{1,0:T(8,128)(2,1)S(1)}, bf16[256,512]{1,0:T(8,128)(2,1)S(1)}, u32[]{:S(2)}, u32[]{:S(2)}) collective-permute-start(bf16[256,512]{1,0:T(8,128)(2,1)S(1)} %convolution_convert_fusion.8), channel_id=1, source_target_pairs={{32,64},{64,32},{33,65},{65,33},{34,66},{66,34},{35,67},{67,35},{3... | collective-permute-start | bytes 786440 | tf_op jit(solution)/shard_map/ppermute | solution.py:51
  74.7 8.1 %collective-permute-start.16 = (bf16[256,512]{1,0:T(8,128)(2,1)S(1)}, bf16[256,512]{1,0:T(8,128)(2,1)S(1)}, u32[]{:S(2)}, u32[]{:S(2)}) collective-permute-start(bf16[256,512]{1,0:T(8,128)(2,1)S(1)} %convolution_convert_fusion.9), channel_id=1, source_target_pairs={{0,32},{32,0},{64,96},{96,64},{1,33},{33,1},{65,97},{97,65},{2,34}... | collective-permute-start | bytes 786440 | tf_op jit(solution)/shard_map/ppermute | solution.py:51
  76.7 6.1 %collective-permute-start.15 = (bf16[256,512]{1,0:T(8,128)(2,1)S(1)}, bf16[256,512]{1,0:T(8,128)(2,1)S(1)}, u32[]{:S(2)}, u32[]{:S(2)}) collective-permute-start(bf16[256,512]{1,0:T(8,128)(2,1)S(1)} %convolution_convert_fusion.10), channel_id=1, source_target_pairs={{0,31},{1,2},{2,1},{3,4},{4,3},{5,6},{6,5},{7,8},{8,7},{9,10},{10,... | collective-permute-start | bytes 786440 | tf_op jit(solution)/shard_map/ppermute | solution.py:41
  77.0 5.9 %collective-permute-start.14 = (bf16[256,512]{1,0:T(8,128)(2,1)S(1)}, bf16[256,512]{1,0:T(8,128)(2,1)S(1)}, u32[]{:S(2)}, u32[]{:S(2)}) collective-permute-start(bf16[256,512]{1,0:T(8,128)(2,1)S(1)} %convolution_convert_fusion.11), channel_id=1, source_target_pairs={{0,1},{1,0},{2,3},{3,2},{4,5},{5,4},{6,7},{7,6},{8,9},{9,8},{10,11... | collective-permute-start | bytes 786440 | tf_op jit(solution)/shard_map/ppermute | solution.py:36
  83.3 7.6 %copy-start.15 = (f32[256,512]{1,0:T(8,128)}, f32[256,512]{1,0:T(8,128)S(1)}, u32[]{:S(2)}) copy-start(f32[256,512]{1,0:T(8,128)S(1)} %get-tuple-element.9) | copy-start | bytes 1572868
  83.8 7.9 %collective-permute-start.18 = (bf16[192,512]{1,0:T(8,128)(2,1)S(1)}, bf16[192,512]{1,0:T(8,128)(2,1)S(1)}, u32[]{:S(2)}, u32[]{:S(2)}) collective-permute-start(bf16[192,512]{1,0:T(8,128)(2,1)S(1)} %get-tuple-element.25), channel_id=1, source_target_pairs={{0,1},{1,0},{2,3},{3,2},{4,5},{5,4},{6,7},{7,6},{8,9},{9,8},{10,11... | collective-permute-start | bytes 589832 | tf_op jit(solution)/shard_map/ppermute | solution.py:36
  90.6 5.1 %collective-permute-start.19 = (bf16[192,512]{1,0:T(8,128)(2,1)S(1)}, bf16[192,512]{1,0:T(8,128)(2,1)S(1)}, u32[]{:S(2)}, u32[]{:S(2)}) collective-permute-start(bf16[192,512]{1,0:T(8,128)(2,1)S(1)} %get-tuple-element.26), channel_id=1, source_target_pairs={{0,31},{1,2},{2,1},{3,4},{4,3},{5,6},{6,5},{7,8},{8,7},{9,10},{10,... | collective-permute-start | bytes 589832 | tf_op jit(solution)/shard_map/ppermute | solution.py:41
  95.8 0.8 copy-start.27
  95.8 2.0 copy-start.28
  104.0 2.9 %copy-start.12 = (bf16[256,512]{1,0:T(8,128)(2,1)S(1)}, bf16[256,512]{1,0:T(8,128)(2,1)}, u32[]{:S(2)}) copy-start(bf16[256,512]{1,0:T(8,128)(2,1)} %copy-done.11) | copy-start | bytes 786436
  106.9 8.9 %copy-start.14 = (bf16[384,512]{1,0:T(8,128)(2,1)S(1)}, bf16[384,512]{1,0:T(8,128)(2,1)}, u32[]{:S(2)}) copy-start(bf16[384,512]{1,0:T(8,128)(2,1)} %get-tuple-element.81) | copy-start | bytes 1179652
  106.9 8.9 %copy-start.19 = (bf16[384,512]{1,0:T(8,128)(2,1)S(1)}, bf16[384,512]{1,0:T(8,128)(2,1)}, u32[]{:S(2)}) copy-start(bf16[384,512]{1,0:T(8,128)(2,1)} %copy-done.18) | copy-start | bytes 1179652
  108.0 10.1 %copy-start.10 = (bf16[256,512]{1,0:T(8,128)(2,1)S(1)}, bf16[256,512]{1,0:T(8,128)(2,1)}, u32[]{:S(2)}) copy-start(bf16[256,512]{1,0:T(8,128)(2,1)} %copy-done.9) | copy-start | bytes 786436
  109.5 10.3 %collective-permute-start.23 = (bf16[256,512]{1,0:T(8,128)(2,1)S(1)}, bf16[256,512]{1,0:T(8,128)(2,1)S(1)}, u32[]{:S(2)}, u32[]{:S(2)}) collective-permute-start(bf16[256,512]{1,0:T(8,128)(2,1)S(1)} %convolution_convert_fusion.7), channel_id=1, source_target_pairs={{32,64},{64,32},{33,65},{65,33},{34,66},{66,34},{35,67},{67,35},{3... | collective-permute-start | bytes 786440 | tf_op jit(solution)/shard_map/ppermute | solution.py:51
  110.1 9.9 %collective-permute-start.22 = (bf16[256,512]{1,0:T(8,128)(2,1)S(1)}, bf16[256,512]{1,0:T(8,128)(2,1)S(1)}, u32[]{:S(2)}, u32[]{:S(2)}) collective-permute-start(bf16[256,512]{1,0:T(8,128)(2,1)S(1)} %convolution_convert_fusion.7), channel_id=1, source_target_pairs={{0,32},{32,0},{64,96},{96,64},{1,33},{33,1},{65,97},{97,65},{2,34}... | collective-permute-start | bytes 786440 | tf_op jit(solution)/shard_map/ppermute | solution.py:51
  111.9 6.6 %collective-permute-start.20 = (bf16[256,512]{1,0:T(8,128)(2,1)S(1)}, bf16[256,512]{1,0:T(8,128)(2,1)S(1)}, u32[]{:S(2)}, u32[]{:S(2)}) collective-permute-start(bf16[256,512]{1,0:T(8,128)(2,1)S(1)} %convolution_convert_fusion.7), channel_id=1, source_target_pairs={{0,1},{1,0},{2,3},{3,2},{4,5},{5,4},{6,7},{7,6},{8,9},{9,8},{10,11... | collective-permute-start | bytes 786440 | tf_op jit(solution)/shard_map/ppermute | solution.py:36
  115.8 6.1 %collective-permute-start.21 = (bf16[256,512]{1,0:T(8,128)(2,1)S(1)}, bf16[256,512]{1,0:T(8,128)(2,1)S(1)}, u32[]{:S(2)}, u32[]{:S(2)}) collective-permute-start(bf16[256,512]{1,0:T(8,128)(2,1)S(1)} %convolution_convert_fusion.7), channel_id=1, source_target_pairs={{0,31},{1,2},{2,1},{3,4},{4,3},{5,6},{6,5},{7,8},{8,7},{9,10},{10,... | collective-permute-start | bytes 786440 | tf_op jit(solution)/shard_map/ppermute | solution.py:41
  121.9 0.7 copy-start.31
  122.6 3.2 %copy-start.13 = (bf16[227,512]{1,0:T(8,128)(2,1)S(1)}, bf16[227,512]{1,0:T(8,128)(2,1)}, u32[]{:S(2)}) copy-start(bf16[227,512]{1,0:T(8,128)(2,1)} %fusion.36) | copy-start | bytes 697348
  131.3 8.4 %copy-start.2 = (bf16[512,512]{1,0:T(8,128)(2,1)S(1)}, bf16[512,512]{1,0:T(8,128)(2,1)}, u32[]{:S(2)}) copy-start(bf16[512,512]{1,0:T(8,128)(2,1)} %convolution_convert_fusion.4) | copy-start | bytes 1572868
  131.3 8.4 %copy-start.5 = (bf16[512,512]{1,0:T(8,128)(2,1)S(1)}, bf16[512,512]{1,0:T(8,128)(2,1)}, u32[]{:S(2)}) copy-start(bf16[512,512]{1,0:T(8,128)(2,1)} %convolution_convert_fusion.2) | copy-start | bytes 1572868
  133.1 6.5 %collective-permute-start.24 = (bf16[1792,512]{1,0:T(8,128)(2,1)S(1)}, bf16[1792,512]{1,0:T(8,128)(2,1)S(1)}, u32[]{:S(2)}, u32[]{:S(2)}) collective-permute-start(bf16[1792,512]{1,0:T(8,128)(2,1)S(1)} %broadcast_select_fusion.2), channel_id=1, source_target_pairs={{0,1},{1,0},{2,3},{3,2},{4,5},{5,4},{6,7},{7,6},{8,9},{9,8},{10,11... | collective-permute-start | bytes 5505032 | tf_op jit(solution)/shard_map/ppermute | solution.py:36
  167.8 57.6 %copy-start.4 = (bf16[512,512]{1,0:T(8,128)(2,1)S(1)}, bf16[512,512]{1,0:T(8,128)(2,1)}, u32[]{:S(2)}) copy-start(bf16[512,512]{1,0:T(8,128)(2,1)} %copy-done.3) | copy-start | bytes 1572868
  167.8 57.6 %copy-start.23 = (bf16[512,227]{0,1:T(8,128)(2,1)S(1)}, bf16[512,227]{0,1:T(8,128)(2,1)}, u32[]{:S(2)}) copy-start(bf16[512,227]{0,1:T(8,128)(2,1)} %param.14) | copy-start | bytes 697348
  167.8 57.6 %copy-start.25 = (bf16[512,227]{0,1:T(8,128)(2,1)S(1)}, bf16[512,227]{0,1:T(8,128)(2,1)}, u32[]{:S(2)}) copy-start(bf16[512,227]{0,1:T(8,128)(2,1)} %param.22) | copy-start | bytes 697348
  223.2 5.7 %collective-permute-start.25 = (bf16[1792,512]{1,0:T(8,128)(2,1)}, bf16[1792,512]{1,0:T(8,128)(2,1)S(1)}, u32[]{:S(2)}, u32[]{:S(2)}) collective-permute-start(bf16[1792,512]{1,0:T(8,128)(2,1)} %all-gather.3.cloned.1.call-done), channel_id=1, source_target_pairs={{0,1},{1,0},{2,3},{3,2},{4,5},{5,4},{6,7},{7,6},{8,9},{9,8},{10,11... | collective-permute-start | bytes 5505032 | tf_op jit(solution)/shard_map/ppermute | solution.py:36
  232.5 3.6 %copy-start.1 = (bf16[512,512]{1,0:T(8,128)(2,1)S(1)}, bf16[512,512]{1,0:T(8,128)(2,1)}, u32[]{:S(2)}) copy-start(bf16[512,512]{1,0:T(8,128)(2,1)} %param.21) | copy-start | bytes 1572868
Sparse Core Ops, SparseCore 0:
  180.2 43.0 all-gather.2

commit v2 on v1

v2 whole, which is shorter than its diff:
```python
import jax
import jax.numpy as jnp
from jax import lax
from jax.experimental import pallas as pl
from jax.experimental.pallas import tpu as pltpu
from jax.sharding import PartitionSpec as P

NEAR = 6
RIM = 64
GROUPS = 5
LANES = 128
HALF = jnp.bfloat16
SINGLE = jnp.float32
MIB = 1024 * 1024


def silu_slope(values):
    sigma = jax.nn.sigmoid(values)
    return sigma * (1.0 + values * (1.0 - sigma))


def matmul(left, right):
    return jnp.dot(left, right, preferred_element_type=SINGLE)


def outer_sum(left, right):
    return lax.dot_general(
        left, right, (((0,), (0,)), ((), ())), preferred_element_type=SINGLE
    )


def back_mul(left, right):
    return lax.dot_general(
        left, right, (((1,), (1,)), ((), ())), preferred_element_type=SINGLE
    )


def swap_on(value):
    count = lax.axis_size("dom")
    return lax.ppermute(value, "dom", [(i, i ^ 1) for i in range(count)])


def swap_off(value):
    count = lax.axis_size("dom")
    return lax.ppermute(
        value, "dom", [(i, (i + (1 if i % 2 else -1)) % count) for i in range(count)]
    )


def swap_band(value, first):
    count = lax.axis_size("band")
    pairs = []
    for low in range(first, count - 1, 2):
        pairs += [(low, low + 1), (low + 1, low)]
    return lax.ppermute(value, "band", pairs)


def swap_all(on, off, north, south):
    return swap_on(on), swap_off(off), swap_band(north, 0), swap_band(south, 1)


def by_partner(slots, odd_dom, odd_band, incoming):
    flip_dom = odd_dom != incoming
    flip_band = odd_band != incoming
    return [
        slots[0],
        jnp.where(flip_dom, slots[2], slots[1]),
        jnp.where(flip_dom, slots[1], slots[2]),
        jnp.where(flip_band, slots[4], slots[3]),
        jnp.where(flip_band, slots[3], slots[4]),
    ]


def whole(body, outs, macs, *args, limit=32):
    moved = sum(a.size * a.dtype.itemsize for a in (*args, *outs))
    return pl.pallas_call(
        body,
        out_shape=outs,
        compiler_params=pltpu.CompilerParams(vmem_limit_bytes=limit * MIB),
        cost_estimate=pl.CostEstimate(flops=2 * macs, bytes_accessed=moved, transcendentals=0),
    )(*args)


def shape(rows, columns, kind):
    return jax.ShapeDtypeStruct((rows, columns), kind)


def odd_along(axis):
    return lax.axis_index(axis) % 2 == 1


def hot(rows, index):
    spots = lax.broadcasted_iota(jnp.int32, (rows, LANES), 0)
    one = [
        jnp.where(spots == index[j : j + 1], 1.0, 0.0).astype(HALF) for j in range(index.shape[0])
    ]
    return jnp.concatenate(one, 1)


def pair_counts(rows, row_count, columns, column_count):
    return back_mul(hot(row_count, rows), hot(column_count, columns)).astype(HALF)


def slots_of(index):
    step = index.shape[0] // GROUPS
    return [index[k * step : (k + 1) * step] for k in range(GROUPS)]


def parcels(grid_ref, grid_send_ref, mesh_recv_ref, mesh_send_ref, near_ref, *outs):
    odd_dom, odd_band = odd_along("dom"), odd_along("band")
    grid_send = by_partner(slots_of(grid_send_ref[...]), odd_dom, odd_band, False)
    mesh_recv = by_partner(slots_of(mesh_recv_ref[...]), odd_dom, odd_band, True)
    mesh_send = by_partner(slots_of(mesh_send_ref[...]), odd_dom, odd_band, False)
    near = near_ref[...]
    near = [near[:, j : j + LANES] for j in range(0, near.shape[1], LANES)]
    rows, variables = grid_ref.shape
    width = outs[0].shape[1]
    grid = grid_ref[...]
    spare = jnp.zeros((rows, width - variables), HALF)
    for p, out in enumerate(outs):
        parts = [mesh_recv[p + 1], mesh_send[p + 1], grid_send[p + 1], *near]
        used = sum(part.shape[0] for part in parts)
        parts.append(jnp.zeros((out.shape[0] - rows - used, LANES), jnp.int32))
        index = jnp.concatenate(parts, 0)
        out[:rows, :variables] = grid
        out[:rows, variables:] = spare
        out[rows:, :LANES] = (index >> 1).astype(SINGLE).astype(HALF)
        out[rows:, LANES:] = (index & 1).astype(SINGLE).astype(HALF)


def embed_own(grid_ref, weight_ref, send_ref, recv_ref, slope_ref, counts_ref, sum_ref):
    step = send_ref.shape[0] // GROUPS
    counts = pair_counts(
        recv_ref[:step], sum_ref.shape[0], send_ref[:step], grid_ref.shape[0]
    )
    pre = matmul(grid_ref[...], weight_ref[...])
    sigma = jax.nn.sigmoid(pre)
    slope_ref[...] = sigma * (1.0 + pre * (1.0 - sigma))
    counts_ref[...] = counts
    sum_ref[...] = matmul(counts, (pre * sigma).astype(HALF))


def embed_far(p, parcel_ref, weight_ref, recv_ref, sum_ref, index_ref, out_ref):
    rows = parcel_ref.shape[0] - index_ref.shape[0]
    packed = parcel_ref[rows:].astype(SINGLE)
    index = (packed[:, :LANES] * 2.0 + packed[:, LANES:]).astype(jnp.int32)
    index_ref[...] = index
    step = recv_ref.shape[0] // GROUPS
    recv = by_partner(slots_of(recv_ref[...]), odd_along("dom"), odd_along("band"), True)[p]
    counts = pair_counts(recv, out_ref.shape[0], index[2 * step : 3 * step], rows)
    pre = matmul(parcel_ref[:rows], weight_ref[...])
    latent = (pre * jax.nn.sigmoid(pre)).astype(HALF)
    out_ref[...] = sum_ref[...] + matmul(counts, latent)


def near_counts(near_ref, on_ref, off_ref, out_ref):
    step = near_ref.shape[0]
    mesh_count = near_ref.shape[1]
    first = on_ref.shape[0] - 2 - 2 * step
    odd_dom = odd_along("dom")
    on, off = on_ref[...], off_ref[...]
    left = jnp.where(odd_dom, on, off)[first + step : first + 2 * step] + (RIM - mesh_count)
    right = jnp.where(odd_dom, off, on)[first : first + step] + (RIM + mesh_count)
    own = near_ref[...] + RIM
    index = jnp.concatenate([left, own, right], 1)
    spots = lax.broadcasted_iota(jnp.int32, out_ref.shape, 0)
    counts = jnp.zeros(out_ref.shape, SINGLE)
    for j in range(step):
        counts = counts + jnp.where(spots == index[j : j + 1], 1.0, 0.0)
    out_ref[...] = counts.astype(HALF)


def grid_counts(send_ref, recv_ref, *refs):
    far, outs = refs[: GROUPS - 1], refs[GROUPS - 1 :]
    odd_dom, odd_band = odd_along("dom"), odd_along("band")
    step = send_ref.shape[0] // GROUPS
    recv = by_partner(slots_of(recv_ref[...]), odd_dom, odd_band, True)
    send = [send_ref[:step]] + [ref[step : 2 * step] for ref in far]
    for p, out in enumerate(outs):
        out[...] = pair_counts(recv[p], out.shape[0], send[p], out.shape[1])


def mesh_counts(send_ref, *refs):
    far, outs = refs[: GROUPS - 1], refs[GROUPS - 1 :]
    step = send_ref.shape[0] // GROUPS
    send = by_partner(slots_of(send_ref[...]), odd_along("dom"), odd_along("band"), False)
    for p, out in enumerate(outs):
        out[...] = pair_counts(far[p][:step], out.shape[0], send[p + 1], out.shape[1])


def gradient_halves(*refs):
    mine_ref, other_ref, wide_ref = refs[-3:]
    odd = lax.axis_index("dom") % 2
    at = 0
    for left, right in zip(refs[:-3:2], refs[1:-3:2], strict=True):
        columns = left.shape[1]
        rows = -(-columns // (2 * LANES)) * LANES
        wide_ref[:columns] = outer_sum(left[...], right[...])
        if columns < 2 * rows:
            wide_ref[columns : 2 * rows] = jnp.zeros((2 * rows - columns, right.shape[1]), SINGLE)
        mine_ref[at : at + rows] = wide_ref[pl.ds(pl.multiple_of(odd * rows, rows), rows)].astype(HALF)
        other_ref[at : at + rows] = wide_ref[
            pl.ds(pl.multiple_of((1 - odd) * rows, rows), rows)
        ].astype(HALF)
        at += rows


def split_gradients(*pairs):
    rows = sum(-(-left.shape[1] // (2 * LANES)) * LANES for left, _ in pairs)
    width = pairs[0][1].shape[1]
    flat = [array for pair in pairs for array in pair]
    macs = sum(left.size * right.shape[1] for left, right in pairs)
    outs = [shape(rows, width, HALF)] * 2
    moved = sum(a.size * a.dtype.itemsize for a in (*flat, *outs))
    mine, other = pl.pallas_call(
        gradient_halves,
        out_shape=outs,
        scratch_shapes=[pltpu.VMEM((width, width), SINGLE)],
        compiler_params=pltpu.CompilerParams(vmem_limit_bytes=32 * MIB),
        cost_estimate=pl.CostEstimate(flops=2 * macs, bytes_accessed=moved, transcendentals=0),
    )(*flat)
    return mine, swap_on(other)


def add_halves(*refs):
    out_ref = refs[-1]
    at = 0
    for mine, other in zip(refs[:-1:2], refs[1:-1:2], strict=True):
        rows = mine.shape[0]
        out_ref[at : at + rows] = (
            mine[...].astype(SINGLE) + other[...].astype(SINGLE)
        ).astype(HALF)
        at += rows


def unpack(part_ref, other_ref, *outs):
    odd = odd_along("dom")
    at = 0
    for out, which, rows in outs_of(outs):
        own = part_ref[at : at + rows].astype(SINGLE)
        far = other_ref[at : at + rows].astype(SINGLE)
        top, bottom = jnp.where(odd, far, own), jnp.where(odd, own, far)
        if which is None:
            out[:rows] = top
            out[rows:] = bottom[: out.shape[0] - rows]
        else:
            out[which, :rows] = top
            out[which, rows:] = bottom
        at += rows


def outs_of(outs):
    embed, encode, self_, near, decode, output = outs
    half = encode.shape[0] // 2
    narrow = -(-embed.shape[0] // (2 * LANES)) * LANES
    return [
        (output, None, narrow),
        (decode, None, half),
        (self_, 1, half),
        (near, 1, half),
        (self_, 0, half),
        (near, 0, half),
        (encode, None, half),
        (embed, None, narrow),
    ]


def reduce_all(part):
    count = lax.axis_size("dom")
    groups = [list(range(c, count, 2)) for c in range(2)]
    chips = count // 2
    width = part.shape[1]
    pieces = lax.all_to_all(
        part.reshape(chips, -1, width), "dom", 0, 0, axis_index_groups=groups
    )
    piece = jnp.sum(pieces.astype(SINGLE), 0).astype(HALF)
    pieces = lax.all_gather(piece, "band", axis=0)
    piece = jnp.sum(pieces.astype(SINGLE), 0).astype(HALF)
    copies = jnp.broadcast_to(piece[None], (chips, *piece.shape))
    return lax.all_to_all(copies, "dom", 0, 0, axis_index_groups=groups).reshape(part.shape)


def shards(
    grid_vars,
    cotangent,
    mesh_static,
    embed_weight,
    encode_weight,
    self_weight,
    neighbor_weight,
    decode_weight,
    output_weight,
    grid_sender,
    mesh_receiver,
    neighbors,
    mesh_sender,
    grid_receiver,
):
    grid_count, variables = grid_vars.shape
    mesh_count, width = mesh_static.shape
    rim = RIM
    odd_dom = odd_along("dom")
    cap = grid_sender.shape[0] // GROUPS

    def sides_out(first, last):
        return jnp.where(odd_dom, first, last), jnp.where(odd_dom, last, first)

    def sides_in(on, off):
        return jnp.where(odd_dom, on, off), jnp.where(odd_dom, off, on)

    grid_send, mesh_recv, mesh_send, grid_recv = (
        index.reshape(-1, LANES) for index in (grid_sender, mesh_receiver, mesh_sender, grid_receiver)
    )
    near = neighbors.T
    index_rows = 3 * (cap // LANES) + NEAR * mesh_count // LANES
    index_rows += -index_rows % 16
    columns = 2 * LANES
    sent = whole(
        parcels,
        [shape(grid_count + index_rows, columns, HALF)] * (GROUPS - 1),
        0,
        grid_vars,
        grid_send,
        mesh_recv,
        mesh_send,
        near,
    )
    arrived = swap_all(*sent)
    slope_embed, to_mesh_own, total = whole(
        embed_own,
        [
            shape(grid_count, width, SINGLE),
            shape(mesh_count, grid_count, HALF),
            shape(mesh_count, width, SINGLE),
        ],
        grid_vars.size * width + mesh_count * grid_count * (cap + width),
        grid_vars,
        embed_weight,
        grid_send,
        mesh_recv,
    )
    wide_weight = jnp.pad(embed_weight, ((0, columns - variables), (0, 0)))
    index = [None] * GROUPS
    for p in range(1, GROUPS):
        index[p], total = whole(
            lambda *refs, p=p: embed_far(p, *refs),
            [shape(index_rows, LANES, jnp.int32), shape(mesh_count, width, SINGLE)],
            grid_count * columns * width + mesh_count * grid_count * (cap + width),
            arrived[p - 1],
            wide_weight,
            mesh_recv,
            total,
        )
    ext = mesh_count + 4 * rim
    (counts,) = whole(
        near_counts, [shape(ext, ext, HALF)], ext * ext * 64, near, index[1], index[2]
    )
    own = slice(2 * rim, 2 * rim + mesh_count)
    to_grid = whole(
        grid_counts,
        [shape(grid_count, mesh_count, HALF)] * GROUPS,
        GROUPS * grid_count * mesh_count * cap,
        mesh_send,
        grid_recv,
        *index[1:],
    )
    to_mesh = to_mesh_own, *whole(
        mesh_counts,
        [shape(mesh_count, grid_count, HALF)] * (GROUPS - 1),
        (GROUPS - 1) * grid_count * mesh_count * cap,
        grid_send,
        *index[1:],
    )

    encode_in = total.astype(HALF)
    encode_pre = matmul(encode_in, encode_weight)
    state = mesh_static.astype(SINGLE) + jax.nn.silu(encode_pre)

    half = state.astype(HALF)
    on, off = sides_out(half[: 2 * rim], half[mesh_count - 2 * rim :])
    left, right = sides_in(swap_on(on), swap_off(off))
    half_0 = jnp.concatenate([left, half, right], 0)
    state_0 = jnp.concatenate([left.astype(SINGLE), state, right.astype(SINGLE)], 0)
    nearby_0 = (outer_sum(counts, half_0) * (1.0 / NEAR)).astype(HALF)
    pre_0 = matmul(half_0, self_weight[0]) + matmul(nearby_0, neighbor_weight[0])
    state_1 = state_0 + jax.nn.silu(pre_0)
    half_1 = state_1.astype(HALF)
    nearby_1 = (outer_sum(counts[:, own], half_1) * (1.0 / NEAR)).astype(HALF)
    pre_1 = matmul(half_1[own], self_weight[1]) + matmul(nearby_1, neighbor_weight[1])
    state_2 = state_1[own] + jax.nn.silu(pre_1)
    final_half = state_2.astype(HALF)

    finals = (final_half,) + swap_all(*[final_half] * 4)
    decode_sum = matmul(to_grid[0], finals[0])
    for p in range(1, GROUPS):
        decode_sum = decode_sum + matmul(to_grid[p], finals[p])
    decode_in = decode_sum.astype(HALF)
    decode_pre = matmul(decode_in, decode_weight)
    hidden = jax.nn.silu(decode_pre).astype(HALF)
    prediction = (grid_vars.astype(SINGLE) + matmul(hidden, output_weight)).astype(HALF)
    hidden_grad = back_mul(cotangent, output_weight)
    decode_grad = (hidden_grad * silu_slope(decode_pre)).astype(HALF)
    decode_in_grad = back_mul(decode_grad, decode_weight).astype(HALF)
    sums = [outer_sum(to_grid[p], decode_in_grad) for p in range(GROUPS)]
    arrived = swap_all(*[block.astype(HALF) for block in sums[1:]])
    halves = [*split_gradients((cotangent, hidden), (decode_in, decode_grad))]
    state_grad = sums[0]
    for block in arrived:
        state_grad = state_grad + block.astype(SINGLE)

    layer_grad_1 = (state_grad * silu_slope(pre_1)).astype(HALF)
    state_grad_half = state_grad.astype(HALF)
    heads = jnp.concatenate([layer_grad_1[: 2 * rim], state_grad_half[:rim]], 0)
    tails = jnp.concatenate(
        [layer_grad_1[mesh_count - 2 * rim :], state_grad_half[mesh_count - rim :]], 0
    )
    on, off = sides_out(heads, tails)
    left, right = sides_in(swap_on(on), swap_off(off))
    halves += split_gradients((half_1[own], layer_grad_1), (nearby_1, layer_grad_1))
    layer_grad = jnp.concatenate([left[: 2 * rim], layer_grad_1, right[: 2 * rim]], 0)
    outside = jnp.zeros((rim, width), SINGLE)
    state_grad = jnp.concatenate(
        [
            outside,
            left[2 * rim :].astype(SINGLE),
            state_grad,
            right[2 * rim :].astype(SINGLE),
            outside,
        ],
        0,
    )
    spread = (matmul(counts, layer_grad) * (1.0 / NEAR)).astype(HALF)
    state_grad = (
        state_grad
        + back_mul(layer_grad, self_weight[1])
        + back_mul(spread, neighbor_weight[1])
    )
    layer_grad = (state_grad * silu_slope(pre_0)).astype(HALF)
    layer_grad_0 = layer_grad[own]
    spread = (matmul(counts[own], layer_grad) * (1.0 / NEAR)).astype(HALF)
    state_grad = (
        state_grad[own]
        + back_mul(layer_grad_0, self_weight[0])
        + back_mul(spread, neighbor_weight[0])
    )
    encode_grad = (state_grad * silu_slope(encode_pre)).astype(HALF)
    encode_in_grad = back_mul(encode_grad, encode_weight).astype(HALF)
    returned = (encode_in_grad,) + swap_all(*[encode_in_grad] * 4)
    halves += split_gradients(
        (half, layer_grad_0), (nearby_0[own], layer_grad_0), (encode_in, encode_grad)
    )
    latent_grad = outer_sum(to_mesh[0], returned[0])
    for p in range(1, GROUPS):
        latent_grad = latent_grad + outer_sum(to_mesh[p], returned[p])
    embed_grad = (latent_grad * slope_embed).astype(HALF)
    halves += split_gradients((grid_vars, embed_grad))

    rows = sum(block.shape[0] for block in halves[::2])
    (part,) = whole(add_halves, [shape(rows, width, HALF)], 0, *halves)
    part = reduce_all(part)
    other = swap_on(part)
    square = shape(width, width, SINGLE)
    pair = jax.ShapeDtypeStruct((2, width, width), SINGLE)
    narrow = shape(variables, width, SINGLE)
    grad_embed, grad_encode, grad_self, grad_near, grad_decode, grad_output = whole(
        unpack, [narrow, square, pair, pair, square, narrow], 0, part, other
    )
    return (
        prediction,
        state_grad,
        grad_embed,
        grad_encode,
        grad_self,
        grad_near,
        grad_decode,
        grad_output.T,
    )


def solution(mesh):
    placed = (
        P(("band", "dom"), None),
        P(("band", "dom"), None),
        P(("band", "dom"), None),
        P(),
        P(),
        P(),
        P(),
        P(),
        P(),
        P(("band", "dom")),
        P(("band", "dom")),
        P(("band", "dom"), None),
        P(("band", "dom")),
        P(("band", "dom")),
    )
    return jax.shard_map(
        shards,
        mesh=mesh,
        in_specs=placed,
        out_specs=(
            P(("band", "dom"), None),
            P(("band", "dom"), None),
            P(),
            P(),
            P(),
            P(),
            P(),
            P(),
        ),
        check_vma=False,
    )
```

time: 244 us -> 199 us (0.82)
  waiting for transfers between devices: 65.8 us -> 16.8 us
  blocking collectives: 38.5 us -> 65 us
  Pallas kernels: 0 us -> 19.7 us
  matrix products: 47.9 us -> 28.6 us
  other arithmetic: 15.5 us -> 2.07 us
  between operations: 14.8 us -> 1.51 us
  local copies, waits for them, and re-layouts: 9.08 us -> 14.1 us
    all_gather x1 -> x0, waiting for transfers between devices: 43.2 us -> none  [reduce_all(): lax.all_gather(piece, 'dom', axis=0, tiled=True, axis_index_groups=groups)]
    all_to_all x1 -> x2, blocking collectives: 27.3 us -> 54 us  [the longest x1 30.1 us: reduce_all(): lax.all_to_all(part.reshape(chips, -1, width), 'dom', 0, 0, axis_index_gr...]
    pallas_call x0 -> x15, Pallas kernels: none -> 19.7 us  [the longest x11 15.5 us: whole(): pl.pallas_call(body, out_shape=outs, compiler_params=pltpu.CompilerParams...]
    dot_general x30 -> x12, matrix products: 21.5 us -> 7.59 us  [matmul(): return jnp.dot(left, right, preferred_element_type=SINGLE)]
    unnamed x64 -> x108, local copies, waits for them, and re-layouts: 1.73 us -> 11.2 us
    ppermute x7 -> x6, waiting for transfers between devices: 14.5 us -> 5.91 us  [swap_off(): lax.ppermute(value, 'dom', [(i, (i + (1 if i % 2 else -1)) % count) for i...]
    ppermute x10 -> x8, waiting for transfers between devices: 0.03 us -> 7.12 us  [swap_band(): return lax.ppermute(value, 'band', pairs)]
    select_n x5 -> x0, other arithmetic: 5.88 us -> none  [the longest x1 1.8 us: reduce_all(): other = jnp.where(odd == 1, halves[0], halves[1])]
  transfers between devices with their start and end apart: 27 -> 25, of which waited for: 11 -> 8; matrix products, arithmetic and copies ran while one was open for 11% -> 10% of each run, Pallas kernels for 0% -> 7%
where the time goes in v2:
time: 199 us; the launch traced here: 198 us
  blocking collectives  65 us (33%)
  starting transfers between devices  50 us (25%)
  matrix products  28.6 us (14%)
  Pallas kernels  19.7 us (10%)
  waiting for transfers between devices  16.8 us (8%)
  local copies, waits for them, and re-layouts  14.1 us (7%)
  other arithmetic  2.07 us (1%)
    ppermute x11, starting transfers between devices, swap_on(): return lax.ppermute(value, 'dom', [(i, i ^ 1) for i in range(count)])  33.4 us
    all_to_all x1, blocking collectives, reduce_all(): lax.all_to_all(part.reshape(chips, -1, width), 'dom', 0, 0, axis_index_gr...  30.1 us
    all_to_all x1, blocking collectives, reduce_all(): lax.all_to_all(copies, 'dom', 0, 0, axis_index_groups=groups)  23.9 us
    pallas_call x11, Pallas kernels, whole(): pl.pallas_call(body, out_shape=outs, compiler_params=pltpu.CompilerParams...  15.5 us
    ppermute x8, starting transfers between devices, swap_band(): return lax.ppermute(value, 'band', pairs)  14.6 us
    dot_general x7, matrix products, back_mul(): lax.dot_general(left, right, (((1,), (1,)), ((), ())), preferred_element_...  12.9 us
    unnamed x108, local copies, waits for them, and re-layouts  11.2 us
    all_gather x1, blocking collectives, reduce_all(): pieces = lax.all_gather(piece, 'band', axis=0)  11 us
  transfers between devices with their start and end apart: 25, of which 8 were waited for; matrix products, arithmetic and copies ran while one was open for 10% of the time, Pallas kernels for 7%

profile of v2, /device:TPU:1, one launch (start us, length us, event | category | flops | bytes accessed | tf_op | source)
XLA Modules:
  0.0 197.7 jit_solution(3553730204579926808)
XLA Ops:
  0.7 1.1 copy.26.grid_ref.refs_0_
  2.5 0.7 copy-done.29
  3.2 0.7 copy-done.32
  4.7 0.9 shard_map.197
  5.5 1.4 collective-permute-start
  6.9 1.6 collective-permute-start.1
  8.5 1.2 collective-permute-start.2
  10.4 1.0 pad.4.refs_1_
  11.4 0.9 copy-done.26
  12.4 0.7 copy-done.30
  13.8 0.9 shard_map.198
  15.4 1.7 shard_map.199
  17.2 1.7 shard_map.200
  19.0 1.8 shard_map.201
  20.8 0.8 shard_map.202
  21.6 1.1 fusion.53
  22.8 5.4 %collective-permute-start.4 = (bf16[128,512]{1,0:T(8,128)(2,1)S(1)}, bf16[128,512]{1,0:T(8,128)(2,1)S(1)}, u32[]{:S(2)}, u32[]{:S(2)}) collective-permute-start(bf16[128,512]{1,0:T(8,128)(2,1)S(1)} %get-tuple-element.104), channel_id=1, source_target_pairs={{0,1},{1,0},{2,3},{3,2},{4,5},{5,4},{6,7},{7,6},{8,9},{9,8},{10,11... | collective-permute-start | bytes 393224 | tf_op jit(solution)/shard_map/ppermute | solution.py:40
  29.2 3.4 %collective-permute-done.5 = bf16[128,512]{1,0:T(8,128)(2,1)S(1)} collective-permute-done((bf16[128,512]{1,0:T(8,128)(2,1)S(1)}, bf16[128,512]{1,0:T(8,128)(2,1)S(1)}, u32[]{:S(2)}, u32[]{:S(2)}) %collective-permute-start.5) | collective-permute-done | bytes 131104 | tf_op jit(solution)/shard_map/ppermute | solution.py:45
  33.2 0.8 copy-done.41
  34.4 1.6 fusion.50
  36.6 1.2 fusion.16
  37.8 3.4 %collective-permute-start.6 = (bf16[256,512]{1,0:T(8,128)(2,1)S(1)}, bf16[256,512]{1,0:T(8,128)(2,1)S(1)}, u32[]{:S(2)}, u32[]{:S(2)}) collective-permute-start(bf16[256,512]{1,0:T(8,128)(2,1)S(1)} %get-tuple-element.108), channel_id=1, source_target_pairs={{0,1},{1,0},{2,3},{3,2},{4,5},{5,4},{6,7},{7,6},{8,9},{9,8},{10,11... | collective-permute-start | bytes 786440 | tf_op jit(solution)/shard_map/ppermute | solution.py:40
  41.2 1.4 shard_map.203
  43.3 5.0 %collective-permute-start.8 = (bf16[256,512]{1,0:T(8,128)(2,1)S(1)}, bf16[256,512]{1,0:T(8,128)(2,1)S(1)}, u32[]{:S(2)}, u32[]{:S(2)}) collective-permute-start(bf16[256,512]{1,0:T(8,128)(2,1)S(1)} %get-tuple-element.108), channel_id=1, source_target_pairs={{0,32},{32,0},{64,96},{96,64},{1,33},{33,1},{65,97},{97,65},{2,34}... | collective-permute-start | bytes 786440 | tf_op jit(solution)/shard_map/ppermute | solution.py:55
  49.2 5.8 %collective-permute-done.8 = bf16[256,512]{1,0:T(8,128)(2,1)S(1)} collective-permute-done((bf16[256,512]{1,0:T(8,128)(2,1)S(1)}, bf16[256,512]{1,0:T(8,128)(2,1)S(1)}, u32[]{:S(2)}, u32[]{:S(2)}) %collective-permute-start.8) | collective-permute-done | bytes 262176 | tf_op jit(solution)/shard_map/ppermute | solution.py:55
  57.6 1.0 convolution_convert_fusion.2
  58.7 1.0 convolution_convert_fusion.3
  59.7 1.0 convolution_convert_fusion.4
  61.0 1.4 collective-permute-start.13
  62.4 3.0 %collective-permute-start.12 = (bf16[256,512]{1,0:T(8,128)(2,1)}, bf16[256,512]{1,0:T(8,128)(2,1)}, u32[]{:S(2)}, u32[]{:S(2)}) collective-permute-start(bf16[256,512]{1,0:T(8,128)(2,1)} %convolution_convert_fusion.3), channel_id=1, source_target_pairs={{0,32},{32,0},{64,96},{96,64},{1,33},{33,1},{65,97},{97,65},{2,34}... | collective-permute-start | bytes 786440 | tf_op jit(solution)/shard_map/ppermute | solution.py:55
  65.4 2.4 %collective-permute-start.10 = (bf16[256,512]{1,0:T(8,128)(2,1)S(1)}, bf16[256,512]{1,0:T(8,128)(2,1)}, u32[]{:S(2)}, u32[]{:S(2)}) collective-permute-start(bf16[256,512]{1,0:T(8,128)(2,1)S(1)} %convolution_convert_fusion.5), channel_id=1, source_target_pairs={{0,1},{1,0},{2,3},{3,2},{4,5},{5,4},{6,7},{7,6},{8,9},{9,8},{10,11... | collective-permute-start | bytes 786440 | tf_op jit(solution)/shard_map/ppermute | solution.py:40
  67.8 1.1 copy.28.refs_0_
  68.9 1.4 collective-permute-done.12
  70.2 1.6 collective-permute-done.11
  71.8 2.1 %multiply_convert_fusion.3 = (bf16[256,512]{1,0:T(8,128)(2,1)S(1)}, bf16[256,512]{1,0:T(8,128)(2,1)S(1)}, f32[256,512]{1,0:T(8,128)S(1)}) fusion(f32[256,512]{1,0:T(8,128)} %get-tuple-element.109, bf16[256,512]{1,0:T(8,128)(2,1)} %collective-permute-done.13, bf16[256,512]{1,0:T(8,128)(2,1)} %collective-permute-done.12, ...), kind=kOutput, calls=%fused_computation.60 | convolution fusion | flops 136577024 | bytes 3407872 | tf_op jit(solution)/shard_map/dot_general | solution.py:27
  74.2 5.5 %collective-permute-start.14 = (bf16[192,512]{1,0:T(8,128)(2,1)S(1)}, bf16[192,512]{1,0:T(8,128)(2,1)S(1)}, u32[]{:S(2)}, u32[]{:S(2)}) collective-permute-start(bf16[192,512]{1,0:T(8,128)(2,1)S(1)} %get-tuple-element.97), channel_id=1, source_target_pairs={{0,1},{1,0},{2,3},{3,2},{4,5},{5,4},{6,7},{7,6},{8,9},{9,8},{10,11... | collective-permute-start | bytes 589832 | tf_op jit(solution)/shard_map/ppermute | solution.py:40
  79.7 1.0 shard_map.208
  81.5 0.7 slice.105.refs_2_
  82.4 1.5 shard_map.205
  83.9 0.7 copy-done.11
  84.6 1.4 shard_map.206
  86.8 1.4 convolution_add_fusion.1
  88.2 3.7 %multiply_convert_fusion = (bf16[512,512]{1,0:T(8,128)(2,1)}, f32[512,512]{1,0:T(8,128)}) fusion(f32[512,512]{1,0:T(8,128)} %get-tuple-element.107, f32[512,512]{1,0:T(8,128)} %convolution_add_fusion.1, bf16[2,512,512]{2,1,0:T(8,128)(2,1)} %param.20, bf16[512,512]{1,0:T(8,128)(2,1)S(1)} %copy-done.8, bf16[128,512]{1,0:T(8,128)(2,1)S(1)} %slice.101, ...), kind=kOutput, calls=%fused_computation.39 | convolution fusion | flops 541589504 | bytes 5242880 | tf_op jit(solution)/shard_map/dot_general | solution.py:33
  91.9 2.3 %fusion.25 = f32[256,512]{1,0:T(8,128)} fusion(bf16[2,512,512]{2,1,0:T(8,128)(2,1)} %param.19, bf16[512,512]{1,0:T(8,128)(2,1)} %get-tuple-element.113), kind=kOutput, calls=%fused_computation.56 | convolution fusion | flops 134217728 | bytes 1310720 | tf_op jit(solution)/shard_map/dot_general | solution.py:33
  94.2 1.0 slice.103.refs_1_.refs_3_
  95.2 3.2 %multiply_convert_fusion.2 = (bf16[256,512]{1,0:T(8,128)(2,1)S(1)}, f32[256,512]{1,0:T(8,128)}) fusion(f32[256,512]{1,0:T(8,128)} %get-tuple-element.106, bf16[2,512,512]{2,1,0:T(8,128)(2,1)} %param.20, bf16[512,512]{1,0:T(8,128)(2,1)} %get-tuple-element.113, bf16[512,512]{1,0:T(8,128)(2,1)} %copy-done.7, f32[256,512]{1,0:T(8,128)} %fusion.25, ...), kind=kOutput, calls=%fused_computation.59 | convolution fusion | flops 270139392 | bytes 3670016 | tf_op jit(solution)/shard_map/dot_general | solution.py:33
  98.3 1.4 convolution_convert_fusion.1
  99.8 0.8 collective-permute-start.22
  100.6 1.9 collective-permute-start.21
  102.5 2.0 collective-permute-start.19
  104.4 0.9 shard_map.207
  106.4 4.1 %collective-permute-start.18 = (bf16[768,512]{1,0:T(8,128)(2,1)S(1)}, bf16[768,512]{1,0:T(8,128)(2,1)S(1)}, u32[]{:S(2)}, u32[]{:S(2)}) collective-permute-start(bf16[768,512]{1,0:T(8,128)(2,1)S(1)} %get-tuple-element.69), channel_id=1, source_target_pairs={{0,1},{1,0},{2,3},{3,2},{4,5},{5,4},{6,7},{7,6},{8,9},{9,8},{10,11... | collective-permute-start | bytes 2359304 | tf_op jit(solution)/shard_map/ppermute | solution.py:40
  111.2 0.9 collective-permute-done.20
  112.9 3.1 %collective-permute-start.23 = (bf16[128,512]{1,0:T(8,128)(2,1)S(1)}, bf16[128,512]{1,0:T(8,128)(2,1)S(1)}, u32[]{:S(2)}, u32[]{:S(2)}) collective-permute-start(bf16[128,512]{1,0:T(8,128)(2,1)S(1)} %get-tuple-element.77), channel_id=1, source_target_pairs={{0,1},{1,0},{2,3},{3,2},{4,5},{5,4},{6,7},{7,6},{8,9},{9,8},{10,11... | collective-permute-start | bytes 393224 | tf_op jit(solution)/shard_map/ppermute | solution.py:40
  116.0 1.0 collective-permute-done.23.refs_7_
  117.0 1.5 shard_map.210
  118.5 30.1 %all_to_all.10 = bf16[16,112,512]{2,1,0:T(8,128)(2,1)} all-to-all(bf16[16,112,512]{2,1,0:T(8,128)(2,1)S(1)} %bitcast.87), channel_id=1, replica_groups={{0,2,4,6,8,10,12,14,16,18,20,22,24,26,28,30},{1,3,5,7,9,11,13,15,17,19,..., dimensions={0} | all-to-all | bytes 3670016 | tf_op jit(solution)/shard_map/all_to_all | solution.py:273
  148.6 1.8 reduce_sum.24
  150.3 11.0 %all-gather = bf16[448,512]{1,0:T(8,128)(2,1)S(1)} all-gather(bf16[112,512]{1,0:T(8,128)(2,1)S(1)} %reduce_sum.24), channel_id=2, replica_groups=mesh['band'=4,'dom'=32] {'band'}, dimensions={0}, use_global_device_ids=true | all-gather | bytes 573440 | tf_op jit(solution)/shard_map/all_gather | solution.py:277
  161.6 23.9 %all_to_all.11 = bf16[16,112,512]{2,1,0:T(8,128)(2,1)S(1)} all-to-all(bf16[16,112,512]{2,1,0:T(8,128)(2,1)S(1)} %broadcast_in_dim.10), channel_id=1, replica_groups={{0,2,4,6,8,10,12,14,16,18,20,22,24,26,28,30},{1,3,5,7,9,11,13,15,17,19,..., dimensions={0} | all-to-all | bytes 3670016 | tf_op jit(solution)/shard_map/all_to_all | solution.py:280
  185.5 5.6 %collective-permute-start.24 = (bf16[1792,512]{1,0:T(8,128)(2,1)S(1)}, bf16[1792,512]{1,0:T(8,128)(2,1)S(1)}, u32[]{:S(2)}, u32[]{:S(2)}) collective-permute-start(bf16[1792,512]{1,0:T(8,128)(2,1)S(1)} %bitcast.85), channel_id=1, source_target_pairs={{0,1},{1,0},{2,3},{3,2},{4,5},{5,4},{6,7},{7,6},{8,9},{9,8},{10,11... | collective-permute-start | bytes 5505032 | tf_op jit(solution)/shard_map/ppermute | solution.py:40
  191.1 1.0 fusion.15
  192.1 2.4 %collective-permute-done.24.other_ref = bf16[1792,512]{1,0:T(8,128)(2,1)S(1)} collective-permute-done((bf16[1792,512]{1,0:T(8,128)(2,1)S(1)}, bf16[1792,512]{1,0:T(8,128)(2,1)S(1)}, u32[]{:S(2)}, u32[]{:S(2)}) %collective-permute-start.24) | collective-permute-done | bytes 1835040 | tf_op jit(solution)/shard_map/ppermute | solution.py:40
  194.5 3.2 %shard_map.211 = (f32[227,512]{1,0:T(8,128)}, f32[512,512]{1,0:T(8,128)}, f32[2,512,512]{2,1,0:T(8,128)}, f32[2,512,512]{2,1,0:T(8,128)}, f32[512,512]{1,0:T(8,128)}, /*index=5*/f32[227,512]{1,0:T(8,128)}) custom-call(bf16[1792,512]{1,0:T(8,128)(2,1)S(1)} %bitcast.86, bf16[1792,512]{1,0:T(8,128)(2,1)S(1)} %collective-permute-done.24.other_ref), custom_call_target="tpu_custom_call" | custom-call | bytes 10891264 | tf_op jit(solution)/shard_map/pallas_call | solution.py:76
  (162 shorter events, 15.1 us)
Async XLA Ops:
  0.6 54.9 %copy-start = (bf16[512,512]{1,0:T(8,128)(2,1)S(1)}, bf16[512,512]{1,0:T(8,128)(2,1)}, u32[]{:S(2)}) copy-start(bf16[512,512]{1,0:T(8,128)(2,1)} %param.21) | copy-start | bytes 1572868
  0.6 14.8 %copy-start.31 = (s32[3840]{0:T(1024)S(1)}, s32[3840]{0:T(1024)}, u32[]{:S(2)}) copy-start(s32[3840]{0:T(1024)} %param.24) | copy-start | bytes 46084
  5.5 9.9 %collective-permute-start = (bf16[544,256]{1,0:T(8,128)(2,1)S(1)}, bf16[544,256]{1,0:T(8,128)(2,1)}, u32[]{:S(2)}, u32[]{:S(2)}) collective-permute-start(bf16[544,256]{1,0:T(8,128)(2,1)S(1)} %get-tuple-element.46), channel_id=1, source_target_pairs={{0,1},{1,0},{2,3},{3,2},{4,5},{5,4},{6,7},{7,6},{8,9},{9,8},{10,11... | collective-permute-start | bytes 835592 | tf_op jit(solution)/shard_map/ppermute | solution.py:40
  6.9 10.2 %collective-permute-start.1 = (bf16[544,256]{1,0:T(8,128)(2,1)}, bf16[544,256]{1,0:T(8,128)(2,1)}, u32[]{:S(2)}, u32[]{:S(2)}) collective-permute-start(bf16[544,256]{1,0:T(8,128)(2,1)} %get-tuple-element.49), channel_id=1, source_target_pairs={{0,31},{1,2},{2,1},{3,4},{4,3},{5,6},{6,5},{7,8},{8,7},{9,10},{10,... | collective-permute-start | bytes 835592 | tf_op jit(solution)/shard_map/ppermute | solution.py:45
  8.5 10.4 %collective-permute-start.2 = (bf16[544,256]{1,0:T(8,128)(2,1)S(1)}, bf16[544,256]{1,0:T(8,128)(2,1)}, u32[]{:S(2)}, u32[]{:S(2)}) collective-permute-start(bf16[544,256]{1,0:T(8,128)(2,1)S(1)} %get-tuple-element.52), channel_id=1, source_target_pairs={{0,32},{32,0},{64,96},{96,64},{1,33},{33,1},{65,97},{97,65},{2,34}... | collective-permute-start | bytes 835592 | tf_op jit(solution)/shard_map/ppermute | solution.py:55
  9.8 11.0 %collective-permute-start.3 = (bf16[544,256]{1,0:T(8,128)(2,1)S(1)}, bf16[544,256]{1,0:T(8,128)(2,1)S(1)}, u32[]{:S(2)}, u32[]{:S(2)}) collective-permute-start(bf16[544,256]{1,0:T(8,128)(2,1)S(1)} %get-tuple-element.55), channel_id=1, source_target_pairs={{32,64},{64,32},{33,65},{65,33},{34,66},{66,34},{35,67},{67,35},{3... | collective-permute-start | bytes 835592 | tf_op jit(solution)/shard_map/ppermute | solution.py:55
  11.4 0.9 copy-start.26
  18.9 2.7 %copy-start.46 = (bf16[512,512]{1,0:T(8,128)(2,1)S(1)}, bf16[512,512]{1,0:T(8,128)(2,1)}, u32[]{:S(2)}) copy-start(bf16[512,512]{1,0:T(8,128)(2,1)} %param.18) | copy-start | bytes 1572868
  18.9 2.7 %copy-start.51 = (bf16[256,512]{1,0:T(8,128)(2,1)S(1)}, bf16[256,512]{1,0:T(8,128)(2,1)}, u32[]{:S(2)}) copy-start(bf16[256,512]{1,0:T(8,128)(2,1)} %param.16) | copy-start | bytes 786436
  21.6 1.2 copy-start.2
  21.6 6.6 %copy-start.28 = (s32[256,6]{0,1:T(8,128)S(1)}, s32[256,6]{0,1:T(8,128)}, u32[]{:S(2)}) copy-start(s32[256,6]{0,1:T(8,128)} %param.25) | copy-start | bytes 18436
  22.7 11.7 %copy-start.4 = (bf16[256,512]{1,0:T(8,128)(2,1)}, bf16[256,512]{1,0:T(8,128)(2,1)S(1)}, u32[]{:S(2)}) copy-start(bf16[256,512]{1,0:T(8,128)(2,1)S(1)} %get-tuple-element.90.refs_0_) | copy-start | bytes 786436
  22.8 6.4 %collective-permute-start.4 = (bf16[128,512]{1,0:T(8,128)(2,1)S(1)}, bf16[128,512]{1,0:T(8,128)(2,1)S(1)}, u32[]{:S(2)}, u32[]{:S(2)}) collective-permute-start(bf16[128,512]{1,0:T(8,128)(2,1)S(1)} %get-tuple-element.104), channel_id=1, source_target_pairs={{0,1},{1,0},{2,3},{3,2},{4,5},{5,4},{6,7},{7,6},{8,9},{9,8},{10,11... | collective-permute-start | bytes 393224 | tf_op jit(solution)/shard_map/ppermute | solution.py:40
  28.2 4.4 %collective-permute-start.5 = (bf16[128,512]{1,0:T(8,128)(2,1)S(1)}, bf16[128,512]{1,0:T(8,128)(2,1)S(1)}, u32[]{:S(2)}, u32[]{:S(2)}) collective-permute-start(bf16[128,512]{1,0:T(8,128)(2,1)S(1)} %get-tuple-element.105), channel_id=1, source_target_pairs={{0,31},{1,2},{2,1},{3,4},{4,3},{5,6},{6,5},{7,8},{8,7},{9,10},{10,... | collective-permute-start | bytes 393224 | tf_op jit(solution)/shard_map/ppermute | solution.py:45
  28.8 7.4 %copy-start.7 = (bf16[512,512]{1,0:T(8,128)(2,1)}, bf16[512,512]{1,0:T(8,128)(2,1)S(1)}, u32[]{:S(2)}) copy-start(bf16[512,512]{1,0:T(8,128)(2,1)S(1)} %shard_map.204) | copy-start | bytes 1572868
  28.8 5.1 %copy-start.47 = (bf16[2,512,512]{2,1,0:T(8,128)(2,1)S(1)}, bf16[2,512,512]{2,1,0:T(8,128)(2,1)}, u32[]{:S(2)}) copy-start(bf16[2,512,512]{2,1,0:T(8,128)(2,1)} %param.20) | copy-start | bytes 3145732
  32.7 1.7 copy-start.39
  36.0 1.8 copy-start.44
  36.6 1.2 copy-start.20
  36.6 4.6 %copy-start.33 = (s32[3840]{0:T(1024)S(1)}, s32[3840]{0:T(1024)}, u32[]{:S(2)}) copy-start(s32[3840]{0:T(1024)} %param.26) | copy-start | bytes 46084
  36.6 4.6 %copy-start.37 = (s32[3840]{0:T(1024)S(1)}, s32[3840]{0:T(1024)}, u32[]{:S(2)}) copy-start(s32[3840]{0:T(1024)} %param.27) | copy-start | bytes 46084
  37.8 10.5 %collective-permute-start.6 = (bf16[256,512]{1,0:T(8,128)(2,1)S(1)}, bf16[256,512]{1,0:T(8,128)(2,1)S(1)}, u32[]{:S(2)}, u32[]{:S(2)}) collective-permute-start(bf16[256,512]{1,0:T(8,128)(2,1)S(1)} %get-tuple-element.108), channel_id=1, source_target_pairs={{0,1},{1,0},{2,3},{3,2},{4,5},{5,4},{6,7},{7,6},{8,9},{9,8},{10,11... | collective-permute-start | bytes 786440 | tf_op jit(solution)/shard_map/ppermute | solution.py:40
  42.6 12.6 %copy-start.17 = (bf16[512,256]{1,0:T(8,128)(2,1)}, bf16[512,256]{1,0:T(8,128)(2,1)S(1)}, u32[]{:S(2)}) copy-start(bf16[512,256]{1,0:T(8,128)(2,1)S(1)} %get-tuple-element.58) | copy-start | bytes 786436
  42.7 6.2 %collective-permute-start.9 = (bf16[256,512]{1,0:T(8,128)(2,1)S(1)}, bf16[256,512]{1,0:T(8,128)(2,1)S(1)}, u32[]{:S(2)}, u32[]{:S(2)}) collective-permute-start(bf16[256,512]{1,0:T(8,128)(2,1)S(1)} %get-tuple-element.108), channel_id=1, source_target_pairs={{32,64},{64,32},{33,65},{65,33},{34,66},{66,34},{35,67},{67,35},{3... | collective-permute-start | bytes 786440 | tf_op jit(solution)/shard_map/ppermute | solution.py:55
  43.3 11.6 %collective-permute-start.8 = (bf16[256,512]{1,0:T(8,128)(2,1)S(1)}, bf16[256,512]{1,0:T(8,128)(2,1)S(1)}, u32[]{:S(2)}, u32[]{:S(2)}) collective-permute-start(bf16[256,512]{1,0:T(8,128)(2,1)S(1)} %get-tuple-element.108), channel_id=1, source_target_pairs={{0,32},{32,0},{64,96},{96,64},{1,33},{33,1},{65,97},{97,65},{2,34}... | collective-permute-start | bytes 786440 | tf_op jit(solution)/shard_map/ppermute | solution.py:55
  48.3 6.9 %collective-permute-start.7 = (bf16[256,512]{1,0:T(8,128)(2,1)S(1)}, bf16[256,512]{1,0:T(8,128)(2,1)S(1)}, u32[]{:S(2)}, u32[]{:S(2)}) collective-permute-start(bf16[256,512]{1,0:T(8,128)(2,1)S(1)} %get-tuple-element.108), channel_id=1, source_target_pairs={{0,31},{1,2},{2,1},{3,4},{4,3},{5,6},{6,5},{7,8},{8,7},{9,10},{10,... | collective-permute-start | bytes 786440 | tf_op jit(solution)/shard_map/ppermute | solution.py:45
  55.6 1.0 copy-start.50
  57.6 7.8 %copy-start.38 = (bf16[512,512]{1,0:T(8,128)(2,1)}, bf16[512,512]{1,0:T(8,128)(2,1)S(1)}, u32[]{:S(2)}) copy-start(bf16[512,512]{1,0:T(8,128)(2,1)S(1)} %convolution_convert_fusion) | copy-start | bytes 1572868
  61.0 7.8 %collective-permute-start.13 = (bf16[256,512]{1,0:T(8,128)(2,1)}, bf16[256,512]{1,0:T(8,128)(2,1)}, u32[]{:S(2)}, u32[]{:S(2)}) collective-permute-start(bf16[256,512]{1,0:T(8,128)(2,1)} %convolution_convert_fusion.2), channel_id=1, source_target_pairs={{32,64},{64,32},{33,65},{65,33},{34,66},{66,34},{35,67},{67,35},{3... | collective-permute-start | bytes 786440 | tf_op jit(solution)/shard_map/ppermute | solution.py:55
  62.4 7.8 %collective-permute-start.12 = (bf16[256,512]{1,0:T(8,128)(2,1)}, bf16[256,512]{1,0:T(8,128)(2,1)}, u32[]{:S(2)}, u32[]{:S(2)}) collective-permute-start(bf16[256,512]{1,0:T(8,128)(2,1)} %convolution_convert_fusion.3), channel_id=1, source_target_pairs={{0,32},{32,0},{64,96},{96,64},{1,33},{33,1},{65,97},{97,65},{2,34}... | collective-permute-start | bytes 786440 | tf_op jit(solution)/shard_map/ppermute | solution.py:55
  65.4 6.4 %collective-permute-start.11 = (bf16[256,512]{1,0:T(8,128)(2,1)}, bf16[256,512]{1,0:T(8,128)(2,1)}, u32[]{:S(2)}, u32[]{:S(2)}) collective-permute-start(bf16[256,512]{1,0:T(8,128)(2,1)} %convolution_convert_fusion.4), channel_id=1, source_target_pairs={{0,31},{1,2},{2,1},{3,4},{4,3},{5,6},{6,5},{7,8},{8,7},{9,10},{10,... | collective-permute-start | bytes 786440 | tf_op jit(solution)/shard_map/ppermute | solution.py:45
  65.4 6.4 %collective-permute-start.10 = (bf16[256,512]{1,0:T(8,128)(2,1)S(1)}, bf16[256,512]{1,0:T(8,128)(2,1)}, u32[]{:S(2)}, u32[]{:S(2)}) collective-permute-start(bf16[256,512]{1,0:T(8,128)(2,1)S(1)} %convolution_convert_fusion.5), channel_id=1, source_target_pairs={{0,1},{1,0},{2,3},{3,2},{4,5},{5,4},{6,7},{7,6},{8,9},{9,8},{10,11... | collective-permute-start | bytes 786440 | tf_op jit(solution)/shard_map/ppermute | solution.py:40
  71.8 7.9 %copy-start.36 = (s32[3840]{0:T(1024)S(1)}, s32[3840]{0:T(1024)}, u32[]{:S(2)}) copy-start(s32[3840]{0:T(1024)} %param.23) | copy-start | bytes 46084
  74.0 7.4 %copy-start.45 = (bf16[512,512]{1,0:T(8,128)(2,1)S(1)}, bf16[512,512]{1,0:T(8,128)(2,1)}, u32[]{:S(2)}) copy-start(bf16[512,512]{1,0:T(8,128)(2,1)} %copy-done.44) | copy-start | bytes 1572868
  74.1 7.4 %copy-start.42 = (bf16[512,512]{1,0:T(8,128)(2,1)S(1)}, bf16[512,512]{1,0:T(8,128)(2,1)}, u32[]{:S(2)}) copy-start(bf16[512,512]{1,0:T(8,128)(2,1)} %copy-done.41) | copy-start | bytes 1572868
  74.1 12.5 %collective-permute-start.15 = (bf16[192,512]{1,0:T(8,128)(2,1)S(1)}, bf16[192,512]{1,0:T(8,128)(2,1)S(1)}, u32[]{:S(2)}, u32[]{:S(2)}) collective-permute-start(bf16[192,512]{1,0:T(8,128)(2,1)S(1)} %get-tuple-element.96), channel_id=1, source_target_pairs={{0,31},{1,2},{2,1},{3,4},{4,3},{5,6},{6,5},{7,8},{8,7},{9,10},{10,... | collective-permute-start | bytes 589832 | tf_op jit(solution)/shard_map/ppermute | solution.py:45
  74.2 12.4 %collective-permute-start.14 = (bf16[192,512]{1,0:T(8,128)(2,1)S(1)}, bf16[192,512]{1,0:T(8,128)(2,1)S(1)}, u32[]{:S(2)}, u32[]{:S(2)}) collective-permute-start(bf16[192,512]{1,0:T(8,128)(2,1)S(1)} %get-tuple-element.97), channel_id=1, source_target_pairs={{0,1},{1,0},{2,3},{3,2},{4,5},{5,4},{6,7},{7,6},{8,9},{9,8},{10,11... | collective-permute-start | bytes 589832 | tf_op jit(solution)/shard_map/ppermute | solution.py:40
  81.4 1.0 copy-start.24
  81.5 3.2 %copy-start.21 = (bf16[256,512]{1,0:T(8,128)(2,1)S(1)}, bf16[256,512]{1,0:T(8,128)(2,1)}, u32[]{:S(2)}) copy-start(bf16[256,512]{1,0:T(8,128)(2,1)} %copy-done.20) | copy-start | bytes 786436
  84.6 2.2 %copy-start.40 = (bf16[2,512,512]{2,1,0:T(8,128)(2,1)S(1)}, bf16[2,512,512]{2,1,0:T(8,128)(2,1)}, u32[]{:S(2)}) copy-start(bf16[2,512,512]{2,1,0:T(8,128)(2,1)} %param.19) | copy-start | bytes 3145732
  84.6 31.4 %collective-permute-start.16 = (bf16[384,512]{1,0:T(8,128)(2,1)}, bf16[384,512]{1,0:T(8,128)(2,1)S(1)}, u32[]{:S(2)}, u32[]{:S(2)}) collective-permute-start(bf16[384,512]{1,0:T(8,128)(2,1)} %get-tuple-element.65), channel_id=1, source_target_pairs={{0,1},{1,0},{2,3},{3,2},{4,5},{5,4},{6,7},{7,6},{8,9},{9,8},{10,11... | collective-permute-start | bytes 1179656 | tf_op jit(solution)/shard_map/ppermute | solution.py:40
  86.1 2.2 %copy-start.9 = (bf16[512,512]{1,0:T(8,128)(2,1)}, bf16[512,512]{1,0:T(8,128)(2,1)S(1)}, u32[]{:S(2)}) copy-start(bf16[512,512]{1,0:T(8,128)(2,1)S(1)} %get-tuple-element.66.refs_2_) | copy-start | bytes 1572868
  86.1 30.0 %collective-permute-start.17 = (bf16[512,512]{1,0:T(8,128)(2,1)}, bf16[512,512]{1,0:T(8,128)(2,1)}, u32[]{:S(2)}, u32[]{:S(2)}) collective-permute-start(bf16[512,512]{1,0:T(8,128)(2,1)} %get-tuple-element.67), channel_id=1, source_target_pairs={{0,1},{1,0},{2,3},{3,2},{4,5},{5,4},{6,7},{7,6},{8,9},{9,8},{10,11... | collective-permute-start | bytes 1572872 | tf_op jit(solution)/shard_map/ppermute | solution.py:40
  86.7 1.5 copy-start.8
  95.1 9.3 %copy-start.3 = (bf16[256,512]{1,0:T(8,128)(2,1)S(1)}, bf16[256,512]{1,0:T(8,128)(2,1)}, u32[]{:S(2)}) copy-start(bf16[256,512]{1,0:T(8,128)(2,1)} %copy-done.2) | copy-start | bytes 786436
  95.1 9.3 %copy-start.5 = (bf16[256,512]{1,0:T(8,128)(2,1)S(1)}, bf16[256,512]{1,0:T(8,128)(2,1)}, u32[]{:S(2)}) copy-start(bf16[256,512]{1,0:T(8,128)(2,1)} %copy-done.4) | copy-start | bytes 786436
  95.1 9.3 %copy-start.6 = (bf16[256,512]{1,0:T(8,128)(2,1)S(1)}, bf16[256,512]{1,0:T(8,128)(2,1)}, u32[]{:S(2)}) copy-start(bf16[256,512]{1,0:T(8,128)(2,1)} %slice.105.refs_2_) | copy-start | bytes 786436
  98.3 7.0 %copy-start.19 = (bf16[256,512]{1,0:T(8,128)(2,1)S(1)}, bf16[256,512]{1,0:T(8,128)(2,1)}, u32[]{:S(2)}) copy-start(bf16[256,512]{1,0:T(8,128)(2,1)} %copy-done.18) | copy-start | bytes 786436
  99.8 6.2 %copy-start.16 = (bf16[256,512]{1,0:T(8,128)(2,1)S(1)}, bf16[256,512]{1,0:T(8,128)(2,1)}, u32[]{:S(2)}) copy-start(bf16[256,512]{1,0:T(8,128)(2,1)} %copy-done.15) | copy-start | bytes 786436
  99.8 6.6 %collective-permute-start.22 = (bf16[256,512]{1,0:T(8,128)(2,1)S(1)}, bf16[256,512]{1,0:T(8,128)(2,1)S(1)}, u32[]{:S(2)}, u32[]{:S(2)}) collective-permute-start(bf16[256,512]{1,0:T(8,128)(2,1)S(1)} %convolution_convert_fusion.1), channel_id=1, source_target_pairs={{32,64},{64,32},{33,65},{65,33},{34,66},{66,34},{35,67},{67,35},{3... | collective-permute-start | bytes 786440 | tf_op jit(solution)/shard_map/ppermute | solution.py:55
  100.6 10.2 %collective-permute-start.21 = (bf16[256,512]{1,0:T(8,128)(2,1)S(1)}, bf16[256,512]{1,0:T(8,128)(2,1)S(1)}, u32[]{:S(2)}, u32[]{:S(2)}) collective-permute-start(bf16[256,512]{1,0:T(8,128)(2,1)S(1)} %convolution_convert_fusion.1), channel_id=1, source_target_pairs={{0,32},{32,0},{64,96},{96,64},{1,33},{33,1},{65,97},{97,65},{2,34}... | collective-permute-start | bytes 786440 | tf_op jit(solution)/shard_map/ppermute | solution.py:55
  102.5 3.2 %collective-permute-start.19 = (bf16[256,512]{1,0:T(8,128)(2,1)S(1)}, bf16[256,512]{1,0:T(8,128)(2,1)S(1)}, u32[]{:S(2)}, u32[]{:S(2)}) collective-permute-start(bf16[256,512]{1,0:T(8,128)(2,1)S(1)} %convolution_convert_fusion.1), channel_id=1, source_target_pairs={{0,1},{1,0},{2,3},{3,2},{4,5},{5,4},{6,7},{7,6},{8,9},{9,8},{10,11... | collective-permute-start | bytes 786440 | tf_op jit(solution)/shard_map/ppermute | solution.py:40
  105.3 5.2 %copy-start.25 = (bf16[256,512]{1,0:T(8,128)(2,1)S(1)}, bf16[256,512]{1,0:T(8,128)(2,1)}, u32[]{:S(2)}) copy-start(bf16[256,512]{1,0:T(8,128)(2,1)} %copy-done.24) | copy-start | bytes 786436
  105.7 6.4 %collective-permute-start.20 = (bf16[256,512]{1,0:T(8,128)(2,1)S(1)}, bf16[256,512]{1,0:T(8,128)(2,1)S(1)}, u32[]{:S(2)}, u32[]{:S(2)}) collective-permute-start(bf16[256,512]{1,0:T(8,128)(2,1)S(1)} %convolution_convert_fusion.1), channel_id=1, source_target_pairs={{0,31},{1,2},{2,1},{3,4},{4,3},{5,6},{6,5},{7,8},{8,7},{9,10},{10,... | collective-permute-start | bytes 786440 | tf_op jit(solution)/shard_map/ppermute | solution.py:45
  106.0 4.8 %copy-start.23 = (bf16[256,512]{1,0:T(8,128)(2,1)S(1)}, bf16[256,512]{1,0:T(8,128)(2,1)}, u32[]{:S(2)}) copy-start(bf16[256,512]{1,0:T(8,128)(2,1)} %copy-done.22) | copy-start | bytes 786436
  106.4 5.7 %copy-start.14 = (bf16[256,512]{1,0:T(8,128)(2,1)S(1)}, bf16[256,512]{1,0:T(8,128)(2,1)}, u32[]{:S(2)}) copy-start(bf16[256,512]{1,0:T(8,128)(2,1)} %copy-done.13) | copy-start | bytes 786436
  106.4 10.7 %collective-permute-start.18 = (bf16[768,512]{1,0:T(8,128)(2,1)S(1)}, bf16[768,512]{1,0:T(8,128)(2,1)S(1)}, u32[]{:S(2)}, u32[]{:S(2)}) collective-permute-start(bf16[768,512]{1,0:T(8,128)(2,1)S(1)} %get-tuple-element.69), channel_id=1, source_target_pairs={{0,1},{1,0},{2,3},{3,2},{4,5},{5,4},{6,7},{7,6},{8,9},{9,8},{10,11... | collective-permute-start | bytes 2359304 | tf_op jit(solution)/shard_map/ppermute | solution.py:40
  112.1 5.0 %copy-start.10 = (bf16[512,512]{1,0:T(8,128)(2,1)S(1)}, bf16[512,512]{1,0:T(8,128)(2,1)}, u32[]{:S(2)}) copy-start(bf16[512,512]{1,0:T(8,128)(2,1)} %copy-done.9) | copy-start | bytes 1572868
  112.1 5.0 %copy-start.12 = (bf16[384,512]{1,0:T(8,128)(2,1)S(1)}, bf16[384,512]{1,0:T(8,128)(2,1)}, u32[]{:S(2)}) copy-start(bf16[384,512]{1,0:T(8,128)(2,1)} %copy-done.11) | copy-start | bytes 1179652
  112.9 4.1 %collective-permute-start.23 = (bf16[128,512]{1,0:T(8,128)(2,1)S(1)}, bf16[128,512]{1,0:T(8,128)(2,1)S(1)}, u32[]{:S(2)}, u32[]{:S(2)}) collective-permute-start(bf16[128,512]{1,0:T(8,128)(2,1)S(1)} %get-tuple-element.77), channel_id=1, source_target_pairs={{0,1},{1,0},{2,3},{3,2},{4,5},{5,4},{6,7},{7,6},{8,9},{9,8},{10,11... | collective-permute-start | bytes 393224 | tf_op jit(solution)/shard_map/ppermute | solution.py:40
  161.6 29.5 %copy-start.43 = (bf16[512,227]{0,1:T(8,128)(2,1)S(1)}, bf16[512,227]{0,1:T(8,128)(2,1)}, u32[]{:S(2)}) copy-start(bf16[512,227]{0,1:T(8,128)(2,1)} %param.14) | copy-start | bytes 697348
  161.6 29.5 %copy-start.49 = (bf16[512,227]{0,1:T(8,128)(2,1)S(1)}, bf16[512,227]{0,1:T(8,128)(2,1)}, u32[]{:S(2)}) copy-start(bf16[512,227]{0,1:T(8,128)(2,1)} %param.22) | copy-start | bytes 697348
  185.5 9.0 %collective-permute-start.24 = (bf16[1792,512]{1,0:T(8,128)(2,1)S(1)}, bf16[1792,512]{1,0:T(8,128)(2,1)S(1)}, u32[]{:S(2)}, u32[]{:S(2)}) collective-permute-start(bf16[1792,512]{1,0:T(8,128)(2,1)S(1)} %bitcast.85), channel_id=1, source_target_pairs={{0,1},{1,0},{2,3},{3,2},{4,5},{5,4},{6,7},{7,6},{8,9},{9,8},{10,11... | collective-permute-start | bytes 5505032 | tf_op jit(solution)/shard_map/ppermute | solution.py:40
  191.1 6.6 %copy-start.1 = (bf16[512,512]{1,0:T(8,128)(2,1)S(1)}, bf16[512,512]{1,0:T(8,128)(2,1)}, u32[]{:S(2)}) copy-start(bf16[512,512]{1,0:T(8,128)(2,1)} %param.21) | copy-start | bytes 1572868
  (13 other events, 9.8 us)

commit v3 on v2

v3 whole, which is shorter than its diff:
```python
import jax
import jax.numpy as jnp
from jax import lax
from jax.experimental import pallas as pl
from jax.experimental.pallas import tpu as pltpu
from jax.sharding import PartitionSpec as P

NEAR = 6
RIM = 64
GROUPS = 5
LANES = 128
HALF = jnp.bfloat16
SINGLE = jnp.float32
MIB = 1024 * 1024
SLOT_ROWS = 6
INDEX_ROWS = 32


def silu_slope(values):
    sigma = jax.nn.sigmoid(values)
    return sigma * (1.0 + values * (1.0 - sigma))


def matmul(left, right):
    return jnp.dot(left, right, preferred_element_type=SINGLE)


def outer_sum(left, right):
    return lax.dot_general(
        left, right, (((0,), (0,)), ((), ())), preferred_element_type=SINGLE
    )


def back_mul(left, right):
    return lax.dot_general(
        left, right, (((1,), (1,)), ((), ())), preferred_element_type=SINGLE
    )


def swap_on(value):
    count = lax.axis_size("dom")
    return lax.ppermute(value, "dom", [(i, i ^ 1) for i in range(count)])


def swap_off(value):
    count = lax.axis_size("dom")
    return lax.ppermute(
        value, "dom", [(i, (i + (1 if i % 2 else -1)) % count) for i in range(count)]
    )


def swap_band(value, first):
    count = lax.axis_size("band")
    pairs = []
    for low in range(first, count - 1, 2):
        pairs += [(low, low + 1), (low + 1, low)]
    return lax.ppermute(value, "band", pairs)


def swap_all(on, off, north, south):
    return swap_on(on), swap_off(off), swap_band(north, 0), swap_band(south, 1)


def by_partner(slots, odd_dom, odd_band, incoming):
    flip_dom = odd_dom != incoming
    flip_band = odd_band != incoming
    return [
        slots[0],
        jnp.where(flip_dom, slots[2], slots[1]),
        jnp.where(flip_dom, slots[1], slots[2]),
        jnp.where(flip_band, slots[4], slots[3]),
        jnp.where(flip_band, slots[3], slots[4]),
    ]


def whole(body, outs, macs, *args, limit=32, scratch=()):
    moved = sum(a.size * a.dtype.itemsize for a in (*args, *outs))
    return pl.pallas_call(
        body,
        out_shape=outs,
        scratch_shapes=scratch,
        compiler_params=pltpu.CompilerParams(vmem_limit_bytes=limit * MIB),
        cost_estimate=pl.CostEstimate(flops=2 * macs, bytes_accessed=moved, transcendentals=0),
    )(*args)


def shape(rows, columns, kind):
    return jax.ShapeDtypeStruct((rows, columns), kind)


def odd_along(axis):
    return lax.axis_index(axis) % 2 == 1


def hot(rows, index):
    spots = lax.broadcasted_iota(jnp.int32, (rows, LANES), 0)
    one = [
        jnp.where(spots == index[j : j + 1], 1.0, 0.0).astype(HALF) for j in range(index.shape[0])
    ]
    return jnp.concatenate(one, 1)


def pair_counts(rows, row_count, columns, column_count):
    return back_mul(hot(row_count, rows), hot(column_count, columns)).astype(HALF)


def slots_of(index):
    step = index.shape[0] // GROUPS
    return [index[k * step : (k + 1) * step] for k in range(GROUPS)]


def fetch(sources, buffers, sems):
    copies = [
        pltpu.make_async_copy(source, buffer, sems.at[i])
        for i, (source, buffer) in enumerate(zip(sources, buffers, strict=True))
    ]
    for copy in copies:
        copy.start()
    for copy in copies:
        copy.wait()


def fetching(body, outs, macs, *args):
    moved = sum(a.size * a.dtype.itemsize for a in (*args, *outs))
    return pl.pallas_call(
        body,
        out_shape=outs,
        in_specs=[pl.BlockSpec(memory_space=pl.ANY)] * len(args),
        scratch_shapes=[pltpu.VMEM(a.shape, a.dtype) for a in args]
        + [pltpu.SemaphoreType.DMA((len(args),))],
        compiler_params=pltpu.CompilerParams(vmem_limit_bytes=32 * MIB),
        cost_estimate=pl.CostEstimate(flops=2 * macs, bytes_accessed=moved, transcendentals=0),
    )(*args)


def parcels(*refs):
    inputs, rest = refs[:5], refs[5:]
    outs, buffers, sems = rest[: GROUPS - 1], rest[GROUPS - 1 : -1], rest[-1]
    fetch(inputs, buffers, sems)
    grid_ref, grid_send_ref, mesh_recv_ref, mesh_send_ref, near_ref = buffers
    odd_dom, odd_band = odd_along("dom"), odd_along("band")
    grid_send = by_partner(slots_of(grid_send_ref[...]), odd_dom, odd_band, False)
    mesh_recv = by_partner(slots_of(mesh_recv_ref[...]), odd_dom, odd_band, True)
    mesh_send = by_partner(slots_of(mesh_send_ref[...]), odd_dom, odd_band, False)
    near = near_ref[...]
    near = [near[:, j : j + LANES] for j in range(0, near.shape[1], LANES)]
    variables, count = grid_ref.shape
    first = outs[0].shape[0] - INDEX_ROWS // 2
    grid = grid_ref[...]
    for p, out in enumerate(outs):
        parts = [mesh_recv[p + 1], mesh_send[p + 1], grid_send[p + 1], *near]
        used = sum(part.shape[0] for part in parts)
        parts.append(jnp.zeros((INDEX_ROWS - used, LANES), jnp.int32))
        index = jnp.concatenate(parts, 0)
        high = (index >> 1).astype(SINGLE)
        low = (index & 1).astype(SINGLE)
        cut = INDEX_ROWS // 2
        out[:variables] = grid
        out[variables:first] = jnp.zeros((first - variables, count), HALF)
        out[first:] = jnp.concatenate([high[:cut], low[:cut], high[cut:], low[cut:]], 1).astype(HALF)


def index_of(packed):
    packed = packed.astype(SINGLE)
    halves = [
        packed[:, j : j + LANES] * 2.0 + packed[:, j + LANES : j + 2 * LANES]
        for j in (0, 2 * LANES)
    ]
    return jnp.concatenate(halves, 0).astype(jnp.int32)


def embed_own(*refs):
    inputs, (slope_ref, sum_ref), buffers, sems = refs[:4], refs[4:6], refs[6:-1], refs[-1]
    fetch(inputs, buffers, sems)
    grid_ref, weight_ref, send_ref, recv_ref = buffers
    step = send_ref.shape[0] // GROUPS
    counts = pair_counts(
        recv_ref[:step], sum_ref.shape[0], send_ref[:step], grid_ref.shape[1]
    )
    pre = outer_sum(grid_ref[...], weight_ref[...])
    sigma = jax.nn.sigmoid(pre)
    slope_ref[...] = sigma * (1.0 + pre * (1.0 - sigma))
    sum_ref[...] = matmul(counts, (pre * sigma).astype(HALF))


def embed_far(p, parcel_ref, weight_ref, recv_ref, sum_ref, index_ref, out_ref):
    index = index_of(parcel_ref[parcel_ref.shape[0] - INDEX_ROWS // 2 :])
    index_ref[...] = index
    step = recv_ref.shape[0] // GROUPS
    recv = by_partner(slots_of(recv_ref[...]), odd_along("dom"), odd_along("band"), True)[p]
    counts = pair_counts(
        recv, out_ref.shape[0], index[2 * step : 3 * step], parcel_ref.shape[1]
    )
    pre = outer_sum(parcel_ref[: weight_ref.shape[0]], weight_ref[...])
    latent = (pre * jax.nn.sigmoid(pre)).astype(HALF)
    out_ref[...] = sum_ref[...] + matmul(counts, latent)


def encode(sum_ref, weight_ref, static_ref, in_ref, slope_ref, state_ref, half_ref, on_ref, off_ref):
    encode_in = sum_ref[...].astype(HALF)
    pre = matmul(encode_in, weight_ref[...])
    sigma = jax.nn.sigmoid(pre)
    state = static_ref[...].astype(SINGLE) + pre * sigma
    half = state.astype(HALF)
    in_ref[...] = encode_in
    slope_ref[...] = sigma * (1.0 + pre * (1.0 - sigma))
    state_ref[...] = state
    half_ref[...] = half
    rows = on_ref.shape[0]
    odd = odd_along("dom")
    head, tail = half[:rows], half[half.shape[0] - rows :]
    on_ref[...] = jnp.where(odd, head, tail)
    off_ref[...] = jnp.where(odd, tail, head)


def near_counts(near_ref, on_ref, off_ref, out_ref, turned_ref):
    step = near_ref.shape[0]
    mesh_count = near_ref.shape[1]
    first = 3 * SLOT_ROWS
    odd_dom = odd_along("dom")
    on, off = on_ref[...], off_ref[...]
    left = jnp.where(odd_dom, on, off)[first + step : first + 2 * step] + (RIM - mesh_count)
    right = jnp.where(odd_dom, off, on)[first : first + step] + (RIM + mesh_count)
    own = near_ref[...] + RIM
    index = jnp.concatenate([left, own, right], 1)
    spots = lax.broadcasted_iota(jnp.int32, out_ref.shape, 0)
    counts = jnp.zeros(out_ref.shape, SINGLE)
    for j in range(step):
        counts = counts + jnp.where(spots == index[j : j + 1], 1.0, 0.0)
    turned_ref[...] = counts.astype(HALF)
    out_ref[...] = counts.T.astype(HALF)


def process(
    half_ref, state_ref, on_ref, off_ref, counts_ref, self_ref, near_ref,
    final_ref, pre_0_ref, pre_1_ref, half_1_ref, nearby_0_ref, nearby_1_ref, whole_ref,
):
    rim = on_ref.shape[0]
    count = half_ref.shape[0]
    own = slice(rim, rim + count)
    odd = odd_along("dom")
    left = jnp.where(odd, on_ref[...], off_ref[...])
    right = jnp.where(odd, off_ref[...], on_ref[...])
    whole_ref[:rim] = left
    whole_ref[own] = half_ref[...]
    whole_ref[rim + count :] = right
    half_0 = whole_ref[...]
    nearby_0 = (matmul(counts_ref[...], half_0) * (1.0 / NEAR)).astype(HALF)
    nearby_0_ref[...] = nearby_0[own]
    pre_0 = matmul(half_0, self_ref[0]) + matmul(nearby_0, near_ref[0])
    pre_0_ref[...] = pre_0
    grown = pre_0 * jax.nn.sigmoid(pre_0)
    state_1 = state_ref[...] + grown[own]
    half_1 = state_1.astype(HALF)
    whole_ref[:rim] = (left.astype(SINGLE) + grown[:rim]).astype(HALF)
    whole_ref[own] = half_1
    whole_ref[rim + count :] = (right.astype(SINGLE) + grown[rim + count :]).astype(HALF)
    half_1_ref[...] = half_1
    nearby_1 = (matmul(counts_ref[own], whole_ref[...]) * (1.0 / NEAR)).astype(HALF)
    nearby_1_ref[...] = nearby_1
    pre_1 = matmul(half_1, self_ref[1]) + matmul(nearby_1, near_ref[1])
    pre_1_ref[...] = pre_1
    final_ref[...] = (state_1 + pre_1 * jax.nn.sigmoid(pre_1)).astype(HALF)


def grid_counts(send_ref, recv_ref, *refs):
    far, (out_ref, turned_ref) = refs[: GROUPS - 1], refs[GROUPS - 1 :]
    odd_dom, odd_band = odd_along("dom"), odd_along("band")
    step = send_ref.shape[0] // GROUPS
    recv = by_partner(slots_of(recv_ref[...]), odd_dom, odd_band, True)
    send = [send_ref[:step]] + [ref[step : 2 * step] for ref in far]
    grids, nodes = out_ref.shape[0], turned_ref.shape[0] // GROUPS
    for p in range(GROUPS):
        at = slice(p * nodes, (p + 1) * nodes)
        to, of = hot(grids, recv[p]), hot(nodes, send[p])
        out_ref[:, at] = back_mul(to, of).astype(HALF)
        turned_ref[at] = back_mul(of, to).astype(HALF)


def mesh_counts(send_ref, recv_ref, *refs):
    far, out_ref = refs[: GROUPS - 1], refs[GROUPS - 1]
    step = send_ref.shape[0] // GROUPS
    send = by_partner(slots_of(send_ref[...]), odd_along("dom"), odd_along("band"), False)
    recv = [recv_ref[:step]] + [ref[:step] for ref in far]
    grids, nodes = out_ref.shape[0], out_ref.shape[1] // GROUPS
    for p in range(GROUPS):
        out_ref[:, p * nodes : (p + 1) * nodes] = pair_counts(send[p], grids, recv[p], nodes)


def decode(*refs):
    finals = refs[:GROUPS]
    counts_ref, turned_ref, weight_ref, back_ref = refs[GROUPS : GROUPS + 4]
    in_ref, hidden_ref, grad_ref, own_ref, *outs = refs[GROUPS + 4 :]
    nodes = own_ref.shape[0]
    total = matmul(counts_ref[:, :nodes], finals[0][...])
    for p in range(1, GROUPS):
        total = total + matmul(counts_ref[:, p * nodes : (p + 1) * nodes], finals[p][...])
    decode_in = total.astype(HALF)
    in_ref[...] = decode_in
    pre = matmul(decode_in, weight_ref[...])
    sigma = jax.nn.sigmoid(pre)
    hidden_ref[...] = (pre * sigma).astype(HALF)
    grad = (back_ref[...] * (sigma * (1.0 + pre * (1.0 - sigma)))).astype(HALF)
    grad_ref[...] = grad
    in_grad = back_mul(grad, weight_ref[...]).astype(HALF)
    own_ref[...] = matmul(turned_ref[:nodes], in_grad)
    for p, out in enumerate(outs):
        out[...] = matmul(turned_ref[(p + 1) * nodes : (p + 2) * nodes], in_grad).astype(HALF)


def gather_back(*refs):
    total = refs[0][...]
    for ref in refs[1:GROUPS]:
        total = total + ref[...].astype(SINGLE)
    slope_ref, state_ref, layer_ref, on_ref, off_ref = refs[GROUPS:]
    state_ref[...] = total
    layer = (total * slope_ref[...]).astype(HALF)
    layer_ref[...] = layer
    half = total.astype(HALF)
    odd = odd_along("dom")
    rim, count = RIM, total.shape[0]
    heads = jnp.concatenate([layer[: 2 * rim], half[:rim]], 0)
    tails = jnp.concatenate([layer[count - 2 * rim :], half[count - rim :]], 0)
    on_ref[...] = jnp.where(odd, heads, tails)
    off_ref[...] = jnp.where(odd, tails, heads)


def process_back(
    state_ref, layer_ref, on_ref, off_ref, turned_ref, slope_0_ref, slope_in_ref,
    self_ref, near_ref, encode_ref, static_ref, layer_0_ref, encode_grad_ref, back_ref, whole_ref,
):
    rim = RIM
    count = state_ref.shape[0]
    own = slice(2 * rim, 2 * rim + count)
    odd = odd_along("dom")
    on, off = on_ref[...], off_ref[...]
    left, right = jnp.where(odd, on, off), jnp.where(odd, off, on)
    whole_ref[: 2 * rim] = left[: 2 * rim]
    whole_ref[own] = layer_ref[...]
    whole_ref[2 * rim + count :] = right[: 2 * rim]
    layer_1 = whole_ref[...]
    spread = (matmul(turned_ref[...], layer_1) * (1.0 / NEAR)).astype(HALF)
    back = back_mul(layer_1, self_ref[1]) + back_mul(spread, near_ref[1])
    state_own = state_ref[...] + back[own]
    first = left[2 * rim :].astype(SINGLE) + back[rim : 2 * rim]
    last = right[2 * rim :].astype(SINGLE) + back[2 * rim + count : 3 * rim + count]
    layer_0 = (state_own * slope_0_ref[own]).astype(HALF)
    layer_0_ref[...] = layer_0
    whole_ref[:rim] = jnp.zeros((rim, back.shape[1]), HALF)
    whole_ref[rim : 2 * rim] = (first * slope_0_ref[rim : 2 * rim]).astype(HALF)
    whole_ref[own] = layer_0
    whole_ref[2 * rim + count : 3 * rim + count] = (
        last * slope_0_ref[2 * rim + count : 3 * rim + count]
    ).astype(HALF)
    whole_ref[3 * rim + count :] = jnp.zeros((rim, back.shape[1]), HALF)
    spread = (matmul(turned_ref[own], whole_ref[...]) * (1.0 / NEAR)).astype(HALF)
    state = state_own + back_mul(layer_0, self_ref[0]) + back_mul(spread, near_ref[0])
    static_ref[...] = state
    grad = (state * slope_in_ref[...]).astype(HALF)
    encode_grad_ref[...] = grad
    back_ref[...] = back_mul(grad, encode_ref[...]).astype(HALF)


def split_rows(count):
    return -(-count // (2 * LANES)) * LANES


def store_halves(value, at, mine_ref, other_ref, wide_ref):
    odd = lax.axis_index("dom") % 2
    count, rows = value.shape[0], split_rows(value.shape[0])
    wide_ref[:count] = value
    if count < 2 * rows:
        wide_ref[count : 2 * rows] = jnp.zeros((2 * rows - count, value.shape[1]), SINGLE)
    mine = pl.ds(pl.multiple_of(odd * rows, rows), rows)
    other = pl.ds(pl.multiple_of((1 - odd) * rows, rows), rows)
    mine_ref[at : at + rows] = wide_ref[mine].astype(HALF)
    other_ref[at : at + rows] = wide_ref[other].astype(HALF)
    return at + rows


def gradient_halves(turned, *refs):
    mine_ref, other_ref, wide_ref = refs[-3:]
    at = 0
    for i, (left, right) in enumerate(zip(refs[:-3:2], refs[1:-3:2], strict=True)):
        product = matmul if i < turned else outer_sum
        value = product(left[...], right[...])
        at = store_halves(value, at, mine_ref, other_ref, wide_ref)


def embed_back(*refs):
    returned = refs[:GROUPS]
    counts_ref, slope_ref, grid_ref, mine_ref, other_ref, wide_ref = refs[GROUPS:]
    nodes = returned[0].shape[0]
    total = matmul(counts_ref[:, :nodes], returned[0][...])
    for p in range(1, GROUPS):
        total = total + matmul(counts_ref[:, p * nodes : (p + 1) * nodes], returned[p][...])
    grad = (total * slope_ref[...]).astype(HALF)
    store_halves(matmul(grid_ref[...], grad), 0, mine_ref, other_ref, wide_ref)


def split_gradients(body, rows, macs, *args):
    width = args[1].shape[1]
    outs = [shape(rows, width, HALF)] * 2
    mine, other = whole(body, outs, macs, *args, scratch=[pltpu.VMEM((width, width), SINGLE)])
    return mine, swap_on(other)


def add_halves(*refs):
    out_ref = refs[-1]
    at = 0
    for mine, other in zip(refs[:-1:2], refs[1:-1:2], strict=True):
        rows = mine.shape[0]
        out_ref[at : at + rows] = (
            mine[...].astype(SINGLE) + other[...].astype(SINGLE)
        ).astype(HALF)
        at += rows


def add_pieces(pieces_ref, out_ref):
    total = pieces_ref[0].astype(SINGLE)
    for i in range(1, pieces_ref.shape[0]):
        total = total + pieces_ref[i].astype(SINGLE)
    out_ref[...] = total.astype(HALF)


def add_bands(*refs):
    out_ref = refs[-1]
    total = refs[0][...].astype(SINGLE)
    for ref in refs[1:-1]:
        total = total + ref[...].astype(SINGLE)
    total = total.astype(HALF)
    for i in range(out_ref.shape[0]):
        out_ref[i] = total


def unpack(part_ref, other_ref, *outs):
    odd = odd_along("dom")
    at = 0
    for out, which, rows in outs_of(outs):
        own = part_ref[at : at + rows].astype(SINGLE)
        far = other_ref[at : at + rows].astype(SINGLE)
        top, bottom = jnp.where(odd, far, own), jnp.where(odd, own, far)
        if which is None:
            out[:rows] = top
            out[rows:] = bottom[: out.shape[0] - rows]
        else:
            out[which, :rows] = top
            out[which, rows:] = bottom
        at += rows


def outs_of(outs):
    embed, encode, self_, near, decode, output = outs
    half = encode.shape[0] // 2
    narrow = -(-embed.shape[0] // (2 * LANES)) * LANES
    return [
        (output, None, narrow),
        (decode, None, half),
        (self_, 1, half),
        (near, 1, half),
        (self_, 0, half),
        (near, 0, half),
        (encode, None, half),
        (embed, None, narrow),
    ]


def reduce_all(part):
    count = lax.axis_size("dom")
    bands = lax.axis_size("band")
    groups = [list(range(c, count, 2)) for c in range(2)]
    chips = count // 2
    rows, width = part.shape[0] // chips, part.shape[1]
    pieces = lax.all_to_all(
        part.reshape(chips, rows, width), "dom", 0, 0, axis_index_groups=groups
    )
    (piece,) = whole(add_pieces, [shape(rows, width, HALF)], 0, pieces)
    others = [
        lax.ppermute(piece, "band", [(i, (i + step) % bands) for i in range(bands)])
        for step in range(1, bands)
    ]
    copies = jax.ShapeDtypeStruct((chips, rows, width), HALF)
    (copies,) = whole(add_bands, [copies], 0, piece, *others)
    return lax.all_to_all(copies, "dom", 0, 0, axis_index_groups=groups).reshape(part.shape)


def shards(
    grid_vars,
    cotangent,
    mesh_static,
    embed_weight,
    encode_weight,
    self_weight,
    neighbor_weight,
    decode_weight,
    output_weight,
    grid_sender,
    mesh_receiver,
    neighbors,
    mesh_sender,
    grid_receiver,
):
    grid_count, variables = grid_vars.shape
    mesh_count, width = mesh_static.shape
    rim = 2 * RIM
    ext = mesh_count + 2 * rim
    grid, cot, near, out_weight = grid_vars.T, cotangent.T, neighbors.T, output_weight.T
    grid_send, mesh_recv, mesh_send, grid_recv = (
        index.reshape(-1, LANES) for index in (grid_sender, mesh_receiver, mesh_sender, grid_receiver)
    )
    step = grid_send.shape[0] // GROUPS * LANES
    nodes = GROUPS * mesh_count
    mesh_rows = shape(mesh_count, width, HALF)
    mesh_full = shape(mesh_count, width, SINGLE)
    grid_rows = shape(grid_count, width, HALF)
    grid_full = shape(grid_count, width, SINGLE)
    parcel = shape(variables + -variables % 16 + INDEX_ROWS // 2, grid_count, HALF)
    sent = fetching(
        parcels, [parcel] * (GROUPS - 1), 0, grid, grid_send, mesh_recv, mesh_send, near
    )
    arrived = swap_all(*sent)
    embed_macs = grid_count * variables * width + mesh_count * grid_count * (step + width)
    slope_embed, total = fetching(
        embed_own, [grid_full, mesh_full], embed_macs, grid, embed_weight, grid_send, mesh_recv
    )
    index = [None] * GROUPS
    for p in range(1, GROUPS):
        index[p], total = whole(
            lambda *refs, p=p: embed_far(p, *refs),
            [shape(INDEX_ROWS, LANES, jnp.int32), mesh_full],
            embed_macs,
            arrived[p - 1],
            embed_weight,
            mesh_recv,
            total,
        )
    encode_in, slope_encode, state, half, on, off = whole(
        encode,
        [mesh_rows, mesh_full, mesh_full, mesh_rows] + [shape(rim, width, HALF)] * 2,
        mesh_count * width * width,
        total,
        encode_weight,
        mesh_static,
    )
    on, off = swap_on(on), swap_off(off)
    counts, turned = whole(
        near_counts, [shape(ext, ext, HALF)] * 2, ext * ext * 64, near, index[1], index[2]
    )
    final_half, pre_0, pre_1, half_1, nearby_0, nearby_1 = whole(
        process,
        [mesh_rows, shape(ext, width, SINGLE), mesh_full, mesh_rows, mesh_rows, mesh_rows],
        (ext + mesh_count) * (ext + 2 * width) * width,
        half,
        state,
        on,
        off,
        counts,
        self_weight,
        neighbor_weight,
        scratch=[pltpu.VMEM((ext, width), HALF)],
    )
    finals = (final_half,) + swap_all(*[final_half] * 4)
    to_grid, from_grid = whole(
        grid_counts,
        [shape(grid_count, nodes, HALF), shape(nodes, grid_count, HALF)],
        2 * nodes * grid_count * step,
        mesh_send,
        grid_recv,
        *index[1:],
    )
    hidden_grad = outer_sum(cot, out_weight)
    decode_in, hidden, decode_grad, state_grad, *sums = whole(
        decode,
        [grid_rows] * 3 + [mesh_full] + [mesh_rows] * (GROUPS - 1),
        2 * grid_count * width * (nodes + width),
        *finals,
        to_grid,
        from_grid,
        decode_weight,
        hidden_grad,
    )
    arrived = swap_all(*sums)
    prediction = (grid.astype(SINGLE) + back_mul(out_weight, hidden)).astype(HALF)
    half_rows = split_rows(width)
    narrow_rows = split_rows(variables)
    square = width * width
    halves = [
        *split_gradients(
            lambda *refs: gradient_halves(1, *refs),
            narrow_rows + half_rows,
            2 * grid_count * square,
            cot,
            hidden,
            decode_in,
            decode_grad,
        )
    ]
    state_grad, layer_1, on, off = whole(
        gather_back,
        [mesh_full, mesh_rows] + [shape(rim + RIM, width, HALF)] * 2,
        0,
        state_grad,
        *arrived,
        silu_slope(pre_1),
    )
    on, off = swap_on(on), swap_off(off)
    state_grad, layer_0, encode_grad, encode_in_grad = whole(
        process_back,
        [mesh_full, mesh_rows, mesh_rows, mesh_rows],
        (ext + mesh_count) * (ext + 2 * width) * width,
        state_grad,
        layer_1,
        on,
        off,
        turned,
        silu_slope(pre_0),
        slope_encode,
        self_weight,
        neighbor_weight,
        encode_weight,
        scratch=[pltpu.VMEM((ext, width), HALF)],
    )
    returned = (encode_in_grad,) + swap_all(*[encode_in_grad] * 4)
    to_mesh = whole(
        mesh_counts,
        [shape(grid_count, nodes, HALF)],
        nodes * grid_count * step,
        grid_send,
        mesh_recv,
        *index[1:],
    )[0]
    layer_1, encode_grad = lax.optimization_barrier((layer_1, encode_grad))
    halves += split_gradients(
        lambda *refs: gradient_halves(0, *refs),
        5 * half_rows,
        5 * mesh_count * square,
        half_1,
        layer_1,
        nearby_1,
        layer_1,
        half,
        layer_0,
        nearby_0,
        layer_0,
        encode_in,
        encode_grad,
    )
    halves += split_gradients(
        embed_back,
        narrow_rows,
        grid_count * width * (nodes + variables),
        *returned,
        to_mesh,
        slope_embed,
        grid,
    )
    rows = sum(block.shape[0] for block in halves[::2])
    (part,) = whole(add_halves, [shape(rows, width, HALF)], 0, *halves)
    part = reduce_all(part)
    other = swap_on(part)
    full = shape(width, width, SINGLE)
    pair = jax.ShapeDtypeStruct((2, width, width), SINGLE)
    narrow = shape(variables, width, SINGLE)
    grad_embed, grad_encode, grad_self, grad_near, grad_decode, grad_output = whole(
        unpack, [narrow, full, pair, pair, full, narrow], 0, part, other
    )
    return (
        prediction.T,
        state_grad,
        grad_embed,
        grad_encode,
        grad_self,
        grad_near,
        grad_decode,
        grad_output.T,
    )


def solution(mesh):
    placed = (
        P(("band", "dom"), None),
        P(("band", "dom"), None),
        P(("band", "dom"), None),
        P(),
        P(),
        P(),
        P(),
        P(),
        P(),
        P(("band", "dom")),
        P(("band", "dom")),
        P(("band", "dom"), None),
        P(("band", "dom")),
        P(("band", "dom")),
    )
    return jax.shard_map(
        shards,
        mesh=mesh,
        in_specs=placed,
        out_specs=(
            P(("band", "dom"), None),
            P(("band", "dom"), None),
            P(),
            P(),
            P(),
            P(),
            P(),
            P(),
        ),
        check_vma=False,
    )
```

time: 199 us -> 158 us (0.79)
  matrix products: 28.6 us -> 1.35 us
  blocking collectives: 65 us -> 54.6 us
  local copies, waits for them, and re-layouts: 14.1 us -> 4.84 us
  Pallas kernels: 19.7 us -> 23.9 us
  waiting for transfers between devices: 16.8 us -> 19.6 us
    dot_general x7 -> x1, matrix products: 12.9 us -> 1.02 us  [back_mul(): lax.dot_general(left, right, (((1,), (1,)), ((), ())), preferred_element_...]
    all_gather x1 -> x0, blocking collectives: 11 us -> none  [reduce_all(): pieces = lax.all_gather(piece, 'band', axis=0)]
    ppermute x0 -> x3, starting transfers between devices: none -> 7.82 us  [reduce_all(): lax.ppermute(piece, 'band', [(i, (i + step) % bands) for i in range(bands)])]
    dot_general x12 -> x1, matrix products: 8.04 us -> 0.34 us  [outer_sum(): lax.dot_general(left, right, (((0,), (0,)), ((), ())), preferred_element_...]
    dot_general x12 -> x0, matrix products: 7.59 us -> none  [matmul(): return jnp.dot(left, right, preferred_element_type=SINGLE)]
    unnamed x108 -> x40, local copies, waits for them, and re-layouts: 11.2 us -> 4.84 us
    ppermute x11 -> x10, starting transfers between devices: 33.4 us -> 27.3 us  [swap_on(): return lax.ppermute(value, 'dom', [(i, i ^ 1) for i in range(count)])]
    ppermute x8, waiting for transfers between devices: 7.12 us -> 2.91 us  [swap_band(): return lax.ppermute(value, 'band', pairs)]
  transfers between devices with their start and end apart: 25 -> 27, of which waited for: 8 -> 11; matrix products, arithmetic and copies ran while one was open for 10% -> 1% of each run, Pallas kernels for 7% -> 7%
where the time goes in v3:
time: 158 us; the launch traced here: 157 us
  blocking collectives  54.6 us (35%)
  starting transfers between devices  51.2 us (32%)
  Pallas kernels  23.9 us (15%)
  waiting for transfers between devices  19.6 us (12%)
  local copies, waits for them, and re-layouts  4.84 us (3%)
    all_to_all x1, blocking collectives, reduce_all(): lax.all_to_all(part.reshape(chips, rows, width), 'dom', 0, 0, axis_index_...  28.1 us
    ppermute x10, starting transfers between devices, swap_on(): return lax.ppermute(value, 'dom', [(i, i ^ 1) for i in range(count)])  27.3 us
    all_to_all x1, blocking collectives, reduce_all(): lax.all_to_all(copies, 'dom', 0, 0, axis_index_groups=groups)  26.5 us
    pallas_call x19, Pallas kernels, whole(): pl.pallas_call(body, out_shape=outs, scratch_shapes=scratch, compiler_par...  21.8 us
    ppermute x8, starting transfers between devices, swap_band(): return lax.ppermute(value, 'band', pairs)  14.3 us
    ppermute x6, waiting for transfers between devices, swap_off(): lax.ppermute(value, 'dom', [(i, (i + (1 if i % 2 else -1)) % count) for i...  9.31 us
    ppermute x3, starting transfers between devices, reduce_all(): lax.ppermute(piece, 'band', [(i, (i + step) % bands) for i in range(bands)])  7.82 us
    unnamed x40, local copies, waits for them, and re-layouts  4.84 us
  transfers between devices with their start and end apart: 27, of which 11 were waited for; matrix products, arithmetic and copies ran while one was open for 1% of the time, Pallas kernels for 7%

profile of v3, /device:TPU:1, one launch (start us, length us, event | category | flops | bytes accessed | tf_op | source)
XLA Modules:
  0.0 157.2 jit_solution(5863649973011982688)
XLA Ops:
  0.7 1.0 copy-done.1
  1.6 0.7 copy-done.8
  2.4 0.7 copy-done.10
  3.1 0.7 copy-done.12
  3.8 0.7 copy-done.14
  4.5 0.5 shard_map.197
  5.0 1.5 collective-permute-start.3
  6.5 1.7 %collective-permute-start.2 = (bf16[256,512]{1,0:T(8,128)(2,1)S(1)}, bf16[256,512]{1,0:T(8,128)(2,1)S(1)}, u32[]{:S(2)}, u32[]{:S(2)}) collective-permute-start(bf16[256,512]{1,0:T(8,128)(2,1)S(1)} %get-tuple-element.70), channel_id=1, source_target_pairs={{0,31},{1,2},{2,1},{3,4},{4,3},{5,6},{6,5},{7,8},{8,7},{9,10},{10,... | collective-permute-start | bytes 786440 | tf_op jit(solution)/shard_map/ppermute | solution.py:47
  8.2 1.2 collective-permute-start.1
  9.4 0.7 collective-permute-start
  10.1 0.9 copy-done.17
  11.0 1.6 %shard_map.198 = (f32[512,512]{1,0:T(8,128)S(1)}, f32[256,512]{1,0:T(8,128)S(1)}) custom-call(bf16[227,512]{1,0:T(8,128)(2,1)S(1)} %bitcast.18, bf16[227,512]{1,0:T(8,128)(2,1)S(1)} %copy-done.17, s32[30,128]{1,0:T(8,128)S(1)} %bitcast.24, s32[30,128]{1,0:T(8,128)S(1)} %bitcast.27), custom_call_target="tpu_custom_call" | custom-call | flops 454557696 | bytes 2068480 | tf_op jit(solution)/shard_map/pallas_call | solution.py:125
  12.6 0.8 shard_map.199
  13.4 0.8 shard_map.200
  14.2 0.8 shard_map.201
  15.1 0.8 shard_map.202
  15.9 0.4 shard_map.203
  16.3 5.4 %collective-permute-start.4 = (bf16[128,512]{1,0:T(8,128)(2,1)S(1)}, bf16[128,512]{1,0:T(8,128)(2,1)S(1)}, u32[]{:S(2)}, u32[]{:S(2)}) collective-permute-start(bf16[128,512]{1,0:T(8,128)(2,1)S(1)} %get-tuple-element.79), channel_id=1, source_target_pairs={{0,1},{1,0},{2,3},{3,2},{4,5},{5,4},{6,7},{7,6},{8,9},{9,8},{10,11... | collective-permute-start | bytes 393224 | tf_op jit(solution)/shard_map/ppermute | solution.py:42
  21.7 0.7 shard_map.204
  22.4 0.3 collective-permute-done.4.on_ref
  22.7 3.4 %collective-permute-done.5.off_ref = bf16[128,512]{1,0:T(8,128)(2,1)S(1)} collective-permute-done((bf16[128,512]{1,0:T(8,128)(2,1)S(1)}, bf16[128,512]{1,0:T(8,128)(2,1)S(1)}, u32[]{:S(2)}, u32[]{:S(2)}) %collective-permute-start.5) | collective-permute-done | bytes 131104 | tf_op jit(solution)/shard_map/ppermute | solution.py:47
  26.1 1.7 %shard_map.205 = (bf16[256,512]{1,0:T(8,128)(2,1)S(1)}, f32[512,512]{1,0:T(8,128)S(1)}, f32[256,512]{1,0:T(8,128)S(1)}, bf16[256,512]{1,0:T(8,128)(2,1)S(1)}, bf...) custom-call(bf16[256,512]{1,0:T(8,128)(2,1)S(1)} %get-tuple-element.77.half_ref.refs_4_, ...), custom_call_target="tpu_custom_call" | custom-call | flops 1207959552 | bytes 6291456 | tf_op jit(solution)/shard_map/pallas_call | solution.py:78
  27.8 3.5 %collective-permute-start.6 = (bf16[256,512]{1,0:T(8,128)(2,1)S(1)}, bf16[256,512]{1,0:T(8,128)(2,1)S(1)}, u32[]{:S(2)}, u32[]{:S(2)}) collective-permute-start(bf16[256,512]{1,0:T(8,128)(2,1)S(1)} %get-tuple-element.84.refs_0_), channel_id=1, source_target_pairs={{0,1},{1,0},{2,3},{3,2},{4,5},{5,4},{6,7},{7,6},{8,9},{9,8},{10,11... | collective-permute-start | bytes 786440 | tf_op jit(solution)/shard_map/ppermute | solution.py:42
  31.3 3.6 %collective-permute-start.8 = (bf16[256,512]{1,0:T(8,128)(2,1)S(1)}, bf16[256,512]{1,0:T(8,128)(2,1)S(1)}, u32[]{:S(2)}, u32[]{:S(2)}) collective-permute-start(bf16[256,512]{1,0:T(8,128)(2,1)S(1)} %get-tuple-element.84.refs_0_), channel_id=1, source_target_pairs={{0,32},{32,0},{64,96},{96,64},{1,33},{33,1},{65,97},{97,65},{2,34}... | collective-permute-start | bytes 786440 | tf_op jit(solution)/shard_map/ppermute | solution.py:57
  34.9 0.8 collective-permute-start.9
  35.8 0.3 fusion.1.refs_8_
  36.2 2.3 %shard_map.206 = (bf16[512,1280]{1,0:T(8,128)(2,1)S(1)}, bf16[1280,512]{1,0:T(8,128)(2,1)S(1)}) custom-call(s32[30,128]{1,0:T(8,128)S(1)} %bitcast.22, s32[30,128]{1,0:T(8,128)S(1)} %bitcast.35, s32[32,128]{1,0:T(8,128)S(1)} %get-tuple-element.81.on_ref.refs_0_, s32[32,128]{1,0:T(8,128)S(1)} %get-tuple-element.82.off_ref.refs_1_, ...), custom_call_target="tpu_custom_call" | custom-call | flops 2013265920 | bytes 2717696 | tf_op jit(solution)/shard_map/pallas_call | solution.py:78
  38.5 1.2 collective-permute-done.8.refs_3_
  39.8 2.4 %shard_map.207 = (bf16[512,512]{1,0:T(8,128)(2,1)S(1)}, bf16[512,512]{1,0:T(8,128)(2,1)S(1)}, bf16[512,512]{1,0:T(8,128)(2,1)S(1)}, f32[256,512]{1,0:T(8,128)S(1...) custom-call(bf16[256,512]{1,0:T(8,128)(2,1)S(1)} %get-tuple-element., ...), custom_call_target="tpu_custom_call" | custom-call | flops 1879048192 | bytes 8650752 | tf_op jit(solution)/shard_map/pallas_call | solution.py:78
  42.1 2.5 %collective-permute-start.10 = (bf16[256,512]{1,0:T(8,128)(2,1)S(1)}, bf16[256,512]{1,0:T(8,128)(2,1)S(1)}, u32[]{:S(2)}, u32[]{:S(2)}) collective-permute-start(bf16[256,512]{1,0:T(8,128)(2,1)S(1)} %get-tuple-element.91), channel_id=1, source_target_pairs={{0,1},{1,0},{2,3},{3,2},{4,5},{5,4},{6,7},{7,6},{8,9},{9,8},{10,11... | collective-permute-start | bytes 786440 | tf_op jit(solution)/shard_map/ppermute | solution.py:42
  44.6 3.3 %collective-permute-start.12 = (bf16[256,512]{1,0:T(8,128)(2,1)S(1)}, bf16[256,512]{1,0:T(8,128)(2,1)S(1)}, u32[]{:S(2)}, u32[]{:S(2)}) collective-permute-start(bf16[256,512]{1,0:T(8,128)(2,1)S(1)} %get-tuple-element.93), channel_id=1, source_target_pairs={{0,32},{32,0},{64,96},{96,64},{1,33},{33,1},{65,97},{97,65},{2,34}... | collective-permute-start | bytes 786440 | tf_op jit(solution)/shard_map/ppermute | solution.py:57
  48.0 0.7 collective-permute-start.13
  48.6 0.2 add_multiply_fusion.1.refs_5_
  48.8 1.9 %collective-permute-done.11.refs_2_ = bf16[256,512]{1,0:T(8,128)(2,1)S(1)} collective-permute-done((bf16[256,512]{1,0:T(8,128)(2,1)S(1)}, bf16[256,512]{1,0:T(8,128)(2,1)S(1)}, u32[]{:S(2)}, u32[]{:S(2)}) %collective-permute-start.11) | collective-permute-done | bytes 262176 | tf_op jit(solution)/shard_map/ppermute | solution.py:47
  50.7 1.7 %collective-permute-done.12.refs_3_ = bf16[256,512]{1,0:T(8,128)(2,1)S(1)} collective-permute-done((bf16[256,512]{1,0:T(8,128)(2,1)S(1)}, bf16[256,512]{1,0:T(8,128)(2,1)S(1)}, u32[]{:S(2)}, u32[]{:S(2)}) %collective-permute-start.12) | collective-permute-done | bytes 262176 | tf_op jit(solution)/shard_map/ppermute | solution.py:57
  52.4 0.2 shard_map.208
  52.6 2.9 %collective-permute-start.14 = (bf16[192,512]{1,0:T(8,128)(2,1)S(1)}, bf16[192,512]{1,0:T(8,128)(2,1)S(1)}, u32[]{:S(2)}, u32[]{:S(2)}) collective-permute-start(bf16[192,512]{1,0:T(8,128)(2,1)S(1)} %get-tuple-element.98), channel_id=1, source_target_pairs={{0,1},{1,0},{2,3},{3,2},{4,5},{5,4},{6,7},{7,6},{8,9},{9,8},{10,11... | collective-permute-start | bytes 589832 | tf_op jit(solution)/shard_map/ppermute | solution.py:42
  55.5 0.4 add_multiply_fusion.slope_0_ref
  55.9 0.7 collective-permute-done.14.on_ref
  56.6 4.0 %collective-permute-done.15.off_ref = bf16[192,512]{1,0:T(8,128)(2,1)S(1)} collective-permute-done((bf16[192,512]{1,0:T(8,128)(2,1)S(1)}, bf16[192,512]{1,0:T(8,128)(2,1)S(1)}, u32[]{:S(2)}, u32[]{:S(2)}) %collective-permute-start.15) | collective-permute-done | bytes 196640 | tf_op jit(solution)/shard_map/ppermute | solution.py:47
  60.6 2.3 %shard_map.209 = (f32[256,512]{1,0:T(8,128)}, bf16[256,512]{1,0:T(8,128)(2,1)S(1)}, bf16[256,512]{1,0:T(8,128)(2,1)S(1)}, bf16[256,512]{1,0:T(8,128)(2,1)S(1)}) custom-call(f32[256,512]{1,0:T(8,128)S(1)} %get-tuple-element.96.state_ref, bf16[256,512]{1,0:T(8,128)(2,1)S(1)} %get-tuple-element.110.layer_ref.refs_1_.refs_3_, ...), custom_call_target="tpu_custom_call" | custom-call | flops 1207959552 | bytes 7208960 | tf_op jit(solution)/shard_map/pallas_call | solution.py:78
  62.9 1.4 shard_map.211
  64.3 3.5 %collective-permute-start.17 = (bf16[1280,512]{1,0:T(8,128)(2,1)S(1)}, bf16[1280,512]{1,0:T(8,128)(2,1)S(1)}, u32[]{:S(2)}, u32[]{:S(2)}) collective-permute-start(bf16[1280,512]{1,0:T(8,128)(2,1)S(1)} %get-tuple-element.117), channel_id=1, source_target_pairs={{0,1},{1,0},{2,3},{3,2},{4,5},{5,4},{6,7},{7,6},{8,9},{9,8},{10,11... | collective-permute-start | bytes 3932168 | tf_op jit(solution)/shard_map/ppermute | solution.py:42
  67.9 3.3 %collective-permute-start.20 = (bf16[256,512]{1,0:T(8,128)(2,1)S(1)}, bf16[256,512]{1,0:T(8,128)(2,1)S(1)}, u32[]{:S(2)}, u32[]{:S(2)}) collective-permute-start(bf16[256,512]{1,0:T(8,128)(2,1)S(1)} %get-tuple-element.118.refs_0_), channel_id=1, source_target_pairs={{0,32},{32,0},{64,96},{96,64},{1,33},{33,1},{65,97},{97,65},{2,34}... | collective-permute-start | bytes 786440 | tf_op jit(solution)/shard_map/ppermute | solution.py:57
  71.3 0.7 collective-permute-start.21
  71.9 0.7 shard_map.210
  72.7 3.4 %collective-permute-start.16 = (bf16[384,512]{1,0:T(8,128)(2,1)S(1)}, bf16[384,512]{1,0:T(8,128)(2,1)S(1)}, u32[]{:S(2)}, u32[]{:S(2)}) collective-permute-start(bf16[384,512]{1,0:T(8,128)(2,1)S(1)} %get-tuple-element.107), channel_id=1, source_target_pairs={{0,1},{1,0},{2,3},{3,2},{4,5},{5,4},{6,7},{7,6},{8,9},{9,8},{10,11... | collective-permute-start | bytes 1179656 | tf_op jit(solution)/shard_map/ppermute | solution.py:42
  76.1 1.4 shard_map.212.refs_5_
  77.5 1.1 shard_map.213
  78.6 1.2 collective-permute-start.22
  79.9 1.0 collective-permute-done.22.refs_5_
  80.9 0.4 shard_map.214
  81.3 28.1 %all_to_all.10.pieces_ref = bf16[16,112,512]{2,1,0:T(8,128)(2,1)S(1)} all-to-all(bf16[16,112,512]{2,1,0:T(8,128)(2,1)S(1)} %bitcast.16), channel_id=1, replica_groups={{0,2,4,6,8,10,12,14,16,18,20,22,24,26,28,30},{1,3,5,7,9,11,13,15,17,19,..., dimensions={0} | all-to-all | bytes 3670016 | tf_op jit(solution)/shard_map/all_to_all | solution.py:474
  109.4 0.2 shard_map.215.refs_0_
  109.7 3.7 %collective-permute-start.23 = (bf16[112,512]{1,0:T(8,128)(2,1)S(1)}, bf16[112,512]{1,0:T(8,128)(2,1)S(1)}, u32[]{:S(2)}, u32[]{:S(2)}) collective-permute-start(bf16[112,512]{1,0:T(8,128)(2,1)S(1)} %shard_map.215.refs_0_), channel_id=1, source_target_pairs={{0,32},{32,64},{64,96},{96,0},{1,33},{33,65},{65,97},{97,1},{2,34}... | collective-permute-start | bytes 344072 | tf_op jit(solution)/shard_map/ppermute | solution.py:479
  113.4 2.1 %collective-permute-start.24 = (bf16[112,512]{1,0:T(8,128)(2,1)S(1)}, bf16[112,512]{1,0:T(8,128)(2,1)S(1)}, u32[]{:S(2)}, u32[]{:S(2)}) collective-permute-start(bf16[112,512]{1,0:T(8,128)(2,1)S(1)} %shard_map.215.refs_0_), channel_id=1, source_target_pairs={{0,64},{32,96},{64,0},{96,32},{1,65},{33,97},{65,1},{97,33},{2,66}... | collective-permute-start | bytes 344072 | tf_op jit(solution)/shard_map/ppermute | solution.py:479
  115.5 2.0 %collective-permute-start.25 = (bf16[112,512]{1,0:T(8,128)(2,1)S(1)}, bf16[112,512]{1,0:T(8,128)(2,1)S(1)}, u32[]{:S(2)}, u32[]{:S(2)}) collective-permute-start(bf16[112,512]{1,0:T(8,128)(2,1)S(1)} %shard_map.215.refs_0_), channel_id=1, source_target_pairs={{0,96},{32,0},{64,32},{96,64},{1,97},{33,1},{65,33},{97,65},{2,98}... | collective-permute-start | bytes 344072 | tf_op jit(solution)/shard_map/ppermute | solution.py:479
  117.5 2.0 %collective-permute-done.24.refs_2_ = bf16[112,512]{1,0:T(8,128)(2,1)S(1)} collective-permute-done((bf16[112,512]{1,0:T(8,128)(2,1)S(1)}, bf16[112,512]{1,0:T(8,128)(2,1)S(1)}, u32[]{:S(2)}, u32[]{:S(2)}) %collective-permute-start.24) | collective-permute-done | bytes 114720 | tf_op jit(solution)/shard_map/ppermute | solution.py:479
  119.5 1.1 collective-permute-done.25.refs_3_
  120.7 26.5 %all_to_all.11 = bf16[16,112,512]{2,1,0:T(8,128)(2,1)S(1)} all-to-all(bf16[16,112,512]{2,1,0:T(8,128)(2,1)S(1)} %shard_map.216), channel_id=1, replica_groups={{0,2,4,6,8,10,12,14,16,18,20,22,24,26,28,30},{1,3,5,7,9,11,13,15,17,19,..., dimensions={0} | all-to-all | bytes 3670016 | tf_op jit(solution)/shard_map/all_to_all | solution.py:484
  147.2 3.3 %collective-permute-start.26 = (bf16[1792,512]{1,0:T(8,128)(2,1)S(1)}, bf16[1792,512]{1,0:T(8,128)(2,1)S(1)}, u32[]{:S(2)}, u32[]{:S(2)}) collective-permute-start(bf16[1792,512]{1,0:T(8,128)(2,1)S(1)} %bitcast.14), channel_id=1, source_target_pairs={{0,1},{1,0},{2,3},{3,2},{4,5},{5,4},{6,7},{7,6},{8,9},{9,8},{10,11... | collective-permute-start | bytes 5505032 | tf_op jit(solution)/shard_map/ppermute | solution.py:42
  150.6 1.0 fusion
  151.6 2.4 %collective-permute-done.26.other_ref = bf16[1792,512]{1,0:T(8,128)(2,1)S(1)} collective-permute-done((bf16[1792,512]{1,0:T(8,128)(2,1)S(1)}, bf16[1792,512]{1,0:T(8,128)(2,1)S(1)}, u32[]{:S(2)}, u32[]{:S(2)}) %collective-permute-start.26) | collective-permute-done | bytes 1835040 | tf_op jit(solution)/shard_map/ppermute | solution.py:42
  154.0 3.2 %shard_map.217 = (f32[227,512]{1,0:T(8,128)}, f32[512,512]{1,0:T(8,128)}, f32[2,512,512]{2,1,0:T(8,128)}, f32[2,512,512]{2,1,0:T(8,128)}, f32[512,512]{1,0:T(8,128)}, /*index=5*/f32[227,512]{1,0:T(8,128)}) custom-call(bf16[1792,512]{1,0:T(8,128)(2,1)S(1)} %bitcast.15, bf16[1792,512]{1,0:T(8,128)(2,1)S(1)} %collective-permute-done.26.other_ref), custom_call_target="tpu_custom_call" | custom-call | bytes 10891264 | tf_op jit(solution)/shard_map/pallas_call | solution.py:78
  (57 shorter events, 0.4 us)
Async XLA Ops:
  0.6 35.1 %copy-start = (bf16[512,227]{0,1:T(8,128)(2,1)S(1)}, bf16[512,227]{0,1:T(8,128)(2,1)}, u32[]{:S(2)}) copy-start(bf16[512,227]{0,1:T(8,128)(2,1)} %param.22) | copy-start | bytes 697348
  0.6 1.0 copy-start.1
  1.6 0.7 copy-start.8
  2.4 0.7 copy-start.10
  3.1 0.7 copy-start.12
  3.8 0.7 copy-start.14
  4.5 8.1 %copy-start.13 = (s32[3840]{0:T(1024)S(1)}, s32[3840]{0:T(1024)}, u32[]{:S(2)}) copy-start(s32[3840]{0:T(1024)} %param.24) | copy-start | bytes 46084
  4.5 8.1 %copy-start.18 = (bf16[227,512]{1,0:T(8,128)(2,1)S(1)}, bf16[227,512]{1,0:T(8,128)(2,1)}, u32[]{:S(2)}) copy-start(bf16[227,512]{1,0:T(8,128)(2,1)} %refs_1_.9) | copy-start | bytes 697348
  5.0 7.6 %collective-permute-start.3 = (bf16[256,512]{1,0:T(8,128)(2,1)S(1)}, bf16[256,512]{1,0:T(8,128)(2,1)S(1)}, u32[]{:S(2)}, u32[]{:S(2)}) collective-permute-start(bf16[256,512]{1,0:T(8,128)(2,1)S(1)} %get-tuple-element.71), channel_id=1, source_target_pairs={{0,1},{1,0},{2,3},{3,2},{4,5},{5,4},{6,7},{7,6},{8,9},{9,8},{10,11... | collective-permute-start | bytes 786440 | tf_op jit(solution)/shard_map/ppermute | solution.py:42
  6.5 6.9 %collective-permute-start.2 = (bf16[256,512]{1,0:T(8,128)(2,1)S(1)}, bf16[256,512]{1,0:T(8,128)(2,1)S(1)}, u32[]{:S(2)}, u32[]{:S(2)}) collective-permute-start(bf16[256,512]{1,0:T(8,128)(2,1)S(1)} %get-tuple-element.70), channel_id=1, source_target_pairs={{0,31},{1,2},{2,1},{3,4},{4,3},{5,6},{6,5},{7,8},{8,7},{9,10},{10,... | collective-permute-start | bytes 786440 | tf_op jit(solution)/shard_map/ppermute | solution.py:47
  8.2 6.1 %collective-permute-start.1 = (bf16[256,512]{1,0:T(8,128)(2,1)S(1)}, bf16[256,512]{1,0:T(8,128)(2,1)S(1)}, u32[]{:S(2)}, u32[]{:S(2)}) collective-permute-start(bf16[256,512]{1,0:T(8,128)(2,1)S(1)} %get-tuple-element.69), channel_id=1, source_target_pairs={{0,32},{32,0},{64,96},{96,64},{1,33},{33,1},{65,97},{97,65},{2,34}... | collective-permute-start | bytes 786440 | tf_op jit(solution)/shard_map/ppermute | solution.py:57
  9.4 5.7 %collective-permute-start = (bf16[256,512]{1,0:T(8,128)(2,1)S(1)}, bf16[256,512]{1,0:T(8,128)(2,1)S(1)}, u32[]{:S(2)}, u32[]{:S(2)}) collective-permute-start(bf16[256,512]{1,0:T(8,128)(2,1)S(1)} %get-tuple-element.68), channel_id=1, source_target_pairs={{32,64},{64,32},{33,65},{65,33},{34,66},{66,34},{35,67},{67,35},{3... | collective-permute-start | bytes 786440 | tf_op jit(solution)/shard_map/ppermute | solution.py:57
  10.1 0.9 copy-start.17
  14.2 1.7 %copy-start.3 = (bf16[512,512]{1,0:T(8,128)(2,1)S(1)}, bf16[512,512]{1,0:T(8,128)(2,1)}, u32[]{:S(2)}) copy-start(bf16[512,512]{1,0:T(8,128)(2,1)} %encode_ref.1) | copy-start | bytes 1572868
  14.2 1.7 %copy-start.6 = (bf16[256,512]{1,0:T(8,128)(2,1)S(1)}, bf16[256,512]{1,0:T(8,128)(2,1)}, u32[]{:S(2)}) copy-start(bf16[256,512]{1,0:T(8,128)(2,1)} %static_ref.1) | copy-start | bytes 786436
  15.0 6.7 %copy-start.15 = (s32[256,6]{0,1:T(8,128)S(1)}, s32[256,6]{0,1:T(8,128)}, u32[]{:S(2)}) copy-start(s32[256,6]{0,1:T(8,128)} %param.25) | copy-start | bytes 18436
  15.0 11.1 %copy-start.4 = (bf16[2,512,512]{2,1,0:T(8,128)(2,1)S(1)}, bf16[2,512,512]{2,1,0:T(8,128)(2,1)}, u32[]{:S(2)}) copy-start(bf16[2,512,512]{2,1,0:T(8,128)(2,1)} %self_ref.3) | copy-start | bytes 3145732
  15.1 11.1 %copy-start.5 = (bf16[2,512,512]{2,1,0:T(8,128)(2,1)S(1)}, bf16[2,512,512]{2,1,0:T(8,128)(2,1)}, u32[]{:S(2)}) copy-start(bf16[2,512,512]{2,1,0:T(8,128)(2,1)} %near_ref.3) | copy-start | bytes 3145732
  16.3 6.4 %collective-permute-start.4 = (bf16[128,512]{1,0:T(8,128)(2,1)S(1)}, bf16[128,512]{1,0:T(8,128)(2,1)S(1)}, u32[]{:S(2)}, u32[]{:S(2)}) collective-permute-start(bf16[128,512]{1,0:T(8,128)(2,1)S(1)} %get-tuple-element.79), channel_id=1, source_target_pairs={{0,1},{1,0},{2,3},{3,2},{4,5},{5,4},{6,7},{7,6},{8,9},{9,8},{10,11... | collective-permute-start | bytes 393224 | tf_op jit(solution)/shard_map/ppermute | solution.py:42
  21.7 4.4 %collective-permute-start.5 = (bf16[128,512]{1,0:T(8,128)(2,1)S(1)}, bf16[128,512]{1,0:T(8,128)(2,1)S(1)}, u32[]{:S(2)}, u32[]{:S(2)}) collective-permute-start(bf16[128,512]{1,0:T(8,128)(2,1)S(1)} %get-tuple-element.80), channel_id=1, source_target_pairs={{0,31},{1,2},{2,1},{3,4},{4,3},{5,6},{6,5},{7,8},{8,7},{9,10},{10,... | collective-permute-start | bytes 393224 | tf_op jit(solution)/shard_map/ppermute | solution.py:47
  26.1 9.7 %copy-start.7 = (bf16[512,227]{0,1:T(8,128)(2,1)S(1)}, bf16[512,227]{0,1:T(8,128)(2,1)}, u32[]{:S(2)}) copy-start(bf16[512,227]{0,1:T(8,128)(2,1)} %param.15) | copy-start | bytes 697348
  26.1 10.0 %copy-start.9 = (s32[3840]{0:T(1024)S(1)}, s32[3840]{0:T(1024)}, u32[]{:S(2)}) copy-start(s32[3840]{0:T(1024)} %param.26) | copy-start | bytes 46084
  26.1 10.0 %copy-start.19 = (s32[3840]{0:T(1024)S(1)}, s32[3840]{0:T(1024)}, u32[]{:S(2)}) copy-start(s32[3840]{0:T(1024)} %param.27) | copy-start | bytes 46084
  27.8 10.7 %collective-permute-start.6 = (bf16[256,512]{1,0:T(8,128)(2,1)S(1)}, bf16[256,512]{1,0:T(8,128)(2,1)S(1)}, u32[]{:S(2)}, u32[]{:S(2)}) collective-permute-start(bf16[256,512]{1,0:T(8,128)(2,1)S(1)} %get-tuple-element.84.refs_0_), channel_id=1, source_target_pairs={{0,1},{1,0},{2,3},{3,2},{4,5},{5,4},{6,7},{7,6},{8,9},{9,8},{10,11... | collective-permute-start | bytes 786440 | tf_op jit(solution)/shard_map/ppermute | solution.py:42
  31.3 7.2 %collective-permute-start.7 = (bf16[256,512]{1,0:T(8,128)(2,1)S(1)}, bf16[256,512]{1,0:T(8,128)(2,1)S(1)}, u32[]{:S(2)}, u32[]{:S(2)}) collective-permute-start(bf16[256,512]{1,0:T(8,128)(2,1)S(1)} %get-tuple-element.84.refs_0_), channel_id=1, source_target_pairs={{0,31},{1,2},{2,1},{3,4},{4,3},{5,6},{6,5},{7,8},{8,7},{9,10},{10,... | collective-permute-start | bytes 786440 | tf_op jit(solution)/shard_map/ppermute | solution.py:47
  31.3 8.5 %collective-permute-start.8 = (bf16[256,512]{1,0:T(8,128)(2,1)S(1)}, bf16[256,512]{1,0:T(8,128)(2,1)S(1)}, u32[]{:S(2)}, u32[]{:S(2)}) collective-permute-start(bf16[256,512]{1,0:T(8,128)(2,1)S(1)} %get-tuple-element.84.refs_0_), channel_id=1, source_target_pairs={{0,32},{32,0},{64,96},{96,64},{1,33},{33,1},{65,97},{97,65},{2,34}... | collective-permute-start | bytes 786440 | tf_op jit(solution)/shard_map/ppermute | solution.py:57
  34.9 4.8 %collective-permute-start.9 = (bf16[256,512]{1,0:T(8,128)(2,1)S(1)}, bf16[256,512]{1,0:T(8,128)(2,1)S(1)}, u32[]{:S(2)}, u32[]{:S(2)}) collective-permute-start(bf16[256,512]{1,0:T(8,128)(2,1)S(1)} %get-tuple-element.84.refs_0_), channel_id=1, source_target_pairs={{32,64},{64,32},{33,65},{65,33},{34,66},{66,34},{35,67},{67,35},{3... | collective-permute-start | bytes 786440 | tf_op jit(solution)/shard_map/ppermute | solution.py:57
  36.1 3.6 %copy-start.16 = (bf16[512,512]{1,0:T(8,128)(2,1)S(1)}, bf16[512,512]{1,0:T(8,128)(2,1)}, u32[]{:S(2)}) copy-start(bf16[512,512]{1,0:T(8,128)(2,1)} %refs_7_.1) | copy-start | bytes 1572868
  42.1 6.7 %collective-permute-start.10 = (bf16[256,512]{1,0:T(8,128)(2,1)S(1)}, bf16[256,512]{1,0:T(8,128)(2,1)S(1)}, u32[]{:S(2)}, u32[]{:S(2)}) collective-permute-start(bf16[256,512]{1,0:T(8,128)(2,1)S(1)} %get-tuple-element.91), channel_id=1, source_target_pairs={{0,1},{1,0},{2,3},{3,2},{4,5},{5,4},{6,7},{7,6},{8,9},{9,8},{10,11... | collective-permute-start | bytes 786440 | tf_op jit(solution)/shard_map/ppermute | solution.py:42
  44.6 6.1 %collective-permute-start.11 = (bf16[256,512]{1,0:T(8,128)(2,1)S(1)}, bf16[256,512]{1,0:T(8,128)(2,1)S(1)}, u32[]{:S(2)}, u32[]{:S(2)}) collective-permute-start(bf16[256,512]{1,0:T(8,128)(2,1)S(1)} %get-tuple-element.92), channel_id=1, source_target_pairs={{0,31},{1,2},{2,1},{3,4},{4,3},{5,6},{6,5},{7,8},{8,7},{9,10},{10,... | collective-permute-start | bytes 786440 | tf_op jit(solution)/shard_map/ppermute | solution.py:47
  44.6 7.8 %collective-permute-start.12 = (bf16[256,512]{1,0:T(8,128)(2,1)S(1)}, bf16[256,512]{1,0:T(8,128)(2,1)S(1)}, u32[]{:S(2)}, u32[]{:S(2)}) collective-permute-start(bf16[256,512]{1,0:T(8,128)(2,1)S(1)} %get-tuple-element.93), channel_id=1, source_target_pairs={{0,32},{32,0},{64,96},{96,64},{1,33},{33,1},{65,97},{97,65},{2,34}... | collective-permute-start | bytes 786440 | tf_op jit(solution)/shard_map/ppermute | solution.py:57
  48.0 4.4 %collective-permute-start.13 = (bf16[256,512]{1,0:T(8,128)(2,1)S(1)}, bf16[256,512]{1,0:T(8,128)(2,1)S(1)}, u32[]{:S(2)}, u32[]{:S(2)}) collective-permute-start(bf16[256,512]{1,0:T(8,128)(2,1)S(1)} %get-tuple-element.94), channel_id=1, source_target_pairs={{32,64},{64,32},{33,65},{65,33},{34,66},{66,34},{35,67},{67,35},{3... | collective-permute-start | bytes 786440 | tf_op jit(solution)/shard_map/ppermute | solution.py:57
  52.6 4.0 %collective-permute-start.14 = (bf16[192,512]{1,0:T(8,128)(2,1)S(1)}, bf16[192,512]{1,0:T(8,128)(2,1)S(1)}, u32[]{:S(2)}, u32[]{:S(2)}) collective-permute-start(bf16[192,512]{1,0:T(8,128)(2,1)S(1)} %get-tuple-element.98), channel_id=1, source_target_pairs={{0,1},{1,0},{2,3},{3,2},{4,5},{5,4},{6,7},{7,6},{8,9},{9,8},{10,11... | collective-permute-start | bytes 589832 | tf_op jit(solution)/shard_map/ppermute | solution.py:42
  55.5 5.1 %collective-permute-start.15 = (bf16[192,512]{1,0:T(8,128)(2,1)S(1)}, bf16[192,512]{1,0:T(8,128)(2,1)S(1)}, u32[]{:S(2)}, u32[]{:S(2)}) collective-permute-start(bf16[192,512]{1,0:T(8,128)(2,1)S(1)} %get-tuple-element.99), channel_id=1, source_target_pairs={{0,31},{1,2},{2,1},{3,4},{4,3},{5,6},{6,5},{7,8},{8,7},{9,10},{10,... | collective-permute-start | bytes 589832 | tf_op jit(solution)/shard_map/ppermute | solution.py:47
  62.9 13.1 %copy-start.11 = (s32[3840]{0:T(1024)S(1)}, s32[3840]{0:T(1024)}, u32[]{:S(2)}) copy-start(s32[3840]{0:T(1024)} %param.23) | copy-start | bytes 46084
  64.3 16.6 %collective-permute-start.17 = (bf16[1280,512]{1,0:T(8,128)(2,1)S(1)}, bf16[1280,512]{1,0:T(8,128)(2,1)S(1)}, u32[]{:S(2)}, u32[]{:S(2)}) collective-permute-start(bf16[1280,512]{1,0:T(8,128)(2,1)S(1)} %get-tuple-element.117), channel_id=1, source_target_pairs={{0,1},{1,0},{2,3},{3,2},{4,5},{5,4},{6,7},{7,6},{8,9},{9,8},{10,11... | collective-permute-start | bytes 3932168 | tf_op jit(solution)/shard_map/ppermute | solution.py:42
  67.8 4.8 %collective-permute-start.18 = (bf16[256,512]{1,0:T(8,128)(2,1)S(1)}, bf16[256,512]{1,0:T(8,128)(2,1)S(1)}, u32[]{:S(2)}, u32[]{:S(2)}) collective-permute-start(bf16[256,512]{1,0:T(8,128)(2,1)S(1)} %get-tuple-element.118.refs_0_), channel_id=1, source_target_pairs={{0,1},{1,0},{2,3},{3,2},{4,5},{5,4},{6,7},{7,6},{8,9},{9,8},{10,11... | collective-permute-start | bytes 786440 | tf_op jit(solution)/shard_map/ppermute | solution.py:42
  67.9 9.6 %collective-permute-start.19 = (bf16[256,512]{1,0:T(8,128)(2,1)S(1)}, bf16[256,512]{1,0:T(8,128)(2,1)S(1)}, u32[]{:S(2)}, u32[]{:S(2)}) collective-permute-start(bf16[256,512]{1,0:T(8,128)(2,1)S(1)} %get-tuple-element.118.refs_0_), channel_id=1, source_target_pairs={{0,31},{1,2},{2,1},{3,4},{4,3},{5,6},{6,5},{7,8},{8,7},{9,10},{10,... | collective-permute-start | bytes 786440 | tf_op jit(solution)/shard_map/ppermute | solution.py:47
  67.9 9.6 %collective-permute-start.20 = (bf16[256,512]{1,0:T(8,128)(2,1)S(1)}, bf16[256,512]{1,0:T(8,128)(2,1)S(1)}, u32[]{:S(2)}, u32[]{:S(2)}) collective-permute-start(bf16[256,512]{1,0:T(8,128)(2,1)S(1)} %get-tuple-element.118.refs_0_), channel_id=1, source_target_pairs={{0,32},{32,0},{64,96},{96,64},{1,33},{33,1},{65,97},{97,65},{2,34}... | collective-permute-start | bytes 786440 | tf_op jit(solution)/shard_map/ppermute | solution.py:57
  71.3 6.3 %collective-permute-start.21 = (bf16[256,512]{1,0:T(8,128)(2,1)S(1)}, bf16[256,512]{1,0:T(8,128)(2,1)S(1)}, u32[]{:S(2)}, u32[]{:S(2)}) collective-permute-start(bf16[256,512]{1,0:T(8,128)(2,1)S(1)} %get-tuple-element.118.refs_0_), channel_id=1, source_target_pairs={{32,64},{64,32},{33,65},{65,33},{34,66},{66,34},{35,67},{67,35},{3... | collective-permute-start | bytes 786440 | tf_op jit(solution)/shard_map/ppermute | solution.py:57
  72.7 4.9 %copy-start.2 = (bf16[512,227]{0,1:T(8,128)(2,1)S(1)}, bf16[512,227]{0,1:T(8,128)(2,1)}, u32[]{:S(2)}) copy-start(bf16[512,227]{0,1:T(8,128)(2,1)} %param.14) | copy-start | bytes 697348
  72.7 7.2 %collective-permute-start.16 = (bf16[384,512]{1,0:T(8,128)(2,1)S(1)}, bf16[384,512]{1,0:T(8,128)(2,1)S(1)}, u32[]{:S(2)}, u32[]{:S(2)}) collective-permute-start(bf16[384,512]{1,0:T(8,128)(2,1)S(1)} %get-tuple-element.107), channel_id=1, source_target_pairs={{0,1},{1,0},{2,3},{3,2},{4,5},{5,4},{6,7},{7,6},{8,9},{9,8},{10,11... | collective-permute-start | bytes 1179656 | tf_op jit(solution)/shard_map/ppermute | solution.py:42
  78.6 2.2 %collective-permute-start.22 = (bf16[128,512]{1,0:T(8,128)(2,1)S(1)}, bf16[128,512]{1,0:T(8,128)(2,1)S(1)}, u32[]{:S(2)}, u32[]{:S(2)}) collective-permute-start(bf16[128,512]{1,0:T(8,128)(2,1)S(1)} %get-tuple-element.121), channel_id=1, source_target_pairs={{0,1},{1,0},{2,3},{3,2},{4,5},{5,4},{6,7},{7,6},{8,9},{9,8},{10,11... | collective-permute-start | bytes 393224 | tf_op jit(solution)/shard_map/ppermute | solution.py:42
  109.7 7.8 %collective-permute-start.23 = (bf16[112,512]{1,0:T(8,128)(2,1)S(1)}, bf16[112,512]{1,0:T(8,128)(2,1)S(1)}, u32[]{:S(2)}, u32[]{:S(2)}) collective-permute-start(bf16[112,512]{1,0:T(8,128)(2,1)S(1)} %shard_map.215.refs_0_), channel_id=1, source_target_pairs={{0,32},{32,64},{64,96},{96,0},{1,33},{33,65},{65,97},{97,1},{2,34}... | collective-permute-start | bytes 344072 | tf_op jit(solution)/shard_map/ppermute | solution.py:479
  113.4 6.1 %collective-permute-start.24 = (bf16[112,512]{1,0:T(8,128)(2,1)S(1)}, bf16[112,512]{1,0:T(8,128)(2,1)S(1)}, u32[]{:S(2)}, u32[]{:S(2)}) collective-permute-start(bf16[112,512]{1,0:T(8,128)(2,1)S(1)} %shard_map.215.refs_0_), channel_id=1, source_target_pairs={{0,64},{32,96},{64,0},{96,32},{1,65},{33,97},{65,1},{97,33},{2,66}... | collective-permute-start | bytes 344072 | tf_op jit(solution)/shard_map/ppermute | solution.py:479
  115.5 5.0 %collective-permute-start.25 = (bf16[112,512]{1,0:T(8,128)(2,1)S(1)}, bf16[112,512]{1,0:T(8,128)(2,1)S(1)}, u32[]{:S(2)}, u32[]{:S(2)}) collective-permute-start(bf16[112,512]{1,0:T(8,128)(2,1)S(1)} %shard_map.215.refs_0_), channel_id=1, source_target_pairs={{0,96},{32,0},{64,32},{96,64},{1,97},{33,1},{65,33},{97,65},{2,98}... | collective-permute-start | bytes 344072 | tf_op jit(solution)/shard_map/ppermute | solution.py:479
  147.2 6.8 %collective-permute-start.26 = (bf16[1792,512]{1,0:T(8,128)(2,1)S(1)}, bf16[1792,512]{1,0:T(8,128)(2,1)S(1)}, u32[]{:S(2)}, u32[]{:S(2)}) collective-permute-start(bf16[1792,512]{1,0:T(8,128)(2,1)S(1)} %bitcast.14), channel_id=1, source_target_pairs={{0,1},{1,0},{2,3},{3,2},{4,5},{5,4},{6,7},{7,6},{8,9},{9,8},{10,11... | collective-permute-start | bytes 5505032 | tf_op jit(solution)/shard_map/ppermute | solution.py:42

commit v4 on v3

--- a/solution.py
+++ b/solution.py
@@ -58,7 +58,10 @@
 
 
 def swap_all(on, off, north, south):
-    return swap_on(on), swap_off(off), swap_band(north, 0), swap_band(south, 1)
+    south = swap_band(south, 1)
+    north = swap_band(north, 0)
+    off = swap_off(off)
+    return swap_on(on), off, north, south
 
 
 def by_partner(slots, odd_dom, odd_band, incoming):
@@ -125,7 +128,7 @@
     return pl.pallas_call(
         body,
         out_shape=outs,
-        in_specs=[pl.BlockSpec(memory_space=pl.ANY)] * len(args),
+        in_specs=[pl.BlockSpec(memory_space=pltpu.HBM)] * len(args),
         scratch_shapes=[pltpu.VMEM(a.shape, a.dtype) for a in args]
         + [pltpu.SemaphoreType.DMA((len(args),))],
         compiler_params=pltpu.CompilerParams(vmem_limit_bytes=32 * MIB),
@@ -134,13 +137,12 @@
 
 
 def parcels(*refs):
-    inputs, rest = refs[:5], refs[5:]
+    inputs, rest = refs[:4], refs[4:]
     outs, buffers, sems = rest[: GROUPS - 1], rest[GROUPS - 1 : -1], rest[-1]
     fetch(inputs, buffers, sems)
-    grid_ref, grid_send_ref, mesh_recv_ref, mesh_send_ref, near_ref = buffers
+    grid_ref, grid_send_ref, mesh_send_ref, near_ref = buffers
     odd_dom, odd_band = odd_along("dom"), odd_along("band")
     grid_send = by_partner(slots_of(grid_send_ref[...]), odd_dom, odd_band, False)
-    mesh_recv = by_partner(slots_of(mesh_recv_ref[...]), odd_dom, odd_band, True)
     mesh_send = by_partner(slots_of(mesh_send_ref[...]), odd_dom, odd_band, False)
     near = near_ref[...]
     near = [near[:, j : j + LANES] for j in range(0, near.shape[1], LANES)]
@@ -148,7 +150,7 @@
     first = outs[0].shape[0] - INDEX_ROWS // 2
     grid = grid_ref[...]
     for p, out in enumerate(outs):
-        parts = [mesh_recv[p + 1], mesh_send[p + 1], grid_send[p + 1], *near]
+        parts = [mesh_send[p + 1], grid_send[p + 1], *near]
         used = sum(part.shape[0] for part in parts)
         parts.append(jnp.zeros((INDEX_ROWS - used, LANES), jnp.int32))
         index = jnp.concatenate(parts, 0)
@@ -183,17 +185,18 @@
     sum_ref[...] = matmul(counts, (pre * sigma).astype(HALF))
 
 
-def embed_far(p, parcel_ref, weight_ref, recv_ref, sum_ref, index_ref, out_ref):
+def embed_far(p, parcel_ref, weight_ref, recv_ref, sum_ref, index_ref, slope_ref, out_ref):
     index = index_of(parcel_ref[parcel_ref.shape[0] - INDEX_ROWS // 2 :])
     index_ref[...] = index
     step = recv_ref.shape[0] // GROUPS
     recv = by_partner(slots_of(recv_ref[...]), odd_along("dom"), odd_along("band"), True)[p]
     counts = pair_counts(
-        recv, out_ref.shape[0], index[2 * step : 3 * step], parcel_ref.shape[1]
+        recv, out_ref.shape[0], index[step : 2 * step], parcel_ref.shape[1]
     )
     pre = outer_sum(parcel_ref[: weight_ref.shape[0]], weight_ref[...])
-    latent = (pre * jax.nn.sigmoid(pre)).astype(HALF)
-    out_ref[...] = sum_ref[...] + matmul(counts, latent)
+    sigma = jax.nn.sigmoid(pre)
+    slope_ref[...] = sigma * (1.0 + pre * (1.0 - sigma))
+    out_ref[...] = sum_ref[...] + matmul(counts, (pre * sigma).astype(HALF))
 
 
 def encode(sum_ref, weight_ref, static_ref, in_ref, slope_ref, state_ref, half_ref, on_ref, off_ref):
@@ -216,7 +219,7 @@
 def near_counts(near_ref, on_ref, off_ref, out_ref, turned_ref):
     step = near_ref.shape[0]
     mesh_count = near_ref.shape[1]
-    first = 3 * SLOT_ROWS
+    first = 2 * SLOT_ROWS
     odd_dom = odd_along("dom")
     on, off = on_ref[...], off_ref[...]
     left = jnp.where(odd_dom, on, off)[first + step : first + 2 * step] + (RIM - mesh_count)
@@ -268,7 +271,7 @@
     odd_dom, odd_band = odd_along("dom"), odd_along("band")
     step = send_ref.shape[0] // GROUPS
     recv = by_partner(slots_of(recv_ref[...]), odd_dom, odd_band, True)
-    send = [send_ref[:step]] + [ref[step : 2 * step] for ref in far]
+    send = [send_ref[:step]] + [ref[:step] for ref in far]
     grids, nodes = out_ref.shape[0], turned_ref.shape[0] // GROUPS
     for p in range(GROUPS):
         at = slice(p * nodes, (p + 1) * nodes)
@@ -280,8 +283,8 @@
 def mesh_counts(send_ref, recv_ref, *refs):
     far, out_ref = refs[: GROUPS - 1], refs[GROUPS - 1]
     step = send_ref.shape[0] // GROUPS
-    send = by_partner(slots_of(send_ref[...]), odd_along("dom"), odd_along("band"), False)
-    recv = [recv_ref[:step]] + [ref[:step] for ref in far]
+    send = [send_ref[:step]] + [ref[step : 2 * step] for ref in far]
+    recv = by_partner(slots_of(recv_ref[...]), odd_along("dom"), odd_along("band"), True)
     grids, nodes = out_ref.shape[0], out_ref.shape[1] // GROUPS
     for p in range(GROUPS):
         out_ref[:, p * nodes : (p + 1) * nodes] = pair_counts(send[p], grids, recv[p], nodes)
@@ -388,21 +391,23 @@
 
 
 def embed_back(*refs):
-    returned = refs[:GROUPS]
-    counts_ref, slope_ref, grid_ref, mine_ref, other_ref, wide_ref = refs[GROUPS:]
-    nodes = returned[0].shape[0]
-    total = matmul(counts_ref[:, :nodes], returned[0][...])
-    for p in range(1, GROUPS):
-        total = total + matmul(counts_ref[:, p * nodes : (p + 1) * nodes], returned[p][...])
-    grad = (total * slope_ref[...]).astype(HALF)
-    store_halves(matmul(grid_ref[...], grad), 0, mine_ref, other_ref, wide_ref)
-
-
-def split_gradients(body, rows, macs, *args):
-    width = args[1].shape[1]
+    back_ref, counts_ref = refs[:2]
+    slopes, grids = refs[2 : 2 + GROUPS], refs[2 + GROUPS : 2 + 2 * GROUPS]
+    mine_ref, other_ref, wide_ref = refs[2 + 2 * GROUPS :]
+    nodes = back_ref.shape[0]
+    variables = grids[0].shape[0]
+    total = None
+    for p in range(GROUPS):
+        latent = matmul(counts_ref[:, p * nodes : (p + 1) * nodes], back_ref[...])
+        grad = (latent * slopes[p][...]).astype(HALF)
+        term = matmul(grids[p][:variables], grad)
+        total = term if total is None else total + term
+    store_halves(total, 0, mine_ref, other_ref, wide_ref)
+
+
+def split_gradients(body, rows, width, macs, *args):
     outs = [shape(rows, width, HALF)] * 2
-    mine, other = whole(body, outs, macs, *args, scratch=[pltpu.VMEM((width, width), SINGLE)])
-    return mine, swap_on(other)
+    return whole(body, outs, macs, *args, scratch=[pltpu.VMEM((width, width), SINGLE)])
 
 
 def add_halves(*refs):
@@ -516,7 +521,7 @@
     grid_full = shape(grid_count, width, SINGLE)
     parcel = shape(variables + -variables % 16 + INDEX_ROWS // 2, grid_count, HALF)
     sent = fetching(
-        parcels, [parcel] * (GROUPS - 1), 0, grid, grid_send, mesh_recv, mesh_send, near
+        parcels, [parcel] * (GROUPS - 1), 0, grid, grid_send, mesh_send, near
     )
     arrived = swap_all(*sent)
     embed_macs = grid_count * variables * width + mesh_count * grid_count * (step + width)
@@ -524,10 +529,12 @@
         embed_own, [grid_full, mesh_full], embed_macs, grid, embed_weight, grid_send, mesh_recv
     )
     index = [None] * GROUPS
+    slopes = [slope_embed] + [None] * (GROUPS - 1)
+    grids = [grid, *arrived]
     for p in range(1, GROUPS):
-        index[p], total = whole(
+        index[p], slopes[p], total = whole(
             lambda *refs, p=p: embed_far(p, *refs),
-            [shape(INDEX_ROWS, LANES, jnp.int32), mesh_full],
+            [shape(INDEX_ROWS, LANES, jnp.int32), grid_full, mesh_full],
             embed_macs,
             arrived[p - 1],
             embed_weight,
@@ -542,7 +549,8 @@
         encode_weight,
         mesh_static,
     )
-    on, off = swap_on(on), swap_off(off)
+    off = swap_off(off)
+    on = swap_on(on)
     counts, turned = whole(
         near_counts, [shape(ext, ext, HALF)] * 2, ext * ext * 64, near, index[1], index[2]
     )
@@ -584,17 +592,17 @@
     half_rows = split_rows(width)
     narrow_rows = split_rows(variables)
     square = width * width
-    halves = [
-        *split_gradients(
-            lambda *refs: gradient_halves(1, *refs),
-            narrow_rows + half_rows,
-            2 * grid_count * square,
-            cot,
-            hidden,
-            decode_in,
-            decode_grad,
-        )
-    ]
+    decode_halves = split_gradients(
+        lambda *refs: gradient_halves(1, *refs),
+        narrow_rows + half_rows,
+        width,
+        2 * grid_count * square,
+        cot,
+        hidden,
+        decode_in,
+        decode_grad,
+    )
+    state_grad, *decode_halves = lax.optimization_barrier((state_grad, *decode_halves))
     state_grad, layer_1, on, off = whole(
         gather_back,
         [mesh_full, mesh_rows] + [shape(rim + RIM, width, HALF)] * 2,
@@ -603,7 +611,19 @@
         *arrived,
         silu_slope(pre_1),
     )
-    on, off = swap_on(on), swap_off(off)
+    off = swap_off(off)
+    on = swap_on(on)
+    layer_halves = split_gradients(
+        lambda *refs: gradient_halves(0, *refs),
+        2 * half_rows,
+        width,
+        2 * mesh_count * square,
+        half_1,
+        layer_1,
+        nearby_1,
+        layer_1,
+    )
+    state_grad, *layer_halves = lax.optimization_barrier((state_grad, *layer_halves))
     state_grad, layer_0, encode_grad, encode_in_grad = whole(
         process_back,
         [mesh_full, mesh_rows, mesh_rows, mesh_rows],
@@ -620,7 +640,6 @@
         encode_weight,
         scratch=[pltpu.VMEM((ext, width), HALF)],
     )
-    returned = (encode_in_grad,) + swap_all(*[encode_in_grad] * 4)
     to_mesh = whole(
         mesh_counts,
         [shape(grid_count, nodes, HALF)],
@@ -629,15 +648,11 @@
         mesh_recv,
         *index[1:],
     )[0]
-    layer_1, encode_grad = lax.optimization_barrier((layer_1, encode_grad))
-    halves += split_gradients(
+    rest_halves = split_gradients(
         lambda *refs: gradient_halves(0, *refs),
-        5 * half_rows,
-        5 * mesh_count * square,
-        half_1,
-        layer_1,
-        nearby_1,
-        layer_1,
+        3 * half_rows,
+        width,
+        3 * mesh_count * square,
         half,
         layer_0,
         nearby_0,
@@ -645,15 +660,19 @@
         encode_in,
         encode_grad,
     )
-    halves += split_gradients(
+    embed_halves = split_gradients(
         embed_back,
         narrow_rows,
-        grid_count * width * (nodes + variables),
-        *returned,
+        width,
+        grid_count * width * (nodes + GROUPS * variables),
+        encode_in_grad,
         to_mesh,
-        slope_embed,
-        grid,
-    )
+        *slopes,
+        *grids,
+    )
+    halves = []
+    for mine, other in (decode_halves, layer_halves, rest_halves, embed_halves):
+        halves += [mine, swap_on(other)]
     rows = sum(block.shape[0] for block in halves[::2])
     (part,) = whole(add_halves, [shape(rows, width, HALF)], 0, *halves)
     part = reduce_all(part)

time: 158 us -> 149 us (0.943)
  starting transfers between devices: 51.2 us -> 41.3 us
  Pallas kernels: 23.9 us -> 25.5 us
    ppermute x10, starting transfers between devices: 27.3 us -> 21.8 us  [swap_on(): return lax.ppermute(value, 'dom', [(i, i ^ 1) for i in range(count)])]
    ppermute x8 -> x6, starting transfers between devices: 14.3 us -> 10.4 us  [swap_band(): return lax.ppermute(value, 'band', pairs)]
    pallas_call x19 -> x20, Pallas kernels: 21.8 us -> 23.4 us  [whole(): pl.pallas_call(body, out_shape=outs, scratch_shapes=scratch, compiler_par...]
    ppermute x8 -> x6, waiting for transfers between devices: 2.91 us -> 4.33 us  [swap_band(): return lax.ppermute(value, 'band', pairs)]
    ppermute x6 -> x5, waiting for transfers between devices: 9.31 us -> 8.57 us  [swap_off(): lax.ppermute(value, 'dom', [(i, (i + (1 if i % 2 else -1)) % count) for i...]
  transfers between devices with their start and end apart: 27 -> 24, of which waited for: 11 -> 11; matrix products, arithmetic and copies ran while one was open for 1% -> 1% of each run, Pallas kernels for 7% -> 8%
where the time goes in v4:
time: 149 us; the launch traced here: 148 us
  blocking collectives  53.9 us (36%)
  starting transfers between devices  41.3 us (28%)
  Pallas kernels  25.5 us (17%)
  waiting for transfers between devices  19.6 us (13%)
  local copies, waits for them, and re-layouts  4.84 us (3%)
    all_to_all x1, blocking collectives, reduce_all(): lax.all_to_all(part.reshape(chips, rows, width), 'dom', 0, 0, axis_index_...  27.2 us
    all_to_all x1, blocking collectives, reduce_all(): lax.all_to_all(copies, 'dom', 0, 0, axis_index_groups=groups)  26.8 us
    pallas_call x20, Pallas kernels, whole(): pl.pallas_call(body, out_shape=outs, scratch_shapes=scratch, compiler_par...  23.4 us
    ppermute x10, starting transfers between devices, swap_on(): return lax.ppermute(value, 'dom', [(i, i ^ 1) for i in range(count)])  21.8 us
    ppermute x6, starting transfers between devices, swap_band(): return lax.ppermute(value, 'band', pairs)  10.4 us
    ppermute x5, waiting for transfers between devices, swap_off(): lax.ppermute(value, 'dom', [(i, (i + (1 if i % 2 else -1)) % count) for i...  8.57 us
    ppermute x3, starting transfers between devices, reduce_all(): lax.ppermute(piece, 'band', [(i, (i + step) % bands) for i in range(bands)])  7.35 us
    unnamed x40, local copies, waits for them, and re-layouts  4.84 us
  transfers between devices with their start and end apart: 24, of which 11 were waited for; matrix products, arithmetic and copies ran while one was open for 1% of the time, Pallas kernels for 8%

profile of v4, /device:TPU:1, one launch (start us, length us, event | category | flops | bytes accessed | tf_op | source)
XLA Modules:
  0.0 148.0 jit_solution(7555454152992218100)
XLA Ops:
  0.7 1.0 copy-done.1
  1.6 0.7 copy-done.8
  2.4 0.7 copy-done.10
  3.1 0.7 copy-done.12
  3.8 0.4 shard_map.197
  4.2 1.5 %collective-permute-start.3 = (bf16[256,512]{1,0:T(8,128)(2,1)S(1)}, bf16[256,512]{1,0:T(8,128)(2,1)S(1)}, u32[]{:S(2)}, u32[]{:S(2)}) collective-permute-start(bf16[256,512]{1,0:T(8,128)(2,1)S(1)} %get-tuple-element.81), channel_id=1, source_target_pairs={{0,1},{1,0},{2,3},{3,2},{4,5},{5,4},{6,7},{7,6},{8,9},{9,8},{10,11... | collective-permute-start | bytes 786440 | tf_op jit(solution)/shard_map/ppermute | solution.py:42
  5.7 1.7 %collective-permute-start.2 = (bf16[256,512]{1,0:T(8,128)(2,1)S(1)}, bf16[256,512]{1,0:T(8,128)(2,1)S(1)}, u32[]{:S(2)}, u32[]{:S(2)}) collective-permute-start(bf16[256,512]{1,0:T(8,128)(2,1)S(1)} %get-tuple-element.80), channel_id=1, source_target_pairs={{0,31},{1,2},{2,1},{3,4},{4,3},{5,6},{6,5},{7,8},{8,7},{9,10},{10,... | collective-permute-start | bytes 786440 | tf_op jit(solution)/shard_map/ppermute | solution.py:47
  7.4 1.2 collective-permute-start.1
  8.6 0.7 collective-permute-start
  9.3 0.9 copy-done.15
  10.3 0.7 copy-done.18
  11.0 1.6 %shard_map.198 = (f32[512,512]{1,0:T(8,128)S(1)}, f32[256,512]{1,0:T(8,128)S(1)}) custom-call(bf16[227,512]{1,0:T(8,128)(2,1)S(1)} %bitcast.18, bf16[227,512]{1,0:T(8,128)(2,1)S(1)} %copy-done.15, s32[30,128]{1,0:T(8,128)S(1)} %bitcast.24, s32[30,128]{1,0:T(8,128)S(1)} %bitcast.29), custom_call_target="tpu_custom_call" | custom-call | flops 454557696 | bytes 2068480 | tf_op jit(solution)/shard_map/pallas_call | solution.py:128
  12.6 0.9 shard_map.199
  13.6 0.9 shard_map.200
  14.6 0.9 shard_map.201
  15.6 0.9 shard_map.202
  16.5 0.4 shard_map.203
  17.0 5.3 %collective-permute-start.4 = (bf16[128,512]{1,0:T(8,128)(2,1)S(1)}, bf16[128,512]{1,0:T(8,128)(2,1)S(1)}, u32[]{:S(2)}, u32[]{:S(2)}) collective-permute-start(bf16[128,512]{1,0:T(8,128)(2,1)S(1)} %get-tuple-element.89), channel_id=1, source_target_pairs={{0,1},{1,0},{2,3},{3,2},{4,5},{5,4},{6,7},{7,6},{8,9},{9,8},{10,11... | collective-permute-start | bytes 393224 | tf_op jit(solution)/shard_map/ppermute | solution.py:42
  22.3 0.7 shard_map.204
  23.1 0.3 collective-permute-done.4.on_ref
  23.3 3.4 %collective-permute-done.5.off_ref = bf16[128,512]{1,0:T(8,128)(2,1)S(1)} collective-permute-done((bf16[128,512]{1,0:T(8,128)(2,1)S(1)}, bf16[128,512]{1,0:T(8,128)(2,1)S(1)}, u32[]{:S(2)}, u32[]{:S(2)}) %collective-permute-start.5) | collective-permute-done | bytes 131104 | tf_op jit(solution)/shard_map/ppermute | solution.py:47
  26.7 1.7 %shard_map.205 = (bf16[256,512]{1,0:T(8,128)(2,1)S(1)}, f32[512,512]{1,0:T(8,128)S(1)}, f32[256,512]{1,0:T(8,128)S(1)}, bf16[256,512]{1,0:T(8,128)(2,1)S(1)}, bf...) custom-call(bf16[256,512]{1,0:T(8,128)(2,1)S(1)} %get-tuple-element.87.half_ref.refs_0_, ...), custom_call_target="tpu_custom_call" | custom-call | flops 1207959552 | bytes 6291456 | tf_op jit(solution)/shard_map/pallas_call | solution.py:81
  28.4 3.5 %collective-permute-start.6 = (bf16[256,512]{1,0:T(8,128)(2,1)S(1)}, bf16[256,512]{1,0:T(8,128)(2,1)S(1)}, u32[]{:S(2)}, u32[]{:S(2)}) collective-permute-start(bf16[256,512]{1,0:T(8,128)(2,1)S(1)} %get-tuple-element.94.refs_0_), channel_id=1, source_target_pairs={{0,1},{1,0},{2,3},{3,2},{4,5},{5,4},{6,7},{7,6},{8,9},{9,8},{10,11... | collective-permute-start | bytes 786440 | tf_op jit(solution)/shard_map/ppermute | solution.py:42
  31.9 3.7 %collective-permute-start.8 = (bf16[256,512]{1,0:T(8,128)(2,1)S(1)}, bf16[256,512]{1,0:T(8,128)(2,1)S(1)}, u32[]{:S(2)}, u32[]{:S(2)}) collective-permute-start(bf16[256,512]{1,0:T(8,128)(2,1)S(1)} %get-tuple-element.94.refs_0_), channel_id=1, source_target_pairs={{0,32},{32,0},{64,96},{96,64},{1,33},{33,1},{65,97},{97,65},{2,34}... | collective-permute-start | bytes 786440 | tf_op jit(solution)/shard_map/ppermute | solution.py:57
  35.6 0.8 collective-permute-start.9
  36.4 0.3 fusion.1.refs_8_
  36.8 2.3 %shard_map.206 = (bf16[512,1280]{1,0:T(8,128)(2,1)S(1)}, bf16[1280,512]{1,0:T(8,128)(2,1)S(1)}) custom-call(s32[30,128]{1,0:T(8,128)S(1)} %bitcast.22, s32[30,128]{1,0:T(8,128)S(1)} %bitcast.28, s32[32,128]{1,0:T(8,128)S(1)} %get-tuple-element.91.on_ref.refs_0_, s32[32,128]{1,0:T(8,128)S(1)} %get-tuple-element.92.off_ref.refs_1_, ...), custom_call_target="tpu_custom_call" | custom-call | flops 2013265920 | bytes 2717696 | tf_op jit(solution)/shard_map/pallas_call | solution.py:81
  39.2 2.2 %collective-permute-done.8.refs_3_ = bf16[256,512]{1,0:T(8,128)(2,1)S(1)} collective-permute-done((bf16[256,512]{1,0:T(8,128)(2,1)S(1)}, bf16[256,512]{1,0:T(8,128)(2,1)S(1)}, u32[]{:S(2)}, u32[]{:S(2)}) %collective-permute-start.8) | collective-permute-done | bytes 262176 | tf_op jit(solution)/shard_map/ppermute | solution.py:57
  41.4 2.4 %shard_map.207 = (bf16[512,512]{1,0:T(8,128)(2,1)S(1)}, bf16[512,512]{1,0:T(8,128)(2,1)S(1)}, bf16[512,512]{1,0:T(8,128)(2,1)S(1)}, f32[256,512]{1,0:T(8,128)S(1...) custom-call(bf16[256,512]{1,0:T(8,128)(2,1)S(1)} %get-tuple-element., ...), custom_call_target="tpu_custom_call" | custom-call | flops 1879048192 | bytes 8650752 | tf_op jit(solution)/shard_map/pallas_call | solution.py:81
  43.7 1.5 %collective-permute-start.10 = (bf16[256,512]{1,0:T(8,128)(2,1)S(1)}, bf16[256,512]{1,0:T(8,128)(2,1)S(1)}, u32[]{:S(2)}, u32[]{:S(2)}) collective-permute-start(bf16[256,512]{1,0:T(8,128)(2,1)S(1)} %get-tuple-element.106), channel_id=1, source_target_pairs={{0,1},{1,0},{2,3},{3,2},{4,5},{5,4},{6,7},{7,6},{8,9},{9,8},{10,11... | collective-permute-start | bytes 786440 | tf_op jit(solution)/shard_map/ppermute | solution.py:42
  45.3 3.4 %collective-permute-start.12 = (bf16[256,512]{1,0:T(8,128)(2,1)S(1)}, bf16[256,512]{1,0:T(8,128)(2,1)S(1)}, u32[]{:S(2)}, u32[]{:S(2)}) collective-permute-start(bf16[256,512]{1,0:T(8,128)(2,1)S(1)} %get-tuple-element.108), channel_id=1, source_target_pairs={{0,32},{32,0},{64,96},{96,64},{1,33},{33,1},{65,97},{97,65},{2,34}... | collective-permute-start | bytes 786440 | tf_op jit(solution)/shard_map/ppermute | solution.py:57
  48.6 0.7 collective-permute-start.13
  49.3 0.2 add_multiply_fusion.1.refs_5_
  49.5 0.7 shard_map.208
  50.2 1.1 collective-permute-done.11.refs_2_
  51.4 2.1 %collective-permute-done.12.refs_3_ = bf16[256,512]{1,0:T(8,128)(2,1)S(1)} collective-permute-done((bf16[256,512]{1,0:T(8,128)(2,1)S(1)}, bf16[256,512]{1,0:T(8,128)(2,1)S(1)}, u32[]{:S(2)}, u32[]{:S(2)}) %collective-permute-start.12) | collective-permute-done | bytes 262176 | tf_op jit(solution)/shard_map/ppermute | solution.py:57
  53.5 0.2 shard_map.209
  53.8 2.5 %collective-permute-start.14 = (bf16[192,512]{1,0:T(8,128)(2,1)S(1)}, bf16[192,512]{1,0:T(8,128)(2,1)S(1)}, u32[]{:S(2)}, u32[]{:S(2)}) collective-permute-start(bf16[192,512]{1,0:T(8,128)(2,1)S(1)} %get-tuple-element.118), channel_id=1, source_target_pairs={{0,1},{1,0},{2,3},{3,2},{4,5},{5,4},{6,7},{7,6},{8,9},{9,8},{10,11... | collective-permute-start | bytes 589832 | tf_op jit(solution)/shard_map/ppermute | solution.py:42
  56.2 0.4 add_multiply_fusion.slope_0_ref
  56.6 0.6 shard_map.210
  57.3 4.0 %collective-permute-done.15.off_ref = bf16[192,512]{1,0:T(8,128)(2,1)S(1)} collective-permute-done((bf16[192,512]{1,0:T(8,128)(2,1)S(1)}, bf16[192,512]{1,0:T(8,128)(2,1)S(1)}, u32[]{:S(2)}, u32[]{:S(2)}) %collective-permute-start.15) | collective-permute-done | bytes 196640 | tf_op jit(solution)/shard_map/ppermute | solution.py:47
  61.3 2.3 %shard_map.211 = (f32[256,512]{1,0:T(8,128)}, bf16[256,512]{1,0:T(8,128)(2,1)S(1)}, bf16[256,512]{1,0:T(8,128)(2,1)S(1)}, bf16[256,512]{1,0:T(8,128)(2,1)S(1)}) custom-call(f32[256,512]{1,0:T(8,128)S(1)} %get-tuple-element.117.state_ref, bf16[256,512]{1,0:T(8,128)(2,1)S(1)} %get-tuple-element.113.refs_1_.refs_3_.layer_ref, ...), custom_call_target="tpu_custom_call" | custom-call | flops 1207959552 | bytes 7208960 | tf_op jit(solution)/shard_map/pallas_call | solution.py:81
  63.6 0.9 shard_map.212
  64.5 3.5 %collective-permute-start.18 = (bf16[768,512]{1,0:T(8,128)(2,1)S(1)}, bf16[768,512]{1,0:T(8,128)(2,1)S(1)}, u32[]{:S(2)}, u32[]{:S(2)}) collective-permute-start(bf16[768,512]{1,0:T(8,128)(2,1)S(1)} %get-tuple-element.133), channel_id=1, source_target_pairs={{0,1},{1,0},{2,3},{3,2},{4,5},{5,4},{6,7},{7,6},{8,9},{9,8},{10,11... | collective-permute-start | bytes 2359304 | tf_op jit(solution)/shard_map/ppermute | solution.py:42
  68.0 0.1 collective-permute-start.17
  68.1 0.4 collective-permute-start.16
  68.5 1.4 shard_map.213.refs_1_
  70.0 1.9 %shard_map.214 = (bf16[128,512]{1,0:T(8,128)(2,1)S(1)}, bf16[128,512]{1,0:T(8,128)(2,1)S(1)}) custom-call(bf16[256,512]{1,0:T(8,128)(2,1)S(1)} %get-tuple-element.134.refs_0_, bf16[512,1280]{1,0:T(8,128)(2,1)S(1)} %shard_map.213.refs_1_, f32[512,512]{1,0:T(8,128)S(1)} %get-tuple-element.135.refs_2_, f32[512,512]{1,0:T(8,128)S(1)} %get-tuple-element.136.refs_3_, ...), custom_call_target="tpu_custom_call" | custom-call | flops 1266155520 | bytes 8358912 | tf_op jit(solution)/shard_map/pallas_call | solution.py:81
  71.8 0.2 collective-permute-start.19
  72.0 1.3 collective-permute-done.19.refs_7_
  73.2 0.4 shard_map.215
  73.7 27.2 %all_to_all.10.pieces_ref = bf16[16,112,512]{2,1,0:T(8,128)(2,1)S(1)} all-to-all(bf16[16,112,512]{2,1,0:T(8,128)(2,1)S(1)} %bitcast.16), channel_id=1, replica_groups={{0,2,4,6,8,10,12,14,16,18,20,22,24,26,28,30},{1,3,5,7,9,11,13,15,17,19,..., dimensions={0} | all-to-all | bytes 3670016 | tf_op jit(solution)/shard_map/all_to_all | solution.py:479
  100.8 0.2 shard_map.216.refs_0_
  101.1 3.7 %collective-permute-start.20 = (bf16[112,512]{1,0:T(8,128)(2,1)S(1)}, bf16[112,512]{1,0:T(8,128)(2,1)S(1)}, u32[]{:S(2)}, u32[]{:S(2)}) collective-permute-start(bf16[112,512]{1,0:T(8,128)(2,1)S(1)} %shard_map.216.refs_0_), channel_id=1, source_target_pairs={{0,32},{32,64},{64,96},{96,0},{1,33},{33,65},{65,97},{97,1},{2,34}... | collective-permute-start | bytes 344072 | tf_op jit(solution)/shard_map/ppermute | solution.py:484
  104.7 1.7 %collective-permute-start.21 = (bf16[112,512]{1,0:T(8,128)(2,1)S(1)}, bf16[112,512]{1,0:T(8,128)(2,1)S(1)}, u32[]{:S(2)}, u32[]{:S(2)}) collective-permute-start(bf16[112,512]{1,0:T(8,128)(2,1)S(1)} %shard_map.216.refs_0_), channel_id=1, source_target_pairs={{0,64},{32,96},{64,0},{96,32},{1,65},{33,97},{65,1},{97,33},{2,66}... | collective-permute-start | bytes 344072 | tf_op jit(solution)/shard_map/ppermute | solution.py:484
  106.4 2.0 %collective-permute-start.22 = (bf16[112,512]{1,0:T(8,128)(2,1)S(1)}, bf16[112,512]{1,0:T(8,128)(2,1)S(1)}, u32[]{:S(2)}, u32[]{:S(2)}) collective-permute-start(bf16[112,512]{1,0:T(8,128)(2,1)S(1)} %shard_map.216.refs_0_), channel_id=1, source_target_pairs={{0,96},{32,0},{64,32},{96,64},{1,97},{33,1},{65,33},{97,65},{2,98}... | collective-permute-start | bytes 344072 | tf_op jit(solution)/shard_map/ppermute | solution.py:484
  108.4 2.1 %collective-permute-done.21.refs_2_ = bf16[112,512]{1,0:T(8,128)(2,1)S(1)} collective-permute-done((bf16[112,512]{1,0:T(8,128)(2,1)S(1)}, bf16[112,512]{1,0:T(8,128)(2,1)S(1)}, u32[]{:S(2)}, u32[]{:S(2)}) %collective-permute-start.21) | collective-permute-done | bytes 114720 | tf_op jit(solution)/shard_map/ppermute | solution.py:484
  110.6 0.6 collective-permute-done.22.refs_3_
  111.1 0.2 shard_map.217
  111.3 26.8 %all_to_all.11 = bf16[16,112,512]{2,1,0:T(8,128)(2,1)S(1)} all-to-all(bf16[16,112,512]{2,1,0:T(8,128)(2,1)S(1)} %shard_map.217), channel_id=1, replica_groups={{0,2,4,6,8,10,12,14,16,18,20,22,24,26,28,30},{1,3,5,7,9,11,13,15,17,19,..., dimensions={0} | all-to-all | bytes 3670016 | tf_op jit(solution)/shard_map/all_to_all | solution.py:489
  138.1 3.3 %collective-permute-start.23 = (bf16[1792,512]{1,0:T(8,128)(2,1)S(1)}, bf16[1792,512]{1,0:T(8,128)(2,1)S(1)}, u32[]{:S(2)}, u32[]{:S(2)}) collective-permute-start(bf16[1792,512]{1,0:T(8,128)(2,1)S(1)} %bitcast.14), channel_id=1, source_target_pairs={{0,1},{1,0},{2,3},{3,2},{4,5},{5,4},{6,7},{7,6},{8,9},{9,8},{10,11... | collective-permute-start | bytes 5505032 | tf_op jit(solution)/shard_map/ppermute | solution.py:42
  141.4 1.0 fusion
  142.4 2.4 %collective-permute-done.23.other_ref = bf16[1792,512]{1,0:T(8,128)(2,1)S(1)} collective-permute-done((bf16[1792,512]{1,0:T(8,128)(2,1)S(1)}, bf16[1792,512]{1,0:T(8,128)(2,1)S(1)}, u32[]{:S(2)}, u32[]{:S(2)}) %collective-permute-start.23) | collective-permute-done | bytes 1835040 | tf_op jit(solution)/shard_map/ppermute | solution.py:42
  144.8 3.2 %shard_map.218 = (f32[227,512]{1,0:T(8,128)}, f32[512,512]{1,0:T(8,128)}, f32[2,512,512]{2,1,0:T(8,128)}, f32[2,512,512]{2,1,0:T(8,128)}, f32[512,512]{1,0:T(8,128)}, /*index=5*/f32[227,512]{1,0:T(8,128)}) custom-call(bf16[1792,512]{1,0:T(8,128)(2,1)S(1)} %bitcast.15, bf16[1792,512]{1,0:T(8,128)(2,1)S(1)} %collective-permute-done.23.other_ref), custom_call_target="tpu_custom_call" | custom-call | bytes 10891264 | tf_op jit(solution)/shard_map/pallas_call | solution.py:81
  (52 shorter events, 0.2 us)
Async XLA Ops:
  0.6 35.8 %copy-start = (bf16[512,227]{0,1:T(8,128)(2,1)S(1)}, bf16[512,227]{0,1:T(8,128)(2,1)}, u32[]{:S(2)}) copy-start(bf16[512,227]{0,1:T(8,128)(2,1)} %param.22) | copy-start | bytes 697348
  0.6 1.0 copy-start.1
  1.6 0.7 copy-start.8
  2.4 0.7 copy-start.10
  3.1 0.7 copy-start.12
  3.8 8.8 %copy-start.16 = (bf16[227,512]{1,0:T(8,128)(2,1)S(1)}, bf16[227,512]{1,0:T(8,128)(2,1)}, u32[]{:S(2)}) copy-start(bf16[227,512]{1,0:T(8,128)(2,1)} %refs_1_.9) | copy-start | bytes 697348
  3.8 8.8 %copy-start.19 = (s32[3840]{0:T(1024)S(1)}, s32[3840]{0:T(1024)}, u32[]{:S(2)}) copy-start(s32[3840]{0:T(1024)} %param.24) | copy-start | bytes 46084
  4.2 8.4 %collective-permute-start.3 = (bf16[256,512]{1,0:T(8,128)(2,1)S(1)}, bf16[256,512]{1,0:T(8,128)(2,1)S(1)}, u32[]{:S(2)}, u32[]{:S(2)}) collective-permute-start(bf16[256,512]{1,0:T(8,128)(2,1)S(1)} %get-tuple-element.81), channel_id=1, source_target_pairs={{0,1},{1,0},{2,3},{3,2},{4,5},{5,4},{6,7},{7,6},{8,9},{9,8},{10,11... | collective-permute-start | bytes 786440 | tf_op jit(solution)/shard_map/ppermute | solution.py:42
  5.7 7.8 %collective-permute-start.2 = (bf16[256,512]{1,0:T(8,128)(2,1)S(1)}, bf16[256,512]{1,0:T(8,128)(2,1)S(1)}, u32[]{:S(2)}, u32[]{:S(2)}) collective-permute-start(bf16[256,512]{1,0:T(8,128)(2,1)S(1)} %get-tuple-element.80), channel_id=1, source_target_pairs={{0,31},{1,2},{2,1},{3,4},{4,3},{5,6},{6,5},{7,8},{8,7},{9,10},{10,... | collective-permute-start | bytes 786440 | tf_op jit(solution)/shard_map/ppermute | solution.py:47
  7.4 7.1 %collective-permute-start.1 = (bf16[256,512]{1,0:T(8,128)(2,1)S(1)}, bf16[256,512]{1,0:T(8,128)(2,1)S(1)}, u32[]{:S(2)}, u32[]{:S(2)}) collective-permute-start(bf16[256,512]{1,0:T(8,128)(2,1)S(1)} %get-tuple-element.79), channel_id=1, source_target_pairs={{0,32},{32,0},{64,96},{96,64},{1,33},{33,1},{65,97},{97,65},{2,34}... | collective-permute-start | bytes 786440 | tf_op jit(solution)/shard_map/ppermute | solution.py:57
  8.6 6.9 %collective-permute-start = (bf16[256,512]{1,0:T(8,128)(2,1)S(1)}, bf16[256,512]{1,0:T(8,128)(2,1)S(1)}, u32[]{:S(2)}, u32[]{:S(2)}) collective-permute-start(bf16[256,512]{1,0:T(8,128)(2,1)S(1)} %get-tuple-element.78), channel_id=1, source_target_pairs={{32,64},{64,32},{33,65},{65,33},{34,66},{66,34},{35,67},{67,35},{3... | collective-permute-start | bytes 786440 | tf_op jit(solution)/shard_map/ppermute | solution.py:57
  9.3 0.9 copy-start.15
  10.3 0.7 copy-start.18
  14.5 2.0 %copy-start.3 = (bf16[512,512]{1,0:T(8,128)(2,1)S(1)}, bf16[512,512]{1,0:T(8,128)(2,1)}, u32[]{:S(2)}) copy-start(bf16[512,512]{1,0:T(8,128)(2,1)} %encode_ref.1) | copy-start | bytes 1572868
  14.5 2.0 %copy-start.6 = (bf16[256,512]{1,0:T(8,128)(2,1)S(1)}, bf16[256,512]{1,0:T(8,128)(2,1)}, u32[]{:S(2)}) copy-start(bf16[256,512]{1,0:T(8,128)(2,1)} %static_ref.1) | copy-start | bytes 786436
  15.5 6.8 %copy-start.13 = (s32[256,6]{0,1:T(8,128)S(1)}, s32[256,6]{0,1:T(8,128)}, u32[]{:S(2)}) copy-start(s32[256,6]{0,1:T(8,128)} %param.25) | copy-start | bytes 18436
  15.5 11.2 %copy-start.4 = (bf16[2,512,512]{2,1,0:T(8,128)(2,1)S(1)}, bf16[2,512,512]{2,1,0:T(8,128)(2,1)}, u32[]{:S(2)}) copy-start(bf16[2,512,512]{2,1,0:T(8,128)(2,1)} %self_ref.3) | copy-start | bytes 3145732
  15.5 11.2 %copy-start.5 = (bf16[2,512,512]{2,1,0:T(8,128)(2,1)S(1)}, bf16[2,512,512]{2,1,0:T(8,128)(2,1)}, u32[]{:S(2)}) copy-start(bf16[2,512,512]{2,1,0:T(8,128)(2,1)} %near_ref.3) | copy-start | bytes 3145732
  17.0 6.3 %collective-permute-start.4 = (bf16[128,512]{1,0:T(8,128)(2,1)S(1)}, bf16[128,512]{1,0:T(8,128)(2,1)S(1)}, u32[]{:S(2)}, u32[]{:S(2)}) collective-permute-start(bf16[128,512]{1,0:T(8,128)(2,1)S(1)} %get-tuple-element.89), channel_id=1, source_target_pairs={{0,1},{1,0},{2,3},{3,2},{4,5},{5,4},{6,7},{7,6},{8,9},{9,8},{10,11... | collective-permute-start | bytes 393224 | tf_op jit(solution)/shard_map/ppermute | solution.py:42
  22.3 4.4 %collective-permute-start.5 = (bf16[128,512]{1,0:T(8,128)(2,1)S(1)}, bf16[128,512]{1,0:T(8,128)(2,1)S(1)}, u32[]{:S(2)}, u32[]{:S(2)}) collective-permute-start(bf16[128,512]{1,0:T(8,128)(2,1)S(1)} %get-tuple-element.90), channel_id=1, source_target_pairs={{0,31},{1,2},{2,1},{3,4},{4,3},{5,6},{6,5},{7,8},{8,7},{9,10},{10,... | collective-permute-start | bytes 393224 | tf_op jit(solution)/shard_map/ppermute | solution.py:47
  26.7 9.7 %copy-start.7 = (bf16[512,227]{0,1:T(8,128)(2,1)S(1)}, bf16[512,227]{0,1:T(8,128)(2,1)}, u32[]{:S(2)}) copy-start(bf16[512,227]{0,1:T(8,128)(2,1)} %param.15) | copy-start | bytes 697348
  26.7 10.1 %copy-start.9 = (s32[3840]{0:T(1024)S(1)}, s32[3840]{0:T(1024)}, u32[]{:S(2)}) copy-start(s32[3840]{0:T(1024)} %param.26) | copy-start | bytes 46084
  26.7 10.1 %copy-start.17 = (s32[3840]{0:T(1024)S(1)}, s32[3840]{0:T(1024)}, u32[]{:S(2)}) copy-start(s32[3840]{0:T(1024)} %param.27) | copy-start | bytes 46084
  28.4 10.7 %collective-permute-start.6 = (bf16[256,512]{1,0:T(8,128)(2,1)S(1)}, bf16[256,512]{1,0:T(8,128)(2,1)S(1)}, u32[]{:S(2)}, u32[]{:S(2)}) collective-permute-start(bf16[256,512]{1,0:T(8,128)(2,1)S(1)} %get-tuple-element.94.refs_0_), channel_id=1, source_target_pairs={{0,1},{1,0},{2,3},{3,2},{4,5},{5,4},{6,7},{7,6},{8,9},{9,8},{10,11... | collective-permute-start | bytes 786440 | tf_op jit(solution)/shard_map/ppermute | solution.py:42
  31.9 7.3 %collective-permute-start.7 = (bf16[256,512]{1,0:T(8,128)(2,1)S(1)}, bf16[256,512]{1,0:T(8,128)(2,1)S(1)}, u32[]{:S(2)}, u32[]{:S(2)}) collective-permute-start(bf16[256,512]{1,0:T(8,128)(2,1)S(1)} %get-tuple-element.94.refs_0_), channel_id=1, source_target_pairs={{0,31},{1,2},{2,1},{3,4},{4,3},{5,6},{6,5},{7,8},{8,7},{9,10},{10,... | collective-permute-start | bytes 786440 | tf_op jit(solution)/shard_map/ppermute | solution.py:47
  31.9 9.4 %collective-permute-start.8 = (bf16[256,512]{1,0:T(8,128)(2,1)S(1)}, bf16[256,512]{1,0:T(8,128)(2,1)S(1)}, u32[]{:S(2)}, u32[]{:S(2)}) collective-permute-start(bf16[256,512]{1,0:T(8,128)(2,1)S(1)} %get-tuple-element.94.refs_0_), channel_id=1, source_target_pairs={{0,32},{32,0},{64,96},{96,64},{1,33},{33,1},{65,97},{97,65},{2,34}... | collective-permute-start | bytes 786440 | tf_op jit(solution)/shard_map/ppermute | solution.py:57
  35.6 5.8 %collective-permute-start.9 = (bf16[256,512]{1,0:T(8,128)(2,1)S(1)}, bf16[256,512]{1,0:T(8,128)(2,1)S(1)}, u32[]{:S(2)}, u32[]{:S(2)}) collective-permute-start(bf16[256,512]{1,0:T(8,128)(2,1)S(1)} %get-tuple-element.94.refs_0_), channel_id=1, source_target_pairs={{32,64},{64,32},{33,65},{65,33},{34,66},{66,34},{35,67},{67,35},{3... | collective-permute-start | bytes 786440 | tf_op jit(solution)/shard_map/ppermute | solution.py:57
  36.8 4.6 %copy-start.14 = (bf16[512,512]{1,0:T(8,128)(2,1)S(1)}, bf16[512,512]{1,0:T(8,128)(2,1)}, u32[]{:S(2)}) copy-start(bf16[512,512]{1,0:T(8,128)(2,1)} %refs_7_.1) | copy-start | bytes 1572868
  43.7 6.5 %collective-permute-start.10 = (bf16[256,512]{1,0:T(8,128)(2,1)S(1)}, bf16[256,512]{1,0:T(8,128)(2,1)S(1)}, u32[]{:S(2)}, u32[]{:S(2)}) collective-permute-start(bf16[256,512]{1,0:T(8,128)(2,1)S(1)} %get-tuple-element.106), channel_id=1, source_target_pairs={{0,1},{1,0},{2,3},{3,2},{4,5},{5,4},{6,7},{7,6},{8,9},{9,8},{10,11... | collective-permute-start | bytes 786440 | tf_op jit(solution)/shard_map/ppermute | solution.py:42
  45.3 6.1 %collective-permute-start.11 = (bf16[256,512]{1,0:T(8,128)(2,1)S(1)}, bf16[256,512]{1,0:T(8,128)(2,1)S(1)}, u32[]{:S(2)}, u32[]{:S(2)}) collective-permute-start(bf16[256,512]{1,0:T(8,128)(2,1)S(1)} %get-tuple-element.107), channel_id=1, source_target_pairs={{0,31},{1,2},{2,1},{3,4},{4,3},{5,6},{6,5},{7,8},{8,7},{9,10},{10,... | collective-permute-start | bytes 786440 | tf_op jit(solution)/shard_map/ppermute | solution.py:47
  45.3 8.2 %collective-permute-start.12 = (bf16[256,512]{1,0:T(8,128)(2,1)S(1)}, bf16[256,512]{1,0:T(8,128)(2,1)S(1)}, u32[]{:S(2)}, u32[]{:S(2)}) collective-permute-start(bf16[256,512]{1,0:T(8,128)(2,1)S(1)} %get-tuple-element.108), channel_id=1, source_target_pairs={{0,32},{32,0},{64,96},{96,64},{1,33},{33,1},{65,97},{97,65},{2,34}... | collective-permute-start | bytes 786440 | tf_op jit(solution)/shard_map/ppermute | solution.py:57
  48.6 4.9 %collective-permute-start.13 = (bf16[256,512]{1,0:T(8,128)(2,1)S(1)}, bf16[256,512]{1,0:T(8,128)(2,1)S(1)}, u32[]{:S(2)}, u32[]{:S(2)}) collective-permute-start(bf16[256,512]{1,0:T(8,128)(2,1)S(1)} %get-tuple-element.109), channel_id=1, source_target_pairs={{32,64},{64,32},{33,65},{65,33},{34,66},{66,34},{35,67},{67,35},{3... | collective-permute-start | bytes 786440 | tf_op jit(solution)/shard_map/ppermute | solution.py:57
  53.8 3.5 %collective-permute-start.14 = (bf16[192,512]{1,0:T(8,128)(2,1)S(1)}, bf16[192,512]{1,0:T(8,128)(2,1)S(1)}, u32[]{:S(2)}, u32[]{:S(2)}) collective-permute-start(bf16[192,512]{1,0:T(8,128)(2,1)S(1)} %get-tuple-element.118), channel_id=1, source_target_pairs={{0,1},{1,0},{2,3},{3,2},{4,5},{5,4},{6,7},{7,6},{8,9},{9,8},{10,11... | collective-permute-start | bytes 589832 | tf_op jit(solution)/shard_map/ppermute | solution.py:42
  56.2 5.1 %collective-permute-start.15 = (bf16[192,512]{1,0:T(8,128)(2,1)S(1)}, bf16[192,512]{1,0:T(8,128)(2,1)S(1)}, u32[]{:S(2)}, u32[]{:S(2)}) collective-permute-start(bf16[192,512]{1,0:T(8,128)(2,1)S(1)} %get-tuple-element.119), channel_id=1, source_target_pairs={{0,31},{1,2},{2,1},{3,4},{4,3},{5,6},{6,5},{7,8},{8,7},{9,10},{10,... | collective-permute-start | bytes 589832 | tf_op jit(solution)/shard_map/ppermute | solution.py:47
  61.3 7.2 %copy-start.11 = (s32[3840]{0:T(1024)S(1)}, s32[3840]{0:T(1024)}, u32[]{:S(2)}) copy-start(s32[3840]{0:T(1024)} %param.23) | copy-start | bytes 46084
  64.5 5.4 %copy-start.2 = (bf16[512,227]{0,1:T(8,128)(2,1)S(1)}, bf16[512,227]{0,1:T(8,128)(2,1)}, u32[]{:S(2)}) copy-start(bf16[512,227]{0,1:T(8,128)(2,1)} %param.14) | copy-start | bytes 697348
  64.5 8.7 %collective-permute-start.18 = (bf16[768,512]{1,0:T(8,128)(2,1)S(1)}, bf16[768,512]{1,0:T(8,128)(2,1)S(1)}, u32[]{:S(2)}, u32[]{:S(2)}) collective-permute-start(bf16[768,512]{1,0:T(8,128)(2,1)S(1)} %get-tuple-element.133), channel_id=1, source_target_pairs={{0,1},{1,0},{2,3},{3,2},{4,5},{5,4},{6,7},{7,6},{8,9},{9,8},{10,11... | collective-permute-start | bytes 2359304 | tf_op jit(solution)/shard_map/ppermute | solution.py:42
  68.0 5.2 %collective-permute-start.17 = (bf16[512,512]{1,0:T(8,128)(2,1)S(1)}, bf16[512,512]{1,0:T(8,128)(2,1)S(1)}, u32[]{:S(2)}, u32[]{:S(2)}) collective-permute-start(bf16[512,512]{1,0:T(8,128)(2,1)S(1)} %get-tuple-element.127), channel_id=1, source_target_pairs={{0,1},{1,0},{2,3},{3,2},{4,5},{5,4},{6,7},{7,6},{8,9},{9,8},{10,11... | collective-permute-start | bytes 1572872 | tf_op jit(solution)/shard_map/ppermute | solution.py:42
  68.1 3.9 %collective-permute-start.16 = (bf16[384,512]{1,0:T(8,128)(2,1)S(1)}, bf16[384,512]{1,0:T(8,128)(2,1)S(1)}, u32[]{:S(2)}, u32[]{:S(2)}) collective-permute-start(bf16[384,512]{1,0:T(8,128)(2,1)S(1)} %get-tuple-element.125), channel_id=1, source_target_pairs={{0,1},{1,0},{2,3},{3,2},{4,5},{5,4},{6,7},{7,6},{8,9},{9,8},{10,11... | collective-permute-start | bytes 1179656 | tf_op jit(solution)/shard_map/ppermute | solution.py:42
  71.8 1.4 collective-permute-start.19
  101.1 7.4 %collective-permute-start.20 = (bf16[112,512]{1,0:T(8,128)(2,1)S(1)}, bf16[112,512]{1,0:T(8,128)(2,1)S(1)}, u32[]{:S(2)}, u32[]{:S(2)}) collective-permute-start(bf16[112,512]{1,0:T(8,128)(2,1)S(1)} %shard_map.216.refs_0_), channel_id=1, source_target_pairs={{0,32},{32,64},{64,96},{96,0},{1,33},{33,65},{65,97},{97,1},{2,34}... | collective-permute-start | bytes 344072 | tf_op jit(solution)/shard_map/ppermute | solution.py:484
  104.7 5.8 %collective-permute-start.21 = (bf16[112,512]{1,0:T(8,128)(2,1)S(1)}, bf16[112,512]{1,0:T(8,128)(2,1)S(1)}, u32[]{:S(2)}, u32[]{:S(2)}) collective-permute-start(bf16[112,512]{1,0:T(8,128)(2,1)S(1)} %shard_map.216.refs_0_), channel_id=1, source_target_pairs={{0,64},{32,96},{64,0},{96,32},{1,65},{33,97},{65,1},{97,33},{2,66}... | collective-permute-start | bytes 344072 | tf_op jit(solution)/shard_map/ppermute | solution.py:484
  106.4 4.7 %collective-permute-start.22 = (bf16[112,512]{1,0:T(8,128)(2,1)S(1)}, bf16[112,512]{1,0:T(8,128)(2,1)S(1)}, u32[]{:S(2)}, u32[]{:S(2)}) collective-permute-start(bf16[112,512]{1,0:T(8,128)(2,1)S(1)} %shard_map.216.refs_0_), channel_id=1, source_target_pairs={{0,96},{32,0},{64,32},{96,64},{1,97},{33,1},{65,33},{97,65},{2,98}... | collective-permute-start | bytes 344072 | tf_op jit(solution)/shard_map/ppermute | solution.py:484
  138.1 6.8 %collective-permute-start.23 = (bf16[1792,512]{1,0:T(8,128)(2,1)S(1)}, bf16[1792,512]{1,0:T(8,128)(2,1)S(1)}, u32[]{:S(2)}, u32[]{:S(2)}) collective-permute-start(bf16[1792,512]{1,0:T(8,128)(2,1)S(1)} %bitcast.14), channel_id=1, source_target_pairs={{0,1},{1,0},{2,3},{3,2},{4,5},{5,4},{6,7},{7,6},{8,9},{9,8},{10,11... | collective-permute-start | bytes 5505032 | tf_op jit(solution)/shard_map/ppermute | solution.py:42

commit v5 on v4

--- a/solution.py
+++ b/solution.py
@@ -123,7 +123,7 @@
         copy.wait()
 
 
-def fetching(body, outs, macs, *args):
+def fetching(body, outs, macs, *args, limit):
     moved = sum(a.size * a.dtype.itemsize for a in (*args, *outs))
     return pl.pallas_call(
         body,
@@ -131,7 +131,7 @@
         in_specs=[pl.BlockSpec(memory_space=pltpu.HBM)] * len(args),
         scratch_shapes=[pltpu.VMEM(a.shape, a.dtype) for a in args]
         + [pltpu.SemaphoreType.DMA((len(args),))],
-        compiler_params=pltpu.CompilerParams(vmem_limit_bytes=32 * MIB),
+        compiler_params=pltpu.CompilerParams(vmem_limit_bytes=limit * MIB),
         cost_estimate=pl.CostEstimate(flops=2 * macs, bytes_accessed=moved, transcendentals=0),
     )(*args)
 
@@ -172,7 +172,7 @@
 
 
 def embed_own(*refs):
-    inputs, (slope_ref, sum_ref), buffers, sems = refs[:4], refs[4:6], refs[6:-1], refs[-1]
+    inputs, (slope_ref, sum_ref, held_ref), buffers, sems = refs[:4], refs[4:7], refs[7:-1], refs[-1]
     fetch(inputs, buffers, sems)
     grid_ref, weight_ref, send_ref, recv_ref = buffers
     step = send_ref.shape[0] // GROUPS
@@ -183,6 +183,7 @@
     sigma = jax.nn.sigmoid(pre)
     slope_ref[...] = sigma * (1.0 + pre * (1.0 - sigma))
     sum_ref[...] = matmul(counts, (pre * sigma).astype(HALF))
+    held_ref[...] = weight_ref[...]
 
 
 def embed_far(p, parcel_ref, weight_ref, recv_ref, sum_ref, index_ref, slope_ref, out_ref):
@@ -438,36 +439,82 @@
         out_ref[i] = total
 
 
-def unpack(part_ref, other_ref, *outs):
+def places(outs):
+    encode, self_, near, decode = outs
+    return [(decode, None), (self_, 1), (near, 1), (self_, 0), (near, 0), (encode, None)]
+
+
+def store_squares(first, half, value_ref, outs, buffer_ref, sems):
+    rows = outs[0].shape[0] // 2
+    spot = pl.ds(pl.multiple_of(half * rows, rows), rows)
+    copies = []
+    for i, (out, which) in enumerate(places(outs)):
+        at = i * rows
+        buffer_ref[at : at + rows] = value_ref[first + at : first + at + rows].astype(SINGLE)
+        target = out.at[spot] if which is None else out.at[which, spot]
+        copies.append(
+            pltpu.make_async_copy(buffer_ref.at[at : at + rows], target, sems.at[i])
+        )
+        copies[-1].start()
+    return copies
+
+
+def unpack_own(part_ref, *refs):
+    outs, (buffer_ref, sems) = refs[:4], refs[4:]
+    first = (part_ref.shape[0] - buffer_ref.shape[0]) // 2
+    half = lax.axis_index("dom") % 2
+    for copy in store_squares(first, half, part_ref, outs, buffer_ref, sems):
+        copy.wait()
+
+
+def unpack_other(part_ref, other_ref, *refs):
+    outs, (embed, output), (buffer_ref, sems) = refs[4:8], refs[8:10], refs[10:]
+    rows = (part_ref.shape[0] - buffer_ref.shape[0]) // 2
+    half = lax.axis_index("dom") % 2
+    copies = store_squares(rows, 1 - half, other_ref, outs, buffer_ref, sems)
     odd = odd_along("dom")
-    at = 0
-    for out, which, rows in outs_of(outs):
+    for out, at in ((output, 0), (embed, part_ref.shape[0] - rows)):
         own = part_ref[at : at + rows].astype(SINGLE)
         far = other_ref[at : at + rows].astype(SINGLE)
-        top, bottom = jnp.where(odd, far, own), jnp.where(odd, own, far)
-        if which is None:
-            out[:rows] = top
-            out[rows:] = bottom[: out.shape[0] - rows]
-        else:
-            out[which, :rows] = top
-            out[which, rows:] = bottom
-        at += rows
-
-
-def outs_of(outs):
-    embed, encode, self_, near, decode, output = outs
-    half = encode.shape[0] // 2
-    narrow = -(-embed.shape[0] // (2 * LANES)) * LANES
-    return [
-        (output, None, narrow),
-        (decode, None, half),
-        (self_, 1, half),
-        (near, 1, half),
-        (self_, 0, half),
-        (near, 0, half),
-        (encode, None, half),
-        (embed, None, narrow),
+        out[:rows] = jnp.where(odd, far, own)
+        out[rows:] = jnp.where(odd, own, far)[: out.shape[0] - rows]
+    for copy in copies:
+        copy.wait()
+
+
+def unpack(part, other, width, variables):
+    full = shape(width, width, SINGLE)
+    pair = jax.ShapeDtypeStruct((2, width, width), SINGLE)
+    narrow = shape(variables, width, SINGLE)
+    squares = [full, pair, pair, full]
+    hbm = pl.BlockSpec(memory_space=pltpu.HBM)
+    vmem = pl.BlockSpec(memory_space=pltpu.VMEM)
+    scratch = [
+        pltpu.VMEM((6 * split_rows(width), width), SINGLE),
+        pltpu.SemaphoreType.DMA((6,)),
     ]
+    params = pltpu.CompilerParams(vmem_limit_bytes=32 * MIB)
+    size = part.size * 6
+    cost = pl.CostEstimate(flops=0, bytes_accessed=size, transcendentals=0)
+    grads = pl.pallas_call(
+        unpack_own,
+        out_shape=squares,
+        in_specs=[vmem],
+        out_specs=[hbm] * 4,
+        scratch_shapes=scratch,
+        compiler_params=params,
+        cost_estimate=cost,
+    )(part)
+    return pl.pallas_call(
+        unpack_other,
+        out_shape=[*squares, narrow, narrow],
+        in_specs=[vmem, vmem] + [hbm] * 4,
+        out_specs=[hbm] * 4 + [vmem] * 2,
+        input_output_aliases={2: 0, 3: 1, 4: 2, 5: 3},
+        scratch_shapes=scratch,
+        compiler_params=params,
+        cost_estimate=cost,
+    )(part, other, *grads)
 
 
 def reduce_all(part):
@@ -521,12 +568,19 @@
     grid_full = shape(grid_count, width, SINGLE)
     parcel = shape(variables + -variables % 16 + INDEX_ROWS // 2, grid_count, HALF)
     sent = fetching(
-        parcels, [parcel] * (GROUPS - 1), 0, grid, grid_send, mesh_send, near
+        parcels, [parcel] * (GROUPS - 1), 0, grid, grid_send, mesh_send, near, limit=58
     )
     arrived = swap_all(*sent)
     embed_macs = grid_count * variables * width + mesh_count * grid_count * (step + width)
-    slope_embed, total = fetching(
-        embed_own, [grid_full, mesh_full], embed_macs, grid, embed_weight, grid_send, mesh_recv
+    slope_embed, total, held_weight = fetching(
+        embed_own,
+        [grid_full, mesh_full, shape(variables, width, HALF)],
+        embed_macs,
+        grid,
+        embed_weight,
+        grid_send,
+        mesh_recv,
+        limit=32,
     )
     index = [None] * GROUPS
     slopes = [slope_embed] + [None] * (GROUPS - 1)
@@ -537,7 +591,7 @@
             [shape(INDEX_ROWS, LANES, jnp.int32), grid_full, mesh_full],
             embed_macs,
             arrived[p - 1],
-            embed_weight,
+            held_weight,
             mesh_recv,
             total,
         )
@@ -602,7 +656,17 @@
         decode_in,
         decode_grad,
     )
-    state_grad, *decode_halves = lax.optimization_barrier((state_grad, *decode_halves))
+    to_mesh = whole(
+        mesh_counts,
+        [shape(grid_count, nodes, HALF)],
+        nodes * grid_count * step,
+        grid_send,
+        mesh_recv,
+        *index[1:],
+    )[0]
+    state_grad, to_mesh, *decode_halves = lax.optimization_barrier(
+        (state_grad, to_mesh, *decode_halves)
+    )
     state_grad, layer_1, on, off = whole(
         gather_back,
         [mesh_full, mesh_rows] + [shape(rim + RIM, width, HALF)] * 2,
@@ -623,7 +687,10 @@
         nearby_1,
         layer_1,
     )
-    state_grad, *layer_halves = lax.optimization_barrier((state_grad, *layer_halves))
+    halves = [decode_halves[0], swap_on(decode_halves[1])]
+    state_grad, *layer_halves, halves[1] = lax.optimization_barrier(
+        (state_grad, *layer_halves, halves[1])
+    )
     state_grad, layer_0, encode_grad, encode_in_grad = whole(
         process_back,
         [mesh_full, mesh_rows, mesh_rows, mesh_rows],
@@ -640,14 +707,6 @@
         encode_weight,
         scratch=[pltpu.VMEM((ext, width), HALF)],
     )
-    to_mesh = whole(
-        mesh_counts,
-        [shape(grid_count, nodes, HALF)],
-        nodes * grid_count * step,
-        grid_send,
-        mesh_recv,
-        *index[1:],
-    )[0]
     rest_halves = split_gradients(
         lambda *refs: gradient_halves(0, *refs),
         3 * half_rows,
@@ -670,18 +729,14 @@
         *slopes,
         *grids,
     )
-    halves = []
-    for mine, other in (decode_halves, layer_halves, rest_halves, embed_halves):
+    for mine, other in (layer_halves, rest_halves, embed_halves):
         halves += [mine, swap_on(other)]
     rows = sum(block.shape[0] for block in halves[::2])
     (part,) = whole(add_halves, [shape(rows, width, HALF)], 0, *halves)
     part = reduce_all(part)
     other = swap_on(part)
-    full = shape(width, width, SINGLE)
-    pair = jax.ShapeDtypeStruct((2, width, width), SINGLE)
-    narrow = shape(variables, width, SINGLE)
-    grad_embed, grad_encode, grad_self, grad_near, grad_decode, grad_output = whole(
-        unpack, [narrow, full, pair, pair, full, narrow], 0, part, other
+    grad_encode, grad_self, grad_near, grad_decode, grad_embed, grad_output = unpack(
+        part, other, width, variables
     )
     return (
         prediction.T,

time: 149 us -> 146 us (0.980)
  waiting for transfers between devices: 19.6 us -> 15.1 us
  Pallas kernels: 25.5 us -> 28.3 us
    pallas_call x0 -> x2, Pallas kernels: none -> 4.41 us  [the longest x1 2.67 us: unpack(): pl.pallas_call(unpack_other, out_shape=[*squares, narrow, narrow], in_spe...]
    pallas_call x20 -> x19, Pallas kernels: 23.4 us -> 20.2 us  [whole(): pl.pallas_call(body, out_shape=outs, scratch_shapes=scratch, compiler_par...]
    ppermute x10, starting transfers between devices: 21.8 us -> 24.1 us  [swap_on(): return lax.ppermute(value, 'dom', [(i, i ^ 1) for i in range(count)])]
    ppermute x10, waiting for transfers between devices: 3.97 us -> 1.87 us  [swap_on(): return lax.ppermute(value, 'dom', [(i, i ^ 1) for i in range(count)])]
    ppermute x6, waiting for transfers between devices: 4.33 us -> 2.69 us  [swap_band(): return lax.ppermute(value, 'band', pairs)]
    pallas_call x2, Pallas kernels: 2.04 us -> 3.67 us  [fetching(): pl.pallas_call(body, out_shape=outs, in_specs=[pl.BlockSpec(memory_space=...]
    unnamed x40 -> x34, local copies, waits for them, and re-layouts: 4.84 us -> 3.39 us
  transfers between devices with their start and end apart: 24 -> 24, of which waited for: 11 -> 8; matrix products, arithmetic and copies ran while one was open for 1% -> 1% of each run, Pallas kernels for 8% -> 10%
where the time goes in v5:
time: 146 us; the launch traced here: 145 us
  blocking collectives  52.6 us (36%)
  starting transfers between devices  42.6 us (29%)
  Pallas kernels  28.3 us (19%)
  waiting for transfers between devices  15.1 us (10%)
  local copies, waits for them, and re-layouts  3.39 us (2%)
    all_to_all x1, blocking collectives, reduce_all(): lax.all_to_all(part.reshape(chips, rows, width), 'dom', 0, 0, axis_index_...  27.2 us
    all_to_all x1, blocking collectives, reduce_all(): lax.all_to_all(copies, 'dom', 0, 0, axis_index_groups=groups)  25.4 us
    ppermute x10, starting transfers between devices, swap_on(): return lax.ppermute(value, 'dom', [(i, i ^ 1) for i in range(count)])  24.1 us
    pallas_call x19, Pallas kernels, whole(): pl.pallas_call(body, out_shape=outs, scratch_shapes=scratch, compiler_par...  20.2 us
    ppermute x6, starting transfers between devices, swap_band(): return lax.ppermute(value, 'band', pairs)  10.4 us
    ppermute x5, waiting for transfers between devices, swap_off(): lax.ppermute(value, 'dom', [(i, (i + (1 if i % 2 else -1)) % count) for i...  7.33 us
    ppermute x3, starting transfers between devices, reduce_all(): lax.ppermute(piece, 'band', [(i, (i + step) % bands) for i in range(bands)])  6.43 us
    pallas_call x2, Pallas kernels, fetching(): pl.pallas_call(body, out_shape=outs, in_specs=[pl.BlockSpec(memory_space=...  3.67 us
  transfers between devices with their start and end apart: 24, of which 8 were waited for; matrix products, arithmetic and copies ran while one was open for 1% of the time, Pallas kernels for 10%

profile of v5, /device:TPU:1, one launch (start us, length us, event | category | flops | bytes accessed | tf_op | source)
XLA Modules:
  0.0 145.2 jit_solution(12486891760696297752)
XLA Ops:
  0.6 0.0 copy-start
  0.7 2.1 %shard_map.197 = (bf16[256,512]{1,0:T(8,128)(2,1)}, bf16[256,512]{1,0:T(8,128)(2,1)}, bf16[256,512]{1,0:T(8,128)(2,1)}, bf16[256,512]{1,0:T(8,128)(2,1)}) custom-call(bf16[227,512]{1,0:T(8,128)(2,1)} %bitcast.18, s32[30,128]{1,0:T(8,128)} %bitcast.22, s32[30,128]{1,0:T(8,128)} %bitcast.25, s32[6,256]{1,0:T(8,128)} %bitcast.27), custom_call_target="tpu_custom_call" | custom-call | bytes 1317888 | tf_op jit(solution)/shard_map/pallas_call | solution.py:128
  2.7 1.5 %collective-permute-start.3 = (bf16[256,512]{1,0:T(8,128)(2,1)}, bf16[256,512]{1,0:T(8,128)(2,1)S(1)}, u32[]{:S(2)}, u32[]{:S(2)}) collective-permute-start(bf16[256,512]{1,0:T(8,128)(2,1)} %get-tuple-element.89), channel_id=1, source_target_pairs={{0,1},{1,0},{2,3},{3,2},{4,5},{5,4},{6,7},{7,6},{8,9},{9,8},{10,11... | collective-permute-start | bytes 786440 | tf_op jit(solution)/shard_map/ppermute | solution.py:42
  4.2 1.7 %collective-permute-start.2 = (bf16[256,512]{1,0:T(8,128)(2,1)}, bf16[256,512]{1,0:T(8,128)(2,1)S(1)}, u32[]{:S(2)}, u32[]{:S(2)}) collective-permute-start(bf16[256,512]{1,0:T(8,128)(2,1)} %get-tuple-element.88), channel_id=1, source_target_pairs={{0,31},{1,2},{2,1},{3,4},{4,3},{5,6},{6,5},{7,8},{8,7},{9,10},{10,... | collective-permute-start | bytes 786440 | tf_op jit(solution)/shard_map/ppermute | solution.py:47
  5.9 1.2 collective-permute-start.1
  7.1 0.7 collective-permute-start
  7.8 0.9 copy-done.1
  8.8 0.7 copy-done.8
  9.5 0.9 copy-done.13
  10.4 0.7 copy-done.14
  11.1 1.6 %shard_map.198 = (f32[512,512]{1,0:T(8,128)S(1)}, f32[256,512]{1,0:T(8,128)S(1)}, bf16[227,512]{1,0:T(8,128)(2,1)S(1)}) custom-call(bf16[227,512]{1,0:T(8,128)(2,1)S(1)} %bitcast.19, bf16[227,512]{1,0:T(8,128)(2,1)S(1)} %copy-done.13, s32[30,128]{1,0:T(8,128)S(1)} %bitcast.23, s32[30,128]{1,0:T(8,128)S(1)} %bitcast.29), custom_call_target="tpu_custom_call" | custom-call | flops 454557696 | bytes 2300928 | tf_op jit(solution)/shard_map/pallas_call | solution.py:128
  12.8 0.9 shard_map.199
  13.7 0.9 shard_map.200
  14.7 0.0 copy-start.3
  14.7 0.0 copy-start.6
  14.7 1.0 shard_map.201
  15.7 0.9 shard_map.202
  16.7 0.4 shard_map.203
  17.2 5.3 %collective-permute-start.4 = (bf16[128,512]{1,0:T(8,128)(2,1)S(1)}, bf16[128,512]{1,0:T(8,128)(2,1)S(1)}, u32[]{:S(2)}, u32[]{:S(2)}) collective-permute-start(bf16[128,512]{1,0:T(8,128)(2,1)S(1)} %get-tuple-element.97), channel_id=1, source_target_pairs={{0,1},{1,0},{2,3},{3,2},{4,5},{5,4},{6,7},{7,6},{8,9},{9,8},{10,11... | collective-permute-start | bytes 393224 | tf_op jit(solution)/shard_map/ppermute | solution.py:42
  22.5 0.3 fusion.1.refs_8_
  22.9 0.7 shard_map.204
  23.6 3.3 %collective-permute-done.5.off_ref = bf16[128,512]{1,0:T(8,128)(2,1)S(1)} collective-permute-done((bf16[128,512]{1,0:T(8,128)(2,1)S(1)}, bf16[128,512]{1,0:T(8,128)(2,1)S(1)}, u32[]{:S(2)}, u32[]{:S(2)}) %collective-permute-start.5) | collective-permute-done | bytes 131104 | tf_op jit(solution)/shard_map/ppermute | solution.py:47
  26.9 1.7 %shard_map.205 = (bf16[256,512]{1,0:T(8,128)(2,1)S(1)}, f32[512,512]{1,0:T(8,128)S(1)}, f32[256,512]{1,0:T(8,128)S(1)}, bf16[256,512]{1,0:T(8,128)(2,1)S(1)}, bf...) custom-call(bf16[256,512]{1,0:T(8,128)(2,1)S(1)} %get-tuple-element.95.half_ref.refs_0_, ...), custom_call_target="tpu_custom_call" | custom-call | flops 1207959552 | bytes 6291456 | tf_op jit(solution)/shard_map/pallas_call | solution.py:81
  28.6 3.5 %collective-permute-start.6 = (bf16[256,512]{1,0:T(8,128)(2,1)S(1)}, bf16[256,512]{1,0:T(8,128)(2,1)S(1)}, u32[]{:S(2)}, u32[]{:S(2)}) collective-permute-start(bf16[256,512]{1,0:T(8,128)(2,1)S(1)} %get-tuple-element.102.refs_0_), channel_id=1, source_target_pairs={{0,1},{1,0},{2,3},{3,2},{4,5},{5,4},{6,7},{7,6},{8,9},{9,8},{10,11... | collective-permute-start | bytes 786440 | tf_op jit(solution)/shard_map/ppermute | solution.py:42
  32.1 3.6 %collective-permute-start.8 = (bf16[256,512]{1,0:T(8,128)(2,1)S(1)}, bf16[256,512]{1,0:T(8,128)(2,1)S(1)}, u32[]{:S(2)}, u32[]{:S(2)}) collective-permute-start(bf16[256,512]{1,0:T(8,128)(2,1)S(1)} %get-tuple-element.102.refs_0_), channel_id=1, source_target_pairs={{0,32},{32,0},{64,96},{96,64},{1,33},{33,1},{65,97},{97,65},{2,34}... | collective-permute-start | bytes 786440 | tf_op jit(solution)/shard_map/ppermute | solution.py:57
  35.7 0.8 collective-permute-start.9
  36.6 1.4 shard_map.208.refs_1_
  38.1 2.3 %shard_map.206 = (bf16[512,1280]{1,0:T(8,128)(2,1)S(1)}, bf16[1280,512]{1,0:T(8,128)(2,1)S(1)}) custom-call(s32[30,128]{1,0:T(8,128)S(1)} %bitcast.26, s32[30,128]{1,0:T(8,128)S(1)} %bitcast.35, s32[32,128]{1,0:T(8,128)S(1)} %get-tuple-element.99.on_ref.refs_0_, s32[32,128]{1,0:T(8,128)S(1)} %get-tuple-element.100.off_ref.refs_1_, ...), custom_call_target="tpu_custom_call" | custom-call | flops 2013265920 | bytes 2717696 | tf_op jit(solution)/shard_map/pallas_call | solution.py:81
  40.4 1.5 %collective-permute-done.8.refs_3_ = bf16[256,512]{1,0:T(8,128)(2,1)S(1)} collective-permute-done((bf16[256,512]{1,0:T(8,128)(2,1)S(1)}, bf16[256,512]{1,0:T(8,128)(2,1)S(1)}, u32[]{:S(2)}, u32[]{:S(2)}) %collective-permute-start.8) | collective-permute-done | bytes 262176 | tf_op jit(solution)/shard_map/ppermute | solution.py:57
  41.9 2.4 %shard_map.207 = (bf16[512,512]{1,0:T(8,128)(2,1)S(1)}, bf16[512,512]{1,0:T(8,128)(2,1)S(1)}, bf16[512,512]{1,0:T(8,128)(2,1)S(1)}, f32[256,512]{1,0:T(8,128)S(1...) custom-call(bf16[256,512]{1,0:T(8,128)(2,1)S(1)} %get-tuple-element., ...), custom_call_target="tpu_custom_call" | custom-call | flops 1879048192 | bytes 8650752 | tf_op jit(solution)/shard_map/pallas_call | solution.py:81
  44.3 1.1 collective-permute-start.10
  45.4 3.4 %collective-permute-start.12 = (bf16[256,512]{1,0:T(8,128)(2,1)S(1)}, bf16[256,512]{1,0:T(8,128)(2,1)S(1)}, u32[]{:S(2)}, u32[]{:S(2)}) collective-permute-start(bf16[256,512]{1,0:T(8,128)(2,1)S(1)} %get-tuple-element.116), channel_id=1, source_target_pairs={{0,32},{32,0},{64,96},{96,64},{1,33},{33,1},{65,97},{97,65},{2,34}... | collective-permute-start | bytes 786440 | tf_op jit(solution)/shard_map/ppermute | solution.py:57
  48.8 0.7 collective-permute-start.13
  49.5 0.7 shard_map.209
  50.2 2.1 %collective-permute-start.14 = (bf16[384,512]{1,0:T(8,128)(2,1)S(1)}, bf16[384,512]{1,0:T(8,128)(2,1)S(1)}, u32[]{:S(2)}, u32[]{:S(2)}) collective-permute-start(bf16[384,512]{1,0:T(8,128)(2,1)S(1)} %get-tuple-element.125), channel_id=1, source_target_pairs={{0,1},{1,0},{2,3},{3,2},{4,5},{5,4},{6,7},{7,6},{8,9},{9,8},{10,11... | collective-permute-start | bytes 1179656 | tf_op jit(solution)/shard_map/ppermute | solution.py:42
  52.3 0.2 add_multiply_fusion.1.refs_5_
  52.5 1.2 collective-permute-done.12.refs_3_
  53.7 0.2 shard_map.210
  53.9 2.5 %collective-permute-start.15 = (bf16[192,512]{1,0:T(8,128)(2,1)S(1)}, bf16[192,512]{1,0:T(8,128)(2,1)S(1)}, u32[]{:S(2)}, u32[]{:S(2)}) collective-permute-start(bf16[192,512]{1,0:T(8,128)(2,1)S(1)} %get-tuple-element.127), channel_id=1, source_target_pairs={{0,1},{1,0},{2,3},{3,2},{4,5},{5,4},{6,7},{7,6},{8,9},{9,8},{10,11... | collective-permute-start | bytes 589832 | tf_op jit(solution)/shard_map/ppermute | solution.py:42
  56.4 0.4 add_multiply_fusion.slope_0_ref
  56.7 0.6 shard_map.211
  57.4 0.1 collective-permute-done.15.on_ref
  57.4 4.0 %collective-permute-done.16.off_ref = bf16[192,512]{1,0:T(8,128)(2,1)S(1)} collective-permute-done((bf16[192,512]{1,0:T(8,128)(2,1)S(1)}, bf16[192,512]{1,0:T(8,128)(2,1)S(1)}, u32[]{:S(2)}, u32[]{:S(2)}) %collective-permute-start.16) | collective-permute-done | bytes 196640 | tf_op jit(solution)/shard_map/ppermute | solution.py:47
  61.5 2.3 %shard_map.212 = (f32[256,512]{1,0:T(8,128)}, bf16[256,512]{1,0:T(8,128)(2,1)S(1)}, bf16[256,512]{1,0:T(8,128)(2,1)S(1)}, bf16[256,512]{1,0:T(8,128)(2,1)S(1)}) custom-call(f32[256,512]{1,0:T(8,128)S(1)} %get-tuple-element.126.state_ref, bf16[256,512]{1,0:T(8,128)(2,1)S(1)} %get-tuple-element.121.refs_1_.refs_3_.layer_ref, ...), custom_call_target="tpu_custom_call" | custom-call | flops 1207959552 | bytes 7208960 | tf_op jit(solution)/shard_map/pallas_call | solution.py:81
  63.8 0.9 shard_map.213
  64.6 3.5 %collective-permute-start.18 = (bf16[768,512]{1,0:T(8,128)(2,1)S(1)}, bf16[768,512]{1,0:T(8,128)(2,1)S(1)}, u32[]{:S(2)}, u32[]{:S(2)}) collective-permute-start(bf16[768,512]{1,0:T(8,128)(2,1)S(1)} %get-tuple-element.142), channel_id=1, source_target_pairs={{0,1},{1,0},{2,3},{3,2},{4,5},{5,4},{6,7},{7,6},{8,9},{9,8},{10,11... | collective-permute-start | bytes 2359304 | tf_op jit(solution)/shard_map/ppermute | solution.py:42
  68.1 0.3 collective-permute-start.17
  68.5 1.8 %shard_map.214 = (bf16[128,512]{1,0:T(8,128)(2,1)S(1)}, bf16[128,512]{1,0:T(8,128)(2,1)S(1)}) custom-call(bf16[256,512]{1,0:T(8,128)(2,1)S(1)} %get-tuple-element.143.refs_0_, bf16[512,1280]{1,0:T(8,128)(2,1)S(1)} %shard_map.208.refs_1_, f32[512,512]{1,0:T(8,128)S(1)} %get-tuple-element.145.refs_2_, f32[512,512]{1,0:T(8,128)S(1)} %get-tuple-element.146.refs_3_, ...), custom_call_target="tpu_custom_call" | custom-call | flops 1266155520 | bytes 8358912 | tf_op jit(solution)/shard_map/pallas_call | solution.py:81
  70.3 0.3 collective-permute-start.19
  70.6 1.2 collective-permute-done.19.refs_7_
  71.7 0.4 shard_map.215
  72.2 27.2 %all_to_all.10.pieces_ref = bf16[16,112,512]{2,1,0:T(8,128)(2,1)S(1)} all-to-all(bf16[16,112,512]{2,1,0:T(8,128)(2,1)S(1)} %bitcast.17), channel_id=1, replica_groups={{0,2,4,6,8,10,12,14,16,18,20,22,24,26,28,30},{1,3,5,7,9,11,13,15,17,19,..., dimensions={0} | all-to-all | bytes 3670016 | tf_op jit(solution)/shard_map/all_to_all | solution.py:526
  99.4 0.2 shard_map.216.refs_0_
  99.6 3.7 %collective-permute-start.20 = (bf16[112,512]{1,0:T(8,128)(2,1)S(1)}, bf16[112,512]{1,0:T(8,128)(2,1)S(1)}, u32[]{:S(2)}, u32[]{:S(2)}) collective-permute-start(bf16[112,512]{1,0:T(8,128)(2,1)S(1)} %shard_map.216.refs_0_), channel_id=1, source_target_pairs={{0,32},{32,64},{64,96},{96,0},{1,33},{33,65},{65,97},{97,1},{2,34}... | collective-permute-start | bytes 344072 | tf_op jit(solution)/shard_map/ppermute | solution.py:531
  103.3 0.8 collective-permute-start.21
  104.1 2.0 %collective-permute-start.22 = (bf16[112,512]{1,0:T(8,128)(2,1)S(1)}, bf16[112,512]{1,0:T(8,128)(2,1)S(1)}, u32[]{:S(2)}, u32[]{:S(2)}) collective-permute-start(bf16[112,512]{1,0:T(8,128)(2,1)S(1)} %shard_map.216.refs_0_), channel_id=1, source_target_pairs={{0,96},{32,0},{64,32},{96,64},{1,97},{33,1},{65,33},{97,65},{2,98}... | collective-permute-start | bytes 344072 | tf_op jit(solution)/shard_map/ppermute | solution.py:531
  106.1 3.3 %collective-permute-done.21.refs_2_ = bf16[112,512]{1,0:T(8,128)(2,1)S(1)} collective-permute-done((bf16[112,512]{1,0:T(8,128)(2,1)S(1)}, bf16[112,512]{1,0:T(8,128)(2,1)S(1)}, u32[]{:S(2)}, u32[]{:S(2)}) %collective-permute-start.21) | collective-permute-done | bytes 114720 | tf_op jit(solution)/shard_map/ppermute | solution.py:531
  109.3 0.2 shard_map.217
  109.5 25.4 %all_to_all.11 = bf16[16,112,512]{2,1,0:T(8,128)(2,1)S(1)} all-to-all(bf16[16,112,512]{2,1,0:T(8,128)(2,1)S(1)} %shard_map.217), channel_id=1, replica_groups={{0,2,4,6,8,10,12,14,16,18,20,22,24,26,28,30},{1,3,5,7,9,11,13,15,17,19,..., dimensions={0} | all-to-all | bytes 3670016 | tf_op jit(solution)/shard_map/all_to_all | solution.py:536
  134.9 4.0 %collective-permute-start.23 = (bf16[1792,512]{1,0:T(8,128)(2,1)S(1)}, bf16[1792,512]{1,0:T(8,128)(2,1)S(1)}, u32[]{:S(2)}, u32[]{:S(2)}) collective-permute-start(bf16[1792,512]{1,0:T(8,128)(2,1)S(1)} %bitcast.14), channel_id=1, source_target_pairs={{0,1},{1,0},{2,3},{3,2},{4,5},{5,4},{6,7},{7,6},{8,9},{9,8},{10,11... | collective-permute-start | bytes 5505032 | tf_op jit(solution)/shard_map/ppermute | solution.py:42
  139.0 1.0 fusion
  140.0 1.7 %shard_map.218 = (f32[512,512]{1,0:T(8,128)}, f32[2,512,512]{2,1,0:T(8,128)}, f32[2,512,512]{2,1,0:T(8,128)}, f32[512,512]{1,0:T(8,128)}) custom-call(bf16[1792,512]{1,0:T(8,128)(2,1)S(1)} %bitcast.15), custom_call_target="tpu_custom_call" | custom-call | bytes 5505024 | tf_op jit(solution)/shard_map/pallas_call | solution.py:499
  141.7 0.6 collective-permute-done.23.other_ref
  142.4 2.7 %shard_map.219 = (f32[512,512]{1,0:T(8,128)}, f32[2,512,512]{2,1,0:T(8,128)}, f32[2,512,512]{2,1,0:T(8,128)}, f32[512,512]{1,0:T(8,128)}, f32[227,512]{1,0:T(8,128)}, /*index=5*/f32[227,512]{1,0:T(8,128)}) custom-call(bf16[1792,512]{1,0:T(8,128)(2,1)S(1)} %bitcast.16, ...), custom_call_target="tpu_custom_call", output_to_operand_aliasing={{0}: (2, {}), {1}: (3, {}), {2}: (4, {}), {3}: (5, {})} | custom-call | bytes 5505024 | tf_op jit(solution)/shard_map/pallas_call | solution.py:508
  (47 shorter events, 0.1 us)
Async XLA Ops:
  0.6 21.9 %copy-start = (bf16[512,227]{0,1:T(8,128)(2,1)S(1)}, bf16[512,227]{0,1:T(8,128)(2,1)}, u32[]{:S(2)}) copy-start(bf16[512,227]{0,1:T(8,128)(2,1)} %param.22) | copy-start | bytes 697348
  0.6 12.1 %copy-start.15 = (s32[3840]{0:T(1024)S(1)}, s32[3840]{0:T(1024)}, u32[]{:S(2)}) copy-start(s32[3840]{0:T(1024)} %param.24) | copy-start | bytes 46084
  2.7 10.0 %collective-permute-start.3 = (bf16[256,512]{1,0:T(8,128)(2,1)}, bf16[256,512]{1,0:T(8,128)(2,1)S(1)}, u32[]{:S(2)}, u32[]{:S(2)}) collective-permute-start(bf16[256,512]{1,0:T(8,128)(2,1)} %get-tuple-element.89), channel_id=1, source_target_pairs={{0,1},{1,0},{2,3},{3,2},{4,5},{5,4},{6,7},{7,6},{8,9},{9,8},{10,11... | collective-permute-start | bytes 786440 | tf_op jit(solution)/shard_map/ppermute | solution.py:42
  4.2 9.5 %collective-permute-start.2 = (bf16[256,512]{1,0:T(8,128)(2,1)}, bf16[256,512]{1,0:T(8,128)(2,1)S(1)}, u32[]{:S(2)}, u32[]{:S(2)}) collective-permute-start(bf16[256,512]{1,0:T(8,128)(2,1)} %get-tuple-element.88), channel_id=1, source_target_pairs={{0,31},{1,2},{2,1},{3,4},{4,3},{5,6},{6,5},{7,8},{8,7},{9,10},{10,... | collective-permute-start | bytes 786440 | tf_op jit(solution)/shard_map/ppermute | solution.py:47
  5.9 8.8 %collective-permute-start.1 = (bf16[256,512]{1,0:T(8,128)(2,1)}, bf16[256,512]{1,0:T(8,128)(2,1)S(1)}, u32[]{:S(2)}, u32[]{:S(2)}) collective-permute-start(bf16[256,512]{1,0:T(8,128)(2,1)} %get-tuple-element.87), channel_id=1, source_target_pairs={{0,32},{32,0},{64,96},{96,64},{1,33},{33,1},{65,97},{97,65},{2,34}... | collective-permute-start | bytes 786440 | tf_op jit(solution)/shard_map/ppermute | solution.py:57
  7.1 8.6 %collective-permute-start = (bf16[256,512]{1,0:T(8,128)(2,1)}, bf16[256,512]{1,0:T(8,128)(2,1)S(1)}, u32[]{:S(2)}, u32[]{:S(2)}) collective-permute-start(bf16[256,512]{1,0:T(8,128)(2,1)} %get-tuple-element.85), channel_id=1, source_target_pairs={{32,64},{64,32},{33,65},{65,33},{34,66},{66,34},{35,67},{67,35},{3... | collective-permute-start | bytes 786440 | tf_op jit(solution)/shard_map/ppermute | solution.py:57
  7.8 0.9 copy-start.1
  8.8 0.7 copy-start.8
  9.5 0.9 copy-start.13
  10.4 0.7 copy-start.14
  14.7 2.0 %copy-start.3 = (bf16[512,512]{1,0:T(8,128)(2,1)S(1)}, bf16[512,512]{1,0:T(8,128)(2,1)}, u32[]{:S(2)}) copy-start(bf16[512,512]{1,0:T(8,128)(2,1)} %encode_ref.1) | copy-start | bytes 1572868
  14.7 2.0 %copy-start.6 = (bf16[256,512]{1,0:T(8,128)(2,1)S(1)}, bf16[256,512]{1,0:T(8,128)(2,1)}, u32[]{:S(2)}) copy-start(bf16[256,512]{1,0:T(8,128)(2,1)} %static_ref.1) | copy-start | bytes 786436
  15.7 6.8 %copy-start.7 = (bf16[512,227]{0,1:T(8,128)(2,1)S(1)}, bf16[512,227]{0,1:T(8,128)(2,1)}, u32[]{:S(2)}) copy-start(bf16[512,227]{0,1:T(8,128)(2,1)} %param.15) | copy-start | bytes 697348
  16.7 6.2 %copy-start.11 = (s32[256,6]{0,1:T(8,128)S(1)}, s32[256,6]{0,1:T(8,128)}, u32[]{:S(2)}) copy-start(s32[256,6]{0,1:T(8,128)} %param.25) | copy-start | bytes 18436
  16.7 10.2 %copy-start.4 = (bf16[2,512,512]{2,1,0:T(8,128)(2,1)S(1)}, bf16[2,512,512]{2,1,0:T(8,128)(2,1)}, u32[]{:S(2)}) copy-start(bf16[2,512,512]{2,1,0:T(8,128)(2,1)} %self_ref.3) | copy-start | bytes 3145732
  16.7 10.2 %copy-start.5 = (bf16[2,512,512]{2,1,0:T(8,128)(2,1)S(1)}, bf16[2,512,512]{2,1,0:T(8,128)(2,1)}, u32[]{:S(2)}) copy-start(bf16[2,512,512]{2,1,0:T(8,128)(2,1)} %near_ref.3) | copy-start | bytes 3145732
  17.2 6.4 %collective-permute-start.4 = (bf16[128,512]{1,0:T(8,128)(2,1)S(1)}, bf16[128,512]{1,0:T(8,128)(2,1)S(1)}, u32[]{:S(2)}, u32[]{:S(2)}) collective-permute-start(bf16[128,512]{1,0:T(8,128)(2,1)S(1)} %get-tuple-element.97), channel_id=1, source_target_pairs={{0,1},{1,0},{2,3},{3,2},{4,5},{5,4},{6,7},{7,6},{8,9},{9,8},{10,11... | collective-permute-start | bytes 393224 | tf_op jit(solution)/shard_map/ppermute | solution.py:42
  22.5 4.4 %collective-permute-start.5 = (bf16[128,512]{1,0:T(8,128)(2,1)S(1)}, bf16[128,512]{1,0:T(8,128)(2,1)S(1)}, u32[]{:S(2)}, u32[]{:S(2)}) collective-permute-start(bf16[128,512]{1,0:T(8,128)(2,1)S(1)} %get-tuple-element.98), channel_id=1, source_target_pairs={{0,31},{1,2},{2,1},{3,4},{4,3},{5,6},{6,5},{7,8},{8,7},{9,10},{10,... | collective-permute-start | bytes 393224 | tf_op jit(solution)/shard_map/ppermute | solution.py:47
  26.9 9.7 %copy-start.9 = (s32[3840]{0:T(1024)S(1)}, s32[3840]{0:T(1024)}, u32[]{:S(2)}) copy-start(s32[3840]{0:T(1024)} %param.23) | copy-start | bytes 46084
  28.6 11.8 %collective-permute-start.6 = (bf16[256,512]{1,0:T(8,128)(2,1)S(1)}, bf16[256,512]{1,0:T(8,128)(2,1)S(1)}, u32[]{:S(2)}, u32[]{:S(2)}) collective-permute-start(bf16[256,512]{1,0:T(8,128)(2,1)S(1)} %get-tuple-element.102.refs_0_), channel_id=1, source_target_pairs={{0,1},{1,0},{2,3},{3,2},{4,5},{5,4},{6,7},{7,6},{8,9},{9,8},{10,11... | collective-permute-start | bytes 786440 | tf_op jit(solution)/shard_map/ppermute | solution.py:42
  32.1 8.4 %collective-permute-start.7 = (bf16[256,512]{1,0:T(8,128)(2,1)S(1)}, bf16[256,512]{1,0:T(8,128)(2,1)S(1)}, u32[]{:S(2)}, u32[]{:S(2)}) collective-permute-start(bf16[256,512]{1,0:T(8,128)(2,1)S(1)} %get-tuple-element.102.refs_0_), channel_id=1, source_target_pairs={{0,31},{1,2},{2,1},{3,4},{4,3},{5,6},{6,5},{7,8},{8,7},{9,10},{10,... | collective-permute-start | bytes 786440 | tf_op jit(solution)/shard_map/ppermute | solution.py:47
  32.1 9.9 %collective-permute-start.8 = (bf16[256,512]{1,0:T(8,128)(2,1)S(1)}, bf16[256,512]{1,0:T(8,128)(2,1)S(1)}, u32[]{:S(2)}, u32[]{:S(2)}) collective-permute-start(bf16[256,512]{1,0:T(8,128)(2,1)S(1)} %get-tuple-element.102.refs_0_), channel_id=1, source_target_pairs={{0,32},{32,0},{64,96},{96,64},{1,33},{33,1},{65,97},{97,65},{2,34}... | collective-permute-start | bytes 786440 | tf_op jit(solution)/shard_map/ppermute | solution.py:57
  35.7 6.2 %collective-permute-start.9 = (bf16[256,512]{1,0:T(8,128)(2,1)S(1)}, bf16[256,512]{1,0:T(8,128)(2,1)S(1)}, u32[]{:S(2)}, u32[]{:S(2)}) collective-permute-start(bf16[256,512]{1,0:T(8,128)(2,1)S(1)} %get-tuple-element.102.refs_0_), channel_id=1, source_target_pairs={{32,64},{64,32},{33,65},{65,33},{34,66},{66,34},{35,67},{67,35},{3... | collective-permute-start | bytes 786440 | tf_op jit(solution)/shard_map/ppermute | solution.py:57
  36.6 1.4 copy-start.10
  36.6 1.4 copy-start.16
  38.0 3.9 %copy-start.12 = (bf16[512,512]{1,0:T(8,128)(2,1)S(1)}, bf16[512,512]{1,0:T(8,128)(2,1)}, u32[]{:S(2)}) copy-start(bf16[512,512]{1,0:T(8,128)(2,1)} %refs_7_.1) | copy-start | bytes 1572868
  44.3 8.2 %collective-permute-start.10 = (bf16[256,512]{1,0:T(8,128)(2,1)S(1)}, bf16[256,512]{1,0:T(8,128)(2,1)S(1)}, u32[]{:S(2)}, u32[]{:S(2)}) collective-permute-start(bf16[256,512]{1,0:T(8,128)(2,1)S(1)} %get-tuple-element.114), channel_id=1, source_target_pairs={{0,1},{1,0},{2,3},{3,2},{4,5},{5,4},{6,7},{7,6},{8,9},{9,8},{10,11... | collective-permute-start | bytes 786440 | tf_op jit(solution)/shard_map/ppermute | solution.py:42
  45.4 7.0 %collective-permute-start.11 = (bf16[256,512]{1,0:T(8,128)(2,1)S(1)}, bf16[256,512]{1,0:T(8,128)(2,1)S(1)}, u32[]{:S(2)}, u32[]{:S(2)}) collective-permute-start(bf16[256,512]{1,0:T(8,128)(2,1)S(1)} %get-tuple-element.115), channel_id=1, source_target_pairs={{0,31},{1,2},{2,1},{3,4},{4,3},{5,6},{6,5},{7,8},{8,7},{9,10},{10,... | collective-permute-start | bytes 786440 | tf_op jit(solution)/shard_map/ppermute | solution.py:47
  45.4 8.2 %collective-permute-start.12 = (bf16[256,512]{1,0:T(8,128)(2,1)S(1)}, bf16[256,512]{1,0:T(8,128)(2,1)S(1)}, u32[]{:S(2)}, u32[]{:S(2)}) collective-permute-start(bf16[256,512]{1,0:T(8,128)(2,1)S(1)} %get-tuple-element.116), channel_id=1, source_target_pairs={{0,32},{32,0},{64,96},{96,64},{1,33},{33,1},{65,97},{97,65},{2,34}... | collective-permute-start | bytes 786440 | tf_op jit(solution)/shard_map/ppermute | solution.py:57
  48.8 4.9 %collective-permute-start.13 = (bf16[256,512]{1,0:T(8,128)(2,1)S(1)}, bf16[256,512]{1,0:T(8,128)(2,1)S(1)}, u32[]{:S(2)}, u32[]{:S(2)}) collective-permute-start(bf16[256,512]{1,0:T(8,128)(2,1)S(1)} %get-tuple-element.117), channel_id=1, source_target_pairs={{32,64},{64,32},{33,65},{65,33},{34,66},{66,34},{35,67},{67,35},{3... | collective-permute-start | bytes 786440 | tf_op jit(solution)/shard_map/ppermute | solution.py:57
  50.2 7.2 %collective-permute-start.14 = (bf16[384,512]{1,0:T(8,128)(2,1)S(1)}, bf16[384,512]{1,0:T(8,128)(2,1)S(1)}, u32[]{:S(2)}, u32[]{:S(2)}) collective-permute-start(bf16[384,512]{1,0:T(8,128)(2,1)S(1)} %get-tuple-element.125), channel_id=1, source_target_pairs={{0,1},{1,0},{2,3},{3,2},{4,5},{5,4},{6,7},{7,6},{8,9},{9,8},{10,11... | collective-permute-start | bytes 1179656 | tf_op jit(solution)/shard_map/ppermute | solution.py:42
  53.9 3.5 %collective-permute-start.15 = (bf16[192,512]{1,0:T(8,128)(2,1)S(1)}, bf16[192,512]{1,0:T(8,128)(2,1)S(1)}, u32[]{:S(2)}, u32[]{:S(2)}) collective-permute-start(bf16[192,512]{1,0:T(8,128)(2,1)S(1)} %get-tuple-element.127), channel_id=1, source_target_pairs={{0,1},{1,0},{2,3},{3,2},{4,5},{5,4},{6,7},{7,6},{8,9},{9,8},{10,11... | collective-permute-start | bytes 589832 | tf_op jit(solution)/shard_map/ppermute | solution.py:42
  56.4 5.1 %collective-permute-start.16 = (bf16[192,512]{1,0:T(8,128)(2,1)S(1)}, bf16[192,512]{1,0:T(8,128)(2,1)S(1)}, u32[]{:S(2)}, u32[]{:S(2)}) collective-permute-start(bf16[192,512]{1,0:T(8,128)(2,1)S(1)} %get-tuple-element.128), channel_id=1, source_target_pairs={{0,31},{1,2},{2,1},{3,4},{4,3},{5,6},{6,5},{7,8},{8,7},{9,10},{10,... | collective-permute-start | bytes 589832 | tf_op jit(solution)/shard_map/ppermute | solution.py:47
  61.5 7.0 %copy-start.2 = (bf16[512,227]{0,1:T(8,128)(2,1)S(1)}, bf16[512,227]{0,1:T(8,128)(2,1)}, u32[]{:S(2)}) copy-start(bf16[512,227]{0,1:T(8,128)(2,1)} %param.14) | copy-start | bytes 697348
  64.6 7.1 %collective-permute-start.18 = (bf16[768,512]{1,0:T(8,128)(2,1)S(1)}, bf16[768,512]{1,0:T(8,128)(2,1)S(1)}, u32[]{:S(2)}, u32[]{:S(2)}) collective-permute-start(bf16[768,512]{1,0:T(8,128)(2,1)S(1)} %get-tuple-element.142), channel_id=1, source_target_pairs={{0,1},{1,0},{2,3},{3,2},{4,5},{5,4},{6,7},{7,6},{8,9},{9,8},{10,11... | collective-permute-start | bytes 2359304 | tf_op jit(solution)/shard_map/ppermute | solution.py:42
  68.1 3.6 %collective-permute-start.17 = (bf16[512,512]{1,0:T(8,128)(2,1)S(1)}, bf16[512,512]{1,0:T(8,128)(2,1)S(1)}, u32[]{:S(2)}, u32[]{:S(2)}) collective-permute-start(bf16[512,512]{1,0:T(8,128)(2,1)S(1)} %get-tuple-element.136), channel_id=1, source_target_pairs={{0,1},{1,0},{2,3},{3,2},{4,5},{5,4},{6,7},{7,6},{8,9},{9,8},{10,11... | collective-permute-start | bytes 1572872 | tf_op jit(solution)/shard_map/ppermute | solution.py:42
  70.3 1.4 collective-permute-start.19
  99.6 6.4 %collective-permute-start.20 = (bf16[112,512]{1,0:T(8,128)(2,1)S(1)}, bf16[112,512]{1,0:T(8,128)(2,1)S(1)}, u32[]{:S(2)}, u32[]{:S(2)}) collective-permute-start(bf16[112,512]{1,0:T(8,128)(2,1)S(1)} %shard_map.216.refs_0_), channel_id=1, source_target_pairs={{0,32},{32,64},{64,96},{96,0},{1,33},{33,65},{65,97},{97,1},{2,34}... | collective-permute-start | bytes 344072 | tf_op jit(solution)/shard_map/ppermute | solution.py:531
  103.3 6.0 %collective-permute-start.21 = (bf16[112,512]{1,0:T(8,128)(2,1)S(1)}, bf16[112,512]{1,0:T(8,128)(2,1)S(1)}, u32[]{:S(2)}, u32[]{:S(2)}) collective-permute-start(bf16[112,512]{1,0:T(8,128)(2,1)S(1)} %shard_map.216.refs_0_), channel_id=1, source_target_pairs={{0,64},{32,96},{64,0},{96,32},{1,65},{33,97},{65,1},{97,33},{2,66}... | collective-permute-start | bytes 344072 | tf_op jit(solution)/shard_map/ppermute | solution.py:531
  104.1 5.2 %collective-permute-start.22 = (bf16[112,512]{1,0:T(8,128)(2,1)S(1)}, bf16[112,512]{1,0:T(8,128)(2,1)S(1)}, u32[]{:S(2)}, u32[]{:S(2)}) collective-permute-start(bf16[112,512]{1,0:T(8,128)(2,1)S(1)} %shard_map.216.refs_0_), channel_id=1, source_target_pairs={{0,96},{32,0},{64,32},{96,64},{1,97},{33,1},{65,33},{97,65},{2,98}... | collective-permute-start | bytes 344072 | tf_op jit(solution)/shard_map/ppermute | solution.py:531
  134.9 7.5 %collective-permute-start.23 = (bf16[1792,512]{1,0:T(8,128)(2,1)S(1)}, bf16[1792,512]{1,0:T(8,128)(2,1)S(1)}, u32[]{:S(2)}, u32[]{:S(2)}) collective-permute-start(bf16[1792,512]{1,0:T(8,128)(2,1)S(1)} %bitcast.14), channel_id=1, source_target_pairs={{0,1},{1,0},{2,3},{3,2},{4,5},{5,4},{6,7},{7,6},{8,9},{9,8},{10,11... | collective-permute-start | bytes 5505032 | tf_op jit(solution)/shard_map/ppermute | solution.py:42

commit v6 on v5

--- a/solution.py
+++ b/solution.py
@@ -249,16 +249,19 @@
     whole_ref[own] = half_ref[...]
     whole_ref[rim + count :] = right
     half_0 = whole_ref[...]
-    nearby_0 = (matmul(counts_ref[...], half_0) * (1.0 / NEAR)).astype(HALF)
-    nearby_0_ref[...] = nearby_0[own]
-    pre_0 = matmul(half_0, self_ref[0]) + matmul(nearby_0, near_ref[0])
+    used = slice(RIM, 3 * RIM + count)
+    nearby_0 = (matmul(counts_ref[used], half_0) * (1.0 / NEAR)).astype(HALF)
+    nearby_0_ref[...] = nearby_0[RIM : RIM + count]
+    pre_0 = matmul(half_0[used], self_ref[0]) + matmul(nearby_0, near_ref[0])
     pre_0_ref[...] = pre_0
     grown = pre_0 * jax.nn.sigmoid(pre_0)
-    state_1 = state_ref[...] + grown[own]
+    state_1 = state_ref[...] + grown[RIM : RIM + count]
     half_1 = state_1.astype(HALF)
-    whole_ref[:rim] = (left.astype(SINGLE) + grown[:rim]).astype(HALF)
+    whole_ref[RIM:rim] = (left[RIM:].astype(SINGLE) + grown[:RIM]).astype(HALF)
     whole_ref[own] = half_1
-    whole_ref[rim + count :] = (right.astype(SINGLE) + grown[rim + count :]).astype(HALF)
+    whole_ref[rim + count : rim + count + RIM] = (
+        right[:RIM].astype(SINGLE) + grown[RIM + count :]
+    ).astype(HALF)
     half_1_ref[...] = half_1
     nearby_1 = (matmul(counts_ref[own], whole_ref[...]) * (1.0 / NEAR)).astype(HALF)
     nearby_1_ref[...] = nearby_1
@@ -267,18 +270,20 @@
     final_ref[...] = (state_1 + pre_1 * jax.nn.sigmoid(pre_1)).astype(HALF)
 
 
-def grid_counts(send_ref, recv_ref, *refs):
-    far, (out_ref, turned_ref) = refs[: GROUPS - 1], refs[GROUPS - 1 :]
+def grid_counts(turned, send_ref, recv_ref, *refs):
+    far, out_ref = refs[: GROUPS - 1], refs[GROUPS - 1]
     odd_dom, odd_band = odd_along("dom"), odd_along("band")
     step = send_ref.shape[0] // GROUPS
     recv = by_partner(slots_of(recv_ref[...]), odd_dom, odd_band, True)
     send = [send_ref[:step]] + [ref[:step] for ref in far]
-    grids, nodes = out_ref.shape[0], turned_ref.shape[0] // GROUPS
+    nodes = out_ref.shape[0 if turned else 1] // GROUPS
+    grids = out_ref.shape[1 if turned else 0]
     for p in range(GROUPS):
         at = slice(p * nodes, (p + 1) * nodes)
-        to, of = hot(grids, recv[p]), hot(nodes, send[p])
-        out_ref[:, at] = back_mul(to, of).astype(HALF)
-        turned_ref[at] = back_mul(of, to).astype(HALF)
+        if turned:
+            out_ref[at] = pair_counts(send[p], nodes, recv[p], grids)
+        else:
+            out_ref[:, at] = pair_counts(recv[p], grids, send[p], nodes)
 
 
 def mesh_counts(send_ref, recv_ref, *refs):
@@ -292,7 +297,7 @@
 
 
 def decode(*refs):
-    finals = refs[:GROUPS]
+    finals = [refs[i] for i in (0, 4, 3, 2, 1)]
     counts_ref, turned_ref, weight_ref, back_ref = refs[GROUPS : GROUPS + 4]
     in_ref, hidden_ref, grad_ref, own_ref, *outs = refs[GROUPS + 4 :]
     nodes = own_ref.shape[0]
@@ -343,19 +348,19 @@
     whole_ref[own] = layer_ref[...]
     whole_ref[2 * rim + count :] = right[: 2 * rim]
     layer_1 = whole_ref[...]
-    spread = (matmul(turned_ref[...], layer_1) * (1.0 / NEAR)).astype(HALF)
-    back = back_mul(layer_1, self_ref[1]) + back_mul(spread, near_ref[1])
-    state_own = state_ref[...] + back[own]
-    first = left[2 * rim :].astype(SINGLE) + back[rim : 2 * rim]
-    last = right[2 * rim :].astype(SINGLE) + back[2 * rim + count : 3 * rim + count]
-    layer_0 = (state_own * slope_0_ref[own]).astype(HALF)
+    used = slice(rim, 3 * rim + count)
+    inner = slice(rim, rim + count)
+    spread = (matmul(turned_ref[used], layer_1) * (1.0 / NEAR)).astype(HALF)
+    back = back_mul(layer_1[used], self_ref[1]) + back_mul(spread, near_ref[1])
+    state_own = state_ref[...] + back[inner]
+    first = left[2 * rim :].astype(SINGLE) + back[:rim]
+    last = right[2 * rim :].astype(SINGLE) + back[rim + count :]
+    layer_0 = (state_own * slope_0_ref[inner]).astype(HALF)
     layer_0_ref[...] = layer_0
     whole_ref[:rim] = jnp.zeros((rim, back.shape[1]), HALF)
-    whole_ref[rim : 2 * rim] = (first * slope_0_ref[rim : 2 * rim]).astype(HALF)
+    whole_ref[rim : 2 * rim] = (first * slope_0_ref[:rim]).astype(HALF)
     whole_ref[own] = layer_0
-    whole_ref[2 * rim + count : 3 * rim + count] = (
-        last * slope_0_ref[2 * rim + count : 3 * rim + count]
-    ).astype(HALF)
+    whole_ref[2 * rim + count : 3 * rim + count] = (last * slope_0_ref[rim + count :]).astype(HALF)
     whole_ref[3 * rim + count :] = jnp.zeros((rim, back.shape[1]), HALF)
     spread = (matmul(turned_ref[own], whole_ref[...]) * (1.0 / NEAR)).astype(HALF)
     state = state_own + back_mul(layer_0, self_ref[0]) + back_mul(spread, near_ref[0])
@@ -397,12 +402,13 @@
     mine_ref, other_ref, wide_ref = refs[2 + 2 * GROUPS :]
     nodes = back_ref.shape[0]
     variables = grids[0].shape[0]
-    total = None
+    grads = []
     for p in range(GROUPS):
         latent = matmul(counts_ref[:, p * nodes : (p + 1) * nodes], back_ref[...])
-        grad = (latent * slopes[p][...]).astype(HALF)
-        term = matmul(grids[p][:variables], grad)
-        total = term if total is None else total + term
+        grads.append((latent * slopes[p][...]).astype(HALF))
+    total = matmul(
+        jnp.concatenate([grid[:variables] for grid in grids], 1), jnp.concatenate(grads, 0)
+    )
     store_halves(total, 0, mine_ref, other_ref, wide_ref)
 
 
@@ -468,16 +474,19 @@
 
 
 def unpack_other(part_ref, other_ref, *refs):
-    outs, (embed, output), (buffer_ref, sems) = refs[4:8], refs[8:10], refs[10:]
+    outs, narrow, (buffer_ref, sems, *held) = refs[4:8], refs[8:10], refs[10:]
     rows = (part_ref.shape[0] - buffer_ref.shape[0]) // 2
     half = lax.axis_index("dom") % 2
-    copies = store_squares(rows, 1 - half, other_ref, outs, buffer_ref, sems)
+    copies = []
     odd = odd_along("dom")
-    for out, at in ((output, 0), (embed, part_ref.shape[0] - rows)):
+    for i, at in enumerate((part_ref.shape[0] - rows, 0)):
         own = part_ref[at : at + rows].astype(SINGLE)
         far = other_ref[at : at + rows].astype(SINGLE)
-        out[:rows] = jnp.where(odd, far, own)
-        out[rows:] = jnp.where(odd, own, far)[: out.shape[0] - rows]
+        held[i][:rows] = jnp.where(odd, far, own)
+        held[i][rows:] = jnp.where(odd, own, far)[: held[i].shape[0] - rows]
+        copies.append(pltpu.make_async_copy(held[i], narrow[i], sems.at[6 + i]))
+        copies[-1].start()
+    copies += store_squares(rows, 1 - half, other_ref, outs, buffer_ref, sems)
     for copy in copies:
         copy.wait()
 
@@ -491,7 +500,7 @@
     vmem = pl.BlockSpec(memory_space=pltpu.VMEM)
     scratch = [
         pltpu.VMEM((6 * split_rows(width), width), SINGLE),
-        pltpu.SemaphoreType.DMA((6,)),
+        pltpu.SemaphoreType.DMA((8,)),
     ]
     params = pltpu.CompilerParams(vmem_limit_bytes=32 * MIB)
     size = part.size * 6
@@ -509,9 +518,9 @@
         unpack_other,
         out_shape=[*squares, narrow, narrow],
         in_specs=[vmem, vmem] + [hbm] * 4,
-        out_specs=[hbm] * 4 + [vmem] * 2,
+        out_specs=[hbm] * 6,
         input_output_aliases={2: 0, 3: 1, 4: 2, 5: 3},
-        scratch_shapes=scratch,
+        scratch_shapes=scratch + [pltpu.VMEM((variables, width), SINGLE)] * 2,
         compiler_params=params,
         cost_estimate=cost,
     )(part, other, *grads)
@@ -608,9 +617,19 @@
     counts, turned = whole(
         near_counts, [shape(ext, ext, HALF)] * 2, ext * ext * 64, near, index[1], index[2]
     )
+    count_macs = nodes * grid_count * step
+    (to_grid,) = whole(
+        lambda *refs: grid_counts(False, *refs),
+        [shape(grid_count, nodes, HALF)],
+        count_macs,
+        mesh_send,
+        grid_recv,
+        *index[1:],
+    )
+    state, to_grid = lax.optimization_barrier((state, to_grid))
     final_half, pre_0, pre_1, half_1, nearby_0, nearby_1 = whole(
         process,
-        [mesh_rows, shape(ext, width, SINGLE), mesh_full, mesh_rows, mesh_rows, mesh_rows],
+        [mesh_rows, shape(ext - rim, width, SINGLE), mesh_full] + [mesh_rows] * 3,
         (ext + mesh_count) * (ext + 2 * width) * width,
         half,
         state,
@@ -621,12 +640,13 @@
         neighbor_weight,
         scratch=[pltpu.VMEM((ext, width), HALF)],
     )
-    finals = (final_half,) + swap_all(*[final_half] * 4)
-    to_grid, from_grid = whole(
-        grid_counts,
-        [shape(grid_count, nodes, HALF), shape(nodes, grid_count, HALF)],
-        2 * nodes * grid_count * step,
-        mesh_send,
+    moved = swap_all(*[final_half] * 4)
+    finals = [final_half] + [moved[p - 1] for p in (4, 3, 2, 1)]
+    (from_grid,) = whole(
+        lambda *refs: grid_counts(True, *refs),
+        [shape(nodes, grid_count, HALF)],
+        count_macs,
+        lax.optimization_barrier((mesh_send, final_half))[0],
         grid_recv,
         *index[1:],
     )
@@ -641,7 +661,8 @@
         decode_weight,
         hidden_grad,
     )
-    arrived = swap_all(*sums)
+    moved = swap_all(*sums)
+    arrived = [moved[p - 1] for p in (1, 2, 3, 4)]
     prediction = (grid.astype(SINGLE) + back_mul(out_weight, hidden)).astype(HALF)
     half_rows = split_rows(width)
     narrow_rows = split_rows(variables)
@@ -659,8 +680,8 @@
     to_mesh = whole(
         mesh_counts,
         [shape(grid_count, nodes, HALF)],
-        nodes * grid_count * step,
-        grid_send,
+        count_macs,
+        lax.optimization_barrier((grid_send, decode_in))[0],
         mesh_recv,
         *index[1:],
     )[0]

time: 146 us -> 146 us (level)
  waiting for transfers between devices: 15.1 us -> 17.4 us
    ppermute x3, waiting for transfers between devices: 3.26 us -> 5.75 us  [reduce_all(): lax.ppermute(piece, 'band', [(i, (i + step) % bands) for i in range(bands)])]
    pallas_call x19 -> x20, Pallas kernels: 20.2 us -> 19.9 us  [whole(): pl.pallas_call(body, out_shape=outs, scratch_shapes=scratch, compiler_par...]
  transfers between devices with their start and end apart: 24 -> 24, of which waited for: 8 -> 9; matrix products, arithmetic and copies ran while one was open for 1% -> 1% of each run, Pallas kernels for 10% -> 10%
where the time goes in v6:
time: 146 us
  blocking collectives  53.1 us (36%)
  starting transfers between devices  41.6 us (28%)
  Pallas kernels  27.4 us (19%)
  waiting for transfers between devices  17.4 us (12%)
  local copies, waits for them, and re-layouts  3.39 us (2%)
    all_to_all x1, blocking collectives, reduce_all(): lax.all_to_all(part.reshape(chips, rows, width), 'dom', 0, 0, axis_index_...  27.6 us
    all_to_all x1, blocking collectives, reduce_all(): lax.all_to_all(copies, 'dom', 0, 0, axis_index_groups=groups)  25.5 us
    ppermute x10, starting transfers between devices, swap_on(): return lax.ppermute(value, 'dom', [(i, i ^ 1) for i in range(count)])  24.1 us
    pallas_call x20, Pallas kernels, whole(): pl.pallas_call(body, out_shape=outs, scratch_shapes=scratch, compiler_par...  19.9 us
    ppermute x6, starting transfers between devices, swap_band(): return lax.ppermute(value, 'band', pairs)  10.4 us
    ppermute x5, waiting for transfers between devices, swap_off(): lax.ppermute(value, 'dom', [(i, (i + (1 if i % 2 else -1)) % count) for i...  6.2 us
    ppermute x3, waiting for transfers between devices, reduce_all(): lax.ppermute(piece, 'band', [(i, (i + step) % bands) for i in range(bands)])  5.75 us
    ppermute x3, starting transfers between devices, reduce_all(): lax.ppermute(piece, 'band', [(i, (i + step) % bands) for i in range(bands)])  5.48 us
  transfers between devices with their start and end apart: 24, of which 9 were waited for; matrix products, arithmetic and copies ran while one was open for 1% of the time, Pallas kernels for 10%

profile of v6, /device:TPU:1, one launch (start us, length us, event | category | flops | bytes accessed | tf_op | source)
XLA Modules:
  0.0 146.1 jit_solution(6934525063230155291)
XLA Ops:
  0.6 0.0 copy-start
  0.6 0.0 copy-start.16
  0.7 2.1 %shard_map.197 = (bf16[256,512]{1,0:T(8,128)(2,1)}, bf16[256,512]{1,0:T(8,128)(2,1)}, bf16[256,512]{1,0:T(8,128)(2,1)}, bf16[256,512]{1,0:T(8,128)(2,1)}) custom-call(bf16[227,512]{1,0:T(8,128)(2,1)} %bitcast.18, s32[30,128]{1,0:T(8,128)} %bitcast.25, s32[30,128]{1,0:T(8,128)} %bitcast.22, s32[6,256]{1,0:T(8,128)} %bitcast.28), custom_call_target="tpu_custom_call" | custom-call | bytes 1317888 | tf_op jit(solution)/shard_map/pallas_call | solution.py:128
  2.7 1.5 %collective-permute-start.3 = (bf16[256,512]{1,0:T(8,128)(2,1)}, bf16[256,512]{1,0:T(8,128)(2,1)S(1)}, u32[]{:S(2)}, u32[]{:S(2)}) collective-permute-start(bf16[256,512]{1,0:T(8,128)(2,1)} %get-tuple-element.91), channel_id=1, source_target_pairs={{0,1},{1,0},{2,3},{3,2},{4,5},{5,4},{6,7},{7,6},{8,9},{9,8},{10,11... | collective-permute-start | bytes 786440 | tf_op jit(solution)/shard_map/ppermute | solution.py:42
  4.2 1.7 %collective-permute-start.2 = (bf16[256,512]{1,0:T(8,128)(2,1)}, bf16[256,512]{1,0:T(8,128)(2,1)S(1)}, u32[]{:S(2)}, u32[]{:S(2)}) collective-permute-start(bf16[256,512]{1,0:T(8,128)(2,1)} %get-tuple-element.90), channel_id=1, source_target_pairs={{0,31},{1,2},{2,1},{3,4},{4,3},{5,6},{6,5},{7,8},{8,7},{9,10},{10,... | collective-permute-start | bytes 786440 | tf_op jit(solution)/shard_map/ppermute | solution.py:47
  5.9 1.2 collective-permute-start.1
  7.1 0.7 collective-permute-start
  7.8 0.9 copy-done.1
  8.8 0.7 copy-done.9
  9.5 0.9 copy-done.13
  10.4 0.7 copy-done.15
  11.1 1.6 %shard_map.198 = (f32[512,512]{1,0:T(8,128)S(1)}, f32[256,512]{1,0:T(8,128)S(1)}, bf16[227,512]{1,0:T(8,128)(2,1)S(1)}) custom-call(bf16[227,512]{1,0:T(8,128)(2,1)S(1)} %bitcast.19, bf16[227,512]{1,0:T(8,128)(2,1)S(1)} %copy-done.13, s32[30,128]{1,0:T(8,128)S(1)} %bitcast.26, s32[30,128]{1,0:T(8,128)S(1)} %bitcast.32), custom_call_target="tpu_custom_call" | custom-call | flops 454557696 | bytes 2300928 | tf_op jit(solution)/shard_map/pallas_call | solution.py:128
  12.8 0.9 shard_map.199
  13.7 0.9 shard_map.200
  14.7 1.0 shard_map.201
  15.7 1.0 shard_map.202
  16.7 0.4 shard_map.203
  17.1 5.3 %collective-permute-start.4 = (bf16[128,512]{1,0:T(8,128)(2,1)S(1)}, bf16[128,512]{1,0:T(8,128)(2,1)S(1)}, u32[]{:S(2)}, u32[]{:S(2)}) collective-permute-start(bf16[128,512]{1,0:T(8,128)(2,1)S(1)} %get-tuple-element.104), channel_id=1, source_target_pairs={{0,1},{1,0},{2,3},{3,2},{4,5},{5,4},{6,7},{7,6},{8,9},{9,8},{10,11... | collective-permute-start | bytes 393224 | tf_op jit(solution)/shard_map/ppermute | solution.py:42
  22.5 1.4 shard_map.204.refs_5_
  24.0 0.7 shard_map.205
  24.7 2.2 %collective-permute-done.5.off_ref = bf16[128,512]{1,0:T(8,128)(2,1)S(1)} collective-permute-done((bf16[128,512]{1,0:T(8,128)(2,1)S(1)}, bf16[128,512]{1,0:T(8,128)(2,1)S(1)}, u32[]{:S(2)}, u32[]{:S(2)}) %collective-permute-start.5) | collective-permute-done | bytes 131104 | tf_op jit(solution)/shard_map/ppermute | solution.py:47
  26.9 1.5 %shard_map.206 = (bf16[256,512]{1,0:T(8,128)(2,1)S(1)}, f32[384,512]{1,0:T(8,128)S(1)}, f32[256,512]{1,0:T(8,128)S(1)}, bf16[256,512]{1,0:T(8,128)(2,1)S(1)}, bf...) custom-call(bf16[256,512]{1,0:T(8,128)(2,1)S(1)} %get-tuple-element.97.half_ref.refs_0_, ...), custom_call_target="tpu_custom_call" | custom-call | flops 1207959552 | bytes 6029312 | tf_op jit(solution)/shard_map/pallas_call | solution.py:81
  28.4 3.5 %collective-permute-start.9 = (bf16[256,512]{1,0:T(8,128)(2,1)S(1)}, bf16[256,512]{1,0:T(8,128)(2,1)S(1)}, u32[]{:S(2)}, u32[]{:S(2)}) collective-permute-start(bf16[256,512]{1,0:T(8,128)(2,1)S(1)} %get-tuple-element.107.refs_0_), channel_id=1, source_target_pairs={{0,1},{1,0},{2,3},{3,2},{4,5},{5,4},{6,7},{7,6},{8,9},{9,8},{10,11... | collective-permute-start | bytes 786440 | tf_op jit(solution)/shard_map/ppermute | solution.py:42
  31.9 3.6 %collective-permute-start.7 = (bf16[256,512]{1,0:T(8,128)(2,1)S(1)}, bf16[256,512]{1,0:T(8,128)(2,1)S(1)}, u32[]{:S(2)}, u32[]{:S(2)}) collective-permute-start(bf16[256,512]{1,0:T(8,128)(2,1)S(1)} %get-tuple-element.107.refs_0_), channel_id=1, source_target_pairs={{0,32},{32,0},{64,96},{96,64},{1,33},{33,1},{65,97},{97,65},{2,34}... | collective-permute-start | bytes 786440 | tf_op jit(solution)/shard_map/ppermute | solution.py:57
  35.5 0.8 collective-permute-start.6
  36.4 0.3 fusion.1.refs_8_
  36.7 1.2 shard_map.207.refs_6_
  38.0 3.7 %collective-permute-done.7.refs_2_ = bf16[256,512]{1,0:T(8,128)(2,1)S(1)} collective-permute-done((bf16[256,512]{1,0:T(8,128)(2,1)S(1)}, bf16[256,512]{1,0:T(8,128)(2,1)S(1)}, u32[]{:S(2)}, u32[]{:S(2)}) %collective-permute-start.7) | collective-permute-done | bytes 262176 | tf_op jit(solution)/shard_map/ppermute | solution.py:57
  41.7 2.4 %shard_map.208 = (bf16[512,512]{1,0:T(8,128)(2,1)S(1)}, bf16[512,512]{1,0:T(8,128)(2,1)S(1)}, bf16[512,512]{1,0:T(8,128)(2,1)S(1)}, f32[256,512]{1,0:T(8,128)S(1...) custom-call(bf16[256,512]{1,0:T(8,128)(2,1)S(1)} %get-tuple-element., ...), custom_call_target="tpu_custom_call" | custom-call | flops 1879048192 | bytes 8650752 | tf_op jit(solution)/shard_map/pallas_call | solution.py:81
  44.1 1.1 collective-permute-start.10
  45.2 3.3 %collective-permute-start.12 = (bf16[256,512]{1,0:T(8,128)(2,1)S(1)}, bf16[256,512]{1,0:T(8,128)(2,1)S(1)}, u32[]{:S(2)}, u32[]{:S(2)}) collective-permute-start(bf16[256,512]{1,0:T(8,128)(2,1)S(1)} %get-tuple-element.120), channel_id=1, source_target_pairs={{0,32},{32,0},{64,96},{96,64},{1,33},{33,1},{65,97},{97,65},{2,34}... | collective-permute-start | bytes 786440 | tf_op jit(solution)/shard_map/ppermute | solution.py:57
  48.6 0.7 collective-permute-start.13
  49.3 1.4 shard_map.209.refs_1_
  50.7 0.7 shard_map.210
  51.4 2.1 %collective-permute-start.14 = (bf16[384,512]{1,0:T(8,128)(2,1)S(1)}, bf16[384,512]{1,0:T(8,128)(2,1)S(1)}, u32[]{:S(2)}, u32[]{:S(2)}) collective-permute-start(bf16[384,512]{1,0:T(8,128)(2,1)S(1)} %get-tuple-element.129), channel_id=1, source_target_pairs={{0,1},{1,0},{2,3},{3,2},{4,5},{5,4},{6,7},{7,6},{8,9},{9,8},{10,11... | collective-permute-start | bytes 1179656 | tf_op jit(solution)/shard_map/ppermute | solution.py:42
  53.5 0.2 add_multiply_fusion.1.refs_5_
  53.7 0.2 shard_map.211
  54.0 2.2 %collective-permute-start.15 = (bf16[192,512]{1,0:T(8,128)(2,1)S(1)}, bf16[192,512]{1,0:T(8,128)(2,1)S(1)}, u32[]{:S(2)}, u32[]{:S(2)}) collective-permute-start(bf16[192,512]{1,0:T(8,128)(2,1)S(1)} %get-tuple-element.131), channel_id=1, source_target_pairs={{0,1},{1,0},{2,3},{3,2},{4,5},{5,4},{6,7},{7,6},{8,9},{9,8},{10,11... | collective-permute-start | bytes 589832 | tf_op jit(solution)/shard_map/ppermute | solution.py:42
  56.2 0.3 add_multiply_fusion.slope_0_ref
  56.4 0.6 shard_map.212
  57.1 0.1 collective-permute-done.15.on_ref
  57.2 4.0 %collective-permute-done.16.off_ref = bf16[192,512]{1,0:T(8,128)(2,1)S(1)} collective-permute-done((bf16[192,512]{1,0:T(8,128)(2,1)S(1)}, bf16[192,512]{1,0:T(8,128)(2,1)S(1)}, u32[]{:S(2)}, u32[]{:S(2)}) %collective-permute-start.16) | collective-permute-done | bytes 196640 | tf_op jit(solution)/shard_map/ppermute | solution.py:47
  61.2 2.2 %shard_map.213 = (f32[256,512]{1,0:T(8,128)}, bf16[256,512]{1,0:T(8,128)(2,1)S(1)}, bf16[256,512]{1,0:T(8,128)(2,1)S(1)}, bf16[256,512]{1,0:T(8,128)(2,1)S(1)}) custom-call(f32[256,512]{1,0:T(8,128)S(1)} %get-tuple-element.130.state_ref, bf16[256,512]{1,0:T(8,128)(2,1)S(1)} %get-tuple-element.125.refs_1_.refs_3_.layer_ref, ...), custom_call_target="tpu_custom_call" | custom-call | flops 1207959552 | bytes 6946816 | tf_op jit(solution)/shard_map/pallas_call | solution.py:81
  63.4 0.9 shard_map.214
  64.3 3.5 %collective-permute-start.18 = (bf16[768,512]{1,0:T(8,128)(2,1)S(1)}, bf16[768,512]{1,0:T(8,128)(2,1)S(1)}, u32[]{:S(2)}, u32[]{:S(2)}) collective-permute-start(bf16[768,512]{1,0:T(8,128)(2,1)S(1)} %get-tuple-element.146), channel_id=1, source_target_pairs={{0,1},{1,0},{2,3},{3,2},{4,5},{5,4},{6,7},{7,6},{8,9},{9,8},{10,11... | collective-permute-start | bytes 2359304 | tf_op jit(solution)/shard_map/ppermute | solution.py:42
  67.8 0.1 collective-permute-start.17
  67.9 1.6 %shard_map.215 = (bf16[128,512]{1,0:T(8,128)(2,1)S(1)}, bf16[128,512]{1,0:T(8,128)(2,1)S(1)}) custom-call(bf16[256,512]{1,0:T(8,128)(2,1)S(1)} %get-tuple-element.147.refs_0_, bf16[512,1280]{1,0:T(8,128)(2,1)S(1)} %shard_map.209.refs_1_, f32[512,512]{1,0:T(8,128)S(1)} %get-tuple-element.149.refs_2_, f32[512,512]{1,0:T(8,128)S(1)} %get-tuple-element.150.refs_3_, ...), custom_call_target="tpu_custom_call" | custom-call | flops 1266155520 | bytes 8358912 | tf_op jit(solution)/shard_map/pallas_call | solution.py:81
  69.5 0.7 collective-permute-start.19
  70.2 1.0 collective-permute-done.19.refs_7_
  71.2 0.4 shard_map.216
  71.6 27.6 %all_to_all.10.pieces_ref = bf16[16,112,512]{2,1,0:T(8,128)(2,1)S(1)} all-to-all(bf16[16,112,512]{2,1,0:T(8,128)(2,1)S(1)} %bitcast.17), channel_id=1, replica_groups={{0,2,4,6,8,10,12,14,16,18,20,22,24,26,28,30},{1,3,5,7,9,11,13,15,17,19,..., dimensions={0} | all-to-all | bytes 3670016 | tf_op jit(solution)/shard_map/all_to_all | solution.py:535
  99.2 0.2 shard_map.217.refs_0_
  99.4 0.7 collective-permute-start.22
  100.1 4.8 %collective-permute-start.21 = (bf16[112,512]{1,0:T(8,128)(2,1)S(1)}, bf16[112,512]{1,0:T(8,128)(2,1)S(1)}, u32[]{:S(2)}, u32[]{:S(2)}) collective-permute-start(bf16[112,512]{1,0:T(8,128)(2,1)S(1)} %shard_map.217.refs_0_), channel_id=1, source_target_pairs={{0,64},{32,96},{64,0},{96,32},{1,65},{33,97},{65,1},{97,33},{2,66}... | collective-permute-start | bytes 344072 | tf_op jit(solution)/shard_map/ppermute | solution.py:540
  104.9 0.4 collective-permute-done.22.refs_3_
  105.3 1.8 %collective-permute-done.21.refs_2_ = bf16[112,512]{1,0:T(8,128)(2,1)S(1)} collective-permute-done((bf16[112,512]{1,0:T(8,128)(2,1)S(1)}, bf16[112,512]{1,0:T(8,128)(2,1)S(1)}, u32[]{:S(2)}, u32[]{:S(2)}) %collective-permute-start.21) | collective-permute-done | bytes 114720 | tf_op jit(solution)/shard_map/ppermute | solution.py:540
  107.1 3.6 %collective-permute-done.20.refs_1_ = bf16[112,512]{1,0:T(8,128)(2,1)S(1)} collective-permute-done((bf16[112,512]{1,0:T(8,128)(2,1)S(1)}, bf16[112,512]{1,0:T(8,128)(2,1)S(1)}, u32[]{:S(2)}, u32[]{:S(2)}) %collective-permute-start.20) | collective-permute-done | bytes 114720 | tf_op jit(solution)/shard_map/ppermute | solution.py:540
  110.7 0.2 shard_map.218
  110.8 25.5 %all_to_all.11 = bf16[16,112,512]{2,1,0:T(8,128)(2,1)S(1)} all-to-all(bf16[16,112,512]{2,1,0:T(8,128)(2,1)S(1)} %shard_map.218), channel_id=1, replica_groups={{0,2,4,6,8,10,12,14,16,18,20,22,24,26,28,30},{1,3,5,7,9,11,13,15,17,19,..., dimensions={0} | all-to-all | bytes 3670016 | tf_op jit(solution)/shard_map/all_to_all | solution.py:545
  136.3 4.0 %collective-permute-start.23 = (bf16[1792,512]{1,0:T(8,128)(2,1)S(1)}, bf16[1792,512]{1,0:T(8,128)(2,1)S(1)}, u32[]{:S(2)}, u32[]{:S(2)}) collective-permute-start(bf16[1792,512]{1,0:T(8,128)(2,1)S(1)} %bitcast.14), channel_id=1, source_target_pairs={{0,1},{1,0},{2,3},{3,2},{4,5},{5,4},{6,7},{7,6},{8,9},{9,8},{10,11... | collective-permute-start | bytes 5505032 | tf_op jit(solution)/shard_map/ppermute | solution.py:42
  140.4 1.0 fusion
  141.4 1.8 %shard_map.219 = (f32[512,512]{1,0:T(8,128)}, f32[2,512,512]{2,1,0:T(8,128)}, f32[2,512,512]{2,1,0:T(8,128)}, f32[512,512]{1,0:T(8,128)}) custom-call(bf16[1792,512]{1,0:T(8,128)(2,1)S(1)} %bitcast.15), custom_call_target="tpu_custom_call" | custom-call | bytes 5505024 | tf_op jit(solution)/shard_map/pallas_call | solution.py:508
  143.2 0.6 collective-permute-done.23.other_ref
  143.8 2.1 %shard_map.220 = (f32[512,512]{1,0:T(8,128)}, f32[2,512,512]{2,1,0:T(8,128)}, f32[2,512,512]{2,1,0:T(8,128)}, f32[512,512]{1,0:T(8,128)}, f32[227,512]{1,0:T(8,128)}, /*index=5*/f32[227,512]{1,0:T(8,128)}) custom-call(bf16[1792,512]{1,0:T(8,128)(2,1)S(1)} %bitcast.16, ...), custom_call_target="tpu_custom_call", output_to_operand_aliasing={{0}: (2, {}), {1}: (3, {}), {2}: (4, {}), {3}: (5, {})} | custom-call | bytes 5505024 | tf_op jit(solution)/shard_map/pallas_call | solution.py:517
  (48 shorter events, 0.1 us)
Async XLA Ops:
  0.6 35.7 %copy-start = (bf16[512,227]{0,1:T(8,128)(2,1)S(1)}, bf16[512,227]{0,1:T(8,128)(2,1)}, u32[]{:S(2)}) copy-start(bf16[512,227]{0,1:T(8,128)(2,1)} %param.22) | copy-start | bytes 697348
  0.6 12.1 %copy-start.16 = (s32[3840]{0:T(1024)S(1)}, s32[3840]{0:T(1024)}, u32[]{:S(2)}) copy-start(s32[3840]{0:T(1024)} %param.24) | copy-start | bytes 46084
  2.7 10.0 %collective-permute-start.3 = (bf16[256,512]{1,0:T(8,128)(2,1)}, bf16[256,512]{1,0:T(8,128)(2,1)S(1)}, u32[]{:S(2)}, u32[]{:S(2)}) collective-permute-start(bf16[256,512]{1,0:T(8,128)(2,1)} %get-tuple-element.91), channel_id=1, source_target_pairs={{0,1},{1,0},{2,3},{3,2},{4,5},{5,4},{6,7},{7,6},{8,9},{9,8},{10,11... | collective-permute-start | bytes 786440 | tf_op jit(solution)/shard_map/ppermute | solution.py:42
  4.2 9.5 %collective-permute-start.2 = (bf16[256,512]{1,0:T(8,128)(2,1)}, bf16[256,512]{1,0:T(8,128)(2,1)S(1)}, u32[]{:S(2)}, u32[]{:S(2)}) collective-permute-start(bf16[256,512]{1,0:T(8,128)(2,1)} %get-tuple-element.90), channel_id=1, source_target_pairs={{0,31},{1,2},{2,1},{3,4},{4,3},{5,6},{6,5},{7,8},{8,7},{9,10},{10,... | collective-permute-start | bytes 786440 | tf_op jit(solution)/shard_map/ppermute | solution.py:47
  5.9 8.8 %collective-permute-start.1 = (bf16[256,512]{1,0:T(8,128)(2,1)}, bf16[256,512]{1,0:T(8,128)(2,1)S(1)}, u32[]{:S(2)}, u32[]{:S(2)}) collective-permute-start(bf16[256,512]{1,0:T(8,128)(2,1)} %get-tuple-element.89), channel_id=1, source_target_pairs={{0,32},{32,0},{64,96},{96,64},{1,33},{33,1},{65,97},{97,65},{2,34}... | collective-permute-start | bytes 786440 | tf_op jit(solution)/shard_map/ppermute | solution.py:57
  7.1 8.6 %collective-permute-start = (bf16[256,512]{1,0:T(8,128)(2,1)}, bf16[256,512]{1,0:T(8,128)(2,1)S(1)}, u32[]{:S(2)}, u32[]{:S(2)}) collective-permute-start(bf16[256,512]{1,0:T(8,128)(2,1)} %get-tuple-element.87), channel_id=1, source_target_pairs={{32,64},{64,32},{33,65},{65,33},{34,66},{66,34},{35,67},{67,35},{3... | collective-permute-start | bytes 786440 | tf_op jit(solution)/shard_map/ppermute | solution.py:57
  7.8 0.9 copy-start.1
  8.8 0.7 copy-start.9
  9.5 0.9 copy-start.13
  10.4 0.7 copy-start.15
  14.7 2.0 %copy-start.3 = (bf16[512,512]{1,0:T(8,128)(2,1)S(1)}, bf16[512,512]{1,0:T(8,128)(2,1)}, u32[]{:S(2)}) copy-start(bf16[512,512]{1,0:T(8,128)(2,1)} %encode_ref.1) | copy-start | bytes 1572868
  14.7 2.0 %copy-start.6 = (bf16[256,512]{1,0:T(8,128)(2,1)S(1)}, bf16[256,512]{1,0:T(8,128)(2,1)}, u32[]{:S(2)}) copy-start(bf16[256,512]{1,0:T(8,128)(2,1)} %static_ref.1) | copy-start | bytes 786436
  15.7 6.8 %copy-start.8 = (s32[3840]{0:T(1024)S(1)}, s32[3840]{0:T(1024)}, u32[]{:S(2)}) copy-start(s32[3840]{0:T(1024)} %param.26) | copy-start | bytes 46084
  15.7 6.8 %copy-start.14 = (s32[3840]{0:T(1024)S(1)}, s32[3840]{0:T(1024)}, u32[]{:S(2)}) copy-start(s32[3840]{0:T(1024)} %param.27) | copy-start | bytes 46084
  17.1 7.6 %collective-permute-start.4 = (bf16[128,512]{1,0:T(8,128)(2,1)S(1)}, bf16[128,512]{1,0:T(8,128)(2,1)S(1)}, u32[]{:S(2)}, u32[]{:S(2)}) collective-permute-start(bf16[128,512]{1,0:T(8,128)(2,1)S(1)} %get-tuple-element.104), channel_id=1, source_target_pairs={{0,1},{1,0},{2,3},{3,2},{4,5},{5,4},{6,7},{7,6},{8,9},{9,8},{10,11... | collective-permute-start | bytes 393224 | tf_op jit(solution)/shard_map/ppermute | solution.py:42
  22.5 4.4 %collective-permute-start.5 = (bf16[128,512]{1,0:T(8,128)(2,1)S(1)}, bf16[128,512]{1,0:T(8,128)(2,1)S(1)}, u32[]{:S(2)}, u32[]{:S(2)}) collective-permute-start(bf16[128,512]{1,0:T(8,128)(2,1)S(1)} %get-tuple-element.105), channel_id=1, source_target_pairs={{0,31},{1,2},{2,1},{3,4},{4,3},{5,6},{6,5},{7,8},{8,7},{9,10},{10,... | collective-permute-start | bytes 393224 | tf_op jit(solution)/shard_map/ppermute | solution.py:47
  22.5 1.5 %copy-start.11 = (s32[256,6]{0,1:T(8,128)S(1)}, s32[256,6]{0,1:T(8,128)}, u32[]{:S(2)}) copy-start(s32[256,6]{0,1:T(8,128)} %param.25) | copy-start | bytes 18436
  22.5 4.4 %copy-start.4 = (bf16[2,512,512]{2,1,0:T(8,128)(2,1)S(1)}, bf16[2,512,512]{2,1,0:T(8,128)(2,1)}, u32[]{:S(2)}) copy-start(bf16[2,512,512]{2,1,0:T(8,128)(2,1)} %self_ref.3) | copy-start | bytes 3145732
  22.5 4.4 %copy-start.5 = (bf16[2,512,512]{2,1,0:T(8,128)(2,1)S(1)}, bf16[2,512,512]{2,1,0:T(8,128)(2,1)}, u32[]{:S(2)}) copy-start(bf16[2,512,512]{2,1,0:T(8,128)(2,1)} %near_ref.3) | copy-start | bytes 3145732
  26.9 9.5 %copy-start.7 = (bf16[512,227]{0,1:T(8,128)(2,1)S(1)}, bf16[512,227]{0,1:T(8,128)(2,1)}, u32[]{:S(2)}) copy-start(bf16[512,227]{0,1:T(8,128)(2,1)} %param.15) | copy-start | bytes 697348
  28.4 9.6 %collective-permute-start.9 = (bf16[256,512]{1,0:T(8,128)(2,1)S(1)}, bf16[256,512]{1,0:T(8,128)(2,1)S(1)}, u32[]{:S(2)}, u32[]{:S(2)}) collective-permute-start(bf16[256,512]{1,0:T(8,128)(2,1)S(1)} %get-tuple-element.107.refs_0_), channel_id=1, source_target_pairs={{0,1},{1,0},{2,3},{3,2},{4,5},{5,4},{6,7},{7,6},{8,9},{9,8},{10,11... | collective-permute-start | bytes 786440 | tf_op jit(solution)/shard_map/ppermute | solution.py:42
  31.9 6.1 %collective-permute-start.8 = (bf16[256,512]{1,0:T(8,128)(2,1)S(1)}, bf16[256,512]{1,0:T(8,128)(2,1)S(1)}, u32[]{:S(2)}, u32[]{:S(2)}) collective-permute-start(bf16[256,512]{1,0:T(8,128)(2,1)S(1)} %get-tuple-element.107.refs_0_), channel_id=1, source_target_pairs={{0,31},{1,2},{2,1},{3,4},{4,3},{5,6},{6,5},{7,8},{8,7},{9,10},{10,... | collective-permute-start | bytes 786440 | tf_op jit(solution)/shard_map/ppermute | solution.py:47
  31.9 9.9 %collective-permute-start.7 = (bf16[256,512]{1,0:T(8,128)(2,1)S(1)}, bf16[256,512]{1,0:T(8,128)(2,1)S(1)}, u32[]{:S(2)}, u32[]{:S(2)}) collective-permute-start(bf16[256,512]{1,0:T(8,128)(2,1)S(1)} %get-tuple-element.107.refs_0_), channel_id=1, source_target_pairs={{0,32},{32,0},{64,96},{96,64},{1,33},{33,1},{65,97},{97,65},{2,34}... | collective-permute-start | bytes 786440 | tf_op jit(solution)/shard_map/ppermute | solution.py:57
  35.5 6.2 %collective-permute-start.6 = (bf16[256,512]{1,0:T(8,128)(2,1)S(1)}, bf16[256,512]{1,0:T(8,128)(2,1)S(1)}, u32[]{:S(2)}, u32[]{:S(2)}) collective-permute-start(bf16[256,512]{1,0:T(8,128)(2,1)S(1)} %get-tuple-element.107.refs_0_), channel_id=1, source_target_pairs={{32,64},{64,32},{33,65},{65,33},{34,66},{66,34},{35,67},{67,35},{3... | collective-permute-start | bytes 786440 | tf_op jit(solution)/shard_map/ppermute | solution.py:57
  36.7 5.0 %copy-start.12 = (bf16[512,512]{1,0:T(8,128)(2,1)S(1)}, bf16[512,512]{1,0:T(8,128)(2,1)}, u32[]{:S(2)}) copy-start(bf16[512,512]{1,0:T(8,128)(2,1)} %refs_7_.1) | copy-start | bytes 1572868
  38.0 11.3 %copy-start.10 = (s32[3840]{0:T(1024)S(1)}, s32[3840]{0:T(1024)}, u32[]{:S(2)}) copy-start(s32[3840]{0:T(1024)} %param.23) | copy-start | bytes 46084
  44.1 9.6 %collective-permute-start.10 = (bf16[256,512]{1,0:T(8,128)(2,1)S(1)}, bf16[256,512]{1,0:T(8,128)(2,1)S(1)}, u32[]{:S(2)}, u32[]{:S(2)}) collective-permute-start(bf16[256,512]{1,0:T(8,128)(2,1)S(1)} %get-tuple-element.118), channel_id=1, source_target_pairs={{0,1},{1,0},{2,3},{3,2},{4,5},{5,4},{6,7},{7,6},{8,9},{9,8},{10,11... | collective-permute-start | bytes 786440 | tf_op jit(solution)/shard_map/ppermute | solution.py:42
  45.2 8.5 %collective-permute-start.11 = (bf16[256,512]{1,0:T(8,128)(2,1)S(1)}, bf16[256,512]{1,0:T(8,128)(2,1)S(1)}, u32[]{:S(2)}, u32[]{:S(2)}) collective-permute-start(bf16[256,512]{1,0:T(8,128)(2,1)S(1)} %get-tuple-element.119), channel_id=1, source_target_pairs={{0,31},{1,2},{2,1},{3,4},{4,3},{5,6},{6,5},{7,8},{8,7},{9,10},{10,... | collective-permute-start | bytes 786440 | tf_op jit(solution)/shard_map/ppermute | solution.py:47
  45.2 8.5 %collective-permute-start.12 = (bf16[256,512]{1,0:T(8,128)(2,1)S(1)}, bf16[256,512]{1,0:T(8,128)(2,1)S(1)}, u32[]{:S(2)}, u32[]{:S(2)}) collective-permute-start(bf16[256,512]{1,0:T(8,128)(2,1)S(1)} %get-tuple-element.120), channel_id=1, source_target_pairs={{0,32},{32,0},{64,96},{96,64},{1,33},{33,1},{65,97},{97,65},{2,34}... | collective-permute-start | bytes 786440 | tf_op jit(solution)/shard_map/ppermute | solution.py:57
  48.6 5.2 %collective-permute-start.13 = (bf16[256,512]{1,0:T(8,128)(2,1)S(1)}, bf16[256,512]{1,0:T(8,128)(2,1)S(1)}, u32[]{:S(2)}, u32[]{:S(2)}) collective-permute-start(bf16[256,512]{1,0:T(8,128)(2,1)S(1)} %get-tuple-element.121), channel_id=1, source_target_pairs={{32,64},{64,32},{33,65},{65,33},{34,66},{66,34},{35,67},{67,35},{3... | collective-permute-start | bytes 786440 | tf_op jit(solution)/shard_map/ppermute | solution.py:57
  51.4 5.7 %collective-permute-start.14 = (bf16[384,512]{1,0:T(8,128)(2,1)S(1)}, bf16[384,512]{1,0:T(8,128)(2,1)S(1)}, u32[]{:S(2)}, u32[]{:S(2)}) collective-permute-start(bf16[384,512]{1,0:T(8,128)(2,1)S(1)} %get-tuple-element.129), channel_id=1, source_target_pairs={{0,1},{1,0},{2,3},{3,2},{4,5},{5,4},{6,7},{7,6},{8,9},{9,8},{10,11... | collective-permute-start | bytes 1179656 | tf_op jit(solution)/shard_map/ppermute | solution.py:42
  54.0 3.2 %collective-permute-start.15 = (bf16[192,512]{1,0:T(8,128)(2,1)S(1)}, bf16[192,512]{1,0:T(8,128)(2,1)S(1)}, u32[]{:S(2)}, u32[]{:S(2)}) collective-permute-start(bf16[192,512]{1,0:T(8,128)(2,1)S(1)} %get-tuple-element.131), channel_id=1, source_target_pairs={{0,1},{1,0},{2,3},{3,2},{4,5},{5,4},{6,7},{7,6},{8,9},{9,8},{10,11... | collective-permute-start | bytes 589832 | tf_op jit(solution)/shard_map/ppermute | solution.py:42
  56.1 5.1 %collective-permute-start.16 = (bf16[192,512]{1,0:T(8,128)(2,1)S(1)}, bf16[192,512]{1,0:T(8,128)(2,1)S(1)}, u32[]{:S(2)}, u32[]{:S(2)}) collective-permute-start(bf16[192,512]{1,0:T(8,128)(2,1)S(1)} %get-tuple-element.132), channel_id=1, source_target_pairs={{0,31},{1,2},{2,1},{3,4},{4,3},{5,6},{6,5},{7,8},{8,7},{9,10},{10,... | collective-permute-start | bytes 589832 | tf_op jit(solution)/shard_map/ppermute | solution.py:47
  61.2 6.6 %copy-start.2 = (bf16[512,227]{0,1:T(8,128)(2,1)S(1)}, bf16[512,227]{0,1:T(8,128)(2,1)}, u32[]{:S(2)}) copy-start(bf16[512,227]{0,1:T(8,128)(2,1)} %param.14) | copy-start | bytes 697348
  64.3 6.9 %collective-permute-start.18 = (bf16[768,512]{1,0:T(8,128)(2,1)S(1)}, bf16[768,512]{1,0:T(8,128)(2,1)S(1)}, u32[]{:S(2)}, u32[]{:S(2)}) collective-permute-start(bf16[768,512]{1,0:T(8,128)(2,1)S(1)} %get-tuple-element.146), channel_id=1, source_target_pairs={{0,1},{1,0},{2,3},{3,2},{4,5},{5,4},{6,7},{7,6},{8,9},{9,8},{10,11... | collective-permute-start | bytes 2359304 | tf_op jit(solution)/shard_map/ppermute | solution.py:42
  67.8 3.4 %collective-permute-start.17 = (bf16[512,512]{1,0:T(8,128)(2,1)S(1)}, bf16[512,512]{1,0:T(8,128)(2,1)S(1)}, u32[]{:S(2)}, u32[]{:S(2)}) collective-permute-start(bf16[512,512]{1,0:T(8,128)(2,1)S(1)} %get-tuple-element.140), channel_id=1, source_target_pairs={{0,1},{1,0},{2,3},{3,2},{4,5},{5,4},{6,7},{7,6},{8,9},{9,8},{10,11... | collective-permute-start | bytes 1572872 | tf_op jit(solution)/shard_map/ppermute | solution.py:42
  69.5 1.7 %collective-permute-start.19 = (bf16[128,512]{1,0:T(8,128)(2,1)S(1)}, bf16[128,512]{1,0:T(8,128)(2,1)S(1)}, u32[]{:S(2)}, u32[]{:S(2)}) collective-permute-start(bf16[128,512]{1,0:T(8,128)(2,1)S(1)} %get-tuple-element.155), channel_id=1, source_target_pairs={{0,1},{1,0},{2,3},{3,2},{4,5},{5,4},{6,7},{7,6},{8,9},{9,8},{10,11... | collective-permute-start | bytes 393224 | tf_op jit(solution)/shard_map/ppermute | solution.py:42
  99.4 5.9 %collective-permute-start.22 = (bf16[112,512]{1,0:T(8,128)(2,1)S(1)}, bf16[112,512]{1,0:T(8,128)(2,1)S(1)}, u32[]{:S(2)}, u32[]{:S(2)}) collective-permute-start(bf16[112,512]{1,0:T(8,128)(2,1)S(1)} %shard_map.217.refs_0_), channel_id=1, source_target_pairs={{0,96},{32,0},{64,32},{96,64},{1,97},{33,1},{65,33},{97,65},{2,98}... | collective-permute-start | bytes 344072 | tf_op jit(solution)/shard_map/ppermute | solution.py:540
  100.1 7.0 %collective-permute-start.21 = (bf16[112,512]{1,0:T(8,128)(2,1)S(1)}, bf16[112,512]{1,0:T(8,128)(2,1)S(1)}, u32[]{:S(2)}, u32[]{:S(2)}) collective-permute-start(bf16[112,512]{1,0:T(8,128)(2,1)S(1)} %shard_map.217.refs_0_), channel_id=1, source_target_pairs={{0,64},{32,96},{64,0},{96,32},{1,65},{33,97},{65,1},{97,33},{2,66}... | collective-permute-start | bytes 344072 | tf_op jit(solution)/shard_map/ppermute | solution.py:540
  104.9 5.8 %collective-permute-start.20 = (bf16[112,512]{1,0:T(8,128)(2,1)S(1)}, bf16[112,512]{1,0:T(8,128)(2,1)S(1)}, u32[]{:S(2)}, u32[]{:S(2)}) collective-permute-start(bf16[112,512]{1,0:T(8,128)(2,1)S(1)} %shard_map.217.refs_0_), channel_id=1, source_target_pairs={{0,32},{32,64},{64,96},{96,0},{1,33},{33,65},{65,97},{97,1},{2,34}... | collective-permute-start | bytes 344072 | tf_op jit(solution)/shard_map/ppermute | solution.py:540
  136.3 7.4 %collective-permute-start.23 = (bf16[1792,512]{1,0:T(8,128)(2,1)S(1)}, bf16[1792,512]{1,0:T(8,128)(2,1)S(1)}, u32[]{:S(2)}, u32[]{:S(2)}) collective-permute-start(bf16[1792,512]{1,0:T(8,128)(2,1)S(1)} %bitcast.14), channel_id=1, source_target_pairs={{0,1},{1,0},{2,3},{3,2},{4,5},{5,4},{6,7},{7,6},{8,9},{9,8},{10,11... | collective-permute-start | bytes 5505032 | tf_op jit(solution)/shard_map/ppermute | solution.py:42

commit v7 on v6

--- a/solution.py
+++ b/solution.py
@@ -594,7 +594,7 @@
     index = [None] * GROUPS
     slopes = [slope_embed] + [None] * (GROUPS - 1)
     grids = [grid, *arrived]
-    for p in range(1, GROUPS):
+    for p in (1, 3, 2, 4):
         index[p], slopes[p], total = whole(
             lambda *refs, p=p: embed_far(p, *refs),
             [shape(INDEX_ROWS, LANES, jnp.int32), grid_full, mesh_full],

time: 146 us -> 146 us (level)
  no operation moved by 1% of the time
where the time goes in v7:
time: 146 us
  blocking collectives  53.1 us (36%)
  starting transfers between devices  41.4 us (28%)
  Pallas kernels  27.4 us (19%)
  waiting for transfers between devices  17.4 us (12%)
  local copies, waits for them, and re-layouts  3.39 us (2%)
    all_to_all x1, blocking collectives, reduce_all(): lax.all_to_all(part.reshape(chips, rows, width), 'dom', 0, 0, axis_index_...  27.6 us
    all_to_all x1, blocking collectives, reduce_all(): lax.all_to_all(copies, 'dom', 0, 0, axis_index_groups=groups)  25.5 us
    ppermute x10, starting transfers between devices, swap_on(): return lax.ppermute(value, 'dom', [(i, i ^ 1) for i in range(count)])  23.6 us
    pallas_call x20, Pallas kernels, whole(): pl.pallas_call(body, out_shape=outs, scratch_shapes=scratch, compiler_par...  19.9 us
    ppermute x6, starting transfers between devices, swap_band(): return lax.ppermute(value, 'band', pairs)  10.5 us
    ppermute x5, waiting for transfers between devices, swap_off(): lax.ppermute(value, 'dom', [(i, (i + (1 if i % 2 else -1)) % count) for i...  6.2 us
    ppermute x3, waiting for transfers between devices, reduce_all(): lax.ppermute(piece, 'band', [(i, (i + step) % bands) for i in range(bands)])  5.75 us
    ppermute x3, starting transfers between devices, reduce_all(): lax.ppermute(piece, 'band', [(i, (i + step) % bands) for i in range(bands)])  5.48 us
  transfers between devices with their start and end apart: 24, of which 9 were waited for; matrix products, arithmetic and copies ran while one was open for 1% of the time, Pallas kernels for 10%

profile of v7, /device:TPU:1, one launch (start us, length us, event | category | flops | bytes accessed | tf_op | source)
XLA Modules:
  0.0 145.8 jit_solution(5238256716493012636)
XLA Ops:
  0.6 0.0 copy-start
  0.6 0.0 copy-start.16
  0.7 2.1 %shard_map.197 = (bf16[256,512]{1,0:T(8,128)(2,1)}, bf16[256,512]{1,0:T(8,128)(2,1)}, bf16[256,512]{1,0:T(8,128)(2,1)}, bf16[256,512]{1,0:T(8,128)(2,1)}) custom-call(bf16[227,512]{1,0:T(8,128)(2,1)} %bitcast.18, s32[30,128]{1,0:T(8,128)} %bitcast.25, s32[30,128]{1,0:T(8,128)} %bitcast.22, s32[6,256]{1,0:T(8,128)} %bitcast.28), custom_call_target="tpu_custom_call" | custom-call | bytes 1317888 | tf_op jit(solution)/shard_map/pallas_call | solution.py:128
  2.7 1.5 %collective-permute-start.3 = (bf16[256,512]{1,0:T(8,128)(2,1)}, bf16[256,512]{1,0:T(8,128)(2,1)S(1)}, u32[]{:S(2)}, u32[]{:S(2)}) collective-permute-start(bf16[256,512]{1,0:T(8,128)(2,1)} %get-tuple-element.91), channel_id=1, source_target_pairs={{0,1},{1,0},{2,3},{3,2},{4,5},{5,4},{6,7},{7,6},{8,9},{9,8},{10,11... | collective-permute-start | bytes 786440 | tf_op jit(solution)/shard_map/ppermute | solution.py:42
  4.2 1.3 collective-permute-start.2
  5.5 1.9 %collective-permute-start.1 = (bf16[256,512]{1,0:T(8,128)(2,1)}, bf16[256,512]{1,0:T(8,128)(2,1)S(1)}, u32[]{:S(2)}, u32[]{:S(2)}) collective-permute-start(bf16[256,512]{1,0:T(8,128)(2,1)} %get-tuple-element.89), channel_id=1, source_target_pairs={{0,31},{1,2},{2,1},{3,4},{4,3},{5,6},{6,5},{7,8},{8,7},{9,10},{10,... | collective-permute-start | bytes 786440 | tf_op jit(solution)/shard_map/ppermute | solution.py:47
  7.4 0.7 collective-permute-start
  8.1 0.9 copy-done.1
  9.0 0.7 copy-done.9
  9.8 0.9 copy-done.13
  10.7 0.7 copy-done.15
  11.4 1.6 %shard_map.198 = (f32[512,512]{1,0:T(8,128)S(1)}, f32[256,512]{1,0:T(8,128)S(1)}, bf16[227,512]{1,0:T(8,128)(2,1)S(1)}) custom-call(bf16[227,512]{1,0:T(8,128)(2,1)S(1)} %bitcast.19, bf16[227,512]{1,0:T(8,128)(2,1)S(1)} %copy-done.13, s32[30,128]{1,0:T(8,128)S(1)} %bitcast.26, s32[30,128]{1,0:T(8,128)S(1)} %bitcast.32), custom_call_target="tpu_custom_call" | custom-call | flops 454557696 | bytes 2300928 | tf_op jit(solution)/shard_map/pallas_call | solution.py:128
  13.1 0.9 shard_map.199
  14.0 1.0 shard_map.200
  15.0 0.9 shard_map.201
  16.0 1.0 shard_map.202
  17.0 0.4 shard_map.203
  17.4 4.8 %collective-permute-start.4 = (bf16[128,512]{1,0:T(8,128)(2,1)S(1)}, bf16[128,512]{1,0:T(8,128)(2,1)S(1)}, u32[]{:S(2)}, u32[]{:S(2)}) collective-permute-start(bf16[128,512]{1,0:T(8,128)(2,1)S(1)} %get-tuple-element.104), channel_id=1, source_target_pairs={{0,1},{1,0},{2,3},{3,2},{4,5},{5,4},{6,7},{7,6},{8,9},{9,8},{10,11... | collective-permute-start | bytes 393224 | tf_op jit(solution)/shard_map/ppermute | solution.py:42
  22.3 1.4 shard_map.204.refs_5_
  23.7 0.7 shard_map.205
  24.4 2.2 %collective-permute-done.5.off_ref = bf16[128,512]{1,0:T(8,128)(2,1)S(1)} collective-permute-done((bf16[128,512]{1,0:T(8,128)(2,1)S(1)}, bf16[128,512]{1,0:T(8,128)(2,1)S(1)}, u32[]{:S(2)}, u32[]{:S(2)}) %collective-permute-start.5) | collective-permute-done | bytes 131104 | tf_op jit(solution)/shard_map/ppermute | solution.py:47
  26.6 1.5 %shard_map.206 = (bf16[256,512]{1,0:T(8,128)(2,1)S(1)}, f32[384,512]{1,0:T(8,128)S(1)}, f32[256,512]{1,0:T(8,128)S(1)}, bf16[256,512]{1,0:T(8,128)(2,1)S(1)}, bf...) custom-call(bf16[256,512]{1,0:T(8,128)(2,1)S(1)} %get-tuple-element.97.half_ref.refs_0_, ...), custom_call_target="tpu_custom_call" | custom-call | flops 1207959552 | bytes 6029312 | tf_op jit(solution)/shard_map/pallas_call | solution.py:81
  28.1 3.5 %collective-permute-start.9 = (bf16[256,512]{1,0:T(8,128)(2,1)S(1)}, bf16[256,512]{1,0:T(8,128)(2,1)S(1)}, u32[]{:S(2)}, u32[]{:S(2)}) collective-permute-start(bf16[256,512]{1,0:T(8,128)(2,1)S(1)} %get-tuple-element.107.refs_0_), channel_id=1, source_target_pairs={{0,1},{1,0},{2,3},{3,2},{4,5},{5,4},{6,7},{7,6},{8,9},{9,8},{10,11... | collective-permute-start | bytes 786440 | tf_op jit(solution)/shard_map/ppermute | solution.py:42
  31.6 3.6 %collective-permute-start.7 = (bf16[256,512]{1,0:T(8,128)(2,1)S(1)}, bf16[256,512]{1,0:T(8,128)(2,1)S(1)}, u32[]{:S(2)}, u32[]{:S(2)}) collective-permute-start(bf16[256,512]{1,0:T(8,128)(2,1)S(1)} %get-tuple-element.107.refs_0_), channel_id=1, source_target_pairs={{0,32},{32,0},{64,96},{96,64},{1,33},{33,1},{65,97},{97,65},{2,34}... | collective-permute-start | bytes 786440 | tf_op jit(solution)/shard_map/ppermute | solution.py:57
  35.2 0.8 collective-permute-start.6
  36.1 0.3 fusion.1.refs_8_
  36.5 1.2 shard_map.207.refs_6_
  37.7 3.7 %collective-permute-done.7.refs_2_ = bf16[256,512]{1,0:T(8,128)(2,1)S(1)} collective-permute-done((bf16[256,512]{1,0:T(8,128)(2,1)S(1)}, bf16[256,512]{1,0:T(8,128)(2,1)S(1)}, u32[]{:S(2)}, u32[]{:S(2)}) %collective-permute-start.7) | collective-permute-done | bytes 262176 | tf_op jit(solution)/shard_map/ppermute | solution.py:57
  41.5 2.3 %shard_map.208 = (bf16[512,512]{1,0:T(8,128)(2,1)S(1)}, bf16[512,512]{1,0:T(8,128)(2,1)S(1)}, bf16[512,512]{1,0:T(8,128)(2,1)S(1)}, f32[256,512]{1,0:T(8,128)S(1...) custom-call(bf16[256,512]{1,0:T(8,128)(2,1)S(1)} %get-tuple-element., ...), custom_call_target="tpu_custom_call" | custom-call | flops 1879048192 | bytes 8650752 | tf_op jit(solution)/shard_map/pallas_call | solution.py:81
  43.8 1.1 collective-permute-start.10
  45.0 3.3 %collective-permute-start.12 = (bf16[256,512]{1,0:T(8,128)(2,1)S(1)}, bf16[256,512]{1,0:T(8,128)(2,1)S(1)}, u32[]{:S(2)}, u32[]{:S(2)}) collective-permute-start(bf16[256,512]{1,0:T(8,128)(2,1)S(1)} %get-tuple-element.120), channel_id=1, source_target_pairs={{0,32},{32,0},{64,96},{96,64},{1,33},{33,1},{65,97},{97,65},{2,34}... | collective-permute-start | bytes 786440 | tf_op jit(solution)/shard_map/ppermute | solution.py:57
  48.3 0.7 collective-permute-start.13
  49.0 1.4 shard_map.209.refs_1_
  50.4 0.7 shard_map.210
  51.1 2.1 %collective-permute-start.14 = (bf16[384,512]{1,0:T(8,128)(2,1)S(1)}, bf16[384,512]{1,0:T(8,128)(2,1)S(1)}, u32[]{:S(2)}, u32[]{:S(2)}) collective-permute-start(bf16[384,512]{1,0:T(8,128)(2,1)S(1)} %get-tuple-element.129), channel_id=1, source_target_pairs={{0,1},{1,0},{2,3},{3,2},{4,5},{5,4},{6,7},{7,6},{8,9},{9,8},{10,11... | collective-permute-start | bytes 1179656 | tf_op jit(solution)/shard_map/ppermute | solution.py:42
  53.2 0.2 add_multiply_fusion.1.refs_5_
  53.5 0.2 shard_map.211
  53.7 2.2 %collective-permute-start.15 = (bf16[192,512]{1,0:T(8,128)(2,1)S(1)}, bf16[192,512]{1,0:T(8,128)(2,1)S(1)}, u32[]{:S(2)}, u32[]{:S(2)}) collective-permute-start(bf16[192,512]{1,0:T(8,128)(2,1)S(1)} %get-tuple-element.131), channel_id=1, source_target_pairs={{0,1},{1,0},{2,3},{3,2},{4,5},{5,4},{6,7},{7,6},{8,9},{9,8},{10,11... | collective-permute-start | bytes 589832 | tf_op jit(solution)/shard_map/ppermute | solution.py:42
  55.9 0.3 add_multiply_fusion.slope_0_ref
  56.2 0.6 shard_map.212
  56.8 0.1 collective-permute-done.15.on_ref
  56.9 4.0 %collective-permute-done.16.off_ref = bf16[192,512]{1,0:T(8,128)(2,1)S(1)} collective-permute-done((bf16[192,512]{1,0:T(8,128)(2,1)S(1)}, bf16[192,512]{1,0:T(8,128)(2,1)S(1)}, u32[]{:S(2)}, u32[]{:S(2)}) %collective-permute-start.16) | collective-permute-done | bytes 196640 | tf_op jit(solution)/shard_map/ppermute | solution.py:47
  61.0 2.2 %shard_map.213 = (f32[256,512]{1,0:T(8,128)}, bf16[256,512]{1,0:T(8,128)(2,1)S(1)}, bf16[256,512]{1,0:T(8,128)(2,1)S(1)}, bf16[256,512]{1,0:T(8,128)(2,1)S(1)}) custom-call(f32[256,512]{1,0:T(8,128)S(1)} %get-tuple-element.130.state_ref, bf16[256,512]{1,0:T(8,128)(2,1)S(1)} %get-tuple-element.125.refs_1_.refs_3_.layer_ref, ...), custom_call_target="tpu_custom_call" | custom-call | flops 1207959552 | bytes 6946816 | tf_op jit(solution)/shard_map/pallas_call | solution.py:81
  63.1 0.9 shard_map.214
  64.0 3.5 %collective-permute-start.18 = (bf16[768,512]{1,0:T(8,128)(2,1)S(1)}, bf16[768,512]{1,0:T(8,128)(2,1)S(1)}, u32[]{:S(2)}, u32[]{:S(2)}) collective-permute-start(bf16[768,512]{1,0:T(8,128)(2,1)S(1)} %get-tuple-element.146), channel_id=1, source_target_pairs={{0,1},{1,0},{2,3},{3,2},{4,5},{5,4},{6,7},{7,6},{8,9},{9,8},{10,11... | collective-permute-start | bytes 2359304 | tf_op jit(solution)/shard_map/ppermute | solution.py:42
  67.5 0.1 collective-permute-start.17
  67.6 1.6 %shard_map.215 = (bf16[128,512]{1,0:T(8,128)(2,1)S(1)}, bf16[128,512]{1,0:T(8,128)(2,1)S(1)}) custom-call(bf16[256,512]{1,0:T(8,128)(2,1)S(1)} %get-tuple-element.147.refs_0_, bf16[512,1280]{1,0:T(8,128)(2,1)S(1)} %shard_map.209.refs_1_, f32[512,512]{1,0:T(8,128)S(1)} %get-tuple-element.149.refs_2_, f32[512,512]{1,0:T(8,128)S(1)} %get-tuple-element.150.refs_3_, ...), custom_call_target="tpu_custom_call" | custom-call | flops 1266155520 | bytes 8358912 | tf_op jit(solution)/shard_map/pallas_call | solution.py:81
  69.2 0.7 collective-permute-start.19
  69.9 1.0 collective-permute-done.19.refs_7_
  70.9 0.4 shard_map.216
  71.3 27.6 %all_to_all.10.pieces_ref = bf16[16,112,512]{2,1,0:T(8,128)(2,1)S(1)} all-to-all(bf16[16,112,512]{2,1,0:T(8,128)(2,1)S(1)} %bitcast.17), channel_id=1, replica_groups={{0,2,4,6,8,10,12,14,16,18,20,22,24,26,28,30},{1,3,5,7,9,11,13,15,17,19,..., dimensions={0} | all-to-all | bytes 3670016 | tf_op jit(solution)/shard_map/all_to_all | solution.py:535
  98.9 0.2 shard_map.217.refs_0_
  99.2 0.7 collective-permute-start.22
  99.8 4.8 %collective-permute-start.21 = (bf16[112,512]{1,0:T(8,128)(2,1)S(1)}, bf16[112,512]{1,0:T(8,128)(2,1)S(1)}, u32[]{:S(2)}, u32[]{:S(2)}) collective-permute-start(bf16[112,512]{1,0:T(8,128)(2,1)S(1)} %shard_map.217.refs_0_), channel_id=1, source_target_pairs={{0,64},{32,96},{64,0},{96,32},{1,65},{33,97},{65,1},{97,33},{2,66}... | collective-permute-start | bytes 344072 | tf_op jit(solution)/shard_map/ppermute | solution.py:540
  104.6 0.4 collective-permute-done.22.refs_3_
  105.0 1.8 %collective-permute-done.21.refs_2_ = bf16[112,512]{1,0:T(8,128)(2,1)S(1)} collective-permute-done((bf16[112,512]{1,0:T(8,128)(2,1)S(1)}, bf16[112,512]{1,0:T(8,128)(2,1)S(1)}, u32[]{:S(2)}, u32[]{:S(2)}) %collective-permute-start.21) | collective-permute-done | bytes 114720 | tf_op jit(solution)/shard_map/ppermute | solution.py:540
  106.8 3.6 %collective-permute-done.20.refs_1_ = bf16[112,512]{1,0:T(8,128)(2,1)S(1)} collective-permute-done((bf16[112,512]{1,0:T(8,128)(2,1)S(1)}, bf16[112,512]{1,0:T(8,128)(2,1)S(1)}, u32[]{:S(2)}, u32[]{:S(2)}) %collective-permute-start.20) | collective-permute-done | bytes 114720 | tf_op jit(solution)/shard_map/ppermute | solution.py:540
  110.4 0.2 shard_map.218
  110.6 25.5 %all_to_all.11 = bf16[16,112,512]{2,1,0:T(8,128)(2,1)S(1)} all-to-all(bf16[16,112,512]{2,1,0:T(8,128)(2,1)S(1)} %shard_map.218), channel_id=1, replica_groups={{0,2,4,6,8,10,12,14,16,18,20,22,24,26,28,30},{1,3,5,7,9,11,13,15,17,19,..., dimensions={0} | all-to-all | bytes 3670016 | tf_op jit(solution)/shard_map/all_to_all | solution.py:545
  136.1 4.0 %collective-permute-start.23 = (bf16[1792,512]{1,0:T(8,128)(2,1)S(1)}, bf16[1792,512]{1,0:T(8,128)(2,1)S(1)}, u32[]{:S(2)}, u32[]{:S(2)}) collective-permute-start(bf16[1792,512]{1,0:T(8,128)(2,1)S(1)} %bitcast.14), channel_id=1, source_target_pairs={{0,1},{1,0},{2,3},{3,2},{4,5},{5,4},{6,7},{7,6},{8,9},{9,8},{10,11... | collective-permute-start | bytes 5505032 | tf_op jit(solution)/shard_map/ppermute | solution.py:42
  140.1 1.0 fusion
  141.1 1.8 %shard_map.219 = (f32[512,512]{1,0:T(8,128)}, f32[2,512,512]{2,1,0:T(8,128)}, f32[2,512,512]{2,1,0:T(8,128)}, f32[512,512]{1,0:T(8,128)}) custom-call(bf16[1792,512]{1,0:T(8,128)(2,1)S(1)} %bitcast.15), custom_call_target="tpu_custom_call" | custom-call | bytes 5505024 | tf_op jit(solution)/shard_map/pallas_call | solution.py:508
  142.9 0.6 collective-permute-done.23.other_ref
  143.5 2.1 %shard_map.220 = (f32[512,512]{1,0:T(8,128)}, f32[2,512,512]{2,1,0:T(8,128)}, f32[2,512,512]{2,1,0:T(8,128)}, f32[512,512]{1,0:T(8,128)}, f32[227,512]{1,0:T(8,128)}, /*index=5*/f32[227,512]{1,0:T(8,128)}) custom-call(bf16[1792,512]{1,0:T(8,128)(2,1)S(1)} %bitcast.16, ...), custom_call_target="tpu_custom_call", output_to_operand_aliasing={{0}: (2, {}), {1}: (3, {}), {2}: (4, {}), {3}: (5, {})} | custom-call | bytes 5505024 | tf_op jit(solution)/shard_map/pallas_call | solution.py:517
  (48 shorter events, 0.1 us)
Async XLA Ops:
  0.6 35.5 %copy-start = (bf16[512,227]{0,1:T(8,128)(2,1)S(1)}, bf16[512,227]{0,1:T(8,128)(2,1)}, u32[]{:S(2)}) copy-start(bf16[512,227]{0,1:T(8,128)(2,1)} %param.22) | copy-start | bytes 697348
  0.6 12.4 %copy-start.16 = (s32[3840]{0:T(1024)S(1)}, s32[3840]{0:T(1024)}, u32[]{:S(2)}) copy-start(s32[3840]{0:T(1024)} %param.24) | copy-start | bytes 46084
  2.7 10.3 %collective-permute-start.3 = (bf16[256,512]{1,0:T(8,128)(2,1)}, bf16[256,512]{1,0:T(8,128)(2,1)S(1)}, u32[]{:S(2)}, u32[]{:S(2)}) collective-permute-start(bf16[256,512]{1,0:T(8,128)(2,1)} %get-tuple-element.91), channel_id=1, source_target_pairs={{0,1},{1,0},{2,3},{3,2},{4,5},{5,4},{6,7},{7,6},{8,9},{9,8},{10,11... | collective-permute-start | bytes 786440 | tf_op jit(solution)/shard_map/ppermute | solution.py:42
  4.2 9.8 %collective-permute-start.2 = (bf16[256,512]{1,0:T(8,128)(2,1)}, bf16[256,512]{1,0:T(8,128)(2,1)S(1)}, u32[]{:S(2)}, u32[]{:S(2)}) collective-permute-start(bf16[256,512]{1,0:T(8,128)(2,1)} %get-tuple-element.90), channel_id=1, source_target_pairs={{0,32},{32,0},{64,96},{96,64},{1,33},{33,1},{65,97},{97,65},{2,34}... | collective-permute-start | bytes 786440 | tf_op jit(solution)/shard_map/ppermute | solution.py:57
  5.5 9.5 %collective-permute-start.1 = (bf16[256,512]{1,0:T(8,128)(2,1)}, bf16[256,512]{1,0:T(8,128)(2,1)S(1)}, u32[]{:S(2)}, u32[]{:S(2)}) collective-permute-start(bf16[256,512]{1,0:T(8,128)(2,1)} %get-tuple-element.89), channel_id=1, source_target_pairs={{0,31},{1,2},{2,1},{3,4},{4,3},{5,6},{6,5},{7,8},{8,7},{9,10},{10,... | collective-permute-start | bytes 786440 | tf_op jit(solution)/shard_map/ppermute | solution.py:47
  7.4 8.6 %collective-permute-start = (bf16[256,512]{1,0:T(8,128)(2,1)}, bf16[256,512]{1,0:T(8,128)(2,1)S(1)}, u32[]{:S(2)}, u32[]{:S(2)}) collective-permute-start(bf16[256,512]{1,0:T(8,128)(2,1)} %get-tuple-element.87), channel_id=1, source_target_pairs={{32,64},{64,32},{33,65},{65,33},{34,66},{66,34},{35,67},{67,35},{3... | collective-permute-start | bytes 786440 | tf_op jit(solution)/shard_map/ppermute | solution.py:57
  8.1 0.9 copy-start.1
  9.0 0.7 copy-start.9
  9.8 0.9 copy-start.13
  10.7 0.7 copy-start.15
  15.0 2.0 %copy-start.3 = (bf16[512,512]{1,0:T(8,128)(2,1)S(1)}, bf16[512,512]{1,0:T(8,128)(2,1)}, u32[]{:S(2)}) copy-start(bf16[512,512]{1,0:T(8,128)(2,1)} %encode_ref.1) | copy-start | bytes 1572868
  15.0 2.0 %copy-start.6 = (bf16[256,512]{1,0:T(8,128)(2,1)S(1)}, bf16[256,512]{1,0:T(8,128)(2,1)}, u32[]{:S(2)}) copy-start(bf16[256,512]{1,0:T(8,128)(2,1)} %static_ref.1) | copy-start | bytes 786436
  16.0 6.3 %copy-start.8 = (s32[3840]{0:T(1024)S(1)}, s32[3840]{0:T(1024)}, u32[]{:S(2)}) copy-start(s32[3840]{0:T(1024)} %param.26) | copy-start | bytes 46084
  16.0 6.3 %copy-start.14 = (s32[3840]{0:T(1024)S(1)}, s32[3840]{0:T(1024)}, u32[]{:S(2)}) copy-start(s32[3840]{0:T(1024)} %param.27) | copy-start | bytes 46084
  17.4 7.0 %collective-permute-start.4 = (bf16[128,512]{1,0:T(8,128)(2,1)S(1)}, bf16[128,512]{1,0:T(8,128)(2,1)S(1)}, u32[]{:S(2)}, u32[]{:S(2)}) collective-permute-start(bf16[128,512]{1,0:T(8,128)(2,1)S(1)} %get-tuple-element.104), channel_id=1, source_target_pairs={{0,1},{1,0},{2,3},{3,2},{4,5},{5,4},{6,7},{7,6},{8,9},{9,8},{10,11... | collective-permute-start | bytes 393224 | tf_op jit(solution)/shard_map/ppermute | solution.py:42
  22.2 4.4 %collective-permute-start.5 = (bf16[128,512]{1,0:T(8,128)(2,1)S(1)}, bf16[128,512]{1,0:T(8,128)(2,1)S(1)}, u32[]{:S(2)}, u32[]{:S(2)}) collective-permute-start(bf16[128,512]{1,0:T(8,128)(2,1)S(1)} %get-tuple-element.105), channel_id=1, source_target_pairs={{0,31},{1,2},{2,1},{3,4},{4,3},{5,6},{6,5},{7,8},{8,7},{9,10},{10,... | collective-permute-start | bytes 393224 | tf_op jit(solution)/shard_map/ppermute | solution.py:47
  22.2 1.5 %copy-start.11 = (s32[256,6]{0,1:T(8,128)S(1)}, s32[256,6]{0,1:T(8,128)}, u32[]{:S(2)}) copy-start(s32[256,6]{0,1:T(8,128)} %param.25) | copy-start | bytes 18436
  22.2 4.4 %copy-start.4 = (bf16[2,512,512]{2,1,0:T(8,128)(2,1)S(1)}, bf16[2,512,512]{2,1,0:T(8,128)(2,1)}, u32[]{:S(2)}) copy-start(bf16[2,512,512]{2,1,0:T(8,128)(2,1)} %self_ref.3) | copy-start | bytes 3145732
  22.3 4.4 %copy-start.5 = (bf16[2,512,512]{2,1,0:T(8,128)(2,1)S(1)}, bf16[2,512,512]{2,1,0:T(8,128)(2,1)}, u32[]{:S(2)}) copy-start(bf16[2,512,512]{2,1,0:T(8,128)(2,1)} %near_ref.3) | copy-start | bytes 3145732
  26.6 9.5 %copy-start.7 = (bf16[512,227]{0,1:T(8,128)(2,1)S(1)}, bf16[512,227]{0,1:T(8,128)(2,1)}, u32[]{:S(2)}) copy-start(bf16[512,227]{0,1:T(8,128)(2,1)} %param.15) | copy-start | bytes 697348
  28.1 9.6 %collective-permute-start.9 = (bf16[256,512]{1,0:T(8,128)(2,1)S(1)}, bf16[256,512]{1,0:T(8,128)(2,1)S(1)}, u32[]{:S(2)}, u32[]{:S(2)}) collective-permute-start(bf16[256,512]{1,0:T(8,128)(2,1)S(1)} %get-tuple-element.107.refs_0_), channel_id=1, source_target_pairs={{0,1},{1,0},{2,3},{3,2},{4,5},{5,4},{6,7},{7,6},{8,9},{9,8},{10,11... | collective-permute-start | bytes 786440 | tf_op jit(solution)/shard_map/ppermute | solution.py:42
  31.6 6.1 %collective-permute-start.8 = (bf16[256,512]{1,0:T(8,128)(2,1)S(1)}, bf16[256,512]{1,0:T(8,128)(2,1)S(1)}, u32[]{:S(2)}, u32[]{:S(2)}) collective-permute-start(bf16[256,512]{1,0:T(8,128)(2,1)S(1)} %get-tuple-element.107.refs_0_), channel_id=1, source_target_pairs={{0,31},{1,2},{2,1},{3,4},{4,3},{5,6},{6,5},{7,8},{8,7},{9,10},{10,... | collective-permute-start | bytes 786440 | tf_op jit(solution)/shard_map/ppermute | solution.py:47
  31.6 9.8 %collective-permute-start.7 = (bf16[256,512]{1,0:T(8,128)(2,1)S(1)}, bf16[256,512]{1,0:T(8,128)(2,1)S(1)}, u32[]{:S(2)}, u32[]{:S(2)}) collective-permute-start(bf16[256,512]{1,0:T(8,128)(2,1)S(1)} %get-tuple-element.107.refs_0_), channel_id=1, source_target_pairs={{0,32},{32,0},{64,96},{96,64},{1,33},{33,1},{65,97},{97,65},{2,34}... | collective-permute-start | bytes 786440 | tf_op jit(solution)/shard_map/ppermute | solution.py:57
  35.2 6.2 %collective-permute-start.6 = (bf16[256,512]{1,0:T(8,128)(2,1)S(1)}, bf16[256,512]{1,0:T(8,128)(2,1)S(1)}, u32[]{:S(2)}, u32[]{:S(2)}) collective-permute-start(bf16[256,512]{1,0:T(8,128)(2,1)S(1)} %get-tuple-element.107.refs_0_), channel_id=1, source_target_pairs={{32,64},{64,32},{33,65},{65,33},{34,66},{66,34},{35,67},{67,35},{3... | collective-permute-start | bytes 786440 | tf_op jit(solution)/shard_map/ppermute | solution.py:57
  36.5 5.0 %copy-start.12 = (bf16[512,512]{1,0:T(8,128)(2,1)S(1)}, bf16[512,512]{1,0:T(8,128)(2,1)}, u32[]{:S(2)}) copy-start(bf16[512,512]{1,0:T(8,128)(2,1)} %refs_7_.1) | copy-start | bytes 1572868
  37.7 11.3 %copy-start.10 = (s32[3840]{0:T(1024)S(1)}, s32[3840]{0:T(1024)}, u32[]{:S(2)}) copy-start(s32[3840]{0:T(1024)} %param.23) | copy-start | bytes 46084
  43.8 9.6 %collective-permute-start.10 = (bf16[256,512]{1,0:T(8,128)(2,1)S(1)}, bf16[256,512]{1,0:T(8,128)(2,1)S(1)}, u32[]{:S(2)}, u32[]{:S(2)}) collective-permute-start(bf16[256,512]{1,0:T(8,128)(2,1)S(1)} %get-tuple-element.118), channel_id=1, source_target_pairs={{0,1},{1,0},{2,3},{3,2},{4,5},{5,4},{6,7},{7,6},{8,9},{9,8},{10,11... | collective-permute-start | bytes 786440 | tf_op jit(solution)/shard_map/ppermute | solution.py:42
  45.0 8.5 %collective-permute-start.11 = (bf16[256,512]{1,0:T(8,128)(2,1)S(1)}, bf16[256,512]{1,0:T(8,128)(2,1)S(1)}, u32[]{:S(2)}, u32[]{:S(2)}) collective-permute-start(bf16[256,512]{1,0:T(8,128)(2,1)S(1)} %get-tuple-element.119), channel_id=1, source_target_pairs={{0,31},{1,2},{2,1},{3,4},{4,3},{5,6},{6,5},{7,8},{8,7},{9,10},{10,... | collective-permute-start | bytes 786440 | tf_op jit(solution)/shard_map/ppermute | solution.py:47
  45.0 8.5 %collective-permute-start.12 = (bf16[256,512]{1,0:T(8,128)(2,1)S(1)}, bf16[256,512]{1,0:T(8,128)(2,1)S(1)}, u32[]{:S(2)}, u32[]{:S(2)}) collective-permute-start(bf16[256,512]{1,0:T(8,128)(2,1)S(1)} %get-tuple-element.120), channel_id=1, source_target_pairs={{0,32},{32,0},{64,96},{96,64},{1,33},{33,1},{65,97},{97,65},{2,34}... | collective-permute-start | bytes 786440 | tf_op jit(solution)/shard_map/ppermute | solution.py:57
  48.3 5.2 %collective-permute-start.13 = (bf16[256,512]{1,0:T(8,128)(2,1)S(1)}, bf16[256,512]{1,0:T(8,128)(2,1)S(1)}, u32[]{:S(2)}, u32[]{:S(2)}) collective-permute-start(bf16[256,512]{1,0:T(8,128)(2,1)S(1)} %get-tuple-element.121), channel_id=1, source_target_pairs={{32,64},{64,32},{33,65},{65,33},{34,66},{66,34},{35,67},{67,35},{3... | collective-permute-start | bytes 786440 | tf_op jit(solution)/shard_map/ppermute | solution.py:57
  51.1 5.7 %collective-permute-start.14 = (bf16[384,512]{1,0:T(8,128)(2,1)S(1)}, bf16[384,512]{1,0:T(8,128)(2,1)S(1)}, u32[]{:S(2)}, u32[]{:S(2)}) collective-permute-start(bf16[384,512]{1,0:T(8,128)(2,1)S(1)} %get-tuple-element.129), channel_id=1, source_target_pairs={{0,1},{1,0},{2,3},{3,2},{4,5},{5,4},{6,7},{7,6},{8,9},{9,8},{10,11... | collective-permute-start | bytes 1179656 | tf_op jit(solution)/shard_map/ppermute | solution.py:42
  53.7 3.2 %collective-permute-start.15 = (bf16[192,512]{1,0:T(8,128)(2,1)S(1)}, bf16[192,512]{1,0:T(8,128)(2,1)S(1)}, u32[]{:S(2)}, u32[]{:S(2)}) collective-permute-start(bf16[192,512]{1,0:T(8,128)(2,1)S(1)} %get-tuple-element.131), channel_id=1, source_target_pairs={{0,1},{1,0},{2,3},{3,2},{4,5},{5,4},{6,7},{7,6},{8,9},{9,8},{10,11... | collective-permute-start | bytes 589832 | tf_op jit(solution)/shard_map/ppermute | solution.py:42
  55.9 5.1 %collective-permute-start.16 = (bf16[192,512]{1,0:T(8,128)(2,1)S(1)}, bf16[192,512]{1,0:T(8,128)(2,1)S(1)}, u32[]{:S(2)}, u32[]{:S(2)}) collective-permute-start(bf16[192,512]{1,0:T(8,128)(2,1)S(1)} %get-tuple-element.132), channel_id=1, source_target_pairs={{0,31},{1,2},{2,1},{3,4},{4,3},{5,6},{6,5},{7,8},{8,7},{9,10},{10,... | collective-permute-start | bytes 589832 | tf_op jit(solution)/shard_map/ppermute | solution.py:47
  61.0 6.6 %copy-start.2 = (bf16[512,227]{0,1:T(8,128)(2,1)S(1)}, bf16[512,227]{0,1:T(8,128)(2,1)}, u32[]{:S(2)}) copy-start(bf16[512,227]{0,1:T(8,128)(2,1)} %param.14) | copy-start | bytes 697348
  64.0 6.9 %collective-permute-start.18 = (bf16[768,512]{1,0:T(8,128)(2,1)S(1)}, bf16[768,512]{1,0:T(8,128)(2,1)S(1)}, u32[]{:S(2)}, u32[]{:S(2)}) collective-permute-start(bf16[768,512]{1,0:T(8,128)(2,1)S(1)} %get-tuple-element.146), channel_id=1, source_target_pairs={{0,1},{1,0},{2,3},{3,2},{4,5},{5,4},{6,7},{7,6},{8,9},{9,8},{10,11... | collective-permute-start | bytes 2359304 | tf_op jit(solution)/shard_map/ppermute | solution.py:42
  67.5 3.4 %collective-permute-start.17 = (bf16[512,512]{1,0:T(8,128)(2,1)S(1)}, bf16[512,512]{1,0:T(8,128)(2,1)S(1)}, u32[]{:S(2)}, u32[]{:S(2)}) collective-permute-start(bf16[512,512]{1,0:T(8,128)(2,1)S(1)} %get-tuple-element.140), channel_id=1, source_target_pairs={{0,1},{1,0},{2,3},{3,2},{4,5},{5,4},{6,7},{7,6},{8,9},{9,8},{10,11... | collective-permute-start | bytes 1572872 | tf_op jit(solution)/shard_map/ppermute | solution.py:42
  69.2 1.7 %collective-permute-start.19 = (bf16[128,512]{1,0:T(8,128)(2,1)S(1)}, bf16[128,512]{1,0:T(8,128)(2,1)S(1)}, u32[]{:S(2)}, u32[]{:S(2)}) collective-permute-start(bf16[128,512]{1,0:T(8,128)(2,1)S(1)} %get-tuple-element.155), channel_id=1, source_target_pairs={{0,1},{1,0},{2,3},{3,2},{4,5},{5,4},{6,7},{7,6},{8,9},{9,8},{10,11... | collective-permute-start | bytes 393224 | tf_op jit(solution)/shard_map/ppermute | solution.py:42
  99.2 5.9 %collective-permute-start.22 = (bf16[112,512]{1,0:T(8,128)(2,1)S(1)}, bf16[112,512]{1,0:T(8,128)(2,1)S(1)}, u32[]{:S(2)}, u32[]{:S(2)}) collective-permute-start(bf16[112,512]{1,0:T(8,128)(2,1)S(1)} %shard_map.217.refs_0_), channel_id=1, source_target_pairs={{0,96},{32,0},{64,32},{96,64},{1,97},{33,1},{65,33},{97,65},{2,98}... | collective-permute-start | bytes 344072 | tf_op jit(solution)/shard_map/ppermute | solution.py:540
  99.8 7.0 %collective-permute-start.21 = (bf16[112,512]{1,0:T(8,128)(2,1)S(1)}, bf16[112,512]{1,0:T(8,128)(2,1)S(1)}, u32[]{:S(2)}, u32[]{:S(2)}) collective-permute-start(bf16[112,512]{1,0:T(8,128)(2,1)S(1)} %shard_map.217.refs_0_), channel_id=1, source_target_pairs={{0,64},{32,96},{64,0},{96,32},{1,65},{33,97},{65,1},{97,33},{2,66}... | collective-permute-start | bytes 344072 | tf_op jit(solution)/shard_map/ppermute | solution.py:540
  104.6 5.8 %collective-permute-start.20 = (bf16[112,512]{1,0:T(8,128)(2,1)S(1)}, bf16[112,512]{1,0:T(8,128)(2,1)S(1)}, u32[]{:S(2)}, u32[]{:S(2)}) collective-permute-start(bf16[112,512]{1,0:T(8,128)(2,1)S(1)} %shard_map.217.refs_0_), channel_id=1, source_target_pairs={{0,32},{32,64},{64,96},{96,0},{1,33},{33,65},{65,97},{97,1},{2,34}... | collective-permute-start | bytes 344072 | tf_op jit(solution)/shard_map/ppermute | solution.py:540
  136.1 7.4 %collective-permute-start.23 = (bf16[1792,512]{1,0:T(8,128)(2,1)S(1)}, bf16[1792,512]{1,0:T(8,128)(2,1)S(1)}, u32[]{:S(2)}, u32[]{:S(2)}) collective-permute-start(bf16[1792,512]{1,0:T(8,128)(2,1)S(1)} %bitcast.14), channel_id=1, source_target_pairs={{0,1},{1,0},{2,3},{3,2},{4,5},{5,4},{6,7},{7,6},{8,9},{9,8},{10,11... | collective-permute-start | bytes 5505032 | tf_op jit(solution)/shard_map/ppermute | solution.py:42

commit v8 on v7

--- a/solution.py
+++ b/solution.py
@@ -133,7 +133,7 @@
         + [pltpu.SemaphoreType.DMA((len(args),))],
         compiler_params=pltpu.CompilerParams(vmem_limit_bytes=limit * MIB),
         cost_estimate=pl.CostEstimate(flops=2 * macs, bytes_accessed=moved, transcendentals=0),
-    )(*args)
+    )(*[pltpu.with_memory_space_constraint(a, pltpu.HBM) for a in args])
 
 
 def parcels(*refs):
@@ -577,7 +577,7 @@
     grid_full = shape(grid_count, width, SINGLE)
     parcel = shape(variables + -variables % 16 + INDEX_ROWS // 2, grid_count, HALF)
     sent = fetching(
-        parcels, [parcel] * (GROUPS - 1), 0, grid, grid_send, mesh_send, near, limit=58
+        parcels, [parcel] * (GROUPS - 1), 0, grid, grid_send, mesh_send, near, limit=32
     )
     arrived = swap_all(*sent)
     embed_macs = grid_count * variables * width + mesh_count * grid_count * (step + width)

time: 146 us -> 143 us (0.979)
  local copies, waits for them, and re-layouts: 3.39 us -> 0.08 us
  starting transfers between devices: 41.4 us -> 43.4 us
  waiting for transfers between devices: 17.4 us -> 15.6 us
    unnamed x34 -> x26, local copies, waits for them, and re-layouts: 3.39 us -> 0.08 us
where the time goes in v8:
time: 143 us
  blocking collectives  54 us (38%)
  starting transfers between devices  43.4 us (30%)
  Pallas kernels  26.9 us (19%)
  waiting for transfers between devices  15.6 us (11%)
    all_to_all x1, blocking collectives, reduce_all(): lax.all_to_all(part.reshape(chips, rows, width), 'dom', 0, 0, axis_index_...  28.5 us
    all_to_all x1, blocking collectives, reduce_all(): lax.all_to_all(copies, 'dom', 0, 0, axis_index_groups=groups)  25.5 us
    ppermute x10, starting transfers between devices, swap_on(): return lax.ppermute(value, 'dom', [(i, i ^ 1) for i in range(count)])  24.8 us
    pallas_call x20, Pallas kernels, whole(): pl.pallas_call(body, out_shape=outs, scratch_shapes=scratch, compiler_par...  19.9 us
    ppermute x6, starting transfers between devices, swap_band(): return lax.ppermute(value, 'band', pairs)  10.7 us
    ppermute x5, waiting for transfers between devices, swap_off(): lax.ppermute(value, 'dom', [(i, (i + (1 if i % 2 else -1)) % count) for i...  6.2 us
    ppermute x3, starting transfers between devices, reduce_all(): lax.ppermute(piece, 'band', [(i, (i + step) % bands) for i in range(bands)])  6.08 us
    ppermute x3, waiting for transfers between devices, reduce_all(): lax.ppermute(piece, 'band', [(i, (i + step) % bands) for i in range(bands)])  5.15 us
  transfers between devices with their start and end apart: 24, of which 9 were waited for; matrix products, arithmetic and copies ran while one was open for 1% of the time, Pallas kernels for 10%

profile of v8, /device:TPU:1, one launch (start us, length us, event | category | flops | bytes accessed | tf_op | source)
XLA Modules:
  0.0 143.1 jit_solution(3942258070718344236)
XLA Ops:
  0.6 0.0 copy-start
  0.6 0.0 copy-start.12
  0.7 1.1 shard_map.197
  1.8 1.5 %collective-permute-start.3 = (bf16[256,512]{1,0:T(8,128)(2,1)S(1)}, bf16[256,512]{1,0:T(8,128)(2,1)S(1)}, u32[]{:S(2)}, u32[]{:S(2)}) collective-permute-start(bf16[256,512]{1,0:T(8,128)(2,1)S(1)} %get-tuple-element.91), channel_id=1, source_target_pairs={{0,1},{1,0},{2,3},{3,2},{4,5},{5,4},{6,7},{7,6},{8,9},{9,8},{10,11... | collective-permute-start | bytes 786440 | tf_op jit(solution)/shard_map/ppermute | solution.py:42
  3.3 1.3 collective-permute-start.2
  4.6 1.9 %collective-permute-start.1 = (bf16[256,512]{1,0:T(8,128)(2,1)S(1)}, bf16[256,512]{1,0:T(8,128)(2,1)S(1)}, u32[]{:S(2)}, u32[]{:S(2)}) collective-permute-start(bf16[256,512]{1,0:T(8,128)(2,1)S(1)} %get-tuple-element.89), channel_id=1, source_target_pairs={{0,31},{1,2},{2,1},{3,4},{4,3},{5,6},{6,5},{7,8},{8,7},{9,10},{10,... | collective-permute-start | bytes 786440 | tf_op jit(solution)/shard_map/ppermute | solution.py:47
  6.5 0.7 collective-permute-start
  7.1 2.1 %shard_map.198 = (f32[512,512]{1,0:T(8,128)S(1)}, f32[256,512]{1,0:T(8,128)S(1)}, bf16[227,512]{1,0:T(8,128)(2,1)S(1)}) custom-call(bf16[227,512]{1,0:T(8,128)(2,1)} %bitcast.19, bf16[227,512]{1,0:T(8,128)(2,1)} %refs_1_.1, s32[30,128]{1,0:T(8,128)} %bitcast.26, s32[30,128]{1,0:T(8,128)} %bitcast.32), custom_call_target="tpu_custom_call" | custom-call | flops 454557696 | bytes 2300928 | tf_op jit(solution)/shard_map/pallas_call | solution.py:128
  9.2 0.9 shard_map.199
  10.2 1.0 collective-permute-done.2.refs_0_.refs_10_
  11.1 0.9 shard_map.200
  12.1 0.0 copy-start.5
  12.1 0.9 shard_map.201
  13.1 1.0 shard_map.202
  14.1 0.4 shard_map.203
  14.5 3.9 %collective-permute-start.4 = (bf16[128,512]{1,0:T(8,128)(2,1)S(1)}, bf16[128,512]{1,0:T(8,128)(2,1)S(1)}, u32[]{:S(2)}, u32[]{:S(2)}) collective-permute-start(bf16[128,512]{1,0:T(8,128)(2,1)S(1)} %get-tuple-element.104), channel_id=1, source_target_pairs={{0,1},{1,0},{2,3},{3,2},{4,5},{5,4},{6,7},{7,6},{8,9},{9,8},{10,11... | collective-permute-start | bytes 393224 | tf_op jit(solution)/shard_map/ppermute | solution.py:42
  18.4 0.0 copy-start.9
  18.4 1.4 shard_map.204.refs_5_
  19.9 0.7 shard_map.205
  20.6 2.2 %collective-permute-done.5.off_ref = bf16[128,512]{1,0:T(8,128)(2,1)S(1)} collective-permute-done((bf16[128,512]{1,0:T(8,128)(2,1)S(1)}, bf16[128,512]{1,0:T(8,128)(2,1)S(1)}, u32[]{:S(2)}, u32[]{:S(2)}) %collective-permute-start.5) | collective-permute-done | bytes 131104 | tf_op jit(solution)/shard_map/ppermute | solution.py:47
  22.8 1.5 %shard_map.206 = (bf16[256,512]{1,0:T(8,128)(2,1)S(1)}, f32[384,512]{1,0:T(8,128)S(1)}, f32[256,512]{1,0:T(8,128)S(1)}, bf16[256,512]{1,0:T(8,128)(2,1)S(1)}, bf...) custom-call(bf16[256,512]{1,0:T(8,128)(2,1)S(1)} %get-tuple-element.97.half_ref.refs_0_, ...), custom_call_target="tpu_custom_call" | custom-call | flops 1207959552 | bytes 6029312 | tf_op jit(solution)/shard_map/pallas_call | solution.py:81
  24.3 3.5 %collective-permute-start.9 = (bf16[256,512]{1,0:T(8,128)(2,1)S(1)}, bf16[256,512]{1,0:T(8,128)(2,1)S(1)}, u32[]{:S(2)}, u32[]{:S(2)}) collective-permute-start(bf16[256,512]{1,0:T(8,128)(2,1)S(1)} %get-tuple-element.107.refs_0_), channel_id=1, source_target_pairs={{0,1},{1,0},{2,3},{3,2},{4,5},{5,4},{6,7},{7,6},{8,9},{9,8},{10,11... | collective-permute-start | bytes 786440 | tf_op jit(solution)/shard_map/ppermute | solution.py:42
  27.8 3.6 %collective-permute-start.7 = (bf16[256,512]{1,0:T(8,128)(2,1)S(1)}, bf16[256,512]{1,0:T(8,128)(2,1)S(1)}, u32[]{:S(2)}, u32[]{:S(2)}) collective-permute-start(bf16[256,512]{1,0:T(8,128)(2,1)S(1)} %get-tuple-element.107.refs_0_), channel_id=1, source_target_pairs={{0,32},{32,0},{64,96},{96,64},{1,33},{33,1},{65,97},{97,65},{2,34}... | collective-permute-start | bytes 786440 | tf_op jit(solution)/shard_map/ppermute | solution.py:57
  31.4 0.8 collective-permute-start.6
  32.3 0.3 fusion.1.refs_8_
  32.6 0.0 copy-start.10
  32.6 1.2 shard_map.207.refs_6_
  33.9 1.6 %collective-permute-done.7.refs_2_ = bf16[256,512]{1,0:T(8,128)(2,1)S(1)} collective-permute-done((bf16[256,512]{1,0:T(8,128)(2,1)S(1)}, bf16[256,512]{1,0:T(8,128)(2,1)S(1)}, u32[]{:S(2)}, u32[]{:S(2)}) %collective-permute-start.7) | collective-permute-done | bytes 262176 | tf_op jit(solution)/shard_map/ppermute | solution.py:57
  35.5 2.3 %shard_map.208 = (bf16[512,512]{1,0:T(8,128)(2,1)S(1)}, bf16[512,512]{1,0:T(8,128)(2,1)S(1)}, bf16[512,512]{1,0:T(8,128)(2,1)S(1)}, f32[256,512]{1,0:T(8,128)S(1...) custom-call(bf16[256,512]{1,0:T(8,128)(2,1)S(1)} %get-tuple-element., ...), custom_call_target="tpu_custom_call" | custom-call | flops 1879048192 | bytes 8650752 | tf_op jit(solution)/shard_map/pallas_call | solution.py:81
  37.8 3.3 %collective-permute-start.10 = (bf16[256,512]{1,0:T(8,128)(2,1)S(1)}, bf16[256,512]{1,0:T(8,128)(2,1)S(1)}, u32[]{:S(2)}, u32[]{:S(2)}) collective-permute-start(bf16[256,512]{1,0:T(8,128)(2,1)S(1)} %get-tuple-element.118), channel_id=1, source_target_pairs={{0,1},{1,0},{2,3},{3,2},{4,5},{5,4},{6,7},{7,6},{8,9},{9,8},{10,11... | collective-permute-start | bytes 786440 | tf_op jit(solution)/shard_map/ppermute | solution.py:42
  41.1 3.6 %collective-permute-start.12 = (bf16[256,512]{1,0:T(8,128)(2,1)S(1)}, bf16[256,512]{1,0:T(8,128)(2,1)S(1)}, u32[]{:S(2)}, u32[]{:S(2)}) collective-permute-start(bf16[256,512]{1,0:T(8,128)(2,1)S(1)} %get-tuple-element.120), channel_id=1, source_target_pairs={{0,32},{32,0},{64,96},{96,64},{1,33},{33,1},{65,97},{97,65},{2,34}... | collective-permute-start | bytes 786440 | tf_op jit(solution)/shard_map/ppermute | solution.py:57
  44.7 0.7 collective-permute-start.13
  45.4 1.4 shard_map.209.refs_1_
  46.8 0.7 shard_map.210
  47.5 3.0 %collective-permute-start.14 = (bf16[384,512]{1,0:T(8,128)(2,1)S(1)}, bf16[384,512]{1,0:T(8,128)(2,1)S(1)}, u32[]{:S(2)}, u32[]{:S(2)}) collective-permute-start(bf16[384,512]{1,0:T(8,128)(2,1)S(1)} %get-tuple-element.129), channel_id=1, source_target_pairs={{0,1},{1,0},{2,3},{3,2},{4,5},{5,4},{6,7},{7,6},{8,9},{9,8},{10,11... | collective-permute-start | bytes 1179656 | tf_op jit(solution)/shard_map/ppermute | solution.py:42
  50.5 0.2 add_multiply_fusion.1.refs_5_
  50.8 0.2 shard_map.211
  51.0 1.3 collective-permute-start.15
  52.3 0.3 add_multiply_fusion.slope_0_ref
  52.6 0.6 shard_map.212
  53.2 0.1 collective-permute-done.15.on_ref
  53.4 4.0 %collective-permute-done.16.off_ref = bf16[192,512]{1,0:T(8,128)(2,1)S(1)} collective-permute-done((bf16[192,512]{1,0:T(8,128)(2,1)S(1)}, bf16[192,512]{1,0:T(8,128)(2,1)S(1)}, u32[]{:S(2)}, u32[]{:S(2)}) %collective-permute-start.16) | collective-permute-done | bytes 196640 | tf_op jit(solution)/shard_map/ppermute | solution.py:47
  57.4 2.2 %shard_map.213 = (f32[256,512]{1,0:T(8,128)}, bf16[256,512]{1,0:T(8,128)(2,1)S(1)}, bf16[256,512]{1,0:T(8,128)(2,1)S(1)}, bf16[256,512]{1,0:T(8,128)(2,1)S(1)}) custom-call(f32[256,512]{1,0:T(8,128)S(1)} %get-tuple-element.130.state_ref, bf16[256,512]{1,0:T(8,128)(2,1)S(1)} %get-tuple-element.125.refs_1_.refs_3_.layer_ref, ...), custom_call_target="tpu_custom_call" | custom-call | flops 1207959552 | bytes 6946816 | tf_op jit(solution)/shard_map/pallas_call | solution.py:81
  59.6 0.9 shard_map.214
  60.5 3.5 %collective-permute-start.18 = (bf16[768,512]{1,0:T(8,128)(2,1)S(1)}, bf16[768,512]{1,0:T(8,128)(2,1)S(1)}, u32[]{:S(2)}, u32[]{:S(2)}) collective-permute-start(bf16[768,512]{1,0:T(8,128)(2,1)S(1)} %get-tuple-element.146), channel_id=1, source_target_pairs={{0,1},{1,0},{2,3},{3,2},{4,5},{5,4},{6,7},{7,6},{8,9},{9,8},{10,11... | collective-permute-start | bytes 2359304 | tf_op jit(solution)/shard_map/ppermute | solution.py:42
  64.0 0.1 collective-permute-start.17
  64.0 1.6 %shard_map.215 = (bf16[128,512]{1,0:T(8,128)(2,1)S(1)}, bf16[128,512]{1,0:T(8,128)(2,1)S(1)}) custom-call(bf16[256,512]{1,0:T(8,128)(2,1)S(1)} %get-tuple-element.147.refs_0_, bf16[512,1280]{1,0:T(8,128)(2,1)S(1)} %shard_map.209.refs_1_, f32[512,512]{1,0:T(8,128)S(1)} %get-tuple-element.149.refs_2_, f32[512,512]{1,0:T(8,128)S(1)} %get-tuple-element.150.refs_3_, ...), custom_call_target="tpu_custom_call" | custom-call | flops 1266155520 | bytes 8358912 | tf_op jit(solution)/shard_map/pallas_call | solution.py:81
  65.6 0.7 collective-permute-start.19
  66.3 1.0 collective-permute-done.19.refs_7_
  67.3 0.4 shard_map.216
  67.8 28.5 %all_to_all.10.pieces_ref = bf16[16,112,512]{2,1,0:T(8,128)(2,1)S(1)} all-to-all(bf16[16,112,512]{2,1,0:T(8,128)(2,1)S(1)} %bitcast.17), channel_id=1, replica_groups={{0,2,4,6,8,10,12,14,16,18,20,22,24,26,28,30},{1,3,5,7,9,11,13,15,17,19,..., dimensions={0} | all-to-all | bytes 3670016 | tf_op jit(solution)/shard_map/all_to_all | solution.py:535
  96.2 0.2 shard_map.217.refs_0_
  96.5 1.9 %collective-permute-start.22 = (bf16[112,512]{1,0:T(8,128)(2,1)S(1)}, bf16[112,512]{1,0:T(8,128)(2,1)S(1)}, u32[]{:S(2)}, u32[]{:S(2)}) collective-permute-start(bf16[112,512]{1,0:T(8,128)(2,1)S(1)} %shard_map.217.refs_0_), channel_id=1, source_target_pairs={{0,96},{32,0},{64,32},{96,64},{1,97},{33,1},{65,33},{97,65},{2,98}... | collective-permute-start | bytes 344072 | tf_op jit(solution)/shard_map/ppermute | solution.py:540
  98.3 3.6 %collective-permute-start.21 = (bf16[112,512]{1,0:T(8,128)(2,1)S(1)}, bf16[112,512]{1,0:T(8,128)(2,1)S(1)}, u32[]{:S(2)}, u32[]{:S(2)}) collective-permute-start(bf16[112,512]{1,0:T(8,128)(2,1)S(1)} %shard_map.217.refs_0_), channel_id=1, source_target_pairs={{0,64},{32,96},{64,0},{96,32},{1,65},{33,97},{65,1},{97,33},{2,66}... | collective-permute-start | bytes 344072 | tf_op jit(solution)/shard_map/ppermute | solution.py:540
  101.9 0.6 collective-permute-start.20
  102.5 1.6 %collective-permute-done.21.refs_2_ = bf16[112,512]{1,0:T(8,128)(2,1)S(1)} collective-permute-done((bf16[112,512]{1,0:T(8,128)(2,1)S(1)}, bf16[112,512]{1,0:T(8,128)(2,1)S(1)}, u32[]{:S(2)}, u32[]{:S(2)}) %collective-permute-start.21) | collective-permute-done | bytes 114720 | tf_op jit(solution)/shard_map/ppermute | solution.py:540
  104.1 3.6 %collective-permute-done.20.refs_1_ = bf16[112,512]{1,0:T(8,128)(2,1)S(1)} collective-permute-done((bf16[112,512]{1,0:T(8,128)(2,1)S(1)}, bf16[112,512]{1,0:T(8,128)(2,1)S(1)}, u32[]{:S(2)}, u32[]{:S(2)}) %collective-permute-start.20) | collective-permute-done | bytes 114720 | tf_op jit(solution)/shard_map/ppermute | solution.py:540
  107.7 0.2 shard_map.218
  107.9 25.5 %all_to_all.11 = bf16[16,112,512]{2,1,0:T(8,128)(2,1)S(1)} all-to-all(bf16[16,112,512]{2,1,0:T(8,128)(2,1)S(1)} %shard_map.218), channel_id=1, replica_groups={{0,2,4,6,8,10,12,14,16,18,20,22,24,26,28,30},{1,3,5,7,9,11,13,15,17,19,..., dimensions={0} | all-to-all | bytes 3670016 | tf_op jit(solution)/shard_map/all_to_all | solution.py:545
  133.4 4.0 %collective-permute-start.23 = (bf16[1792,512]{1,0:T(8,128)(2,1)S(1)}, bf16[1792,512]{1,0:T(8,128)(2,1)S(1)}, u32[]{:S(2)}, u32[]{:S(2)}) collective-permute-start(bf16[1792,512]{1,0:T(8,128)(2,1)S(1)} %bitcast.14), channel_id=1, source_target_pairs={{0,1},{1,0},{2,3},{3,2},{4,5},{5,4},{6,7},{7,6},{8,9},{9,8},{10,11... | collective-permute-start | bytes 5505032 | tf_op jit(solution)/shard_map/ppermute | solution.py:42
  137.4 1.0 fusion
  138.4 1.8 %shard_map.219 = (f32[512,512]{1,0:T(8,128)}, f32[2,512,512]{2,1,0:T(8,128)}, f32[2,512,512]{2,1,0:T(8,128)}, f32[512,512]{1,0:T(8,128)}) custom-call(bf16[1792,512]{1,0:T(8,128)(2,1)S(1)} %bitcast.15), custom_call_target="tpu_custom_call" | custom-call | bytes 5505024 | tf_op jit(solution)/shard_map/pallas_call | solution.py:508
  140.2 0.6 collective-permute-done.23.other_ref
  140.8 2.1 %shard_map.220 = (f32[512,512]{1,0:T(8,128)}, f32[2,512,512]{2,1,0:T(8,128)}, f32[2,512,512]{2,1,0:T(8,128)}, f32[512,512]{1,0:T(8,128)}, f32[227,512]{1,0:T(8,128)}, /*index=5*/f32[227,512]{1,0:T(8,128)}) custom-call(bf16[1792,512]{1,0:T(8,128)(2,1)S(1)} %bitcast.16, ...), custom_call_target="tpu_custom_call", output_to_operand_aliasing={{0}: (2, {}), {1}: (3, {}), {2}: (4, {}), {3}: (5, {})} | custom-call | bytes 5505024 | tf_op jit(solution)/shard_map/pallas_call | solution.py:517
  (40 shorter events, 0.1 us)
Async XLA Ops:
  0.6 31.7 %copy-start = (bf16[512,227]{0,1:T(8,128)(2,1)S(1)}, bf16[512,227]{0,1:T(8,128)(2,1)}, u32[]{:S(2)}) copy-start(bf16[512,227]{0,1:T(8,128)(2,1)} %param.22) | copy-start | bytes 697348
  0.6 8.6 %copy-start.12 = (s32[3840]{0:T(1024)S(1)}, s32[3840]{0:T(1024)}, u32[]{:S(2)}) copy-start(s32[3840]{0:T(1024)} %param.24) | copy-start | bytes 46084
  1.8 7.4 %collective-permute-start.3 = (bf16[256,512]{1,0:T(8,128)(2,1)S(1)}, bf16[256,512]{1,0:T(8,128)(2,1)S(1)}, u32[]{:S(2)}, u32[]{:S(2)}) collective-permute-start(bf16[256,512]{1,0:T(8,128)(2,1)S(1)} %get-tuple-element.91), channel_id=1, source_target_pairs={{0,1},{1,0},{2,3},{3,2},{4,5},{5,4},{6,7},{7,6},{8,9},{9,8},{10,11... | collective-permute-start | bytes 786440 | tf_op jit(solution)/shard_map/ppermute | solution.py:42
  3.3 7.9 %collective-permute-start.2 = (bf16[256,512]{1,0:T(8,128)(2,1)S(1)}, bf16[256,512]{1,0:T(8,128)(2,1)S(1)}, u32[]{:S(2)}, u32[]{:S(2)}) collective-permute-start(bf16[256,512]{1,0:T(8,128)(2,1)S(1)} %get-tuple-element.90), channel_id=1, source_target_pairs={{0,32},{32,0},{64,96},{96,64},{1,33},{33,1},{65,97},{97,65},{2,34}... | collective-permute-start | bytes 786440 | tf_op jit(solution)/shard_map/ppermute | solution.py:57
  4.6 7.5 %collective-permute-start.1 = (bf16[256,512]{1,0:T(8,128)(2,1)S(1)}, bf16[256,512]{1,0:T(8,128)(2,1)S(1)}, u32[]{:S(2)}, u32[]{:S(2)}) collective-permute-start(bf16[256,512]{1,0:T(8,128)(2,1)S(1)} %get-tuple-element.89), channel_id=1, source_target_pairs={{0,31},{1,2},{2,1},{3,4},{4,3},{5,6},{6,5},{7,8},{8,7},{9,10},{10,... | collective-permute-start | bytes 786440 | tf_op jit(solution)/shard_map/ppermute | solution.py:47
  6.5 6.6 %collective-permute-start = (bf16[256,512]{1,0:T(8,128)(2,1)S(1)}, bf16[256,512]{1,0:T(8,128)(2,1)S(1)}, u32[]{:S(2)}, u32[]{:S(2)}) collective-permute-start(bf16[256,512]{1,0:T(8,128)(2,1)S(1)} %get-tuple-element.87), channel_id=1, source_target_pairs={{32,64},{64,32},{33,65},{65,33},{34,66},{66,34},{35,67},{67,35},{3... | collective-permute-start | bytes 786440 | tf_op jit(solution)/shard_map/ppermute | solution.py:57
  12.1 2.0 %copy-start.2 = (bf16[512,512]{1,0:T(8,128)(2,1)S(1)}, bf16[512,512]{1,0:T(8,128)(2,1)}, u32[]{:S(2)}) copy-start(bf16[512,512]{1,0:T(8,128)(2,1)} %encode_ref.1) | copy-start | bytes 1572868
  12.1 2.0 %copy-start.5 = (bf16[256,512]{1,0:T(8,128)(2,1)S(1)}, bf16[256,512]{1,0:T(8,128)(2,1)}, u32[]{:S(2)}) copy-start(bf16[256,512]{1,0:T(8,128)(2,1)} %static_ref.1) | copy-start | bytes 786436
  13.1 5.3 %copy-start.7 = (s32[3840]{0:T(1024)S(1)}, s32[3840]{0:T(1024)}, u32[]{:S(2)}) copy-start(s32[3840]{0:T(1024)} %param.26) | copy-start | bytes 46084
  13.1 5.3 %copy-start.11 = (s32[3840]{0:T(1024)S(1)}, s32[3840]{0:T(1024)}, u32[]{:S(2)}) copy-start(s32[3840]{0:T(1024)} %param.27) | copy-start | bytes 46084
  14.5 6.1 %collective-permute-start.4 = (bf16[128,512]{1,0:T(8,128)(2,1)S(1)}, bf16[128,512]{1,0:T(8,128)(2,1)S(1)}, u32[]{:S(2)}, u32[]{:S(2)}) collective-permute-start(bf16[128,512]{1,0:T(8,128)(2,1)S(1)} %get-tuple-element.104), channel_id=1, source_target_pairs={{0,1},{1,0},{2,3},{3,2},{4,5},{5,4},{6,7},{7,6},{8,9},{9,8},{10,11... | collective-permute-start | bytes 393224 | tf_op jit(solution)/shard_map/ppermute | solution.py:42
  18.4 4.4 %collective-permute-start.5 = (bf16[128,512]{1,0:T(8,128)(2,1)S(1)}, bf16[128,512]{1,0:T(8,128)(2,1)S(1)}, u32[]{:S(2)}, u32[]{:S(2)}) collective-permute-start(bf16[128,512]{1,0:T(8,128)(2,1)S(1)} %get-tuple-element.105), channel_id=1, source_target_pairs={{0,31},{1,2},{2,1},{3,4},{4,3},{5,6},{6,5},{7,8},{8,7},{9,10},{10,... | collective-permute-start | bytes 393224 | tf_op jit(solution)/shard_map/ppermute | solution.py:47
  18.4 1.5 %copy-start.9 = (s32[256,6]{0,1:T(8,128)S(1)}, s32[256,6]{0,1:T(8,128)}, u32[]{:S(2)}) copy-start(s32[256,6]{0,1:T(8,128)} %param.25) | copy-start | bytes 18436
  18.4 4.4 %copy-start.3 = (bf16[2,512,512]{2,1,0:T(8,128)(2,1)S(1)}, bf16[2,512,512]{2,1,0:T(8,128)(2,1)}, u32[]{:S(2)}) copy-start(bf16[2,512,512]{2,1,0:T(8,128)(2,1)} %self_ref.3) | copy-start | bytes 3145732
  18.4 4.4 %copy-start.4 = (bf16[2,512,512]{2,1,0:T(8,128)(2,1)S(1)}, bf16[2,512,512]{2,1,0:T(8,128)(2,1)}, u32[]{:S(2)}) copy-start(bf16[2,512,512]{2,1,0:T(8,128)(2,1)} %near_ref.3) | copy-start | bytes 3145732
  22.8 9.5 %copy-start.6 = (bf16[512,227]{0,1:T(8,128)(2,1)S(1)}, bf16[512,227]{0,1:T(8,128)(2,1)}, u32[]{:S(2)}) copy-start(bf16[512,227]{0,1:T(8,128)(2,1)} %param.15) | copy-start | bytes 697348
  24.3 9.6 %collective-permute-start.9 = (bf16[256,512]{1,0:T(8,128)(2,1)S(1)}, bf16[256,512]{1,0:T(8,128)(2,1)S(1)}, u32[]{:S(2)}, u32[]{:S(2)}) collective-permute-start(bf16[256,512]{1,0:T(8,128)(2,1)S(1)} %get-tuple-element.107.refs_0_), channel_id=1, source_target_pairs={{0,1},{1,0},{2,3},{3,2},{4,5},{5,4},{6,7},{7,6},{8,9},{9,8},{10,11... | collective-permute-start | bytes 786440 | tf_op jit(solution)/shard_map/ppermute | solution.py:42
  27.8 6.1 %collective-permute-start.8 = (bf16[256,512]{1,0:T(8,128)(2,1)S(1)}, bf16[256,512]{1,0:T(8,128)(2,1)S(1)}, u32[]{:S(2)}, u32[]{:S(2)}) collective-permute-start(bf16[256,512]{1,0:T(8,128)(2,1)S(1)} %get-tuple-element.107.refs_0_), channel_id=1, source_target_pairs={{0,31},{1,2},{2,1},{3,4},{4,3},{5,6},{6,5},{7,8},{8,7},{9,10},{10,... | collective-permute-start | bytes 786440 | tf_op jit(solution)/shard_map/ppermute | solution.py:47
  27.8 7.7 %collective-permute-start.7 = (bf16[256,512]{1,0:T(8,128)(2,1)S(1)}, bf16[256,512]{1,0:T(8,128)(2,1)S(1)}, u32[]{:S(2)}, u32[]{:S(2)}) collective-permute-start(bf16[256,512]{1,0:T(8,128)(2,1)S(1)} %get-tuple-element.107.refs_0_), channel_id=1, source_target_pairs={{0,32},{32,0},{64,96},{96,64},{1,33},{33,1},{65,97},{97,65},{2,34}... | collective-permute-start | bytes 786440 | tf_op jit(solution)/shard_map/ppermute | solution.py:57
  31.4 4.1 %collective-permute-start.6 = (bf16[256,512]{1,0:T(8,128)(2,1)S(1)}, bf16[256,512]{1,0:T(8,128)(2,1)S(1)}, u32[]{:S(2)}, u32[]{:S(2)}) collective-permute-start(bf16[256,512]{1,0:T(8,128)(2,1)S(1)} %get-tuple-element.107.refs_0_), channel_id=1, source_target_pairs={{32,64},{64,32},{33,65},{65,33},{34,66},{66,34},{35,67},{67,35},{3... | collective-permute-start | bytes 786440 | tf_op jit(solution)/shard_map/ppermute | solution.py:57
  32.6 2.8 %copy-start.10 = (bf16[512,512]{1,0:T(8,128)(2,1)S(1)}, bf16[512,512]{1,0:T(8,128)(2,1)}, u32[]{:S(2)}) copy-start(bf16[512,512]{1,0:T(8,128)(2,1)} %refs_7_.1) | copy-start | bytes 1572868
  33.9 11.5 %copy-start.8 = (s32[3840]{0:T(1024)S(1)}, s32[3840]{0:T(1024)}, u32[]{:S(2)}) copy-start(s32[3840]{0:T(1024)} %param.23) | copy-start | bytes 46084
  37.8 12.9 %collective-permute-start.10 = (bf16[256,512]{1,0:T(8,128)(2,1)S(1)}, bf16[256,512]{1,0:T(8,128)(2,1)S(1)}, u32[]{:S(2)}, u32[]{:S(2)}) collective-permute-start(bf16[256,512]{1,0:T(8,128)(2,1)S(1)} %get-tuple-element.118), channel_id=1, source_target_pairs={{0,1},{1,0},{2,3},{3,2},{4,5},{5,4},{6,7},{7,6},{8,9},{9,8},{10,11... | collective-permute-start | bytes 786440 | tf_op jit(solution)/shard_map/ppermute | solution.py:42
  41.1 9.6 %collective-permute-start.11 = (bf16[256,512]{1,0:T(8,128)(2,1)S(1)}, bf16[256,512]{1,0:T(8,128)(2,1)S(1)}, u32[]{:S(2)}, u32[]{:S(2)}) collective-permute-start(bf16[256,512]{1,0:T(8,128)(2,1)S(1)} %get-tuple-element.119), channel_id=1, source_target_pairs={{0,31},{1,2},{2,1},{3,4},{4,3},{5,6},{6,5},{7,8},{8,7},{9,10},{10,... | collective-permute-start | bytes 786440 | tf_op jit(solution)/shard_map/ppermute | solution.py:47
  41.1 9.6 %collective-permute-start.12 = (bf16[256,512]{1,0:T(8,128)(2,1)S(1)}, bf16[256,512]{1,0:T(8,128)(2,1)S(1)}, u32[]{:S(2)}, u32[]{:S(2)}) collective-permute-start(bf16[256,512]{1,0:T(8,128)(2,1)S(1)} %get-tuple-element.120), channel_id=1, source_target_pairs={{0,32},{32,0},{64,96},{96,64},{1,33},{33,1},{65,97},{97,65},{2,34}... | collective-permute-start | bytes 786440 | tf_op jit(solution)/shard_map/ppermute | solution.py:57
  44.7 6.0 %collective-permute-start.13 = (bf16[256,512]{1,0:T(8,128)(2,1)S(1)}, bf16[256,512]{1,0:T(8,128)(2,1)S(1)}, u32[]{:S(2)}, u32[]{:S(2)}) collective-permute-start(bf16[256,512]{1,0:T(8,128)(2,1)S(1)} %get-tuple-element.121), channel_id=1, source_target_pairs={{32,64},{64,32},{33,65},{65,33},{34,66},{66,34},{35,67},{67,35},{3... | collective-permute-start | bytes 786440 | tf_op jit(solution)/shard_map/ppermute | solution.py:57
  47.5 5.7 %collective-permute-start.14 = (bf16[384,512]{1,0:T(8,128)(2,1)S(1)}, bf16[384,512]{1,0:T(8,128)(2,1)S(1)}, u32[]{:S(2)}, u32[]{:S(2)}) collective-permute-start(bf16[384,512]{1,0:T(8,128)(2,1)S(1)} %get-tuple-element.129), channel_id=1, source_target_pairs={{0,1},{1,0},{2,3},{3,2},{4,5},{5,4},{6,7},{7,6},{8,9},{9,8},{10,11... | collective-permute-start | bytes 1179656 | tf_op jit(solution)/shard_map/ppermute | solution.py:42
  51.0 2.4 %collective-permute-start.15 = (bf16[192,512]{1,0:T(8,128)(2,1)S(1)}, bf16[192,512]{1,0:T(8,128)(2,1)S(1)}, u32[]{:S(2)}, u32[]{:S(2)}) collective-permute-start(bf16[192,512]{1,0:T(8,128)(2,1)S(1)} %get-tuple-element.131), channel_id=1, source_target_pairs={{0,1},{1,0},{2,3},{3,2},{4,5},{5,4},{6,7},{7,6},{8,9},{9,8},{10,11... | collective-permute-start | bytes 589832 | tf_op jit(solution)/shard_map/ppermute | solution.py:42
  52.3 5.1 %collective-permute-start.16 = (bf16[192,512]{1,0:T(8,128)(2,1)S(1)}, bf16[192,512]{1,0:T(8,128)(2,1)S(1)}, u32[]{:S(2)}, u32[]{:S(2)}) collective-permute-start(bf16[192,512]{1,0:T(8,128)(2,1)S(1)} %get-tuple-element.132), channel_id=1, source_target_pairs={{0,31},{1,2},{2,1},{3,4},{4,3},{5,6},{6,5},{7,8},{8,7},{9,10},{10,... | collective-permute-start | bytes 589832 | tf_op jit(solution)/shard_map/ppermute | solution.py:47
  57.4 6.6 %copy-start.1 = (bf16[512,227]{0,1:T(8,128)(2,1)S(1)}, bf16[512,227]{0,1:T(8,128)(2,1)}, u32[]{:S(2)}) copy-start(bf16[512,227]{0,1:T(8,128)(2,1)} %param.14) | copy-start | bytes 697348
  60.5 6.9 %collective-permute-start.18 = (bf16[768,512]{1,0:T(8,128)(2,1)S(1)}, bf16[768,512]{1,0:T(8,128)(2,1)S(1)}, u32[]{:S(2)}, u32[]{:S(2)}) collective-permute-start(bf16[768,512]{1,0:T(8,128)(2,1)S(1)} %get-tuple-element.146), channel_id=1, source_target_pairs={{0,1},{1,0},{2,3},{3,2},{4,5},{5,4},{6,7},{7,6},{8,9},{9,8},{10,11... | collective-permute-start | bytes 2359304 | tf_op jit(solution)/shard_map/ppermute | solution.py:42
  64.0 3.4 %collective-permute-start.17 = (bf16[512,512]{1,0:T(8,128)(2,1)S(1)}, bf16[512,512]{1,0:T(8,128)(2,1)S(1)}, u32[]{:S(2)}, u32[]{:S(2)}) collective-permute-start(bf16[512,512]{1,0:T(8,128)(2,1)S(1)} %get-tuple-element.140), channel_id=1, source_target_pairs={{0,1},{1,0},{2,3},{3,2},{4,5},{5,4},{6,7},{7,6},{8,9},{9,8},{10,11... | collective-permute-start | bytes 1572872 | tf_op jit(solution)/shard_map/ppermute | solution.py:42
  65.6 1.7 %collective-permute-start.19 = (bf16[128,512]{1,0:T(8,128)(2,1)S(1)}, bf16[128,512]{1,0:T(8,128)(2,1)S(1)}, u32[]{:S(2)}, u32[]{:S(2)}) collective-permute-start(bf16[128,512]{1,0:T(8,128)(2,1)S(1)} %get-tuple-element.155), channel_id=1, source_target_pairs={{0,1},{1,0},{2,3},{3,2},{4,5},{5,4},{6,7},{7,6},{8,9},{9,8},{10,11... | collective-permute-start | bytes 393224 | tf_op jit(solution)/shard_map/ppermute | solution.py:42
  96.5 6.1 %collective-permute-start.22 = (bf16[112,512]{1,0:T(8,128)(2,1)S(1)}, bf16[112,512]{1,0:T(8,128)(2,1)S(1)}, u32[]{:S(2)}, u32[]{:S(2)}) collective-permute-start(bf16[112,512]{1,0:T(8,128)(2,1)S(1)} %shard_map.217.refs_0_), channel_id=1, source_target_pairs={{0,96},{32,0},{64,32},{96,64},{1,97},{33,1},{65,33},{97,65},{2,98}... | collective-permute-start | bytes 344072 | tf_op jit(solution)/shard_map/ppermute | solution.py:540
  98.3 5.8 %collective-permute-start.21 = (bf16[112,512]{1,0:T(8,128)(2,1)S(1)}, bf16[112,512]{1,0:T(8,128)(2,1)S(1)}, u32[]{:S(2)}, u32[]{:S(2)}) collective-permute-start(bf16[112,512]{1,0:T(8,128)(2,1)S(1)} %shard_map.217.refs_0_), channel_id=1, source_target_pairs={{0,64},{32,96},{64,0},{96,32},{1,65},{33,97},{65,1},{97,33},{2,66}... | collective-permute-start | bytes 344072 | tf_op jit(solution)/shard_map/ppermute | solution.py:540
  101.9 5.8 %collective-permute-start.20 = (bf16[112,512]{1,0:T(8,128)(2,1)S(1)}, bf16[112,512]{1,0:T(8,128)(2,1)S(1)}, u32[]{:S(2)}, u32[]{:S(2)}) collective-permute-start(bf16[112,512]{1,0:T(8,128)(2,1)S(1)} %shard_map.217.refs_0_), channel_id=1, source_target_pairs={{0,32},{32,64},{64,96},{96,0},{1,33},{33,65},{65,97},{97,1},{2,34}... | collective-permute-start | bytes 344072 | tf_op jit(solution)/shard_map/ppermute | solution.py:540
  133.4 7.4 %collective-permute-start.23 = (bf16[1792,512]{1,0:T(8,128)(2,1)S(1)}, bf16[1792,512]{1,0:T(8,128)(2,1)S(1)}, u32[]{:S(2)}, u32[]{:S(2)}) collective-permute-start(bf16[1792,512]{1,0:T(8,128)(2,1)S(1)} %bitcast.14), channel_id=1, source_target_pairs={{0,1},{1,0},{2,3},{3,2},{4,5},{5,4},{6,7},{7,6},{8,9},{9,8},{10,11... | collective-permute-start | bytes 5505032 | tf_op jit(solution)/shard_map/ppermute | solution.py:42

commit v9 on v8

--- a/solution.py
+++ b/solution.py
@@ -181,7 +181,7 @@
     )
     pre = outer_sum(grid_ref[...], weight_ref[...])
     sigma = jax.nn.sigmoid(pre)
-    slope_ref[...] = sigma * (1.0 + pre * (1.0 - sigma))
+    slope_ref[...] = (sigma * (1.0 + pre * (1.0 - sigma))).astype(HALF)
     sum_ref[...] = matmul(counts, (pre * sigma).astype(HALF))
     held_ref[...] = weight_ref[...]
 
@@ -196,7 +196,7 @@
     )
     pre = outer_sum(parcel_ref[: weight_ref.shape[0]], weight_ref[...])
     sigma = jax.nn.sigmoid(pre)
-    slope_ref[...] = sigma * (1.0 + pre * (1.0 - sigma))
+    slope_ref[...] = (sigma * (1.0 + pre * (1.0 - sigma))).astype(HALF)
     out_ref[...] = sum_ref[...] + matmul(counts, (pre * sigma).astype(HALF))
 
 
@@ -215,6 +215,12 @@
     head, tail = half[:rows], half[half.shape[0] - rows :]
     on_ref[...] = jnp.where(odd, head, tail)
     off_ref[...] = jnp.where(odd, tail, head)
+
+
+def embed_last(p, parcel_ref, weight_ref, recv_ref, sum_ref, encode_ref, static_ref, *refs):
+    index_ref, slope_ref, outs, total_ref = refs[0], refs[1], refs[2:-1], refs[-1]
+    embed_far(p, parcel_ref, weight_ref, recv_ref, sum_ref, index_ref, slope_ref, total_ref)
+    encode(total_ref, encode_ref, static_ref, *outs)
 
 
 def near_counts(near_ref, on_ref, off_ref, out_ref, turned_ref):
@@ -405,7 +411,7 @@
     grads = []
     for p in range(GROUPS):
         latent = matmul(counts_ref[:, p * nodes : (p + 1) * nodes], back_ref[...])
-        grads.append((latent * slopes[p][...]).astype(HALF))
+        grads.append((latent * slopes[p][...].astype(SINGLE)).astype(HALF))
     total = matmul(
         jnp.concatenate([grid[:variables] for grid in grids], 1), jnp.concatenate(grads, 0)
     )
@@ -583,7 +589,7 @@
     embed_macs = grid_count * variables * width + mesh_count * grid_count * (step + width)
     slope_embed, total, held_weight = fetching(
         embed_own,
-        [grid_full, mesh_full, shape(variables, width, HALF)],
+        [grid_rows, mesh_full, shape(variables, width, HALF)],
         embed_macs,
         grid,
         embed_weight,
@@ -594,23 +600,29 @@
     index = [None] * GROUPS
     slopes = [slope_embed] + [None] * (GROUPS - 1)
     grids = [grid, *arrived]
-    for p in (1, 3, 2, 4):
+    embedded = [shape(INDEX_ROWS, LANES, jnp.int32), grid_rows]
+    for p in (1, 3, 2):
         index[p], slopes[p], total = whole(
             lambda *refs, p=p: embed_far(p, *refs),
-            [shape(INDEX_ROWS, LANES, jnp.int32), grid_full, mesh_full],
+            [*embedded, mesh_full],
             embed_macs,
             arrived[p - 1],
             held_weight,
             mesh_recv,
             total,
         )
-    encode_in, slope_encode, state, half, on, off = whole(
-        encode,
-        [mesh_rows, mesh_full, mesh_full, mesh_rows] + [shape(rim, width, HALF)] * 2,
-        mesh_count * width * width,
+    index[4], slopes[4], encode_in, slope_encode, state, half, on, off = whole(
+        lambda *refs: embed_last(4, *refs),
+        [*embedded, mesh_rows, mesh_full, mesh_full, mesh_rows]
+        + [shape(rim, width, HALF)] * 2,
+        embed_macs + mesh_count * width * width,
+        arrived[3],
+        held_weight,
+        mesh_recv,
         total,
         encode_weight,
         mesh_static,
+        scratch=[pltpu.VMEM((mesh_count, width), SINGLE)],
     )
     off = swap_off(off)
     on = swap_on(on)

time: 143 us -> 143 us (level)
    pallas_call x20 -> x19, Pallas kernels: 19.9 us -> 19.8 us  [whole(): pl.pallas_call(body, out_shape=outs, scratch_shapes=scratch, compiler_par...]
where the time goes in v9:
time: 143 us
  blocking collectives  54 us (38%)
  starting transfers between devices  43.4 us (30%)
  Pallas kernels  26.9 us (19%)
  waiting for transfers between devices  15.6 us (11%)
    all_to_all x1, blocking collectives, reduce_all(): lax.all_to_all(part.reshape(chips, rows, width), 'dom', 0, 0, axis_index_...  28.5 us
    all_to_all x1, blocking collectives, reduce_all(): lax.all_to_all(copies, 'dom', 0, 0, axis_index_groups=groups)  25.5 us
    ppermute x10, starting transfers between devices, swap_on(): return lax.ppermute(value, 'dom', [(i, i ^ 1) for i in range(count)])  24.8 us
    pallas_call x19, Pallas kernels, whole(): pl.pallas_call(body, out_shape=outs, scratch_shapes=scratch, compiler_par...  19.8 us
    ppermute x6, starting transfers between devices, swap_band(): return lax.ppermute(value, 'band', pairs)  10.7 us
    ppermute x5, waiting for transfers between devices, swap_off(): lax.ppermute(value, 'dom', [(i, (i + (1 if i % 2 else -1)) % count) for i...  6.2 us
    ppermute x3, starting transfers between devices, reduce_all(): lax.ppermute(piece, 'band', [(i, (i + step) % bands) for i in range(bands)])  6.06 us
    ppermute x3, waiting for transfers between devices, reduce_all(): lax.ppermute(piece, 'band', [(i, (i + step) % bands) for i in range(bands)])  5.16 us
  transfers between devices with their start and end apart: 24, of which 9 were waited for; matrix products, arithmetic and copies ran while one was open for 1% of the time, Pallas kernels for 10%

profile of v9, /device:TPU:1, one launch (start us, length us, event | category | flops | bytes accessed | tf_op | source)
XLA Modules:
  0.0 143.0 jit_solution(10825522120052211204)
XLA Ops:
  0.6 0.0 copy-start
  0.6 0.0 copy-start.12
  0.7 1.1 shard_map.197
  1.8 1.5 %collective-permute-start.3 = (bf16[256,512]{1,0:T(8,128)(2,1)S(1)}, bf16[256,512]{1,0:T(8,128)(2,1)S(1)}, u32[]{:S(2)}, u32[]{:S(2)}) collective-permute-start(bf16[256,512]{1,0:T(8,128)(2,1)S(1)} %get-tuple-element.90), channel_id=1, source_target_pairs={{0,1},{1,0},{2,3},{3,2},{4,5},{5,4},{6,7},{7,6},{8,9},{9,8},{10,11... | collective-permute-start | bytes 786440 | tf_op jit(solution)/shard_map/ppermute | solution.py:42
  3.3 1.3 collective-permute-start.2
  4.6 1.9 %collective-permute-start.1 = (bf16[256,512]{1,0:T(8,128)(2,1)S(1)}, bf16[256,512]{1,0:T(8,128)(2,1)S(1)}, u32[]{:S(2)}, u32[]{:S(2)}) collective-permute-start(bf16[256,512]{1,0:T(8,128)(2,1)S(1)} %get-tuple-element.88), channel_id=1, source_target_pairs={{0,31},{1,2},{2,1},{3,4},{4,3},{5,6},{6,5},{7,8},{8,7},{9,10},{10,... | collective-permute-start | bytes 786440 | tf_op jit(solution)/shard_map/ppermute | solution.py:47
  6.5 0.7 collective-permute-start
  7.1 2.1 %shard_map.198 = (bf16[512,512]{1,0:T(8,128)(2,1)S(1)}, f32[256,512]{1,0:T(8,128)S(1)}, bf16[227,512]{1,0:T(8,128)(2,1)S(1)}) custom-call(bf16[227,512]{1,0:T(8,128)(2,1)} %bitcast.19, bf16[227,512]{1,0:T(8,128)(2,1)} %refs_1_.1, s32[30,128]{1,0:T(8,128)} %bitcast.26, s32[30,128]{1,0:T(8,128)} %bitcast.32), custom_call_target="tpu_custom_call" | custom-call | flops 454557696 | bytes 1776640 | tf_op jit(solution)/shard_map/pallas_call | solution.py:128
  9.2 1.0 shard_map.199
  10.2 0.0 copy-start.4
  10.2 0.9 collective-permute-done.2.refs_0_.refs_10_
  11.1 1.0 shard_map.200
  12.1 0.0 copy-start.6
  12.1 0.0 copy-start.11
  12.1 1.0 shard_map.201
  13.1 1.3 shard_map.202
  14.5 3.9 %collective-permute-start.4 = (bf16[128,512]{1,0:T(8,128)(2,1)S(1)}, bf16[128,512]{1,0:T(8,128)(2,1)S(1)}, u32[]{:S(2)}, u32[]{:S(2)}) collective-permute-start(bf16[128,512]{1,0:T(8,128)(2,1)S(1)} %get-tuple-element.102), channel_id=1, source_target_pairs={{0,1},{1,0},{2,3},{3,2},{4,5},{5,4},{6,7},{7,6},{8,9},{9,8},{10,11... | collective-permute-start | bytes 393224 | tf_op jit(solution)/shard_map/ppermute | solution.py:42
  18.4 0.0 copy-start.3
  18.4 1.4 shard_map.203.refs_5_
  19.8 0.7 shard_map.204
  20.6 2.2 %collective-permute-done.5.off_ref = bf16[128,512]{1,0:T(8,128)(2,1)S(1)} collective-permute-done((bf16[128,512]{1,0:T(8,128)(2,1)S(1)}, bf16[128,512]{1,0:T(8,128)(2,1)S(1)}, u32[]{:S(2)}, u32[]{:S(2)}) %collective-permute-start.5) | collective-permute-done | bytes 131104 | tf_op jit(solution)/shard_map/ppermute | solution.py:47
  22.8 1.5 %shard_map.205 = (bf16[256,512]{1,0:T(8,128)(2,1)S(1)}, f32[384,512]{1,0:T(8,128)S(1)}, f32[256,512]{1,0:T(8,128)S(1)}, bf16[256,512]{1,0:T(8,128)(2,1)S(1)}, bf...) custom-call(bf16[256,512]{1,0:T(8,128)(2,1)S(1)} %get-tuple-element.95.half_ref.refs_0_, ...), custom_call_target="tpu_custom_call" | custom-call | flops 1207959552 | bytes 6029312 | tf_op jit(solution)/shard_map/pallas_call | solution.py:81
  24.2 3.5 %collective-permute-start.9 = (bf16[256,512]{1,0:T(8,128)(2,1)S(1)}, bf16[256,512]{1,0:T(8,128)(2,1)S(1)}, u32[]{:S(2)}, u32[]{:S(2)}) collective-permute-start(bf16[256,512]{1,0:T(8,128)(2,1)S(1)} %get-tuple-element.105.refs_0_), channel_id=1, source_target_pairs={{0,1},{1,0},{2,3},{3,2},{4,5},{5,4},{6,7},{7,6},{8,9},{9,8},{10,11... | collective-permute-start | bytes 786440 | tf_op jit(solution)/shard_map/ppermute | solution.py:42
  27.7 3.6 %collective-permute-start.7 = (bf16[256,512]{1,0:T(8,128)(2,1)S(1)}, bf16[256,512]{1,0:T(8,128)(2,1)S(1)}, u32[]{:S(2)}, u32[]{:S(2)}) collective-permute-start(bf16[256,512]{1,0:T(8,128)(2,1)S(1)} %get-tuple-element.105.refs_0_), channel_id=1, source_target_pairs={{0,32},{32,0},{64,96},{96,64},{1,33},{33,1},{65,97},{97,65},{2,34}... | collective-permute-start | bytes 786440 | tf_op jit(solution)/shard_map/ppermute | solution.py:57
  31.4 0.8 collective-permute-start.6
  32.3 0.3 fusion.1.refs_8_
  32.6 1.2 shard_map.206.refs_6_
  33.9 1.6 %collective-permute-done.7.refs_2_ = bf16[256,512]{1,0:T(8,128)(2,1)S(1)} collective-permute-done((bf16[256,512]{1,0:T(8,128)(2,1)S(1)}, bf16[256,512]{1,0:T(8,128)(2,1)S(1)}, u32[]{:S(2)}, u32[]{:S(2)}) %collective-permute-start.7) | collective-permute-done | bytes 262176 | tf_op jit(solution)/shard_map/ppermute | solution.py:57
  35.5 2.4 %shard_map.207 = (bf16[512,512]{1,0:T(8,128)(2,1)S(1)}, bf16[512,512]{1,0:T(8,128)(2,1)S(1)}, bf16[512,512]{1,0:T(8,128)(2,1)S(1)}, f32[256,512]{1,0:T(8,128)S(1...) custom-call(bf16[256,512]{1,0:T(8,128)(2,1)S(1)} %get-tuple-element., ...), custom_call_target="tpu_custom_call" | custom-call | flops 1879048192 | bytes 8650752 | tf_op jit(solution)/shard_map/pallas_call | solution.py:81
  37.8 3.3 %collective-permute-start.10 = (bf16[256,512]{1,0:T(8,128)(2,1)S(1)}, bf16[256,512]{1,0:T(8,128)(2,1)S(1)}, u32[]{:S(2)}, u32[]{:S(2)}) collective-permute-start(bf16[256,512]{1,0:T(8,128)(2,1)S(1)} %get-tuple-element.116), channel_id=1, source_target_pairs={{0,1},{1,0},{2,3},{3,2},{4,5},{5,4},{6,7},{7,6},{8,9},{9,8},{10,11... | collective-permute-start | bytes 786440 | tf_op jit(solution)/shard_map/ppermute | solution.py:42
  41.1 3.6 %collective-permute-start.12 = (bf16[256,512]{1,0:T(8,128)(2,1)S(1)}, bf16[256,512]{1,0:T(8,128)(2,1)S(1)}, u32[]{:S(2)}, u32[]{:S(2)}) collective-permute-start(bf16[256,512]{1,0:T(8,128)(2,1)S(1)} %get-tuple-element.118), channel_id=1, source_target_pairs={{0,32},{32,0},{64,96},{96,64},{1,33},{33,1},{65,97},{97,65},{2,34}... | collective-permute-start | bytes 786440 | tf_op jit(solution)/shard_map/ppermute | solution.py:57
  44.6 0.7 collective-permute-start.13
  45.3 1.4 shard_map.208.refs_1_
  46.8 0.7 shard_map.209
  47.5 3.0 %collective-permute-start.14 = (bf16[384,512]{1,0:T(8,128)(2,1)S(1)}, bf16[384,512]{1,0:T(8,128)(2,1)S(1)}, u32[]{:S(2)}, u32[]{:S(2)}) collective-permute-start(bf16[384,512]{1,0:T(8,128)(2,1)S(1)} %get-tuple-element.127), channel_id=1, source_target_pairs={{0,1},{1,0},{2,3},{3,2},{4,5},{5,4},{6,7},{7,6},{8,9},{9,8},{10,11... | collective-permute-start | bytes 1179656 | tf_op jit(solution)/shard_map/ppermute | solution.py:42
  50.5 0.2 add_multiply_fusion.1.refs_5_
  50.7 0.2 shard_map.210
  50.9 1.3 collective-permute-start.15
  52.2 0.3 add_multiply_fusion.slope_0_ref
  52.5 0.6 shard_map.211
  53.2 0.1 collective-permute-done.15.on_ref
  53.3 4.0 %collective-permute-done.16.off_ref = bf16[192,512]{1,0:T(8,128)(2,1)S(1)} collective-permute-done((bf16[192,512]{1,0:T(8,128)(2,1)S(1)}, bf16[192,512]{1,0:T(8,128)(2,1)S(1)}, u32[]{:S(2)}, u32[]{:S(2)}) %collective-permute-start.16) | collective-permute-done | bytes 196640 | tf_op jit(solution)/shard_map/ppermute | solution.py:47
  57.3 2.2 %shard_map.212 = (f32[256,512]{1,0:T(8,128)}, bf16[256,512]{1,0:T(8,128)(2,1)S(1)}, bf16[256,512]{1,0:T(8,128)(2,1)S(1)}, bf16[256,512]{1,0:T(8,128)(2,1)S(1)}) custom-call(f32[256,512]{1,0:T(8,128)S(1)} %get-tuple-element.128.state_ref, bf16[256,512]{1,0:T(8,128)(2,1)S(1)} %get-tuple-element.123.refs_1_.refs_3_.layer_ref, ...), custom_call_target="tpu_custom_call" | custom-call | flops 1207959552 | bytes 6946816 | tf_op jit(solution)/shard_map/pallas_call | solution.py:81
  59.5 0.9 shard_map.213
  60.4 3.5 %collective-permute-start.18 = (bf16[768,512]{1,0:T(8,128)(2,1)S(1)}, bf16[768,512]{1,0:T(8,128)(2,1)S(1)}, u32[]{:S(2)}, u32[]{:S(2)}) collective-permute-start(bf16[768,512]{1,0:T(8,128)(2,1)S(1)} %get-tuple-element.144), channel_id=1, source_target_pairs={{0,1},{1,0},{2,3},{3,2},{4,5},{5,4},{6,7},{7,6},{8,9},{9,8},{10,11... | collective-permute-start | bytes 2359304 | tf_op jit(solution)/shard_map/ppermute | solution.py:42
  63.9 0.1 collective-permute-start.17
  64.0 1.6 %shard_map.214 = (bf16[128,512]{1,0:T(8,128)(2,1)S(1)}, bf16[128,512]{1,0:T(8,128)(2,1)S(1)}) custom-call(bf16[256,512]{1,0:T(8,128)(2,1)S(1)} %get-tuple-element.145.refs_0_, bf16[512,1280]{1,0:T(8,128)(2,1)S(1)} %shard_map.208.refs_1_, bf16[512,512]{1,0:T(8,128)(2,1)S(1)} %get-tuple-element.147.refs_2_, bf16[512,512]{1,0:T(8,128)(2,1)S(1)} %get-tuple-element.148.refs_3_, ...), custom_call_target="tpu_custom_call" | custom-call | flops 1266155520 | bytes 5737472 | tf_op jit(solution)/shard_map/pallas_call | solution.py:81
  65.5 0.7 collective-permute-start.19
  66.3 1.0 collective-permute-done.19.refs_7_
  67.2 0.4 shard_map.215
  67.7 28.5 %all_to_all.10.pieces_ref = bf16[16,112,512]{2,1,0:T(8,128)(2,1)S(1)} all-to-all(bf16[16,112,512]{2,1,0:T(8,128)(2,1)S(1)} %bitcast.17), channel_id=1, replica_groups={{0,2,4,6,8,10,12,14,16,18,20,22,24,26,28,30},{1,3,5,7,9,11,13,15,17,19,..., dimensions={0} | all-to-all | bytes 3670016 | tf_op jit(solution)/shard_map/all_to_all | solution.py:541
  96.1 0.2 shard_map.216.refs_0_
  96.4 1.9 %collective-permute-start.22 = (bf16[112,512]{1,0:T(8,128)(2,1)S(1)}, bf16[112,512]{1,0:T(8,128)(2,1)S(1)}, u32[]{:S(2)}, u32[]{:S(2)}) collective-permute-start(bf16[112,512]{1,0:T(8,128)(2,1)S(1)} %shard_map.216.refs_0_), channel_id=1, source_target_pairs={{0,96},{32,0},{64,32},{96,64},{1,97},{33,1},{65,33},{97,65},{2,98}... | collective-permute-start | bytes 344072 | tf_op jit(solution)/shard_map/ppermute | solution.py:546
  98.2 3.6 %collective-permute-start.21 = (bf16[112,512]{1,0:T(8,128)(2,1)S(1)}, bf16[112,512]{1,0:T(8,128)(2,1)S(1)}, u32[]{:S(2)}, u32[]{:S(2)}) collective-permute-start(bf16[112,512]{1,0:T(8,128)(2,1)S(1)} %shard_map.216.refs_0_), channel_id=1, source_target_pairs={{0,64},{32,96},{64,0},{96,32},{1,65},{33,97},{65,1},{97,33},{2,66}... | collective-permute-start | bytes 344072 | tf_op jit(solution)/shard_map/ppermute | solution.py:546
  101.8 0.6 collective-permute-start.20
  102.4 1.6 %collective-permute-done.21.refs_2_ = bf16[112,512]{1,0:T(8,128)(2,1)S(1)} collective-permute-done((bf16[112,512]{1,0:T(8,128)(2,1)S(1)}, bf16[112,512]{1,0:T(8,128)(2,1)S(1)}, u32[]{:S(2)}, u32[]{:S(2)}) %collective-permute-start.21) | collective-permute-done | bytes 114720 | tf_op jit(solution)/shard_map/ppermute | solution.py:546
  104.0 3.6 %collective-permute-done.20.refs_1_ = bf16[112,512]{1,0:T(8,128)(2,1)S(1)} collective-permute-done((bf16[112,512]{1,0:T(8,128)(2,1)S(1)}, bf16[112,512]{1,0:T(8,128)(2,1)S(1)}, u32[]{:S(2)}, u32[]{:S(2)}) %collective-permute-start.20) | collective-permute-done | bytes 114720 | tf_op jit(solution)/shard_map/ppermute | solution.py:546
  107.6 0.2 shard_map.217
  107.8 25.5 %all_to_all.11 = bf16[16,112,512]{2,1,0:T(8,128)(2,1)S(1)} all-to-all(bf16[16,112,512]{2,1,0:T(8,128)(2,1)S(1)} %shard_map.217), channel_id=1, replica_groups={{0,2,4,6,8,10,12,14,16,18,20,22,24,26,28,30},{1,3,5,7,9,11,13,15,17,19,..., dimensions={0} | all-to-all | bytes 3670016 | tf_op jit(solution)/shard_map/all_to_all | solution.py:551
  133.3 4.0 %collective-permute-start.23 = (bf16[1792,512]{1,0:T(8,128)(2,1)S(1)}, bf16[1792,512]{1,0:T(8,128)(2,1)S(1)}, u32[]{:S(2)}, u32[]{:S(2)}) collective-permute-start(bf16[1792,512]{1,0:T(8,128)(2,1)S(1)} %bitcast.14), channel_id=1, source_target_pairs={{0,1},{1,0},{2,3},{3,2},{4,5},{5,4},{6,7},{7,6},{8,9},{9,8},{10,11... | collective-permute-start | bytes 5505032 | tf_op jit(solution)/shard_map/ppermute | solution.py:42
  137.3 1.0 fusion
  138.3 1.8 %shard_map.218 = (f32[512,512]{1,0:T(8,128)}, f32[2,512,512]{2,1,0:T(8,128)}, f32[2,512,512]{2,1,0:T(8,128)}, f32[512,512]{1,0:T(8,128)}) custom-call(bf16[1792,512]{1,0:T(8,128)(2,1)S(1)} %bitcast.15), custom_call_target="tpu_custom_call" | custom-call | bytes 5505024 | tf_op jit(solution)/shard_map/pallas_call | solution.py:514
  140.1 0.6 collective-permute-done.23.other_ref
  140.7 2.1 %shard_map.219 = (f32[512,512]{1,0:T(8,128)}, f32[2,512,512]{2,1,0:T(8,128)}, f32[2,512,512]{2,1,0:T(8,128)}, f32[512,512]{1,0:T(8,128)}, f32[227,512]{1,0:T(8,128)}, /*index=5*/f32[227,512]{1,0:T(8,128)}) custom-call(bf16[1792,512]{1,0:T(8,128)(2,1)S(1)} %bitcast.16, ...), custom_call_target="tpu_custom_call", output_to_operand_aliasing={{0}: (2, {}), {1}: (3, {}), {2}: (4, {}), {3}: (5, {})} | custom-call | bytes 5505024 | tf_op jit(solution)/shard_map/pallas_call | solution.py:523
  (39 shorter events, 0.1 us)
Async XLA Ops:
  0.6 31.6 %copy-start = (bf16[512,227]{0,1:T(8,128)(2,1)S(1)}, bf16[512,227]{0,1:T(8,128)(2,1)}, u32[]{:S(2)}) copy-start(bf16[512,227]{0,1:T(8,128)(2,1)} %param.22) | copy-start | bytes 697348
  0.6 8.6 %copy-start.12 = (s32[3840]{0:T(1024)S(1)}, s32[3840]{0:T(1024)}, u32[]{:S(2)}) copy-start(s32[3840]{0:T(1024)} %param.24) | copy-start | bytes 46084
  1.8 7.4 %collective-permute-start.3 = (bf16[256,512]{1,0:T(8,128)(2,1)S(1)}, bf16[256,512]{1,0:T(8,128)(2,1)S(1)}, u32[]{:S(2)}, u32[]{:S(2)}) collective-permute-start(bf16[256,512]{1,0:T(8,128)(2,1)S(1)} %get-tuple-element.90), channel_id=1, source_target_pairs={{0,1},{1,0},{2,3},{3,2},{4,5},{5,4},{6,7},{7,6},{8,9},{9,8},{10,11... | collective-permute-start | bytes 786440 | tf_op jit(solution)/shard_map/ppermute | solution.py:42
  3.3 7.9 %collective-permute-start.2 = (bf16[256,512]{1,0:T(8,128)(2,1)S(1)}, bf16[256,512]{1,0:T(8,128)(2,1)S(1)}, u32[]{:S(2)}, u32[]{:S(2)}) collective-permute-start(bf16[256,512]{1,0:T(8,128)(2,1)S(1)} %get-tuple-element.89), channel_id=1, source_target_pairs={{0,32},{32,0},{64,96},{96,64},{1,33},{33,1},{65,97},{97,65},{2,34}... | collective-permute-start | bytes 786440 | tf_op jit(solution)/shard_map/ppermute | solution.py:57
  4.6 7.5 %collective-permute-start.1 = (bf16[256,512]{1,0:T(8,128)(2,1)S(1)}, bf16[256,512]{1,0:T(8,128)(2,1)S(1)}, u32[]{:S(2)}, u32[]{:S(2)}) collective-permute-start(bf16[256,512]{1,0:T(8,128)(2,1)S(1)} %get-tuple-element.88), channel_id=1, source_target_pairs={{0,31},{1,2},{2,1},{3,4},{4,3},{5,6},{6,5},{7,8},{8,7},{9,10},{10,... | collective-permute-start | bytes 786440 | tf_op jit(solution)/shard_map/ppermute | solution.py:47
  6.5 6.6 %collective-permute-start = (bf16[256,512]{1,0:T(8,128)(2,1)S(1)}, bf16[256,512]{1,0:T(8,128)(2,1)S(1)}, u32[]{:S(2)}, u32[]{:S(2)}) collective-permute-start(bf16[256,512]{1,0:T(8,128)(2,1)S(1)} %get-tuple-element.86), channel_id=1, source_target_pairs={{32,64},{64,32},{33,65},{65,33},{34,66},{66,34},{35,67},{67,35},{3... | collective-permute-start | bytes 786440 | tf_op jit(solution)/shard_map/ppermute | solution.py:57
  10.2 2.9 %copy-start.4 = (bf16[512,512]{1,0:T(8,128)(2,1)S(1)}, bf16[512,512]{1,0:T(8,128)(2,1)}, u32[]{:S(2)}) copy-start(bf16[512,512]{1,0:T(8,128)(2,1)} %encode_ref.1) | copy-start | bytes 1572868
  10.2 2.9 %copy-start.10 = (bf16[256,512]{1,0:T(8,128)(2,1)S(1)}, bf16[256,512]{1,0:T(8,128)(2,1)}, u32[]{:S(2)}) copy-start(bf16[256,512]{1,0:T(8,128)(2,1)} %refs_5_.1) | copy-start | bytes 786436
  12.1 6.2 %copy-start.6 = (s32[3840]{0:T(1024)S(1)}, s32[3840]{0:T(1024)}, u32[]{:S(2)}) copy-start(s32[3840]{0:T(1024)} %param.26) | copy-start | bytes 46084
  12.1 6.2 %copy-start.11 = (s32[3840]{0:T(1024)S(1)}, s32[3840]{0:T(1024)}, u32[]{:S(2)}) copy-start(s32[3840]{0:T(1024)} %param.27) | copy-start | bytes 46084
  14.5 6.1 %collective-permute-start.4 = (bf16[128,512]{1,0:T(8,128)(2,1)S(1)}, bf16[128,512]{1,0:T(8,128)(2,1)S(1)}, u32[]{:S(2)}, u32[]{:S(2)}) collective-permute-start(bf16[128,512]{1,0:T(8,128)(2,1)S(1)} %get-tuple-element.102), channel_id=1, source_target_pairs={{0,1},{1,0},{2,3},{3,2},{4,5},{5,4},{6,7},{7,6},{8,9},{9,8},{10,11... | collective-permute-start | bytes 393224 | tf_op jit(solution)/shard_map/ppermute | solution.py:42
  18.3 4.4 %collective-permute-start.5 = (bf16[128,512]{1,0:T(8,128)(2,1)S(1)}, bf16[128,512]{1,0:T(8,128)(2,1)S(1)}, u32[]{:S(2)}, u32[]{:S(2)}) collective-permute-start(bf16[128,512]{1,0:T(8,128)(2,1)S(1)} %get-tuple-element.103), channel_id=1, source_target_pairs={{0,31},{1,2},{2,1},{3,4},{4,3},{5,6},{6,5},{7,8},{8,7},{9,10},{10,... | collective-permute-start | bytes 393224 | tf_op jit(solution)/shard_map/ppermute | solution.py:47
  18.4 1.5 %copy-start.8 = (s32[256,6]{0,1:T(8,128)S(1)}, s32[256,6]{0,1:T(8,128)}, u32[]{:S(2)}) copy-start(s32[256,6]{0,1:T(8,128)} %param.25) | copy-start | bytes 18436
  18.4 4.4 %copy-start.2 = (bf16[2,512,512]{2,1,0:T(8,128)(2,1)S(1)}, bf16[2,512,512]{2,1,0:T(8,128)(2,1)}, u32[]{:S(2)}) copy-start(bf16[2,512,512]{2,1,0:T(8,128)(2,1)} %self_ref.3) | copy-start | bytes 3145732
  18.4 4.4 %copy-start.3 = (bf16[2,512,512]{2,1,0:T(8,128)(2,1)S(1)}, bf16[2,512,512]{2,1,0:T(8,128)(2,1)}, u32[]{:S(2)}) copy-start(bf16[2,512,512]{2,1,0:T(8,128)(2,1)} %near_ref.3) | copy-start | bytes 3145732
  22.7 9.5 %copy-start.5 = (bf16[512,227]{0,1:T(8,128)(2,1)S(1)}, bf16[512,227]{0,1:T(8,128)(2,1)}, u32[]{:S(2)}) copy-start(bf16[512,227]{0,1:T(8,128)(2,1)} %param.15) | copy-start | bytes 697348
  24.2 9.6 %collective-permute-start.9 = (bf16[256,512]{1,0:T(8,128)(2,1)S(1)}, bf16[256,512]{1,0:T(8,128)(2,1)S(1)}, u32[]{:S(2)}, u32[]{:S(2)}) collective-permute-start(bf16[256,512]{1,0:T(8,128)(2,1)S(1)} %get-tuple-element.105.refs_0_), channel_id=1, source_target_pairs={{0,1},{1,0},{2,3},{3,2},{4,5},{5,4},{6,7},{7,6},{8,9},{9,8},{10,11... | collective-permute-start | bytes 786440 | tf_op jit(solution)/shard_map/ppermute | solution.py:42
  27.7 6.1 %collective-permute-start.8 = (bf16[256,512]{1,0:T(8,128)(2,1)S(1)}, bf16[256,512]{1,0:T(8,128)(2,1)S(1)}, u32[]{:S(2)}, u32[]{:S(2)}) collective-permute-start(bf16[256,512]{1,0:T(8,128)(2,1)S(1)} %get-tuple-element.105.refs_0_), channel_id=1, source_target_pairs={{0,31},{1,2},{2,1},{3,4},{4,3},{5,6},{6,5},{7,8},{8,7},{9,10},{10,... | collective-permute-start | bytes 786440 | tf_op jit(solution)/shard_map/ppermute | solution.py:47
  27.7 7.7 %collective-permute-start.7 = (bf16[256,512]{1,0:T(8,128)(2,1)S(1)}, bf16[256,512]{1,0:T(8,128)(2,1)S(1)}, u32[]{:S(2)}, u32[]{:S(2)}) collective-permute-start(bf16[256,512]{1,0:T(8,128)(2,1)S(1)} %get-tuple-element.105.refs_0_), channel_id=1, source_target_pairs={{0,32},{32,0},{64,96},{96,64},{1,33},{33,1},{65,97},{97,65},{2,34}... | collective-permute-start | bytes 786440 | tf_op jit(solution)/shard_map/ppermute | solution.py:57
  31.4 4.1 %collective-permute-start.6 = (bf16[256,512]{1,0:T(8,128)(2,1)S(1)}, bf16[256,512]{1,0:T(8,128)(2,1)S(1)}, u32[]{:S(2)}, u32[]{:S(2)}) collective-permute-start(bf16[256,512]{1,0:T(8,128)(2,1)S(1)} %get-tuple-element.105.refs_0_), channel_id=1, source_target_pairs={{32,64},{64,32},{33,65},{65,33},{34,66},{66,34},{35,67},{67,35},{3... | collective-permute-start | bytes 786440 | tf_op jit(solution)/shard_map/ppermute | solution.py:57
  32.6 2.9 %copy-start.9 = (bf16[512,512]{1,0:T(8,128)(2,1)S(1)}, bf16[512,512]{1,0:T(8,128)(2,1)}, u32[]{:S(2)}) copy-start(bf16[512,512]{1,0:T(8,128)(2,1)} %refs_7_.1) | copy-start | bytes 1572868
  33.8 11.5 %copy-start.7 = (s32[3840]{0:T(1024)S(1)}, s32[3840]{0:T(1024)}, u32[]{:S(2)}) copy-start(s32[3840]{0:T(1024)} %param.23) | copy-start | bytes 46084
  37.8 12.8 %collective-permute-start.10 = (bf16[256,512]{1,0:T(8,128)(2,1)S(1)}, bf16[256,512]{1,0:T(8,128)(2,1)S(1)}, u32[]{:S(2)}, u32[]{:S(2)}) collective-permute-start(bf16[256,512]{1,0:T(8,128)(2,1)S(1)} %get-tuple-element.116), channel_id=1, source_target_pairs={{0,1},{1,0},{2,3},{3,2},{4,5},{5,4},{6,7},{7,6},{8,9},{9,8},{10,11... | collective-permute-start | bytes 786440 | tf_op jit(solution)/shard_map/ppermute | solution.py:42
  41.1 9.6 %collective-permute-start.11 = (bf16[256,512]{1,0:T(8,128)(2,1)S(1)}, bf16[256,512]{1,0:T(8,128)(2,1)S(1)}, u32[]{:S(2)}, u32[]{:S(2)}) collective-permute-start(bf16[256,512]{1,0:T(8,128)(2,1)S(1)} %get-tuple-element.117), channel_id=1, source_target_pairs={{0,31},{1,2},{2,1},{3,4},{4,3},{5,6},{6,5},{7,8},{8,7},{9,10},{10,... | collective-permute-start | bytes 786440 | tf_op jit(solution)/shard_map/ppermute | solution.py:47
  41.1 9.6 %collective-permute-start.12 = (bf16[256,512]{1,0:T(8,128)(2,1)S(1)}, bf16[256,512]{1,0:T(8,128)(2,1)S(1)}, u32[]{:S(2)}, u32[]{:S(2)}) collective-permute-start(bf16[256,512]{1,0:T(8,128)(2,1)S(1)} %get-tuple-element.118), channel_id=1, source_target_pairs={{0,32},{32,0},{64,96},{96,64},{1,33},{33,1},{65,97},{97,65},{2,34}... | collective-permute-start | bytes 786440 | tf_op jit(solution)/shard_map/ppermute | solution.py:57
  44.6 6.0 %collective-permute-start.13 = (bf16[256,512]{1,0:T(8,128)(2,1)S(1)}, bf16[256,512]{1,0:T(8,128)(2,1)S(1)}, u32[]{:S(2)}, u32[]{:S(2)}) collective-permute-start(bf16[256,512]{1,0:T(8,128)(2,1)S(1)} %get-tuple-element.119), channel_id=1, source_target_pairs={{32,64},{64,32},{33,65},{65,33},{34,66},{66,34},{35,67},{67,35},{3... | collective-permute-start | bytes 786440 | tf_op jit(solution)/shard_map/ppermute | solution.py:57
  47.5 5.7 %collective-permute-start.14 = (bf16[384,512]{1,0:T(8,128)(2,1)S(1)}, bf16[384,512]{1,0:T(8,128)(2,1)S(1)}, u32[]{:S(2)}, u32[]{:S(2)}) collective-permute-start(bf16[384,512]{1,0:T(8,128)(2,1)S(1)} %get-tuple-element.127), channel_id=1, source_target_pairs={{0,1},{1,0},{2,3},{3,2},{4,5},{5,4},{6,7},{7,6},{8,9},{9,8},{10,11... | collective-permute-start | bytes 1179656 | tf_op jit(solution)/shard_map/ppermute | solution.py:42
  50.9 2.4 %collective-permute-start.15 = (bf16[192,512]{1,0:T(8,128)(2,1)S(1)}, bf16[192,512]{1,0:T(8,128)(2,1)S(1)}, u32[]{:S(2)}, u32[]{:S(2)}) collective-permute-start(bf16[192,512]{1,0:T(8,128)(2,1)S(1)} %get-tuple-element.129), channel_id=1, source_target_pairs={{0,1},{1,0},{2,3},{3,2},{4,5},{5,4},{6,7},{7,6},{8,9},{9,8},{10,11... | collective-permute-start | bytes 589832 | tf_op jit(solution)/shard_map/ppermute | solution.py:42
  52.2 5.1 %collective-permute-start.16 = (bf16[192,512]{1,0:T(8,128)(2,1)S(1)}, bf16[192,512]{1,0:T(8,128)(2,1)S(1)}, u32[]{:S(2)}, u32[]{:S(2)}) collective-permute-start(bf16[192,512]{1,0:T(8,128)(2,1)S(1)} %get-tuple-element.130), channel_id=1, source_target_pairs={{0,31},{1,2},{2,1},{3,4},{4,3},{5,6},{6,5},{7,8},{8,7},{9,10},{10,... | collective-permute-start | bytes 589832 | tf_op jit(solution)/shard_map/ppermute | solution.py:47
  57.3 6.6 %copy-start.1 = (bf16[512,227]{0,1:T(8,128)(2,1)S(1)}, bf16[512,227]{0,1:T(8,128)(2,1)}, u32[]{:S(2)}) copy-start(bf16[512,227]{0,1:T(8,128)(2,1)} %param.14) | copy-start | bytes 697348
  60.4 6.9 %collective-permute-start.18 = (bf16[768,512]{1,0:T(8,128)(2,1)S(1)}, bf16[768,512]{1,0:T(8,128)(2,1)S(1)}, u32[]{:S(2)}, u32[]{:S(2)}) collective-permute-start(bf16[768,512]{1,0:T(8,128)(2,1)S(1)} %get-tuple-element.144), channel_id=1, source_target_pairs={{0,1},{1,0},{2,3},{3,2},{4,5},{5,4},{6,7},{7,6},{8,9},{9,8},{10,11... | collective-permute-start | bytes 2359304 | tf_op jit(solution)/shard_map/ppermute | solution.py:42
  63.9 3.4 %collective-permute-start.17 = (bf16[512,512]{1,0:T(8,128)(2,1)S(1)}, bf16[512,512]{1,0:T(8,128)(2,1)S(1)}, u32[]{:S(2)}, u32[]{:S(2)}) collective-permute-start(bf16[512,512]{1,0:T(8,128)(2,1)S(1)} %get-tuple-element.138), channel_id=1, source_target_pairs={{0,1},{1,0},{2,3},{3,2},{4,5},{5,4},{6,7},{7,6},{8,9},{9,8},{10,11... | collective-permute-start | bytes 1572872 | tf_op jit(solution)/shard_map/ppermute | solution.py:42
  65.5 1.7 %collective-permute-start.19 = (bf16[128,512]{1,0:T(8,128)(2,1)S(1)}, bf16[128,512]{1,0:T(8,128)(2,1)S(1)}, u32[]{:S(2)}, u32[]{:S(2)}) collective-permute-start(bf16[128,512]{1,0:T(8,128)(2,1)S(1)} %get-tuple-element.153), channel_id=1, source_target_pairs={{0,1},{1,0},{2,3},{3,2},{4,5},{5,4},{6,7},{7,6},{8,9},{9,8},{10,11... | collective-permute-start | bytes 393224 | tf_op jit(solution)/shard_map/ppermute | solution.py:42
  96.4 6.1 %collective-permute-start.22 = (bf16[112,512]{1,0:T(8,128)(2,1)S(1)}, bf16[112,512]{1,0:T(8,128)(2,1)S(1)}, u32[]{:S(2)}, u32[]{:S(2)}) collective-permute-start(bf16[112,512]{1,0:T(8,128)(2,1)S(1)} %shard_map.216.refs_0_), channel_id=1, source_target_pairs={{0,96},{32,0},{64,32},{96,64},{1,97},{33,1},{65,33},{97,65},{2,98}... | collective-permute-start | bytes 344072 | tf_op jit(solution)/shard_map/ppermute | solution.py:546
  98.2 5.8 %collective-permute-start.21 = (bf16[112,512]{1,0:T(8,128)(2,1)S(1)}, bf16[112,512]{1,0:T(8,128)(2,1)S(1)}, u32[]{:S(2)}, u32[]{:S(2)}) collective-permute-start(bf16[112,512]{1,0:T(8,128)(2,1)S(1)} %shard_map.216.refs_0_), channel_id=1, source_target_pairs={{0,64},{32,96},{64,0},{96,32},{1,65},{33,97},{65,1},{97,33},{2,66}... | collective-permute-start | bytes 344072 | tf_op jit(solution)/shard_map/ppermute | solution.py:546
  101.8 5.8 %collective-permute-start.20 = (bf16[112,512]{1,0:T(8,128)(2,1)S(1)}, bf16[112,512]{1,0:T(8,128)(2,1)S(1)}, u32[]{:S(2)}, u32[]{:S(2)}) collective-permute-start(bf16[112,512]{1,0:T(8,128)(2,1)S(1)} %shard_map.216.refs_0_), channel_id=1, source_target_pairs={{0,32},{32,64},{64,96},{96,0},{1,33},{33,65},{65,97},{97,1},{2,34}... | collective-permute-start | bytes 344072 | tf_op jit(solution)/shard_map/ppermute | solution.py:546
  133.3 7.4 %collective-permute-start.23 = (bf16[1792,512]{1,0:T(8,128)(2,1)S(1)}, bf16[1792,512]{1,0:T(8,128)(2,1)S(1)}, u32[]{:S(2)}, u32[]{:S(2)}) collective-permute-start(bf16[1792,512]{1,0:T(8,128)(2,1)S(1)} %bitcast.14), channel_id=1, source_target_pairs={{0,1},{1,0},{2,3},{3,2},{4,5},{5,4},{6,7},{7,6},{8,9},{9,8},{10,11... | collective-permute-start | bytes 5505032 | tf_op jit(solution)/shard_map/ppermute | solution.py:42
